TPU v7x, 32 devices: a whole 2x2x4 slice. The times are simulated.
32 devices in a mesh: grp: 2 (over x), rep: 16 (over z, y, core).
Axes of the slice: x: 2, y: 2, z: 4, core: 2. Of those that a mesh axis runs over, the one named last changes fastest.
Arguments:
- tokens: bfloat16 [2, 4096, 2048], P(None, ('grp', 'rep')), may hold values from -6 to 6
- attn_gain: bfloat16 [2048], P('grp'), may hold values from 0.5 to 1.5
- w_query: bfloat16 [2048, 2048], P('grp'), may hold values from -0.25 to 0.25
- w_key: bfloat16 [2048, 2048], P('grp'), may hold values from -0.125 to 0.125
- w_value: bfloat16 [2048, 2048], P('grp'), may hold values from -0.125 to 0.125
- w_output: bfloat16 [2048, 2048], P('grp'), may hold values from -0.5 to 0.5
- mlp_gain: bfloat16 [2048], P('grp'), may hold values from 0.5 to 1.5
- w_gate: bfloat16 [2048, 4096], P('grp'), may hold values from -0.125 to 0.125
- w_up: bfloat16 [2048, 4096], P('grp'), may hold values from -0.125 to 0.125
- w_down: bfloat16 [4096, 2048], P('grp'), may hold values from -0.1875 to 0.1875
- out_grad: bfloat16 [2, 4096, 2048], P(None, ('grp', 'rep')), may hold values from -6 to 6
- lengths: int32 [2, 4], replicated, may hold values from 1 to 64, 128 in all within a row
Outputs:
- block_out: bfloat16 [2, 4096, 2048], P(None, ('grp', 'rep'))
- token_grad: bfloat16 [2, 4096, 2048], P(None, ('grp', 'rep'))
- attn_gain_grad: float32 [2048], P(('grp', 'rep'))
- query_grad: float32 [2048, 2048], P(('grp', 'rep'))
- key_grad: float32 [2048, 2048], P(('grp', 'rep'))
- value_grad: float32 [2048, 2048], P(('grp', 'rep'))
- output_grad: float32 [2048, 2048], P(('grp', 'rep'))
- mlp_gain_grad: float32 [2048], P(('grp', 'rep'))
- gate_grad: float32 [2048, 4096], P(('grp', 'rep'))
- up_grad: float32 [2048, 4096], P(('grp', 'rep'))
- down_grad: float32 [4096, 2048], P(('grp', 'rep'))
Inputs may be any that keep to these rules, and one draw needn't show every extreme that they name: `lengths`: each row sums to 128 and its largest entry is 64.
All inputs are finite; a program needn't handle non-finite values.
Results may differ from a plain program's by a relative error of at most 0.018.
Values may be sent and summed in bfloat16 or wider, within the bound.
A program may use at most 448 MiB of HBM per device.

v0:
```python
import math

import jax
import jax.numpy as jnp
from jax import lax
from jax.sharding import PartitionSpec as P

HD = 64
WINDOW = 2048


epsilon = 1e-05
rope_base = 10000.0
masked_score = -1e30


def from_behind(value, axis, steps):
    count = lax.axis_size(axis)
    first, last = (max(0, -steps), min(count, count - steps))
    return lax.ppermute(value, axis, [(source, source + steps) for source in range(first, last)])


def rms_scale(values):
    return lax.rsqrt(jnp.mean(values * values, axis=-1, keepdims=True) + epsilon)


def norm_backward(values, gain_full, grad_normed):
    inverse = rms_scale(values)
    normed = values * inverse
    gain_grad = jnp.sum(grad_normed * normed, axis=0)
    weighted = grad_normed * gain_full
    return (
        inverse * (weighted - normed * jnp.mean(weighted * normed, axis=-1, keepdims=True)),
        gain_grad,
    )


def rotary(values, cosine, sine_table):
    half_width = values.shape[-1] // 2
    first_half = values[..., :half_width]
    second_half = values[..., half_width:]
    return jnp.concatenate(
        [
            first_half * cosine - second_half * sine_table,
            second_half * cosine + first_half * sine_table,
        ],
        axis=-1,
    )


def pick_rows(rows_block, row_ids):
    return jnp.take(rows_block, row_ids, axis=0)


def take_rows(values, row_ids):
    return jax.vmap(pick_rows)(values, row_ids)


def gather_attn(attn_gain, w_query, w_key, w_value, w_output):
    return (
        lax.all_gather(attn_gain, "grp", axis=0, tiled=True),
        lax.all_gather(w_query, "grp", axis=0, tiled=True),
        lax.all_gather(w_key, "grp", axis=0, tiled=True),
        lax.all_gather(w_value, "grp", axis=0, tiled=True),
        lax.all_gather(w_output, "grp", axis=0, tiled=True),
    )


def gather_mlp(mlp_gain, w_gate, w_up, w_down):
    return (
        lax.all_gather(mlp_gain, "grp", axis=0, tiled=True),
        lax.all_gather(w_gate, "grp", axis=0, tiled=True),
        lax.all_gather(w_up, "grp", axis=0, tiled=True),
        lax.all_gather(w_down, "grp", axis=0, tiled=True),
    )


def reduce_attn(gain_grad, query_grad, key_grad, value_grad, output_grad):
    return (
        lax.psum_scatter(gain_grad, ("grp", "rep"), scatter_dimension=0, tiled=True),
        lax.psum_scatter(query_grad, ("grp", "rep"), scatter_dimension=0, tiled=True),
        lax.psum_scatter(key_grad, ("grp", "rep"), scatter_dimension=0, tiled=True),
        lax.psum_scatter(value_grad, ("grp", "rep"), scatter_dimension=0, tiled=True),
        lax.psum_scatter(output_grad, ("grp", "rep"), scatter_dimension=0, tiled=True),
    )


def reduce_mlp(gain_grad, gate_grad, up_grad, down_grad):
    return (
        lax.psum_scatter(gain_grad, ("grp", "rep"), scatter_dimension=0, tiled=True),
        lax.psum_scatter(gate_grad, ("grp", "rep"), scatter_dimension=0, tiled=True),
        lax.psum_scatter(up_grad, ("grp", "rep"), scatter_dimension=0, tiled=True),
        lax.psum_scatter(down_grad, ("grp", "rep"), scatter_dimension=0, tiled=True),
    )


def pass_on(carried, unused):
    arrived = from_behind(carried, ("grp", "rep"), 1)
    return (arrived, arrived)


def pass_back(running, portion):
    arrived = from_behind(running.astype(jnp.bfloat16), ("grp", "rep"), -1).astype(running.dtype)
    return (arrived + portion, None)


def body(
    tokens,
    attn_gain,
    w_query,
    w_key,
    w_value,
    w_output,
    mlp_gain,
    w_gate,
    w_up,
    w_down,
    out_grad,
    lengths,
):
    devices = lax.axis_size(("grp", "rep"))
    rank_here = lax.axis_index(("grp", "rep"))
    micro_count, row_count, model_width = tokens.shape
    per_dev = row_count // devices
    head_count = model_width // HD
    reach_count = (WINDOW + row_count - 2) // row_count
    head_group = math.gcd(head_count, 4)
    group_count = head_count // head_group
    score_scale = 1.0 / math.sqrt(HD)
    unit_ids = jnp.arange(row_count, dtype=jnp.int32)
    seq_ends = jnp.cumsum(lengths, axis=1)
    starts = seq_ends - lengths
    seq_order = jnp.arange(lengths.shape[1], dtype=jnp.int32)
    earlier = seq_order[None, :] < seq_order[:, None]
    dealt_start = jnp.sum(jnp.where(earlier[None], lengths[:, None, :], 0), axis=2)
    seq_of = jnp.sum((seq_ends[:, None, :] <= unit_ids[None, :, None]).astype(jnp.int32), axis=2)
    seq_dealt = jnp.take_along_axis(dealt_start, seq_of, axis=1)
    unit_of = seq_dealt + unit_ids[None, :] - jnp.take_along_axis(starts, seq_of, axis=1)
    micro_ids = jnp.arange(micro_count, dtype=jnp.int32)[:, None]
    source_unit = (
        jnp.zeros((micro_count, row_count), jnp.int32)
        .at[micro_ids, unit_of]
        .set(jnp.broadcast_to(unit_ids[None, :], unit_of.shape))
    )
    unit_begin = (
        jnp.zeros((micro_count, row_count), jnp.int32).at[micro_ids, unit_of].set(seq_dealt)
    )
    local_ids = jnp.arange(row_count, dtype=jnp.int32)
    local_step = local_ids % per_dev
    local_source = local_ids // per_dev
    distance = jnp.arange(reach_count + 1, dtype=jnp.int32)
    owner_dev = rank_here - distance
    owner_ok = owner_dev >= 0
    owner_unit = jnp.maximum(owner_dev, 0)[:, None] * per_dev + local_step[None, :]
    key_begin = unit_begin[:, owner_unit]
    key_pos = (owner_unit[None] - key_begin) * devices + local_source[None, None, :]
    query_begin = key_begin[:, 0]
    query_pos = key_pos[:, 0]
    allowed = (
        owner_ok[None, None, :, None]
        & (query_begin[:, :, None, None] == key_begin[:, None, :, :])
        & (key_pos[:, None, :, :] <= query_pos[:, :, None, None])
        & (query_pos[:, :, None, None] - key_pos[:, None, :, :] < WINDOW)
    )
    mask_full = allowed[:, None]
    half_width = HD // 2
    frequency = jnp.power(rope_base, -2.0 * jnp.arange(half_width, dtype=jnp.float32) / HD)
    angles = query_pos.astype(jnp.float32)[:, :, None] * frequency[None, None, :]
    cosine = jnp.cos(angles)[:, :, None, :]
    sine_table = jnp.sin(angles)[:, :, None, :]
    head_shape = (micro_count, row_count, head_count, HD)
    block_shape = (micro_count, row_count, model_width)
    gathered = gather_attn(attn_gain, w_query, w_key, w_value, w_output)
    gain_one = gathered[0].astype(jnp.float32)
    inputs = tokens.astype(jnp.float32).reshape(micro_count * row_count, model_width)
    normed_in = (inputs * rms_scale(inputs) * gain_one).astype(jnp.bfloat16)
    queries = jnp.dot(normed_in, gathered[1], preferred_element_type=jnp.float32).astype(
        jnp.bfloat16
    )
    keys_in = jnp.dot(normed_in, gathered[2], preferred_element_type=jnp.float32).astype(
        jnp.bfloat16
    )
    values_in = jnp.dot(normed_in, gathered[3], preferred_element_type=jnp.float32).astype(
        jnp.bfloat16
    )
    dealt = (
        lax.all_to_all(
            take_rows(queries.reshape(block_shape), source_unit),
            ("grp", "rep"),
            split_axis=1,
            concat_axis=1,
            tiled=True,
        ),
        lax.all_to_all(
            take_rows(keys_in.reshape(block_shape), source_unit),
            ("grp", "rep"),
            split_axis=1,
            concat_axis=1,
            tiled=True,
        ),
        lax.all_to_all(
            take_rows(values_in.reshape(block_shape), source_unit),
            ("grp", "rep"),
            split_axis=1,
            concat_axis=1,
            tiled=True,
        ),
    )
    rot_q = rotary(dealt[0].reshape(head_shape).astype(jnp.float32), cosine, sine_table).astype(
        jnp.bfloat16
    )
    rot_k = rotary(dealt[1].reshape(head_shape).astype(jnp.float32), cosine, sine_table).astype(
        jnp.bfloat16
    )
    own_pair = jnp.stack([rot_k.reshape(block_shape), dealt[2]], axis=0)
    last_pair, farther = lax.scan(pass_on, own_pair, None, length=reach_count)
    context = jnp.concatenate([own_pair[None], farther], axis=0).reshape(
        reach_count + 1, 2, micro_count, row_count, head_count, HD
    )

    def group_scores(query_part, pair_part):
        scores = (
            jnp.einsum(
                "mqge,dmkge->mgqdk", query_part, pair_part[:, 0], preferred_element_type=jnp.float32
            )
            * score_scale
        )
        return jnp.where(mask_full, scores, masked_score)

    def forward_group(group_index, carried):
        attended_all, log_all = carried
        head_start = group_index * head_group
        query_part = lax.dynamic_slice_in_dim(rot_q, head_start, head_group, axis=2)
        pair_part = lax.dynamic_slice_in_dim(context, head_start, head_group, axis=4)
        scores = group_scores(query_part, pair_part)
        row_max = jnp.max(scores, axis=(3, 4), keepdims=True)
        weights_exp = jnp.exp(scores - row_max)
        row_sum = jnp.sum(weights_exp, axis=(3, 4), keepdims=True)
        soft_probs = (weights_exp / row_sum).astype(jnp.bfloat16)
        attended = jnp.einsum(
            "mgqdk,dmkge->mqge", soft_probs, pair_part[:, 1], preferred_element_type=jnp.float32
        ).astype(jnp.bfloat16)
        attended_all = lax.dynamic_update_slice_in_dim(attended_all, attended, head_start, axis=2)
        log_all = lax.dynamic_update_slice_in_dim(
            log_all, row_max + jnp.log(row_sum), head_start, axis=1
        )
        return (attended_all, log_all)

    attended_heads, log_sum = lax.fori_loop(
        0,
        group_count,
        forward_group,
        (
            jnp.zeros(head_shape, jnp.bfloat16),
            jnp.zeros((micro_count, head_count, row_count, 1, 1), jnp.float32),
        ),
    )
    returned = lax.all_to_all(
        attended_heads.reshape(block_shape), ("grp", "rep"), split_axis=1, concat_axis=1, tiled=True
    )
    attn_rows = take_rows(returned, unit_of).reshape(micro_count * row_count, model_width)
    mixed = inputs + jnp.dot(attn_rows, gathered[4], preferred_element_type=jnp.float32)
    mlp_set = gather_mlp(mlp_gain, w_gate, w_up, w_down)
    gain_two = mlp_set[0].astype(jnp.float32)
    normed_mid = (mixed * rms_scale(mixed) * gain_two).astype(jnp.bfloat16)
    gate_pre = jnp.dot(normed_mid, mlp_set[1], preferred_element_type=jnp.float32)
    up_pre = jnp.dot(normed_mid, mlp_set[2], preferred_element_type=jnp.float32)
    gate_sig = jax.nn.sigmoid(gate_pre)
    gate_silu = gate_pre * gate_sig
    hidden = (gate_silu * up_pre).astype(jnp.bfloat16)
    block_out = (mixed + jnp.dot(hidden, mlp_set[3], preferred_element_type=jnp.float32)).astype(
        jnp.bfloat16
    )
    mlp_set = gather_mlp(mlp_gain, w_gate, w_up, w_down)
    out_rows = out_grad.reshape(micro_count * row_count, model_width)
    down_grad = jnp.einsum("tf,td->fd", hidden, out_rows, preferred_element_type=jnp.float32)
    grad_hidden = jnp.einsum("td,fd->tf", out_rows, mlp_set[3], preferred_element_type=jnp.float32)
    grad_gate = (grad_hidden * up_pre * gate_sig * (1.0 + gate_pre * (1.0 - gate_sig))).astype(
        jnp.bfloat16
    )
    grad_up = (grad_hidden * gate_silu).astype(jnp.bfloat16)
    gate_grad = jnp.einsum("td,tf->df", normed_mid, grad_gate, preferred_element_type=jnp.float32)
    up_grad = jnp.einsum("td,tf->df", normed_mid, grad_up, preferred_element_type=jnp.float32)
    grad_mid = jnp.einsum(
        "tf,df->td", grad_gate, mlp_set[1], preferred_element_type=jnp.float32
    ) + jnp.einsum("tf,df->td", grad_up, mlp_set[2], preferred_element_type=jnp.float32)
    grad_norm_mid, mlp_gain_grad = norm_backward(mixed, gain_two, grad_mid)
    grad_mixed = out_rows.astype(jnp.float32) + grad_norm_mid
    mlp_sums = reduce_mlp(mlp_gain_grad, gate_grad, up_grad, down_grad)
    gathered = gather_attn(attn_gain, w_query, w_key, w_value, w_output)
    grad_branch = grad_mixed.astype(jnp.bfloat16)
    output_grad = jnp.einsum(
        "td,te->de", attn_rows, grad_branch, preferred_element_type=jnp.float32
    )
    grad_att = jnp.einsum(
        "te,de->td", grad_branch, gathered[4], preferred_element_type=jnp.float32
    ).astype(jnp.bfloat16)
    grad_dealt = lax.all_to_all(
        take_rows(grad_att.reshape(block_shape), source_unit),
        ("grp", "rep"),
        split_axis=1,
        concat_axis=1,
        tiled=True,
    )
    grad_heads = grad_dealt.reshape(head_shape)

    def backward_group(group_index, carried):
        query_total, pair_total = carried
        head_start = group_index * head_group
        query_part = lax.dynamic_slice_in_dim(rot_q, head_start, head_group, axis=2)
        grad_part = lax.dynamic_slice_in_dim(grad_heads, head_start, head_group, axis=2)
        pair_part = lax.dynamic_slice_in_dim(context, head_start, head_group, axis=4)
        log_part = lax.dynamic_slice_in_dim(log_sum, head_start, head_group, axis=1)
        scores = group_scores(query_part, pair_part)
        soft_probs = jnp.exp(scores - log_part)
        grad_probs = jnp.einsum(
            "mqge,dmkge->mgqdk", grad_part, pair_part[:, 1], preferred_element_type=jnp.float32
        )
        inner_sum = jnp.sum(soft_probs * grad_probs, axis=(3, 4), keepdims=True)
        grad_scores = (soft_probs * (grad_probs - inner_sum)).astype(jnp.bfloat16)
        query_piece = (
            jnp.einsum(
                "mgqdk,dmkge->mqge",
                grad_scores,
                pair_part[:, 0],
                preferred_element_type=jnp.float32,
            )
            * score_scale
        )
        key_part = (
            jnp.einsum(
                "mgqdk,mqge->dmkge", grad_scores, query_part, preferred_element_type=jnp.float32
            )
            * score_scale
        )
        value_part = jnp.einsum(
            "mgqdk,mqge->dmkge",
            soft_probs.astype(jnp.bfloat16),
            grad_part,
            preferred_element_type=jnp.float32,
        )
        query_total = lax.dynamic_update_slice_in_dim(query_total, query_piece, head_start, axis=2)
        pair_total = lax.dynamic_update_slice_in_dim(
            pair_total, jnp.stack([key_part, value_part], axis=1), head_start, axis=4
        )
        return (query_total, pair_total)

    query_total, pair_total = lax.fori_loop(
        0,
        group_count,
        backward_group,
        (
            jnp.zeros(head_shape, jnp.float32),
            jnp.zeros((reach_count + 1, 2) + head_shape, jnp.float32),
        ),
    )
    partials = pair_total.reshape(reach_count + 1, 2, micro_count, row_count, model_width)
    own_total, unused_out = lax.scan(
        pass_back, partials[reach_count], partials[:reach_count], reverse=True
    )
    query_back = rotary(query_total, cosine, -sine_table).astype(jnp.bfloat16)
    key_back = rotary(own_total[0].reshape(head_shape), cosine, -sine_table).astype(jnp.bfloat16)
    value_back = own_total[1].astype(jnp.bfloat16)
    grad_back = (
        lax.all_to_all(
            query_back.reshape(block_shape), ("grp", "rep"), split_axis=1, concat_axis=1, tiled=True
        ),
        lax.all_to_all(
            key_back.reshape(block_shape), ("grp", "rep"), split_axis=1, concat_axis=1, tiled=True
        ),
        lax.all_to_all(value_back, ("grp", "rep"), split_axis=1, concat_axis=1, tiled=True),
    )
    query_rows = take_rows(grad_back[0], unit_of).reshape(micro_count * row_count, model_width)
    key_rows = take_rows(grad_back[1], unit_of).reshape(micro_count * row_count, model_width)
    value_rows = take_rows(grad_back[2], unit_of).reshape(micro_count * row_count, model_width)
    query_grad = jnp.einsum("td,te->de", normed_in, query_rows, preferred_element_type=jnp.float32)
    key_grad = jnp.einsum("td,te->de", normed_in, key_rows, preferred_element_type=jnp.float32)
    value_grad = jnp.einsum("td,te->de", normed_in, value_rows, preferred_element_type=jnp.float32)
    grad_in = jnp.einsum("te,de->td", query_rows, gathered[1], preferred_element_type=jnp.float32)
    grad_in = grad_in + jnp.einsum(
        "te,de->td", key_rows, gathered[2], preferred_element_type=jnp.float32
    )
    grad_in = grad_in + jnp.einsum(
        "te,de->td", value_rows, gathered[3], preferred_element_type=jnp.float32
    )
    grad_norm_in, attn_gain_grad = norm_backward(inputs, gain_one, grad_in)
    token_grad = (grad_mixed + grad_norm_in).astype(jnp.bfloat16)
    attn_sums = reduce_attn(attn_gain_grad, query_grad, key_grad, value_grad, output_grad)
    return (
        block_out.reshape(block_shape),
        token_grad.reshape(block_shape),
        attn_sums[0],
        attn_sums[1],
        attn_sums[2],
        attn_sums[3],
        attn_sums[4],
        mlp_sums[0],
        mlp_sums[1],
        mlp_sums[2],
        mlp_sums[3],
    )


def solution(mesh):
    in_specs = (
        P(None, ("grp", "rep"), None),
        P("grp"),
        P("grp", None),
        P("grp", None),
        P("grp", None),
        P("grp", None),
        P("grp"),
        P("grp", None),
        P("grp", None),
        P("grp", None),
        P(None, ("grp", "rep"), None),
        P(),
    )
    out_specs = (
        P(None, ("grp", "rep"), None),
        P(None, ("grp", "rep"), None),
        P(("grp", "rep")),
        P(("grp", "rep"), None),
        P(("grp", "rep"), None),
        P(("grp", "rep"), None),
        P(("grp", "rep"), None),
        P(("grp", "rep")),
        P(("grp", "rep"), None),
        P(("grp", "rep"), None),
        P(("grp", "rep"), None),
    )
    return jax.shard_map(body, mesh=mesh, in_specs=in_specs, out_specs=out_specs, check_vma=False)
```

profile of v0, /device:TPU:0, one launch (start us, length us, event | category | flops | bytes accessed | tf_op | source)
XLA Modules:
  0.0 4213.4 jit_solution(2860450741598323863)
XLA Ops:
  35.8 80.5 %all-gather.12.cloned.1.call-done = bf16[2048,2048]{1,0:T(8,128)(2,1)} async-done(((bf16[1024,2048]{1,0:T(8,128)(2,1)}), bf16[2048,2048]{1,0:T(8,128)(2,1)}) %all-gather.12.cloned.1.call-update) | async-done | bytes 8388624 | tf_op jit(solution)/shard_map/all_gather | solution.py:62
  126.4 95.5 %all-gather.8.cloned.1.call-done = bf16[2048,2048]{1,0:T(8,128)(2,1)} async-done(((bf16[1024,2048]{1,0:T(8,128)(2,1)}), bf16[2048,2048]{1,0:T(8,128)(2,1)}) %all-gather.8.cloned.1.call-update) | async-done | bytes 8388624 | tf_op jit(solution)/shard_map/all_gather | solution.py:63
  232.2 95.3 %all-gather.10.cloned.1.call-done = bf16[2048,2048]{1,0:T(8,128)(2,1)} async-done(((bf16[1024,2048]{1,0:T(8,128)(2,1)}), bf16[2048,2048]{1,0:T(8,128)(2,1)}) %all-gather.10.cloned.1.call-update) | async-done | bytes 8388624 | tf_op jit(solution)/shard_map/all_gather | solution.py:64
  345.5 31.8 all_to_all.40
  444.9 530.4 %while.58 = (s32[]{:T(128)}, bf16[2,2,128,2048]{3,2,1,0:T(8,128)(2,1)}, bf16[16,2,2,128,2048]{3,4,2,1,0:T(8,128)(2,1)}, s32[]{:T(128)}) while((s32[]{:T(128)}, bf16[2,2,128,2048]{3,2,1,0:T(8,128)(2,1)}, bf16[16,2,2,128,2048]{3,4,2,1,0:T(8,128)(2,1)}, s32[]{:T(128)}) %tuple.160), condition=%wide.region_7.10_spmd, body=%wide.region_6.9_spmd.sunk | while | flops 2 | bytes 20971624 | solution.py:216
  457.3 23.4 collective-permute-start
  491.5 23.9 collective-permute-start
  526.2 23.7 collective-permute-start
  560.7 23.7 collective-permute-start
  595.3 23.7 collective-permute-start
  629.8 23.7 collective-permute-start
  664.3 23.7 collective-permute-start
  698.8 23.7 collective-permute-start
  733.4 23.7 collective-permute-start
  767.9 23.7 collective-permute-start
  802.4 23.7 collective-permute-start
  837.0 23.7 collective-permute-start
  871.5 23.7 collective-permute-start
  906.0 23.7 collective-permute-start
  940.6 23.8 collective-permute-start
  975.2 24.1 pad_maximum_fusion
  999.3 24.2 copy.257
  1023.7 94.3 %while.60 = (s32[]{:T(128)}, bf16[2,128,32,64]{1,3,2,0:T(8,128)(2,1)S(1)}, f32[2,32,128,1,1]{2,1,0,4,3:T(8,128)S(1)}, bf16[17,2,2,128,32,64]{3,5,0,4,2,1:T(8,128...) while((s32[]{:T(128)}, ...), condition=%wide.region_11.14_spmd.clone, body=%wide.region_8.13_spmd.clone.sunk | while | flops 601127936 | bytes 33757916 | solution.py:249
  1120.2 82.9 %all-to-all-start.3 = ((bf16[2,128,2048]{2,0,1:T(2,128)(2,1)}), bf16[2,128,2048]{2,0,1:T(2,128)(2,1)}, u32[]{:S(2)}, u32[]{:S(2)}) async-start(bf16[2,128,2048]{2,0,1:T(2,128)(2,1)} %copy.258), calls=%async_computation.3 | async-start | bytes 2097152 | tf_op jit(solution)/shard_map/all_to_all | solution.py:258
  1210.2 20.2 all-to-all-done.3
  1265.2 134.5 %all-gather.20.cloned.1.call-done = bf16[4096,2048]{1,0:T(8,128)(2,1)} async-done(((bf16[2048,2048]{1,0:T(8,128)(2,1)}), bf16[4096,2048]{1,0:T(8,128)(2,1)}) %all-gather.20.cloned.1.call-update) | async-done | bytes 16777232 | tf_op jit(solution)/shard_map/all_gather | solution.py:74
  1470.7 24.8 all-to-all-done.4
  1500.0 23.0 broadcast_in_dim.170
  1522.9 202.2 %while.61 = (s32[]{:T(128)}, f32[2,128,32,64]{1,3,2,0:T(8,128)}, f32[17,2,2,128,32,64]{3,5,0,4,2,1:T(8,128)}, bf16[17,2,2,128,32,64]{3,5,0,4,2,1:T(8,128)(2,1)},...) while((s32[]{:T(128)}, f32[2,128,32,64]{1,3,2,0:T(8,128)}, ...), condition=%wide.region_16.19_spmd.clone, body=%wide.region_14.18_spmd.clone.sunk | while | flops 1466792960 | bytes 103354096 | solution.py:348
  1730.0 46.3 %copy.266 = f32[17,2,2,128,32,64]{3,5,4,2,1,0:T(8,128)} copy(f32[17,2,2,128,32,64]{3,5,0,4,2,1:T(8,128)} %get-tuple-element.349) | data formatting | bytes 142606336 | tf_op jit(solution)/shard_map/while | solution.py:348
  1776.3 43.7 %slice.127 = f32[16,2,2,128,32,64]{3,5,4,2,1,0:T(8,128)} slice(f32[17,2,2,128,32,64]{3,5,4,2,1,0:T(8,128)} %copy.266), slice={[0:16], [0:2], [0:2], [0:128], [0:32], [0:64]} | slice | bytes 134217728 | tf_op jit(solution)/shard_map/slice | solution.py:359
  1825.5 552.7 %while.59 = (s32[]{:T(128)}, f32[2,2,128,2048]{3,2,1,0:T(8,128)}, f32[16,2,2,128,2048]{3,4,2,1,0:T(8,128)}, s32[]{:T(128)}, s32[]{:T(128)}) while((s32[]{:T(128)}, f32[2,2,128,2048]{3,2,1,0:T(8,128)}, f32[16,2,2,128,2048]{3,4,2,1,0:T(8,128)}, s32[]{:T(128)}, s32[]{:T(128)}) %tuple.169), condition=%wide.region_18.21_spmd, body=%wide.region_17.20_spmd.sunk | while | flops 3145731 | bytes 41943156 | solution.py:358
  1892.6 16.4 collective-permute-done.1
  1928.3 16.4 collective-permute-done.1
  1963.9 16.4 collective-permute-done.1
  1999.6 16.4 collective-permute-done.1
  2035.2 16.4 collective-permute-done.1
  2070.9 16.4 collective-permute-done.1
  2388.4 75.8 %all-to-all-start.6 = ((bf16[2,128,2048]{2,0,1:T(2,128)(2,1)}), bf16[2,128,2048]{2,0,1:T(2,128)(2,1)S(1)}, u32[]{:S(2)}, u32[]{:S(2)}) async-start(bf16[2,128,2048]{2,0,1:T(2,128)(2,1)} %copy.270), calls=%async_computation.6 | async-start | bytes 2097152 | tf_op jit(solution)/shard_map/all_to_all | solution.py:368
  2471.4 20.1 all-to-all-done.6
  2497.4 23.8 all-to-all-done.7
  2665.7 41.6 all-reduce.2
  2711.7 41.0 reduce-scatter.12.cloned.1.call-done
  2752.7 188.0 %reduce-scatter.8.cloned.1.call-done = f32[64,2048]{1,0:T(8,128)} async-done(((f32[2048,2048]{1,0:T(8,128)}), f32[64,2048]{1,0:T(8,128)}) %reduce-scatter.8.cloned.1.call-update) | async-done | bytes 524304 | tf_op jit(solution)/shard_map/reduce_scatter | solution.py:81
  2940.7 187.5 %reduce-scatter.10.cloned.1.call-done = f32[64,2048]{1,0:T(8,128)} async-done(((f32[2048,2048]{1,0:T(8,128)}), f32[64,2048]{1,0:T(8,128)}) %reduce-scatter.10.cloned.1.call-update) | async-done | bytes 524304 | tf_op jit(solution)/shard_map/reduce_scatter | solution.py:82
  3128.2 357.6 %reduce-scatter.18.cloned.1.call-done = f32[64,4096]{1,0:T(8,128)} async-done(((f32[2048,4096]{1,0:T(8,128)}), f32[64,4096]{1,0:T(8,128)}) %reduce-scatter.18.cloned.1.call-update) | async-done | bytes 1048592 | tf_op jit(solution)/shard_map/reduce_scatter | solution.py:92
  3485.9 360.5 %reduce-scatter.16.cloned.1.call-done = f32[64,4096]{1,0:T(8,128)} async-done(((f32[2048,4096]{1,0:T(8,128)}), f32[64,4096]{1,0:T(8,128)}) %reduce-scatter.16.cloned.1.call-update) | async-done | bytes 1048592 | tf_op jit(solution)/shard_map/reduce_scatter | solution.py:91
  3846.3 360.3 %reduce-scatter.20.cloned.1.call-done = f32[128,2048]{1,0:T(8,128)} async-done(((f32[4096,2048]{1,0:T(8,128)}), f32[128,2048]{1,0:T(8,128)}) %reduce-scatter.20.cloned.1.call-update) | async-done | bytes 1048592 | tf_op jit(solution)/shard_map/reduce_scatter | solution.py:93
  (515 shorter events, 1360.0 us)
Async XLA Ops:
  7.2 109.1 %all-gather.12.cloned.1.call-start = ((), (), s32[]{:S(2)}) async-start(), calls=%async_computation.17 | async-start | bytes 12582912 | tf_op jit(solution)/shard_map/all_gather | solution.py:62
  7.9 214.0 %all-gather.8.cloned.1.call-start = ((), (), s32[]{:S(2)}) async-start(), calls=%async_computation.15 | async-start | bytes 12582912 | tf_op jit(solution)/shard_map/all_gather | solution.py:63
  8.7 318.8 %all-gather.10.cloned.1.call-start = ((), (), s32[]{:S(2)}) async-start(), calls=%async_computation.16 | async-start | bytes 12582912 | tf_op jit(solution)/shard_map/all_gather | solution.py:64
  9.4 1227.1 %all-gather.14.cloned.1.call-start = ((), (), s32[]{:S(2)}) async-start(), calls=%async_computation.18 | async-start | bytes 12582912 | tf_op jit(solution)/shard_map/all_gather | solution.py:65
  10.0 1234.4 %all-gather.18.cloned.1.call-start = ((), (), s32[]{:S(2)}) async-start(), calls=%async_computation.20 | async-start | bytes 25165824 | tf_op jit(solution)/shard_map/all_gather | solution.py:73
  10.6 1244.3 %all-gather.16.cloned.1.call-start = ((), (), s32[]{:S(2)}) async-start(), calls=%async_computation.19 | async-start | bytes 25165824 | tf_op jit(solution)/shard_map/all_gather | solution.py:72
  377.3 29.9 all-to-all-start
  380.0 1019.7 %all-gather.20.cloned.1.call-start = ((), (), s32[]{:S(2)}) async-start(), calls=%async_computation.21 | async-start | bytes 25165824 | tf_op jit(solution)/shard_map/all_gather | solution.py:74
  407.2 30.3 all-to-all-start.1
  491.5 27.8 collective-permute-start
  526.2 27.6 collective-permute-start
  560.7 27.6 collective-permute-start
  595.3 27.6 collective-permute-start
  629.8 27.6 collective-permute-start
  664.3 27.6 collective-permute-start
  698.8 27.6 collective-permute-start
  733.4 27.6 collective-permute-start
  767.9 27.6 collective-permute-start
  802.4 27.6 collective-permute-start
  837.0 27.6 collective-permute-start
  871.5 27.6 collective-permute-start
  906.0 27.6 collective-permute-start
  940.6 27.7 collective-permute-start
  1120.2 110.2 %all-to-all-start.3 = ((bf16[2,128,2048]{2,0,1:T(2,128)(2,1)}), bf16[2,128,2048]{2,0,1:T(2,128)(2,1)}, u32[]{:S(2)}, u32[]{:S(2)}) async-start(bf16[2,128,2048]{2,0,1:T(2,128)(2,1)} %copy.258), calls=%async_computation.3 | async-start | bytes 2097152 | tf_op jit(solution)/shard_map/all_to_all | solution.py:258
  1458.3 37.3 all-to-all-start.4
  1462.4 1249.3 %reduce-scatter.14.cloned.1.call-start = ((), (), s32[]{:S(2)}) async-start(), calls=%async_computation.25 | async-start | bytes 17301504 | tf_op jit(solution)/shard_map/reduce_scatter | solution.py:84
  1881.5 27.5 collective-permute-start.1
  1917.2 27.5 collective-permute-start.1
  1952.8 27.5 collective-permute-start.1
  1988.5 27.5 collective-permute-start.1
  2024.1 27.5 collective-permute-start.1
  2059.8 27.5 collective-permute-start.1
  2095.4 27.5 collective-permute-start.1
  2131.1 27.5 collective-permute-start.1
  2202.4 27.5 collective-permute-start.1
  2238.0 27.5 collective-permute-start.1
  2273.7 27.5 collective-permute-start.1
  2309.3 27.5 collective-permute-start.1
  2345.0 27.5 collective-permute-start.1
  2388.4 103.0 %all-to-all-start.6 = ((bf16[2,128,2048]{2,0,1:T(2,128)(2,1)}), bf16[2,128,2048]{2,0,1:T(2,128)(2,1)S(1)}, u32[]{:S(2)}, u32[]{:S(2)}) async-start(bf16[2,128,2048]{2,0,1:T(2,128)(2,1)} %copy.270), calls=%async_computation.6 | async-start | bytes 2097152 | tf_op jit(solution)/shard_map/all_to_all | solution.py:368
  2491.4 29.8 all-to-all-start.7
  2521.3 30.6 all-to-all-start.5
  2524.7 228.0 %reduce-scatter.12.cloned.1.call-start = ((), (), s32[]{:S(2)}) async-start(), calls=%async_computation.24 | async-start | bytes 17301504 | tf_op jit(solution)/shard_map/reduce_scatter | solution.py:83
  2570.8 370.0 %reduce-scatter.8.cloned.1.call-start = ((), (), s32[]{:S(2)}) async-start(), calls=%async_computation.22 | async-start | bytes 17301504 | tf_op jit(solution)/shard_map/reduce_scatter | solution.py:81
  2579.2 549.1 %reduce-scatter.10.cloned.1.call-start = ((), (), s32[]{:S(2)}) async-start(), calls=%async_computation.23 | async-start | bytes 17301504 | tf_op jit(solution)/shard_map/reduce_scatter | solution.py:82
  2587.6 898.2 %reduce-scatter.18.cloned.1.call-start = ((), (), s32[]{:S(2)}) async-start(), calls=%async_computation.27 | async-start | bytes 34603008 | tf_op jit(solution)/shard_map/reduce_scatter | solution.py:92
  2603.9 1242.4 %reduce-scatter.16.cloned.1.call-start = ((), (), s32[]{:S(2)}) async-start(), calls=%async_computation.26 | async-start | bytes 34603008 | tf_op jit(solution)/shard_map/reduce_scatter | solution.py:91
  2619.1 1587.6 %reduce-scatter.20.cloned.1.call-start = ((), (), s32[]{:S(2)}) async-start(), calls=%async_computation.28 | async-start | bytes 34603008 | tf_op jit(solution)/shard_map/reduce_scatter | solution.py:93
  (51 other events, 1841.1 us)
Sparse Core Ops, SparseCore 0:
  9.6 106.6 all-gather.11
  117.8 104.0 all-gather.7
  223.4 104.0 all-gather.9
  328.9 137.7 all-gather.13
  468.0 218.5 all-gather.17
  688.0 450.3 all-gather.15
  1140.0 259.6 all-gather.19
  1470.8 185.6 reduce-scatter.13
  2570.9 181.7 reduce-scatter.11
  2755.4 185.2 reduce-scatter.7
  2943.6 184.5 reduce-scatter.9
  3130.9 354.8 reduce-scatter.17
  3488.7 357.5 reduce-scatter.15
  3849.1 357.5 reduce-scatter.19
where the time goes:
time: 4230 us; the launch traced here: 4210 us
  waiting for transfers between devices  2330 us (55%)
  starting transfers between devices  553 us (13%)
  local copies, waits for them, and re-layouts  539 us (13%)
  matrix products  400 us (9%)
  other arithmetic  287 us (7%)
  blocking collectives  85.7 us (2%)
    ppermute x32, starting transfers between devices, from_behind(): lax.ppermute(value, axis, [(source, source + steps) for source in range(f...  378 us
    reduce_scatter x1, waiting for transfers between devices, reduce_mlp(): lax.psum_scatter(gate_grad, ('grp', 'rep'), scatter_dimension=0, tiled=True)  360 us
    reduce_scatter x1, waiting for transfers between devices, reduce_mlp(): lax.psum_scatter(down_grad, ('grp', 'rep'), scatter_dimension=0, tiled=True)  360 us
    reduce_scatter x1, waiting for transfers between devices, reduce_mlp(): lax.psum_scatter(up_grad, ('grp', 'rep'), scatter_dimension=0, tiled=True)  358 us
    ppermute x32, waiting for transfers between devices, from_behind(): lax.ppermute(value, axis, [(source, source + steps) for source in range(f...  305 us
    reduce_scatter x1, waiting for transfers between devices, reduce_attn(): lax.psum_scatter(query_grad, ('grp', 'rep'), scatter_dimension=0, tiled=T...  188 us
    reduce_scatter x1, waiting for transfers between devices, reduce_attn(): lax.psum_scatter(key_grad, ('grp', 'rep'), scatter_dimension=0, tiled=True)  187 us
    dynamic_slice x32, local copies, waits for them, and re-layouts, body(): lax.scan(pass_back, partials[reach_count], partials[:reach_count], revers...  157 us
  transfers between devices with their start and end apart: 53, of which 48 were waited for; matrix products, arithmetic and copies ran while one was open for 28% of the time, Pallas kernels for 0%

commit v1 on v0

--- a/solution.py
+++ b/solution.py
@@ -1,8 +1,11 @@
+import functools
 import math
 
 import jax
 import jax.numpy as jnp
 from jax import lax
+from jax.experimental import pallas as pl
+from jax.experimental.pallas import tpu as pltpu
 from jax.sharding import PartitionSpec as P
 
 HD = 64
@@ -12,6 +15,11 @@
 epsilon = 1e-05
 rope_base = 10000.0
 masked_score = -1e30
+BOTH = ("grp", "rep")
+LANES = 128
+UNIT_BLOCK = 8
+UNIT_PAIR = 16
+KERNEL_VMEM = 56 * 1024 * 1024
 
 
 def from_behind(value, axis, steps):
@@ -104,7 +112,7 @@
     return (arrived + portion, None)
 
 
-def body(
+def ring_body(
     tokens,
     attn_gain,
     w_query,
@@ -401,6 +409,722 @@
     )
 
 
+def contract(left_side, right_side, left_dim, right_dim, kind=jnp.float32):
+    return lax.dot_general(
+        left_side,
+        right_side,
+        (((left_dim,), (right_dim,)), ((), ())),
+        preferred_element_type=jnp.float32,
+    ).astype(kind)
+
+
+def swap_halves(values):
+    lane = lax.broadcasted_iota(jnp.int32, values.shape, 1)
+    ahead = pltpu.roll(values, LANES - HD // 2, 1)
+    behind = pltpu.roll(values, HD // 2, 1)
+    return jnp.where(lane % HD < HD // 2, -ahead, behind)
+
+
+def pair_angles(unit_at, cos_unit, sin_unit, cos_part, sin_part):
+    unit_cos = cos_unit[pl.ds(unit_at, UNIT_PAIR), :][None]
+    unit_sin = sin_unit[pl.ds(unit_at, UNIT_PAIR), :][None]
+    part_cos = cos_part[...][:, None, :]
+    part_sin = sin_part[...][:, None, :]
+    cosine = unit_cos * part_cos - unit_sin * part_sin
+    sine = unit_sin * part_cos + unit_cos * part_sin
+    return cosine, sine
+
+
+def key_offsets(block):
+    row = lax.broadcasted_iota(jnp.int32, (block, block), 0)
+    return (row % UNIT_BLOCK) * (block // UNIT_BLOCK) + row // UNIT_BLOCK
+
+
+def query_offsets(block):
+    column = lax.broadcasted_iota(jnp.int32, (block, block), 1)
+    return (column % UNIT_BLOCK) * (block // UNIT_BLOCK) + column // UNIT_BLOCK
+
+
+def attend_kernel(
+    slot_ref,
+    first_ref,
+    plain_ref,
+    cos_unit,
+    sin_unit,
+    cos_part,
+    sin_part,
+    low_ref,
+    qkv_ref,
+    att_ref,
+    out_ref,
+    log_ref,
+    query_ref,
+    key_ref,
+    value_ref,
+    query_t,
+    value_t,
+    key_at,
+    causal_at,
+):
+    parts, units, _ = qkv_ref.shape
+    block = parts * UNIT_BLOCK
+    pairs = units // UNIT_PAIR
+    key_at[...] = key_offsets(block)
+    causal_at[...] = jnp.where(key_offsets(block) <= query_offsets(block), 0.0, masked_score)
+    extra = value_t.shape[2] - HD
+
+    def lay_out(pair, unused):
+        unit_at = pl.multiple_of(pair * UNIT_PAIR, UNIT_PAIR)
+        rows = jnp.stack(
+            [qkv_ref[slot_ref[part], pl.ds(unit_at, UNIT_PAIR), :] for part in range(parts)]
+        )
+        cosine, sine = pair_angles(unit_at, cos_unit, sin_unit, cos_part, sin_part)
+        flat = (parts * UNIT_PAIR, LANES)
+        cosine = cosine.reshape(flat)
+        sine = sine.reshape(flat)
+
+        def rotated(values):
+            values = values.astype(jnp.float32).reshape(flat)
+            turned = values * cosine + swap_halves(values) * sine
+            return turned.reshape(parts, UNIT_PAIR, LANES)
+
+        query = rotated(rows[:, :, :LANES]) * (1.0 / math.sqrt(HD))
+        key = rotated(rows[:, :, LANES : 2 * LANES])
+        value = rows[:, :, 2 * LANES :].astype(jnp.float32)
+        for half in range(UNIT_PAIR // UNIT_BLOCK):
+            at = pair * (UNIT_PAIR // UNIT_BLOCK) + half
+            cut = slice(half * UNIT_BLOCK, (half + 1) * UNIT_BLOCK)
+            query_rows = query[:, cut].reshape(block, LANES)
+            value_rows = value[:, cut].reshape(block, LANES)
+            query_ref[at] = query_rows.astype(jnp.bfloat16)
+            key_ref[at] = key[:, cut].reshape(block, LANES).astype(jnp.bfloat16)
+            value_ref[at] = value_rows.astype(jnp.bfloat16)
+            turned = jnp.transpose(query_rows)
+            row = lax.broadcasted_iota(jnp.int32, turned.shape, 0)
+            query_t[0, at] = jnp.where(row < HD, turned, 0.0).astype(jnp.bfloat16)
+            query_t[1, at] = jnp.where(row < HD, 0.0, turned).astype(jnp.bfloat16)
+            turned = jnp.transpose(value_rows).astype(jnp.bfloat16)
+            for head in range(2):
+                value_t[head, at, pl.ds(0, HD), :] = turned[head * HD : (head + 1) * HD]
+                value_t[head, at, pl.ds(HD, extra), :] = jnp.ones((extra, block), jnp.bfloat16)
+        return unused
+
+    lax.fori_loop(0, pairs, lay_out, 0)
+
+    def query_block(at):
+        low = low_ref[at, 0:1, :]
+
+        def step(key_block, carried, causal, bounded):
+            new = []
+            for head in range(2):
+                top, total = carried[2 * head : 2 * head + 2]
+                scores = jnp.dot(
+                    key_ref[key_block], query_t[head, at], preferred_element_type=jnp.float32
+                )
+                if causal:
+                    scores = scores + causal_at[...]
+                if bounded:
+                    scores = jnp.where(
+                        key_at[...] >= low - key_block * block, scores, masked_score
+                    )
+                high = jnp.maximum(top, jnp.max(scores, axis=0, keepdims=True))
+                weights = jnp.exp(scores - high).astype(jnp.bfloat16)
+                total = total * jnp.exp(top - high) + jnp.dot(
+                    value_t[head, key_block], weights, preferred_element_type=jnp.float32
+                )
+                new += [high, total]
+            return tuple(new)
+
+        empty = (
+            jnp.full((1, block), masked_score, jnp.float32),
+            jnp.zeros((HD + extra, block), jnp.float32),
+        )
+        carried = step(at, empty * 2, True, True)
+        carried = lax.fori_loop(
+            first_ref[at],
+            plain_ref[at],
+            lambda key_block, held: step(key_block, held, False, True),
+            carried,
+        )
+        carried = lax.fori_loop(
+            plain_ref[at],
+            at,
+            lambda key_block, held: step(key_block, held, False, False),
+            carried,
+        )
+        heads = []
+        for head in range(2):
+            top, total = carried[2 * head : 2 * head + 2]
+            heads.append(total[:HD] / total[HD : HD + 1])
+            log_ref[at, head : head + 1, :] = top + jnp.log(total[HD : HD + 1])
+        both = jnp.concatenate(heads, axis=0)
+        out_ref[at] = both
+        return jnp.transpose(both).reshape(parts, UNIT_BLOCK, LANES)
+
+    def query_pair(pair, unused):
+        halves = UNIT_PAIR // UNIT_BLOCK
+        done = [query_block(pair * halves + half) for half in range(halves)]
+        unit_at = pl.multiple_of(pair * UNIT_PAIR, UNIT_PAIR)
+        att_ref[:, pl.ds(unit_at, UNIT_PAIR), :] = jnp.concatenate(done, axis=1).astype(
+            jnp.bfloat16
+        )
+        return unused
+
+    lax.fori_loop(0, pairs, query_pair, 0)
+
+
+def attend_back_kernel(
+    slot_ref,
+    first_ref,
+    plain_ref,
+    cos_unit,
+    sin_unit,
+    cos_part,
+    sin_part,
+    low_ref,
+    query_ref,
+    key_ref,
+    value_ref,
+    out_ref,
+    log_ref,
+    grad_ref,
+    back_ref,
+    key_t,
+    key_total,
+    value_total,
+    key_at,
+    causal_at,
+):
+    parts, units, _ = grad_ref.shape
+    block = parts * UNIT_BLOCK
+    pairs = units // UNIT_PAIR
+    halves = UNIT_PAIR // UNIT_BLOCK
+    key_at[...] = key_offsets(block)
+    causal_at[...] = jnp.where(key_offsets(block) <= query_offsets(block), 0.0, masked_score)
+
+    def lay_out(at, unused):
+        key_t[at] = jnp.transpose(key_ref[at].astype(jnp.float32)).astype(jnp.bfloat16)
+        key_total[at] = jnp.zeros((block, LANES), jnp.float32)
+        value_total[at] = jnp.zeros((block, LANES), jnp.float32)
+        return unused
+
+    lax.fori_loop(0, pairs * halves, lay_out, 0)
+
+    def split_heads(values, axis):
+        place = lax.broadcasted_iota(jnp.int32, values.shape, axis)
+        zero = jnp.zeros_like(values)
+        return [
+            jnp.where(place < HD, values, zero).astype(jnp.bfloat16),
+            jnp.where(place < HD, zero, values).astype(jnp.bfloat16),
+        ]
+
+    def query_block(at, grad_rows):
+        low = low_ref[at, 0:1, :]
+        query_rows = query_ref[at].astype(jnp.float32)
+        query_heads = jnp.concatenate(split_heads(query_rows, 1), axis=0)
+        grad_heads = jnp.concatenate(split_heads(grad_rows, 1), axis=0)
+        query_t = split_heads(jnp.transpose(query_rows), 0)
+        grad_turned = jnp.transpose(grad_rows)
+        grad_t = split_heads(grad_turned, 0)
+        product = grad_turned * out_ref[at]
+        inner = [
+            jnp.sum(product[head * HD : (head + 1) * HD], axis=0, keepdims=True)
+            for head in range(2)
+        ]
+        logs = [log_ref[at, head : head + 1, :] for head in range(2)]
+
+        def step(key_block, carried, causal, bounded):
+            probs, slopes, new = [], [], []
+            for head in range(2):
+                scores = jnp.dot(
+                    key_ref[key_block], query_t[head], preferred_element_type=jnp.float32
+                )
+                if causal:
+                    scores = scores + causal_at[...]
+                if bounded:
+                    scores = jnp.where(
+                        key_at[...] >= low - key_block * block, scores, masked_score
+                    )
+                soft = jnp.exp(scores - logs[head])
+                grad_probs = jnp.dot(
+                    value_ref[key_block], grad_t[head], preferred_element_type=jnp.float32
+                )
+                slope = (soft * (grad_probs - inner[head])).astype(jnp.bfloat16)
+                probs.append(soft.astype(jnp.bfloat16))
+                slopes.append(slope)
+                new.append(
+                    carried[head]
+                    + jnp.dot(
+                        key_t[key_block, pl.ds(head * HD, HD), :],
+                        slope,
+                        preferred_element_type=jnp.float32,
+                    )
+                )
+            value_total[key_block] += jnp.dot(
+                jnp.concatenate(probs, axis=1), grad_heads, preferred_element_type=jnp.float32
+            )
+            key_total[key_block] += jnp.dot(
+                jnp.concatenate(slopes, axis=1), query_heads, preferred_element_type=jnp.float32
+            )
+            return tuple(new)
+
+        carried = step(at, (jnp.zeros((HD, block), jnp.float32),) * 2, True, True)
+        carried = lax.fori_loop(
+            first_ref[at],
+            plain_ref[at],
+            lambda key_block, held: step(key_block, held, False, True),
+            carried,
+        )
+        carried = lax.fori_loop(
+            plain_ref[at],
+            at,
+            lambda key_block, held: step(key_block, held, False, False),
+            carried,
+        )
+        return jnp.transpose(jnp.concatenate(carried, axis=0)) * (1.0 / math.sqrt(HD))
+
+    def turn_back(rows, cosine, sine):
+        flat = (parts * UNIT_PAIR, LANES)
+        rows = jnp.concatenate(
+            [one.reshape(parts, UNIT_BLOCK, LANES) for one in rows], axis=1
+        ).reshape(flat)
+        turned = rows * cosine.reshape(flat) - swap_halves(rows) * sine.reshape(flat)
+        return turned.reshape(parts, UNIT_PAIR, LANES).astype(jnp.bfloat16)
+
+    def put(values, unit_at, lane_at):
+        for part in range(parts):
+            back_ref[slot_ref[part], pl.ds(unit_at, UNIT_PAIR), pl.ds(lane_at, LANES)] = values[part]
+
+    def query_pair(pair, unused):
+        unit_at = pl.multiple_of(pair * UNIT_PAIR, UNIT_PAIR)
+        grads = grad_ref[:, pl.ds(unit_at, UNIT_PAIR), :].astype(jnp.float32)
+        done = [
+            query_block(
+                pair * halves + half,
+                grads[:, half * UNIT_BLOCK : (half + 1) * UNIT_BLOCK].reshape(block, LANES),
+            )
+            for half in range(halves)
+        ]
+        cosine, sine = pair_angles(unit_at, cos_unit, sin_unit, cos_part, sin_part)
+        put(turn_back(done, cosine, sine), unit_at, 0)
+        return unused
+
+    lax.fori_loop(0, pairs, query_pair, 0)
+
+    def key_pair(pair, unused):
+        unit_at = pl.multiple_of(pair * UNIT_PAIR, UNIT_PAIR)
+        cosine, sine = pair_angles(unit_at, cos_unit, sin_unit, cos_part, sin_part)
+        ids = [pair * halves + half for half in range(halves)]
+        put(turn_back([key_total[at] for at in ids], cosine, sine), unit_at, LANES)
+        values = jnp.concatenate(
+            [value_total[at].reshape(parts, UNIT_BLOCK, LANES) for at in ids], axis=1
+        ).astype(jnp.bfloat16)
+        put(values, unit_at, 2 * LANES)
+        return unused
+
+    lax.fori_loop(0, pairs, key_pair, 0)
+
+
+def attend(tables, qkv):
+    parts, units, _ = qkv.shape
+    block = parts * UNIT_BLOCK
+    blocks = units // UNIT_BLOCK
+    smem = pl.BlockSpec(memory_space=pltpu.SMEM)
+    vmem = pl.BlockSpec(memory_space=pltpu.VMEM)
+    rows = jax.ShapeDtypeStruct((blocks, block, LANES), jnp.bfloat16)
+    extra = UNIT_PAIR
+    return pl.pallas_call(
+        attend_kernel,
+        out_shape=(
+            jax.ShapeDtypeStruct((parts, units, LANES), jnp.bfloat16),
+            jax.ShapeDtypeStruct((blocks, LANES, block), jnp.float32),
+            jax.ShapeDtypeStruct((blocks, 8, block), jnp.float32),
+            rows,
+            rows,
+            rows,
+        ),
+        in_specs=[smem] * 3 + [vmem] * 6,
+        out_specs=(vmem,) * 6,
+        scratch_shapes=[
+            pltpu.VMEM((2, blocks, LANES, block), jnp.bfloat16),
+            pltpu.VMEM((2, blocks, HD + extra, block), jnp.bfloat16),
+            pltpu.VMEM((block, block), jnp.int32),
+            pltpu.VMEM((block, block), jnp.float32),
+        ],
+        compiler_params=pltpu.CompilerParams(vmem_limit_bytes=KERNEL_VMEM),
+        cost_estimate=pl.CostEstimate(
+            flops=20 * 10**9, bytes_accessed=16 << 20, transcendentals=20 * 10**6
+        ),
+        name="attend",
+    )(*tables, qkv)
+
+
+def attend_back(tables, query, key, value, out, log, grad):
+    parts, units, _ = grad.shape
+    block = parts * UNIT_BLOCK
+    blocks = units // UNIT_BLOCK
+    smem = pl.BlockSpec(memory_space=pltpu.SMEM)
+    vmem = pl.BlockSpec(memory_space=pltpu.VMEM)
+    return pl.pallas_call(
+        attend_back_kernel,
+        out_shape=jax.ShapeDtypeStruct((parts, units, 3 * LANES), jnp.bfloat16),
+        in_specs=[smem] * 3 + [vmem] * 11,
+        out_specs=vmem,
+        scratch_shapes=[
+            pltpu.VMEM((blocks, LANES, block), jnp.bfloat16),
+            pltpu.VMEM((blocks, block, LANES), jnp.float32),
+            pltpu.VMEM((blocks, block, LANES), jnp.float32),
+            pltpu.VMEM((block, block), jnp.int32),
+            pltpu.VMEM((block, block), jnp.float32),
+        ],
+        compiler_params=pltpu.CompilerParams(vmem_limit_bytes=KERNEL_VMEM),
+        cost_estimate=pl.CostEstimate(
+            flops=50 * 10**9, bytes_accessed=16 << 20, transcendentals=20 * 10**6
+        ),
+        name="attend_back",
+    )(*tables, query, key, value, out, log, grad)
+
+
+def attention_tables(lengths, grp_here, rep_here, units):
+    reps = lax.axis_size("rep")
+    parts = lax.axis_size("grp") * reps
+    block = parts * UNIT_BLOCK
+    blocks = units // UNIT_BLOCK
+    own = lax.dynamic_index_in_dim(lengths, grp_here, 0, keepdims=False)
+    ends = jnp.cumsum(own)
+    unit_ids = jnp.arange(units, dtype=jnp.int32)
+    begin = jnp.max(
+        jnp.where(ends[None, :] <= unit_ids[:, None], ends[None, :], 0), axis=1
+    ).astype(jnp.int32)
+    part_ids = jnp.arange(parts, dtype=jnp.int32)
+    offset = part_ids % reps ^ rep_here
+    slot = offset * lax.axis_size("grp") + (part_ids // reps ^ grp_here)
+    frequency = jnp.power(
+        rope_base, -2.0 * (jnp.arange(LANES) % (HD // 2)).astype(jnp.float32) / HD
+    )
+    unit_angle = ((unit_ids - begin) * parts).astype(jnp.float32)[:, None] * frequency[None, :]
+    part_angle = part_ids.astype(jnp.float32)[:, None] * frequency[None, :]
+    low = jnp.maximum(
+        (begin * parts)[:, None], unit_ids[:, None] * parts + part_ids[None, :] - (WINDOW - 1)
+    )
+    low = low.reshape(blocks, UNIT_BLOCK, parts)
+    least = jnp.min(low, axis=(1, 2))
+    most = jnp.max(low, axis=(1, 2))
+    block_ids = jnp.arange(blocks, dtype=jnp.int32)
+    first = jnp.maximum(least, 0) // block
+    plain = jnp.clip((most + block - 1) // block, first, block_ids)
+    low_rows = jnp.broadcast_to(
+        low.transpose(0, 2, 1).reshape(blocks, 1, block), (blocks, 8, block)
+    )
+    return (
+        slot,
+        first,
+        plain,
+        jnp.cos(unit_angle),
+        jnp.sin(unit_angle),
+        jnp.cos(part_angle),
+        jnp.sin(part_angle),
+        low_rows,
+    )
+
+
+def swap(value, grp_step, rep_step):
+    groups, reps = lax.axis_size("grp"), lax.axis_size("rep")
+    pairs = [
+        (grp * reps + rep, (grp ^ grp_step) * reps + (rep ^ rep_step))
+        for grp in range(groups)
+        for rep in range(reps)
+    ]
+    return lax.ppermute(value, BOTH, pairs)
+
+
+def ordered(flag, own, other, axis=0):
+    return jnp.where(
+        flag == 0,
+        jnp.concatenate([own, other], axis=axis),
+        jnp.concatenate([other, own], axis=axis),
+    )
+
+
+def pick(value, index, axis):
+    return lax.dynamic_index_in_dim(value, index, axis, keepdims=False)
+
+
+def halve(value, axis, bit, grp_step, rep_step):
+    kept = pick(value, bit, axis)
+    sent = pick(value, 1 - bit, axis).astype(jnp.bfloat16)
+    arrived = swap(sent, grp_step, rep_step)
+    return kept.astype(jnp.float32) + arrived.astype(jnp.float32)
+
+
+def narrow(value):
+    return value.astype(jnp.bfloat16)
+
+
+def heads_body(
+    tokens,
+    attn_gain,
+    w_query,
+    w_key,
+    w_value,
+    w_output,
+    mlp_gain,
+    w_gate,
+    w_up,
+    w_down,
+    out_grad,
+    lengths,
+):
+    groups, reps = lax.axis_size("grp"), lax.axis_size("rep")
+    here, there = lax.axis_index("grp"), lax.axis_index("rep")
+    core = there % 2
+    micro_count, row_count, width = tokens.shape
+    rows = micro_count * row_count
+    hidden_width = w_gate.shape[1]
+    half_width = width // groups
+    own_width = hidden_width // (2 * groups)
+    stripes = reps // 2
+
+    gain_one = ordered(here, attn_gain, swap(attn_gain, 1, 0)).astype(jnp.float32)
+    gain_two = ordered(here, mlp_gain, swap(mlp_gain, 1, 0)).astype(jnp.float32)
+    inputs = tokens.astype(jnp.float32)
+    normed_in = (inputs * rms_scale(inputs) * gain_one).astype(jnp.bfloat16)
+    base = jnp.stack(
+        [pick(normed_in, here, 0), swap(pick(normed_in, 1 - here, 0), 1, 0)], axis=0
+    ).reshape(groups * row_count, width)
+
+    def own_columns(weight):
+        return lax.dynamic_slice_in_dim(weight, there * LANES, LANES, axis=1)
+
+    w_heads = jnp.concatenate(
+        [own_columns(w_query), own_columns(w_key), own_columns(w_value)], axis=1
+    )
+    w_heads = ordered(here, w_heads, swap(w_heads, 1, 0))
+
+    chunks = {0: base}
+    for step in range(reps - 4, 0, -4):
+        chunks[step] = swap(base, 0, step)
+    for step in [0] + list(range(reps - 4, 0, -4)):
+        chunks[step + 2] = swap(chunks[step], 0, 2)
+    for step in [0] + list(range(reps - 4, 0, -4)):
+        for part in (0, 2):
+            chunks[step + part + 1] = swap(chunks[step + part], 0, 1)
+    qkv = jnp.concatenate(
+        [jnp.dot(chunks[step], w_heads, preferred_element_type=jnp.float32).astype(jnp.bfloat16) for step in range(reps)],
+        axis=0,
+    ).reshape(reps * groups, row_count, 3 * LANES)
+
+    output_other = swap(
+        lax.dynamic_slice_in_dim(w_output, core * (half_width // 2), half_width // 2, axis=0), 1, 0
+    )
+    output_other = ordered(core, output_other, swap(output_other, 0, 1))
+    w_output_full = ordered(here, w_output, output_other)
+
+    def striped(weight):
+        return weight.reshape(half_width, groups, stripes, 2, LANES)
+
+    def own_stripes(weight, grp):
+        cut = pick(pick(striped(weight), grp, 1), core, 2)
+        return cut.reshape(half_width, own_width)
+
+    w_in = jnp.concatenate([own_stripes(w_gate, here), own_stripes(w_up, here)], axis=1)
+    w_in_other = swap(
+        jnp.concatenate([own_stripes(w_gate, 1 - here), own_stripes(w_up, 1 - here)], axis=1), 1, 0
+    )
+    w_in = ordered(here, w_in, w_in_other)
+    w_out = pick(w_down.reshape(stripes, 2, LANES, width), core, 1).reshape(own_width, width)
+
+    def gather_quad(value):
+        across = swap(value, 1, 0)
+        return jnp.concatenate([value, swap(value, 0, 1), across, swap(across, 0, 1)], axis=0)
+
+    out_rows = out_grad.reshape(rows, width)
+    out_quad = gather_quad(out_rows)
+    grad_hidden = contract(out_quad, w_out, 1, 1)
+
+    tables = attention_tables(lengths, here, there, row_count)
+    attended, out_heads, log_sum, query, key, value = attend(tables, qkv)
+    returned = lax.all_to_all(attended, BOTH, split_axis=0, concat_axis=0, tiled=True)
+    attn_rows = (
+        returned.reshape(groups, reps, row_count, LANES).transpose(0, 2, 1, 3).reshape(rows, width)
+    )
+    mixed = inputs.reshape(rows, width) + jnp.dot(
+        attn_rows, w_output_full, preferred_element_type=jnp.float32
+    )
+    normed_mid = (mixed * rms_scale(mixed) * gain_two).astype(jnp.bfloat16)
+    mid_quad = gather_quad(normed_mid)
+    gate_up = jnp.dot(mid_quad, w_in, preferred_element_type=jnp.float32)
+    gate_pre, up_pre = gate_up[:, :own_width], gate_up[:, own_width:]
+    gate_sig = jax.nn.sigmoid(gate_pre)
+    gate_silu = gate_pre * gate_sig
+    hidden = (gate_silu * up_pre).astype(jnp.bfloat16)
+    grad_gate = (grad_hidden * up_pre * gate_sig * (1.0 + gate_pre * (1.0 - gate_sig))).astype(
+        jnp.bfloat16
+    )
+    grad_up = (grad_hidden * gate_silu).astype(jnp.bfloat16)
+    grad_in_mlp = jnp.concatenate([grad_gate, grad_up], axis=1)
+
+    def scatter_quad(parts):
+        parts = parts.reshape(2, 2, rows, width)
+        both = parts[:, 0].astype(jnp.float32) + swap(narrow(parts[:, 1]), 0, 1).astype(jnp.float32)
+        return both[0] + swap(narrow(both[1]), 1, 0).astype(jnp.float32)
+
+    grad_mid = scatter_quad(contract(grad_in_mlp, w_in, 1, 1, jnp.bfloat16))
+    grad_norm_mid, unused_gain = norm_backward(mixed, gain_two, grad_mid)
+    grad_mixed = out_rows.astype(jnp.float32) + grad_norm_mid
+    grad_branch = grad_mixed.astype(jnp.bfloat16)
+    grad_att = contract(grad_branch, w_output_full, 1, 1, jnp.bfloat16)
+    grad_heads = lax.all_to_all(
+        grad_att.reshape(groups, row_count, reps, LANES)
+        .transpose(0, 2, 1, 3)
+        .reshape(groups * reps, row_count, LANES),
+        BOTH,
+        split_axis=0,
+        concat_axis=0,
+        tiled=True,
+    )
+
+    block_out = (
+        mixed + scatter_quad(jnp.dot(hidden, w_out, preferred_element_type=jnp.float32).astype(jnp.bfloat16))
+    ).astype(jnp.bfloat16)
+
+    bits = [(there // step) % 2 for step in (1, 2)]
+    far = [1 << place for place in range(2, reps.bit_length() - 1)]
+
+    def scatter_stripes(parts):
+        lead, rest = parts.shape[0], parts.shape[2:]
+        parts = halve(parts.reshape((lead, stripes // 2, 2) + rest), 2, bits[1], 0, 2)
+        for step in far:
+            count = parts.shape[1]
+            parts = halve(
+                narrow(parts).reshape((lead, count // 2, 2) + rest), 2, (there // step) % 2, 0, step
+            )
+        return parts[:, 0]
+
+    mlp_in_grad = contract(mid_quad, grad_in_mlp, 0, 0, jnp.bfloat16)
+    own_rows = width // (groups * reps)
+    mlp_in_part = narrow(
+        scatter_stripes(
+            mlp_in_grad.reshape(groups, stripes, 2, own_rows, 2 * own_width)
+        )
+    )
+    down_grad = scatter_stripes(
+        contract(hidden, out_quad, 0, 0, jnp.bfloat16).reshape(1, stripes, LANES, width)
+    )[0]
+
+    kept = pick(mlp_in_part, here, 0)
+    crossed = swap(pick(mlp_in_part, 1 - here, 0), 1, 0)
+    columns = []
+    for part in (kept, crossed):
+        columns.append(pick(part, core, 0))
+        columns.append(swap(pick(part, 1 - core, 0), 0, 1))
+    by_grp = [
+        jnp.where(
+            core == 0,
+            jnp.stack([columns[2 * at], columns[2 * at + 1]], axis=1),
+            jnp.stack([columns[2 * at + 1], columns[2 * at]], axis=1),
+        )
+        for at in range(2)
+    ]
+    pieces = jnp.where(
+        here == 0,
+        jnp.stack([by_grp[0], by_grp[1]], axis=1),
+        jnp.stack([by_grp[1], by_grp[0]], axis=1),
+    )
+    pieces = pieces.reshape(own_rows, groups, 2, 2, stripes, LANES).transpose(3, 0, 1, 4, 2, 5)
+    pieces = pieces.reshape(2, own_rows, hidden_width).astype(jnp.float32)
+    gate_grad, up_grad = pieces[0], pieces[1]
+
+    output_part = contract(attn_rows, grad_branch, 0, 0, jnp.bfloat16)
+    output_part = output_part.reshape(groups, stripes, 2, own_rows, width)
+    output_part = halve(output_part, 2, core, 0, 1)
+    output_part = halve(narrow(output_part), 0, here, 1, 0)
+    output_grad = scatter_stripes(narrow(output_part)[None])[0]
+
+    back = attend_back(tables, query, key, value, out_heads, log_sum, grad_heads)
+    back = back.reshape(reps, groups * row_count, 3 * LANES)
+
+    grad_in = None
+    for step in list(range(reps - 4, 0, -4)) + [0]:
+        summed = None
+        for part in (2, 0):
+            away = swap(contract(back[step + part + 1], w_heads, 1, 1, jnp.bfloat16), 0, 1)
+            total = contract(back[step + part], w_heads, 1, 1) + away.astype(jnp.float32)
+            if part == 2:
+                summed = swap(narrow(total), 0, 2).astype(jnp.float32)
+            else:
+                summed = summed + total
+        if step:
+            summed = swap(narrow(summed), 0, step).astype(jnp.float32)
+        grad_in = summed if grad_in is None else grad_in + summed
+    grad_in = grad_in.reshape(groups, row_count, width)
+    grad_in = ordered(here, grad_in[:1], swap(narrow(grad_in[1:]), 1, 0).astype(jnp.float32))
+    grad_norm_in, unused_gain = norm_backward(
+        inputs.reshape(rows, width), gain_one, grad_in.reshape(rows, width)
+    )
+    token_grad = (grad_mixed + grad_norm_in).astype(jnp.bfloat16)
+
+    gathered_rows = jnp.concatenate([chunks[step] for step in range(reps)], axis=0)
+    heads_grad = contract(gathered_rows, back.reshape(reps * groups * row_count, 3 * LANES), 0, 0)
+    heads_grad = halve(heads_grad.reshape(groups, half_width, 3 * LANES), 0, here, 1, 0)
+    heads_grad = lax.all_to_all(
+        narrow(heads_grad).reshape(reps, own_rows, 3 * LANES),
+        "rep",
+        split_axis=0,
+        concat_axis=0,
+        tiled=True,
+    )
+    heads_grad = (
+        heads_grad.reshape(reps, own_rows, 3, LANES)
+        .transpose(2, 1, 0, 3)
+        .reshape(3, own_rows, width)
+        .astype(jnp.float32)
+    )
+
+    def own_part(value):
+        return lax.dynamic_slice_in_dim(value, there * own_rows, own_rows, axis=0).astype(
+            jnp.float32
+        )
+
+    attn_gain_grad = (
+        jnp.sum(own_part(w_query) * heads_grad[0], axis=1)
+        + jnp.sum(own_part(w_key) * heads_grad[1], axis=1)
+        + jnp.sum(own_part(w_value) * heads_grad[2], axis=1)
+    ) / own_part(attn_gain)
+    mlp_gain_grad = (
+        jnp.sum(own_part(w_gate) * gate_grad, axis=1) + jnp.sum(own_part(w_up) * up_grad, axis=1)
+    ) / own_part(mlp_gain)
+    block_shape = tokens.shape
+    return (
+        block_out.reshape(block_shape),
+        token_grad.reshape(block_shape),
+        attn_gain_grad,
+        heads_grad[0],
+        heads_grad[1],
+        heads_grad[2],
+        output_grad,
+        mlp_gain_grad,
+        gate_grad,
+        up_grad,
+        down_grad,
+    )
+
+
+def pick_body(*arrays):
+    tokens = arrays[0]
+    groups, reps = lax.axis_size("grp"), lax.axis_size("rep")
+    fits = (
+        groups == 2
+        and tokens.shape[0] == groups
+        and tokens.shape[2] == reps * LANES
+        and reps % 4 == 0
+        and reps & (reps - 1) == 0
+        and tokens.shape[1] % UNIT_PAIR == 0
+        and arrays[7].shape[1] % (2 * groups * LANES) == 0
+    )
+    return heads_body(*arrays) if fits else ring_body(*arrays)
+
+
 def solution(mesh):
     in_specs = (
         P(None, ("grp", "rep"), None),
@@ -429,4 +1153,4 @@
         P(("grp", "rep"), None),
         P(("grp", "rep"), None),
     )
-    return jax.shard_map(body, mesh=mesh, in_specs=in_specs, out_specs=out_specs, check_vma=False)
+    return jax.shard_map(pick_body, mesh=mesh, in_specs=in_specs, out_specs=out_specs, check_vma=False)

time: 4230 us -> 1110 us (0.26)
  waiting for transfers between devices: 2330 us -> 517 us
  starting transfers between devices: 553 us -> 129 us
  local copies, waits for them, and re-layouts: 539 us -> 146 us
  matrix products: 400 us -> 149 us
  other arithmetic: 287 us -> 61.2 us
  Pallas kernels: 0 us -> 102 us
  blocking collectives: 85.7 us -> 0 us
    reduce_scatter x7 -> x0, waiting for transfers between devices: 1490 us -> none  [the longest x1 360 us: reduce_mlp(): lax.psum_scatter(gate_grad, ('grp', 'rep'), scatter_dimension=0, tiled=True)]
    all_gather x7 -> x0, waiting for transfers between devices: 406 us -> none  [the longest x1 134 us: gather_mlp(): lax.all_gather(w_down, 'grp', axis=0, tiled=True)]
    ppermute x32 -> x63, starting transfers between devices: 378 us -> 94 us  [swap(): return lax.ppermute(value, BOTH, pairs)]
    dot_general x77 -> x42, matrix products: 400 us -> 149 us  [the longest x23 95.7 us: contract(): lax.dot_general(left_side, right_side, (((left_dim,), (right_dim,)), ((),...]
    ppermute x32 -> x63, waiting for transfers between devices: 305 us -> 507 us  [swap(): return lax.ppermute(value, BOTH, pairs)]
    all_to_all x7 -> x3, starting transfers between devices: 175 us -> 34.5 us  [the longest x1 27.2 us: heads_body(): lax.all_to_all(attended, BOTH, split_axis=0, concat_axis=0, tiled=True)]
    dynamic_slice x32 -> x6, local copies, waits for them, and re-layouts: 157 us -> 16.9 us  [the longest x3 11.7 us: pick(): return lax.dynamic_index_in_dim(value, index, axis, keepdims=False)]
    all_to_all x7 -> x3, waiting for transfers between devices: 122 us -> 9.85 us  [the longest x1 9.84 us: heads_body(): lax.all_to_all(attended, BOTH, split_axis=0, concat_axis=0, tiled=True)]
  transfers between devices with their start and end apart: 53 -> 66, of which waited for: 48 -> 24; matrix products, arithmetic and copies ran while one was open for 28% -> 27% of each run, Pallas kernels for 0% -> 9%
where the time goes in v1:
time: 1110 us
  waiting for transfers between devices  517 us (47%)
  matrix products  149 us (13%)
  local copies, waits for them, and re-layouts  146 us (13%)
  starting transfers between devices  129 us (12%)
  Pallas kernels  102 us (9%)
  other arithmetic  61.2 us (6%)
    ppermute x63, waiting for transfers between devices, swap(): return lax.ppermute(value, BOTH, pairs)  507 us
    dot_general x23, matrix products, contract(): lax.dot_general(left_side, right_side, (((left_dim,), (right_dim,)), ((),...  95.7 us
    ppermute x63, starting transfers between devices, swap(): return lax.ppermute(value, BOTH, pairs)  94 us
    unnamed x195, local copies, waits for them, and re-layouts  64 us
    pallas_call x1, Pallas kernels, attend_back(): pl.pallas_call(attend_back_kernel, out_shape=jax.ShapeDtypeStruct((parts,...  53.9 us
    pallas_call x1, Pallas kernels, attend(): pl.pallas_call(attend_kernel, out_shape=(jax.ShapeDtypeStruct((parts, uni...  48.4 us
    all_to_all x1, starting transfers between devices, heads_body(): lax.all_to_all(attended, BOTH, split_axis=0, concat_axis=0, tiled=True)  27.2 us
  transfers between devices with their start and end apart: 66, of which 24 were waited for; matrix products, arithmetic and copies ran while one was open for 27% of the time, Pallas kernels for 9%

profile of v1, /device:TPU:0, one launch (start us, length us, event | category | flops | bytes accessed | tf_op | source)
XLA Modules:
  0.0 1105.8 jit_solution(5380194788679769602)
XLA Ops:
  0.7 6.4 copy.74
  22.2 12.0 %copy.77 = bf16[1024,4096]{0,1:T(8,128)(2,1)} copy(bf16[1024,4096]{1,0:T(8,128)(2,1)} %param.20) | data formatting | bytes 16777216 | tf_op args[8]
  34.2 12.1 %copy.76 = bf16[1024,4096]{0,1:T(8,128)(2,1)} copy(bf16[1024,4096]{1,0:T(8,128)(2,1)} %param.19) | data formatting | bytes 16777216 | tf_op args[7]
  46.3 13.7 %collective-permute-done = bf16[1024]{0:T(1024)(128)(2,1)S(1)} collective-permute-done((bf16[1024]{0:T(1024)(128)(2,1)S(1)}, bf16[1024]{0:T(1024)(128)(2,1)S(1)}, u32[]{:S(2)}, u32[]{:S(2)}) %collective-permute-start) | collective-permute-done | bytes 2080 | tf_op jit(solution)/shard_map/ppermute | solution.py:838
  63.3 6.7 constant_dynamic-slice_fusion.6
  70.0 17.2 %collective-permute-done.1 = bf16[128,2048]{1,0:T(8,128)(2,1)S(1)} collective-permute-done((bf16[128,2048]{1,0:T(8,128)(2,1)S(1)}, bf16[128,2048]{1,0:T(8,128)(2,1)S(1)}, u32[]{:S(2)}, u32[]{:S(2)}) %collective-permute-start.1) | collective-permute-done | bytes 524320 | tf_op jit(solution)/shard_map/ppermute | solution.py:838
  93.6 4.9 constant_dynamic-slice_fusion.3
  104.0 8.9 collective-permute-done.4
  112.9 11.6 %collective-permute-done.6 = bf16[256,2048]{1,0:T(8,128)(2,1)} collective-permute-done((bf16[256,2048]{1,0:T(8,128)(2,1)}, bf16[256,2048]{1,0:T(8,128)(2,1)}, u32[]{:S(2)}, u32[]{:S(2)}) %collective-permute-start.6) | collective-permute-done | bytes 1048608 | tf_op jit(solution)/shard_map/ppermute | solution.py:838
  132.3 18.3 %collective-permute-done.10 = bf16[256,2048]{1,0:T(8,128)(2,1)S(1)} collective-permute-done((bf16[256,2048]{1,0:T(8,128)(2,1)}, bf16[256,2048]{1,0:T(8,128)(2,1)S(1)}, u32[]{:S(2)}, u32[]{:S(2)}) %collective-permute-start.10) | collective-permute-done | bytes 1048608 | tf_op jit(solution)/shard_map/ppermute | solution.py:838
  158.5 19.1 %collective-permute-done.14 = bf16[256,2048]{1,0:T(8,128)(2,1)S(1)} collective-permute-done((bf16[256,2048]{1,0:T(8,128)(2,1)}, bf16[256,2048]{1,0:T(8,128)(2,1)S(1)}, u32[]{:S(2)}, u32[]{:S(2)}) %collective-permute-start.14) | collective-permute-done | bytes 1048608 | tf_op jit(solution)/shard_map/ppermute | solution.py:838
  183.5 19.2 %collective-permute-done.16 = bf16[256,2048]{1,0:T(8,128)(2,1)S(1)} collective-permute-done((bf16[256,2048]{1,0:T(8,128)(2,1)S(1)}, bf16[256,2048]{1,0:T(8,128)(2,1)S(1)}, u32[]{:S(2)}, u32[]{:S(2)}) %collective-permute-start.16) | collective-permute-done | bytes 1048608 | tf_op jit(solution)/shard_map/ppermute | solution.py:838
  211.0 48.4 %attend.1 = (bf16[32,128,128]{2,1,0:T(8,128)(2,1)}, f32[16,128,256]{2,1,0:T(8,128)}, f32[16,8,256]{2,1,0:T(8,128)}, bf16[16,256,128]{2,1,0:T(8,128)(2,1)}, bf16[...) custom-call(s32[32]{0:T(128)} %fusion.61.slot_ref, s32[16]{0:T(128)} %get-tuple-element.34.first_ref, ...), custom_call_target="tpu_custom_call" | custom-call | flops 20000000000 | bytes 16777216 | tf_op jit(solution)/shard_map/attend/pallas_call | solution.py:736
  259.3 27.2 %all-to-all-start = ((bf16[32,128,128]{2,1,0:T(8,128)(2,1)}), bf16[32,128,128]{2,1,0:T(8,128)(2,1)S(1)}, u32[]{:S(2)}, u32[]{:S(2)}) async-start(bf16[32,128,128]{2,1,0:T(8,128)(2,1)} %get-tuple-element.17), calls=%async_computation | async-start | bytes 2097152 | tf_op jit(solution)/shard_map/all_to_all | solution.py:947
  297.2 6.6 maximum_select_fusion.2
  303.9 9.8 all-to-all-done
  314.4 9.4 multiply_reduce_fusion.2
  331.2 17.8 %collective-permute-done.22 = bf16[256,2048]{1,0:T(8,128)(2,1)} collective-permute-done((bf16[256,2048]{1,0:T(8,128)(2,1)S(1)}, bf16[256,2048]{1,0:T(8,128)(2,1)}, u32[]{:S(2)}, u32[]{:S(2)}) %collective-permute-start.22) | collective-permute-done | bytes 1048608 | tf_op jit(solution)/shard_map/ppermute | solution.py:838
  354.3 21.4 %copy.85 = bf16[2048,4096]{1,0:T(8,128)(2,1)} copy(bf16[2048,4096]{0,1:T(8,128)(2,1)} %bitcast.55) | data formatting | bytes 33554432 | tf_op jit(solution)/shard_map/dot_general | solution.py:413
  375.7 20.7 %fusion.49 = f32[1024,2048]{1,0:T(8,128)} fusion(bf16[256,2048]{1,0:T(8,128)(2,1)} %collective-permute-done.23, bf16[256,2048]{1,0:T(8,128)(2,1)} %collective-permute-done.22, bf16[256,2048]{1,0:T(8,128)(2,1)} %collective-permute-done.21, bf16[256,2048]{1,0:T(8,128)(2,1)S(1)} %multiply_convert_fusion.3, bf16[1024,2048]{0,1:T(8,128)(2,1)} %collective-permute-done.24, ...), kind=kOutput, calls=%fused_computation.151 | convolution fusion | flops 8661237760 | bytes 20971520 | tf_op jit(solution)/shard_map/dot_general | solution.py:956
  396.4 12.2 %multiply_convert_fusion.1 = (bf16[1024,1024]{1,0:T(8,128)(2,1)}, bf16[1024,1024]{1,0:T(8,128)(2,1)}, bf16[1024,1024]{1,0:T(8,128)(2,1)}) fusion(f32[1024,2048]{1,0:T(8,128)} %fusion.49, bf16[1024,2048]{1,0:T(8,128)(2,1)S(1)} %bitcast.342, bf16[256,2048]{1,0:T(8,128)(2,1)} %collective-permute-done.29, bf16[256,2048]{1,0:T(8,128)(2,1)} %collective-permute-done.28, ...), kind=kOutput, calls=%fused_computation.24 | convolution fusion | flops 4327473152 | bytes 23068672 | tf_op jit(solution)/shard_map/dot_general | solution.py:413
  408.6 18.0 %convolution_convert_fusion.2 = bf16[1024,2048]{1,0:T(8,128)(2,1)} fusion(bf16[1024,1024]{1,0:T(8,128)(2,1)} %get-tuple-element.36, bf16[1024,1024]{1,0:T(8,128)(2,1)} %get-tuple-element.35, bf16[1024,2048]{0,1:T(8,128)(2,1)} %collective-permute-done.24, bf16[1024,1024]{0,1:T(8,128)(2,1)} %bitcast.355, bf16[1024,1024]{0,1:T(8,128)(2,1)} %bitcast.357, ...), kind=kOutput, calls=%fused_computation.28 | convolution fusion | flops 8654946304 | bytes 16777216 | tf_op jit(solution)/shard_map/dot_general | solution.py:413
  430.5 6.7 convolution_convert_fusion.4
  438.8 12.0 %convolution_convert_fusion = bf16[2048,2048]{1,0:T(8,128)(2,1)S(1)} fusion(bf16[1024,1024]{1,0:T(8,128)(2,1)} %get-tuple-element.36, bf16[1024,1024]{1,0:T(8,128)(2,1)} %get-tuple-element.35, bf16[256,2048]{1,0:T(8,128)(2,1)} %collective-permute-done.23, bf16[256,2048]{1,0:T(8,128)(2,1)} %collective-permute-done.22, ...), kind=kOutput, calls=%fused_computation.6 | convolution fusion | flops 8619294720 | bytes 16777216 | tf_op jit(solution)/shard_map/dot_general | solution.py:413
  456.2 6.8 convolution_convert_fusion.3
  472.2 121.5 %collective-permute-done.60 = bf16[1,4,128,2048]{3,2,1,0:T(8,128)(2,1)S(1)} collective-permute-done((bf16[1,4,128,2048]{3,2,1,0:T(8,128)(2,1)S(1)}, bf16[1,4,128,2048]{3,2,1,0:T(8,128)(2,1)S(1)}, u32[]{:S(2)}, u32[]{:S(2)}) %collective-permute-start.60) | collective-permute-done | bytes 2097184 | tf_op jit(solution)/shard_map/ppermute | solution.py:838
  595.6 17.2 %collective-permute-start.61 = (bf16[1,2,128,2048]{3,2,1,0:T(8,128)(2,1)}, bf16[1,2,128,2048]{3,2,1,0:T(8,128)(2,1)}, u32[]{:S(2)}, u32[]{:S(2)}) collective-permute-start(bf16[1,2,128,2048]{3,2,1,0:T(8,128)(2,1)} %dynamic-slice_bitcast_fusion.5), channel_id=1, source_target_pairs={{0,4},{1,5},{2,6},{3,7},{4,0},{5,1},{6,2},{7,3},{8,12},{9,13},{10,... | collective-permute-start | bytes 3145736 | tf_op jit(solution)/shard_map/ppermute | solution.py:838
  613.4 4.2 multiply_add_fusion
  626.0 17.2 %collective-permute-done.61 = bf16[1,2,128,2048]{3,2,1,0:T(8,128)(2,1)} collective-permute-done((bf16[1,2,128,2048]{3,2,1,0:T(8,128)(2,1)}, bf16[1,2,128,2048]{3,2,1,0:T(8,128)(2,1)}, u32[]{:S(2)}, u32[]{:S(2)}) %collective-permute-start.61) | collective-permute-done | bytes 1048608 | tf_op jit(solution)/shard_map/ppermute | solution.py:838
  652.9 21.7 %collective-permute-done.62 = bf16[1,1,128,2048]{3,2,1,0:T(8,128)(2,1)S(1)} collective-permute-done((bf16[1,1,128,2048]{3,2,1,0:T(8,128)(2,1)S(1)}, bf16[1,1,128,2048]{3,2,1,0:T(8,128)(2,1)S(1)}, u32[]{:S(2)}, u32[]{:S(2)}) %collective-permute-start.62) | collective-permute-done | bytes 524320 | tf_op jit(solution)/shard_map/ppermute | solution.py:838
  675.7 4.1 fusion
  683.3 53.9 %attend_back.1 = bf16[32,128,384]{2,1,0:T(8,128)(2,1)} custom-call(s32[32]{0:T(128)} %fusion.61.slot_ref, s32[16]{0:T(128)} %get-tuple-element.34.first_ref, s32[16]{0:T(128)} %get-tuple-element.33.plain_ref, f32[128,128]{1,0:T(8,128)} %get-tuple-element.76.cos_unit, f32[128,128]{1,0:T(8,128)} %get-tuple-element.75.sin_unit, ...), custom_call_target="tpu_custom_call" | custom-call | flops 49999998976 | bytes 16777216 | tf_op jit(solution)/shard_map/attend_back/pallas_call | solution.py:768
  743.4 12.3 %fusion.78 = f32[2,1024,384]{2,1,0:T(8,128)S(1)} fusion(bf16[2,1024,4096]{2,1,0:T(8,128)(2,1)} %bitcast.325, bf16[4096,384,1]{1,0,2:T(8,128)(2,1)S(1)} %bitcast.353), kind=kOutput, calls=%fused_computation.257 | convolution fusion | flops 6442450944 | bytes 23068672 | tf_op jit(solution)/shard_map/dot_general | solution.py:413
  755.9 8.0 collective-permute-start.48
  769.1 12.9 %collective-permute-done.48 = bf16[1024,384]{1,0:T(8,128)(2,1)S(1)} collective-permute-done((bf16[1024,384]{1,0:T(8,128)(2,1)S(1)}, bf16[1024,384]{1,0:T(8,128)(2,1)S(1)}, u32[]{:S(2)}, u32[]{:S(2)}) %collective-permute-start.48) | collective-permute-done | bytes 786464 | tf_op jit(solution)/shard_map/ppermute | solution.py:838
  801.2 38.0 %collective-permute-done.55 = bf16[2,2,2,64,2048]{4,3,2,1,0:T(8,128)(2,1)} collective-permute-done((bf16[2,2,2,64,2048]{4,3,2,1,0:T(8,128)(2,1)}, bf16[2,2,2,64,2048]{4,3,2,1,0:T(8,128)(2,1)}, u32[]{:S(2)}, u32[]{:S(2)}) %collective-permute-start.55) | collective-permute-done | bytes 2097184 | tf_op jit(solution)/shard_map/ppermute | solution.py:838
  847.0 18.4 %collective-permute-done.37 = bf16[256,2048]{1,0:T(8,128)(2,1)S(1)} collective-permute-done((bf16[256,2048]{1,0:T(8,128)(2,1)S(1)}, bf16[256,2048]{1,0:T(8,128)(2,1)S(1)}, u32[]{:S(2)}, u32[]{:S(2)}) %collective-permute-start.37) | collective-permute-done | bytes 1048608 | tf_op jit(solution)/shard_map/ppermute | solution.py:838
  868.1 19.8 %collective-permute-done.33 = bf16[256,2048]{1,0:T(8,128)(2,1)S(1)} collective-permute-done((bf16[256,2048]{1,0:T(8,128)(2,1)S(1)}, bf16[256,2048]{1,0:T(8,128)(2,1)S(1)}, u32[]{:S(2)}, u32[]{:S(2)}) %collective-permute-start.33) | collective-permute-done | bytes 1048608 | tf_op jit(solution)/shard_map/ppermute | solution.py:838
  896.7 12.5 %collective-permute-done.56 = bf16[2,1,2,64,2048]{4,3,2,1,0:T(8,128)(2,1)S(1)} collective-permute-done((bf16[2,1,2,64,2048]{4,3,2,1,0:T(8,128)(2,1)S(1)}, bf16[2,1,2,64,2048]{4,3,2,1,0:T(8,128)(2,1)S(1)}, u32[]{:S(2)}, u32[]{:S(2)}) %collective-permute-start.56) | collective-permute-done | bytes 1048608 | tf_op jit(solution)/shard_map/ppermute | solution.py:838
  914.5 4.7 fusion.77
  921.9 27.0 %collective-permute-done.58 = bf16[2,64,2048]{2,1,0:T(8,128)(2,1)} collective-permute-done((bf16[2,64,2048]{2,1,0:T(8,128)(2,1)}, bf16[2,64,2048]{2,1,0:T(8,128)(2,1)}, u32[]{:S(2)}, u32[]{:S(2)}) %collective-permute-start.58) | collective-permute-done | bytes 524320 | tf_op jit(solution)/shard_map/ppermute | solution.py:838
  976.1 24.3 %collective-permute-done.43 = bf16[256,2048]{1,0:T(8,128)(2,1)} collective-permute-done((bf16[256,2048]{1,0:T(8,128)(2,1)}, bf16[256,2048]{1,0:T(8,128)(2,1)}, u32[]{:S(2)}, u32[]{:S(2)}) %collective-permute-start.43) | collective-permute-done | bytes 1048608 | tf_op jit(solution)/shard_map/ppermute | solution.py:838
  1000.4 26.4 %collective-permute-done.39 = bf16[256,2048]{1,0:T(8,128)(2,1)} collective-permute-done((bf16[256,2048]{1,0:T(8,128)(2,1)}, bf16[256,2048]{1,0:T(8,128)(2,1)}, u32[]{:S(2)}, u32[]{:S(2)}) %collective-permute-start.39) | collective-permute-done | bytes 1048608 | tf_op jit(solution)/shard_map/ppermute | solution.py:838
  1035.8 10.5 collective-permute-done.47
  1046.4 10.8 collective-permute-done.51
  1057.6 23.1 %collective-permute-start.52 = (bf16[1,2,64,2048]{3,2,1,0:T(8,128)(2,1)S(1)}, bf16[1,2,64,2048]{3,2,1,0:T(8,128)(2,1)S(1)}, u32[]{:S(2)}, u32[]{:S(2)}) collective-permute-start(bf16[1,2,64,2048]{3,2,1,0:T(8,128)(2,1)S(1)} %dynamic-slice_bitcast_fusion.8), channel_id=1, source_target_pairs={{0,4},{1,5},{2,6},{3,7},{4,0},{5,1},{6,2},{7,3},{8,12},{9,13},{10,... | collective-permute-start | bytes 1572872 | tf_op jit(solution)/shard_map/ppermute | solution.py:838
  1081.4 10.3 collective-permute-done.52
  1095.2 9.6 collective-permute-done.53
  (428 shorter events, 228.0 us)
Async XLA Ops:
  10.3 196.6 %collective-permute-start.18 = (bf16[512,2048]{0,1:T(8,128)(2,1)}, bf16[512,2048]{0,1:T(8,128)(2,1)}, u32[]{:S(2)}, u32[]{:S(2)}) collective-permute-start(bf16[512,2048]{0,1:T(8,128)(2,1)} %constant_dynamic-slice_fusion.8), channel_id=1, source_target_pairs={{0,16},{1,17},{2,18},{3,19},{4,20},{5,21},{6,22},{7,23},{8,24},{9,... | collective-permute-start | bytes 6291464 | tf_op jit(solution)/shard_map/ppermute | solution.py:838
  13.2 46.8 %collective-permute-start = (bf16[1024]{0:T(1024)(128)(2,1)S(1)}, bf16[1024]{0:T(1024)(128)(2,1)S(1)}, u32[]{:S(2)}, u32[]{:S(2)}) collective-permute-start(bf16[1024]{0:T(1024)(128)(2,1)S(1)} %copy-done.78), channel_id=1, source_target_pairs={{0,16},{1,17},{2,18},{3,19},{4,20},{5,21},{6,22},{7,23},{8,24},{9,... | collective-permute-start | bytes 6152 | tf_op jit(solution)/shard_map/ppermute | solution.py:838
  17.0 84.4 %collective-permute-start.2 = (bf16[1024,384]{1,0:T(8,128)(2,1)}, bf16[1024,384]{1,0:T(8,128)(2,1)}, u32[]{:S(2)}, u32[]{:S(2)}) collective-permute-start(bf16[1024,384]{1,0:T(8,128)(2,1)} %pad_maximum_fusion.7), channel_id=1, source_target_pairs={{0,16},{1,17},{2,18},{3,19},{4,20},{5,21},{6,22},{7,23},{8,24},{9,... | collective-permute-start | bytes 2359304 | tf_op jit(solution)/shard_map/ppermute | solution.py:838
  60.4 26.8 %collective-permute-start.1 = (bf16[128,2048]{1,0:T(8,128)(2,1)S(1)}, bf16[128,2048]{1,0:T(8,128)(2,1)S(1)}, u32[]{:S(2)}, u32[]{:S(2)}) collective-permute-start(bf16[128,2048]{1,0:T(8,128)(2,1)S(1)} %get-tuple-element.68), channel_id=1, source_target_pairs={{0,16},{1,17},{2,18},{3,19},{4,20},{5,21},{6,22},{7,23},{8,24},{9,... | collective-permute-start | bytes 1572872 | tf_op jit(solution)/shard_map/ppermute | solution.py:838
  90.0 34.5 %collective-permute-start.6 = (bf16[256,2048]{1,0:T(8,128)(2,1)}, bf16[256,2048]{1,0:T(8,128)(2,1)}, u32[]{:S(2)}, u32[]{:S(2)}) collective-permute-start(bf16[256,2048]{1,0:T(8,128)(2,1)} %bitcast.7), channel_id=1, source_target_pairs={{0,4},{1,5},{2,6},{3,7},{4,0},{5,1},{6,2},{7,3},{8,12},{9,13},{10,... | collective-permute-start | bytes 3145736 | tf_op jit(solution)/shard_map/ppermute | solution.py:838
  98.4 31.0 %collective-permute-start.3 = (bf16[256,2048]{1,0:T(8,128)(2,1)}, bf16[256,2048]{1,0:T(8,128)(2,1)S(1)}, u32[]{:S(2)}, u32[]{:S(2)}) collective-permute-start(bf16[256,2048]{1,0:T(8,128)(2,1)} %bitcast.7), channel_id=1, source_target_pairs={{0,1},{1,0},{2,3},{3,2},{4,5},{5,4},{6,7},{7,6},{8,9},{9,8},{10,11... | collective-permute-start | bytes 3145736 | tf_op jit(solution)/shard_map/ppermute | solution.py:838
  101.4 49.2 %collective-permute-start.10 = (bf16[256,2048]{1,0:T(8,128)(2,1)}, bf16[256,2048]{1,0:T(8,128)(2,1)S(1)}, u32[]{:S(2)}, u32[]{:S(2)}) collective-permute-start(bf16[256,2048]{1,0:T(8,128)(2,1)} %bitcast.7), channel_id=1, source_target_pairs={{0,8},{1,9},{2,10},{3,11},{4,12},{5,13},{6,14},{7,15},{8,0},{9,1},... | collective-permute-start | bytes 3145736 | tf_op jit(solution)/shard_map/ppermute | solution.py:838
  112.9 40.2 %collective-permute-start.5 = (bf16[256,2048]{1,0:T(8,128)(2,1)}, bf16[256,2048]{1,0:T(8,128)(2,1)S(1)}, u32[]{:S(2)}, u32[]{:S(2)}) collective-permute-start(bf16[256,2048]{1,0:T(8,128)(2,1)} %collective-permute-done.4), channel_id=1, source_target_pairs={{0,1},{1,0},{2,3},{3,2},{4,5},{5,4},{6,7},{7,6},{8,9},{9,8},{10,11... | collective-permute-start | bytes 3145736 | tf_op jit(solution)/shard_map/ppermute | solution.py:838
  124.5 29.1 %collective-permute-start.8 = (bf16[256,2048]{1,0:T(8,128)(2,1)}, bf16[256,2048]{1,0:T(8,128)(2,1)S(1)}, u32[]{:S(2)}, u32[]{:S(2)}) collective-permute-start(bf16[256,2048]{1,0:T(8,128)(2,1)} %collective-permute-done.6), channel_id=1, source_target_pairs={{0,2},{1,3},{2,0},{3,1},{4,6},{5,7},{6,4},{7,5},{8,10},{9,11},{10,... | collective-permute-start | bytes 3145736 | tf_op jit(solution)/shard_map/ppermute | solution.py:838
  129.5 26.9 %collective-permute-start.7 = (bf16[256,2048]{1,0:T(8,128)(2,1)}, bf16[256,2048]{1,0:T(8,128)(2,1)S(1)}, u32[]{:S(2)}, u32[]{:S(2)}) collective-permute-start(bf16[256,2048]{1,0:T(8,128)(2,1)} %collective-permute-done.6), channel_id=1, source_target_pairs={{0,1},{1,0},{2,3},{3,2},{4,5},{5,4},{6,7},{7,6},{8,9},{9,8},{10,11... | collective-permute-start | bytes 3145736 | tf_op jit(solution)/shard_map/ppermute | solution.py:838
  150.6 26.9 %collective-permute-start.14 = (bf16[256,2048]{1,0:T(8,128)(2,1)}, bf16[256,2048]{1,0:T(8,128)(2,1)S(1)}, u32[]{:S(2)}, u32[]{:S(2)}) collective-permute-start(bf16[256,2048]{1,0:T(8,128)(2,1)} %bitcast.7), channel_id=1, source_target_pairs={{0,12},{1,13},{2,14},{3,15},{4,8},{5,9},{6,10},{7,11},{8,4},{9,5},... | collective-permute-start | bytes 3145736 | tf_op jit(solution)/shard_map/ppermute | solution.py:838
  177.5 111.4 %collective-permute-start.28 = (bf16[256,2048]{1,0:T(8,128)(2,1)}, bf16[256,2048]{1,0:T(8,128)(2,1)}, u32[]{:S(2)}, u32[]{:S(2)}) collective-permute-start(bf16[256,2048]{1,0:T(8,128)(2,1)} %bitcast.25), channel_id=1, source_target_pairs={{0,16},{1,17},{2,18},{3,19},{4,20},{5,21},{6,22},{7,23},{8,24},{9,... | collective-permute-start | bytes 3145736 | tf_op jit(solution)/shard_map/ppermute | solution.py:838
  202.7 193.7 %collective-permute-start.27 = (bf16[256,2048]{1,0:T(8,128)(2,1)}, bf16[256,2048]{1,0:T(8,128)(2,1)}, u32[]{:S(2)}, u32[]{:S(2)}) collective-permute-start(bf16[256,2048]{1,0:T(8,128)(2,1)} %bitcast.25), channel_id=1, source_target_pairs={{0,1},{1,0},{2,3},{3,2},{4,5},{5,4},{6,7},{7,6},{8,9},{9,8},{10,11... | collective-permute-start | bytes 3145736 | tf_op jit(solution)/shard_map/ppermute | solution.py:838
  204.8 81.8 %collective-permute-start.20 = (bf16[1024]{0:T(1024)(128)(2,1)S(1)}, bf16[1024]{0:T(1024)(128)(2,1)S(1)}, u32[]{:S(2)}, u32[]{:S(2)}) collective-permute-start(bf16[1024]{0:T(1024)(128)(2,1)S(1)} %copy-done.77), channel_id=1, source_target_pairs={{0,16},{1,17},{2,18},{3,19},{4,20},{5,21},{6,22},{7,23},{8,24},{9,... | collective-permute-start | bytes 6152 | tf_op jit(solution)/shard_map/ppermute | solution.py:838
  206.9 168.8 %collective-permute-start.24 = (bf16[1024,2048]{0,1:T(8,128)(2,1)}, bf16[1024,2048]{0,1:T(8,128)(2,1)}, u32[]{:S(2)}, u32[]{:S(2)}) collective-permute-start(bf16[1024,2048]{0,1:T(8,128)(2,1)} %pad_maximum_fusion.1), channel_id=1, source_target_pairs={{0,16},{1,17},{2,18},{3,19},{4,20},{5,21},{6,22},{7,23},{8,24},{9,... | collective-permute-start | bytes 12582920 | tf_op jit(solution)/shard_map/ppermute | solution.py:838
  208.5 88.7 %collective-permute-start.19 = (bf16[512,2048]{0,1:T(8,128)(2,1)}, bf16[512,2048]{0,1:T(8,128)(2,1)}, u32[]{:S(2)}, u32[]{:S(2)}) collective-permute-start(bf16[512,2048]{0,1:T(8,128)(2,1)} %collective-permute-done.18), channel_id=1, source_target_pairs={{0,1},{1,0},{2,3},{3,2},{4,5},{5,4},{6,7},{7,6},{8,9},{9,8},{10,11... | collective-permute-start | bytes 6291464 | tf_op jit(solution)/shard_map/ppermute | solution.py:838
  259.3 54.4 %all-to-all-start = ((bf16[32,128,128]{2,1,0:T(8,128)(2,1)}), bf16[32,128,128]{2,1,0:T(8,128)(2,1)S(1)}, u32[]{:S(2)}, u32[]{:S(2)}) async-start(bf16[32,128,128]{2,1,0:T(8,128)(2,1)} %get-tuple-element.17), calls=%async_computation | async-start | bytes 2097152 | tf_op jit(solution)/shard_map/all_to_all | solution.py:947
  289.0 107.4 %collective-permute-start.29 = (bf16[256,2048]{1,0:T(8,128)(2,1)}, bf16[256,2048]{1,0:T(8,128)(2,1)}, u32[]{:S(2)}, u32[]{:S(2)}) collective-permute-start(bf16[256,2048]{1,0:T(8,128)(2,1)} %collective-permute-done.28), channel_id=1, source_target_pairs={{0,1},{1,0},{2,3},{3,2},{4,5},{5,4},{6,7},{7,6},{8,9},{9,8},{10,11... | collective-permute-start | bytes 3145736 | tf_op jit(solution)/shard_map/ppermute | solution.py:838
  331.1 44.5 %collective-permute-start.21 = (bf16[256,2048]{1,0:T(8,128)(2,1)S(1)}, bf16[256,2048]{1,0:T(8,128)(2,1)}, u32[]{:S(2)}, u32[]{:S(2)}) collective-permute-start(bf16[256,2048]{1,0:T(8,128)(2,1)S(1)} %multiply_convert_fusion.3), channel_id=1, source_target_pairs={{0,1},{1,0},{2,3},{3,2},{4,5},{5,4},{6,7},{7,6},{8,9},{9,8},{10,11... | collective-permute-start | bytes 3145736 | tf_op jit(solution)/shard_map/ppermute | solution.py:838
  430.0 34.6 %collective-permute-start.30 = (bf16[2,256,2048]{2,1,0:T(8,128)(2,1)}, bf16[2,256,2048]{2,1,0:T(8,128)(2,1)}, u32[]{:S(2)}, u32[]{:S(2)}) collective-permute-start(bf16[2,256,2048]{2,1,0:T(8,128)(2,1)} %slice_bitcast_fusion.1), channel_id=1, source_target_pairs={{0,1},{1,0},{2,3},{3,2},{4,5},{5,4},{6,7},{7,6},{8,9},{9,8},{10,11... | collective-permute-start | bytes 6291464 | tf_op jit(solution)/shard_map/ppermute | solution.py:838
  438.8 29.3 %collective-permute-start.25 = (bf16[2,256,2048]{2,1,0:T(8,128)(2,1)}, bf16[2,256,2048]{2,1,0:T(8,128)(2,1)}, u32[]{:S(2)}, u32[]{:S(2)}) collective-permute-start(bf16[2,256,2048]{2,1,0:T(8,128)(2,1)} %slice_bitcast_fusion.4), channel_id=1, source_target_pairs={{0,1},{1,0},{2,3},{3,2},{4,5},{5,4},{6,7},{7,6},{8,9},{9,8},{10,11... | collective-permute-start | bytes 6291464 | tf_op jit(solution)/shard_map/ppermute | solution.py:838
  455.5 220.2 %collective-permute-start.54 = (bf16[2,4,2,64,2048]{4,3,2,1,0:T(8,128)(2,1)}, bf16[2,4,2,64,2048]{4,3,2,1,0:T(8,128)(2,1)}, u32[]{:S(2)}, u32[]{:S(2)}) collective-permute-start(bf16[2,4,2,64,2048]{4,3,2,1,0:T(8,128)(2,1)} %dynamic-slice_bitcast_fusion), channel_id=1, source_target_pairs={{0,2},{1,3},{2,0},{3,1},{4,6},{5,7},{6,4},{7,5},{8,10},{9,11},{10,... | collective-permute-start | bytes 12582920 | tf_op jit(solution)/shard_map/ppermute | solution.py:838
  463.2 130.5 %collective-permute-start.60 = (bf16[1,4,128,2048]{3,2,1,0:T(8,128)(2,1)S(1)}, bf16[1,4,128,2048]{3,2,1,0:T(8,128)(2,1)S(1)}, u32[]{:S(2)}, u32[]{:S(2)}) collective-permute-start(bf16[1,4,128,2048]{3,2,1,0:T(8,128)(2,1)S(1)} %dynamic-slice_bitcast_fusion.2), channel_id=1, source_target_pairs={{0,2},{1,3},{2,0},{3,1},{4,6},{5,7},{6,4},{7,5},{8,10},{9,11},{10,... | collective-permute-start | bytes 6291464 | tf_op jit(solution)/shard_map/ppermute | solution.py:838
  467.6 145.1 %collective-permute-start.31 = (bf16[256,2048]{1,0:T(8,128)(2,1)S(1)}, bf16[256,2048]{1,0:T(8,128)(2,1)S(1)}, u32[]{:S(2)}, u32[]{:S(2)}) collective-permute-start(bf16[256,2048]{1,0:T(8,128)(2,1)S(1)} %fusion.41), channel_id=1, source_target_pairs={{0,16},{1,17},{2,18},{3,19},{4,20},{5,21},{6,22},{7,23},{8,24},{9,... | collective-permute-start | bytes 3145736 | tf_op jit(solution)/shard_map/ppermute | solution.py:838
  470.4 143.0 %collective-permute-start.26 = (bf16[256,2048]{1,0:T(8,128)(2,1)S(1)}, bf16[256,2048]{1,0:T(8,128)(2,1)S(1)}, u32[]{:S(2)}, u32[]{:S(2)}) collective-permute-start(bf16[256,2048]{1,0:T(8,128)(2,1)S(1)} %fusion.40), channel_id=1, source_target_pairs={{0,16},{1,17},{2,18},{3,19},{4,20},{5,21},{6,22},{7,23},{8,24},{9,... | collective-permute-start | bytes 3145736 | tf_op jit(solution)/shard_map/ppermute | solution.py:838
  595.6 47.6 %collective-permute-start.61 = (bf16[1,2,128,2048]{3,2,1,0:T(8,128)(2,1)}, bf16[1,2,128,2048]{3,2,1,0:T(8,128)(2,1)}, u32[]{:S(2)}, u32[]{:S(2)}) collective-permute-start(bf16[1,2,128,2048]{3,2,1,0:T(8,128)(2,1)} %dynamic-slice_bitcast_fusion.5), channel_id=1, source_target_pairs={{0,4},{1,5},{2,6},{3,7},{4,0},{5,1},{6,2},{7,3},{8,12},{9,13},{10,... | collective-permute-start | bytes 3145736 | tf_op jit(solution)/shard_map/ppermute | solution.py:838
  622.3 60.9 %all-to-all-start.1 = ((bf16[32,128,128]{2,1,0:T(8,128)(2,1)}), bf16[32,128,128]{2,1,0:T(8,128)(2,1)}, u32[]{:S(2)}, u32[]{:S(2)}) async-start(bf16[32,128,128]{2,1,0:T(8,128)(2,1)} %bitcast.345), calls=%async_computation.1 | async-start | bytes 2097152 | tf_op jit(solution)/shard_map/all_to_all | solution.py:977
  645.4 29.2 %collective-permute-start.62 = (bf16[1,1,128,2048]{3,2,1,0:T(8,128)(2,1)S(1)}, bf16[1,1,128,2048]{3,2,1,0:T(8,128)(2,1)S(1)}, u32[]{:S(2)}, u32[]{:S(2)}) collective-permute-start(bf16[1,1,128,2048]{3,2,1,0:T(8,128)(2,1)S(1)} %constant_dynamic-slice_fusion), channel_id=1, source_target_pairs={{0,8},{1,9},{2,10},{3,11},{4,12},{5,13},{6,14},{7,15},{8,0},{9,1},... | collective-permute-start | bytes 1572872 | tf_op jit(solution)/shard_map/ppermute | solution.py:838
  652.9 236.8 %collective-permute-start.49 = (bf16[2,8,64,2048]{3,2,1,0:T(8,128)(2,1)}, bf16[2,8,64,2048]{3,2,1,0:T(8,128)(2,1)}, u32[]{:S(2)}, u32[]{:S(2)}) collective-permute-start(bf16[2,8,64,2048]{3,2,1,0:T(8,128)(2,1)} %dynamic-slice_bitcast_fusion.1), channel_id=1, source_target_pairs={{0,1},{1,0},{2,3},{3,2},{4,5},{5,4},{6,7},{7,6},{8,9},{9,8},{10,11... | collective-permute-start | bytes 12582920 | tf_op jit(solution)/shard_map/ppermute | solution.py:838
  741.2 46.1 %collective-permute-start.44 = (bf16[256,2048]{1,0:T(8,128)(2,1)S(1)}, bf16[256,2048]{1,0:T(8,128)(2,1)S(1)}, u32[]{:S(2)}, u32[]{:S(2)}) collective-permute-start(bf16[256,2048]{1,0:T(8,128)(2,1)S(1)} %convolution_convert_fusion.6), channel_id=1, source_target_pairs={{0,1},{1,0},{2,3},{3,2},{4,5},{5,4},{6,7},{7,6},{8,9},{9,8},{10,11... | collective-permute-start | bytes 3145736 | tf_op jit(solution)/shard_map/ppermute | solution.py:838
  742.0 43.6 %collective-permute-start.40 = (bf16[256,2048]{1,0:T(8,128)(2,1)S(1)}, bf16[256,2048]{1,0:T(8,128)(2,1)S(1)}, u32[]{:S(2)}, u32[]{:S(2)}) collective-permute-start(bf16[256,2048]{1,0:T(8,128)(2,1)S(1)} %convolution_convert_fusion.8), channel_id=1, source_target_pairs={{0,1},{1,0},{2,3},{3,2},{4,5},{5,4},{6,7},{7,6},{8,9},{9,8},{10,11... | collective-permute-start | bytes 3145736 | tf_op jit(solution)/shard_map/ppermute | solution.py:838
  743.3 44.5 %collective-permute-start.36 = (bf16[256,2048]{1,0:T(8,128)(2,1)S(1)}, bf16[256,2048]{1,0:T(8,128)(2,1)S(1)}, u32[]{:S(2)}, u32[]{:S(2)}) collective-permute-start(bf16[256,2048]{1,0:T(8,128)(2,1)S(1)} %convolution_convert_fusion.10), channel_id=1, source_target_pairs={{0,1},{1,0},{2,3},{3,2},{4,5},{5,4},{6,7},{7,6},{8,9},{9,8},{10,11... | collective-permute-start | bytes 3145736 | tf_op jit(solution)/shard_map/ppermute | solution.py:838
  782.0 57.3 %collective-permute-start.55 = (bf16[2,2,2,64,2048]{4,3,2,1,0:T(8,128)(2,1)}, bf16[2,2,2,64,2048]{4,3,2,1,0:T(8,128)(2,1)}, u32[]{:S(2)}, u32[]{:S(2)}) collective-permute-start(bf16[2,2,2,64,2048]{4,3,2,1,0:T(8,128)(2,1)} %dynamic-slice_bitcast_fusion.3), channel_id=1, source_target_pairs={{0,4},{1,5},{2,6},{3,7},{4,0},{5,1},{6,2},{7,3},{8,12},{9,13},{10,... | collective-permute-start | bytes 6291464 | tf_op jit(solution)/shard_map/ppermute | solution.py:838
  787.8 51.8 %collective-permute-start.41 = (bf16[256,2048]{1,0:T(8,128)(2,1)}, bf16[256,2048]{1,0:T(8,128)(2,1)}, u32[]{:S(2)}, u32[]{:S(2)}) collective-permute-start(bf16[256,2048]{1,0:T(8,128)(2,1)} %fusion.8), channel_id=1, source_target_pairs={{0,2},{1,3},{2,0},{3,1},{4,6},{5,7},{6,4},{7,5},{8,10},{9,11},{10,... | collective-permute-start | bytes 3145736 | tf_op jit(solution)/shard_map/ppermute | solution.py:838
  790.4 122.3 %all-to-all-start.2 = ((bf16[16,64,384]{2,1,0:T(8,128)(2,1)}), bf16[16,64,384]{2,1,0:T(8,128)(2,1)S(1)}, u32[]{:S(2)}, u32[]{:S(2)}) async-start(bf16[16,64,384]{2,1,0:T(8,128)(2,1)} %bitcast.61), calls=%async_computation.2 | async-start | bytes 1572864 | tf_op jit(solution)/shard_map/all_to_all | solution.py:1070
  798.1 48.9 %collective-permute-start.38 = (bf16[256,2048]{1,0:T(8,128)(2,1)S(1)}, bf16[256,2048]{1,0:T(8,128)(2,1)S(1)}, u32[]{:S(2)}, u32[]{:S(2)}) collective-permute-start(bf16[256,2048]{1,0:T(8,128)(2,1)S(1)} %copy-done.60), channel_id=1, source_target_pairs={{0,1},{1,0},{2,3},{3,2},{4,5},{5,4},{6,7},{7,6},{8,9},{9,8},{10,11... | collective-permute-start | bytes 3145736 | tf_op jit(solution)/shard_map/ppermute | solution.py:838
  800.9 67.2 %collective-permute-start.34 = (bf16[256,2048]{1,0:T(8,128)(2,1)S(1)}, bf16[256,2048]{1,0:T(8,128)(2,1)S(1)}, u32[]{:S(2)}, u32[]{:S(2)}) collective-permute-start(bf16[256,2048]{1,0:T(8,128)(2,1)S(1)} %copy-done.59), channel_id=1, source_target_pairs={{0,1},{1,0},{2,3},{3,2},{4,5},{5,4},{6,7},{7,6},{8,9},{9,8},{10,11... | collective-permute-start | bytes 3145736 | tf_op jit(solution)/shard_map/ppermute | solution.py:838
  839.7 48.2 %collective-permute-start.33 = (bf16[256,2048]{1,0:T(8,128)(2,1)S(1)}, bf16[256,2048]{1,0:T(8,128)(2,1)S(1)}, u32[]{:S(2)}, u32[]{:S(2)}) collective-permute-start(bf16[256,2048]{1,0:T(8,128)(2,1)S(1)} %fusion.6), channel_id=1, source_target_pairs={{0,2},{1,3},{2,0},{3,1},{4,6},{5,7},{6,4},{7,5},{8,10},{9,11},{10,... | collective-permute-start | bytes 3145736 | tf_op jit(solution)/shard_map/ppermute | solution.py:838
  847.0 107.5 %collective-permute-start.46 = (bf16[256,2048]{1,0:T(8,128)(2,1)}, bf16[256,2048]{1,0:T(8,128)(2,1)S(1)}, u32[]{:S(2)}, u32[]{:S(2)}) collective-permute-start(bf16[256,2048]{1,0:T(8,128)(2,1)} %convolution_convert_fusion.5), channel_id=1, source_target_pairs={{0,1},{1,0},{2,3},{3,2},{4,5},{5,4},{6,7},{7,6},{8,9},{9,8},{10,11... | collective-permute-start | bytes 3145736 | tf_op jit(solution)/shard_map/ppermute | solution.py:838
  865.4 110.6 %collective-permute-start.45 = (bf16[256,2048]{1,0:T(8,128)(2,1)}, bf16[256,2048]{1,0:T(8,128)(2,1)}, u32[]{:S(2)}, u32[]{:S(2)}) collective-permute-start(bf16[256,2048]{1,0:T(8,128)(2,1)} %fusion.9), channel_id=1, source_target_pairs={{0,2},{1,3},{2,0},{3,1},{4,6},{5,7},{6,4},{7,5},{8,10},{9,11},{10,... | collective-permute-start | bytes 3145736 | tf_op jit(solution)/shard_map/ppermute | solution.py:838
  868.1 41.1 %collective-permute-start.56 = (bf16[2,1,2,64,2048]{4,3,2,1,0:T(8,128)(2,1)S(1)}, bf16[2,1,2,64,2048]{4,3,2,1,0:T(8,128)(2,1)S(1)}, u32[]{:S(2)}, u32[]{:S(2)}) collective-permute-start(bf16[2,1,2,64,2048]{4,3,2,1,0:T(8,128)(2,1)S(1)} %constant_dynamic-slice_fusion.1), channel_id=1, source_target_pairs={{0,8},{1,9},{2,10},{3,11},{4,12},{5,13},{6,14},{7,15},{8,0},{9,1},... | collective-permute-start | bytes 3145736 | tf_op jit(solution)/shard_map/ppermute | solution.py:838
  895.0 135.2 %collective-permute-start.50 = (bf16[8,64,2048]{2,1,0:T(8,128)(2,1)}, bf16[8,64,2048]{2,1,0:T(8,128)(2,1)}, u32[]{:S(2)}, u32[]{:S(2)}) collective-permute-start(bf16[8,64,2048]{2,1,0:T(8,128)(2,1)} %dynamic-slice_bitcast_fusion.4), channel_id=1, source_target_pairs={{0,16},{1,17},{2,18},{3,19},{4,20},{5,21},{6,22},{7,23},{8,24},{9,... | collective-permute-start | bytes 6291464 | tf_op jit(solution)/shard_map/ppermute | solution.py:838
  910.5 38.4 %collective-permute-start.58 = (bf16[2,64,2048]{2,1,0:T(8,128)(2,1)}, bf16[2,64,2048]{2,1,0:T(8,128)(2,1)}, u32[]{:S(2)}, u32[]{:S(2)}) collective-permute-start(bf16[2,64,2048]{2,1,0:T(8,128)(2,1)} %dynamic-slice_bitcast_fusion.7), channel_id=1, source_target_pairs={{0,16},{1,17},{2,18},{3,19},{4,20},{5,21},{6,22},{7,23},{8,24},{9,... | collective-permute-start | bytes 1572872 | tf_op jit(solution)/shard_map/ppermute | solution.py:838
  912.0 42.6 %collective-permute-start.57 = (bf16[64,2048]{1,0:T(8,128)(2,1)}, bf16[64,2048]{1,0:T(8,128)(2,1)}, u32[]{:S(2)}, u32[]{:S(2)}) collective-permute-start(bf16[64,2048]{1,0:T(8,128)(2,1)} %get-tuple-element.66), channel_id=1, source_target_pairs={{0,1},{1,0},{2,3},{3,2},{4,5},{5,4},{6,7},{7,6},{8,9},{9,8},{10,11... | collective-permute-start | bytes 786440 | tf_op jit(solution)/shard_map/ppermute | solution.py:838
  954.5 45.9 %collective-permute-start.43 = (bf16[256,2048]{1,0:T(8,128)(2,1)}, bf16[256,2048]{1,0:T(8,128)(2,1)}, u32[]{:S(2)}, u32[]{:S(2)}) collective-permute-start(bf16[256,2048]{1,0:T(8,128)(2,1)} %add_convert_fusion.1), channel_id=1, source_target_pairs={{0,4},{1,5},{2,6},{3,7},{4,0},{5,1},{6,2},{7,3},{8,12},{9,13},{10,... | collective-permute-start | bytes 3145736 | tf_op jit(solution)/shard_map/ppermute | solution.py:838
  954.6 72.2 %collective-permute-start.39 = (bf16[256,2048]{1,0:T(8,128)(2,1)}, bf16[256,2048]{1,0:T(8,128)(2,1)}, u32[]{:S(2)}, u32[]{:S(2)}) collective-permute-start(bf16[256,2048]{1,0:T(8,128)(2,1)} %add_convert_fusion.2), channel_id=1, source_target_pairs={{0,8},{1,9},{2,10},{3,11},{4,12},{5,13},{6,14},{7,15},{8,0},{9,1},... | collective-permute-start | bytes 3145736 | tf_op jit(solution)/shard_map/ppermute | solution.py:838
  955.3 71.5 %collective-permute-start.35 = (bf16[256,2048]{1,0:T(8,128)(2,1)}, bf16[256,2048]{1,0:T(8,128)(2,1)}, u32[]{:S(2)}, u32[]{:S(2)}) collective-permute-start(bf16[256,2048]{1,0:T(8,128)(2,1)} %add_convert_fusion.3), channel_id=1, source_target_pairs={{0,12},{1,13},{2,14},{3,15},{4,8},{5,9},{6,10},{7,11},{8,4},{9,5},... | collective-permute-start | bytes 3145736 | tf_op jit(solution)/shard_map/ppermute | solution.py:838
  1057.6 34.0 %collective-permute-start.52 = (bf16[1,2,64,2048]{3,2,1,0:T(8,128)(2,1)S(1)}, bf16[1,2,64,2048]{3,2,1,0:T(8,128)(2,1)S(1)}, u32[]{:S(2)}, u32[]{:S(2)}) collective-permute-start(bf16[1,2,64,2048]{3,2,1,0:T(8,128)(2,1)S(1)} %dynamic-slice_bitcast_fusion.8), channel_id=1, source_target_pairs={{0,4},{1,5},{2,6},{3,7},{4,0},{5,1},{6,2},{7,3},{8,12},{9,13},{10,... | collective-permute-start | bytes 1572872 | tf_op jit(solution)/shard_map/ppermute | solution.py:838
  (103 other events, 2105.9 us)

commit v2 on v1

--- a/solution.py
+++ b/solution.py
@@ -861,6 +861,516 @@
     return value.astype(jnp.bfloat16)
 
 
+MESH_IDS = pl.DeviceIdType.MESH
+
+
+def flipped(index, step):
+    return index + step - 2 * step * ((index // step) % 2)
+
+
+def lowest(offset):
+    return offset & -offset
+
+
+def arrivals(reps):
+    far = [step for step in range(4, reps, 4)]
+    far.sort(key=lambda step: (bin(step).count("1"), step))
+    order = [(2, 0), (0, 1)]
+    for at, step in enumerate(far):
+        if bin(step).count("1") == 1:
+            order.append((step, 0))
+    order.append((2, 1))
+    for step in far:
+        if bin(step).count("1") == 1:
+            order.append((step, 1))
+    single = [step for step in far if bin(step).count("1") == 1]
+    double = [step for step in far if bin(step).count("1") > 1]
+    rest = []
+    for step in single[:1]:
+        rest.append((step + 2, 0))
+    for step in double:
+        rest.append((step, 0))
+    for step in single[:1]:
+        rest.append((step + 2, 1))
+    for step in double:
+        rest.append((step, 1))
+    for step in single[1:] + double:
+        rest += [(step + 2, 0), (step + 2, 1)]
+    return order + rest
+
+
+def link_of(offset, part, reps):
+    if reps > 8 and offset == reps - 2 and part == 1:
+        return 4
+    return lowest(offset)
+
+
+def gather_kernel(
+    tokens_ref,
+    gain_ref,
+    w_query,
+    w_key,
+    w_value,
+    normed_out,
+    qkv_ref,
+    weight_ref,
+    raw,
+    normed,
+    gains,
+    weight_sem,
+    out_sem,
+    send_sem,
+    recv_sem,
+    side_send,
+    side_recv,
+):
+    here, there = lax.axis_index("grp"), lax.axis_index("rep")
+    reps = raw.shape[0]
+    slots = normed.shape[0]
+    row_count, width = raw.shape[2:]
+    steps = [1 << place for place in range(reps.bit_length() - 1)]
+    across = (1 - here, there)
+
+    def neighbour(step):
+        return (here, flipped(there, step))
+
+    barrier = pltpu.get_barrier_semaphore()
+    for target in [across] + [neighbour(step) for step in steps]:
+        pl.semaphore_signal(barrier, inc=1, device_id=target, device_id_type=MESH_IDS)
+    local = []
+    for at, weight in enumerate((w_query, w_key, w_value)):
+        local.append(
+            pltpu.make_async_copy(
+                weight.at[:, pl.ds(pl.multiple_of(there * LANES, LANES), LANES)],
+                weight_ref.at[here, :, pl.ds(at * LANES, LANES)],
+                weight_sem.at[at],
+            )
+        )
+        local[-1].start()
+    raw[0, 0] = tokens_ref[here]
+    gains[here] = gain_ref[...]
+    pl.semaphore_wait(barrier, len(steps) + 1)
+
+    def side(at, source, target_ref):
+        return pltpu.make_async_remote_copy(
+            src_ref=source,
+            dst_ref=target_ref,
+            send_sem=side_send.at[at],
+            recv_sem=side_recv.at[at],
+            device_id=across,
+            device_id_type=MESH_IDS,
+        )
+
+    def rows_copy(offset, part):
+        if offset == 0:
+            return pltpu.make_async_remote_copy(
+                src_ref=tokens_ref.at[1 - here],
+                dst_ref=raw.at[0, 1],
+                send_sem=send_sem.at[1],
+                recv_sem=recv_sem.at[1],
+                device_id=across,
+                device_id_type=MESH_IDS,
+            )
+        step = link_of(offset, part, reps)
+        return pltpu.make_async_remote_copy(
+            src_ref=raw.at[offset - step, part],
+            dst_ref=raw.at[offset, part],
+            send_sem=send_sem.at[2 * offset + part],
+            recv_sem=recv_sem.at[2 * offset + part],
+            device_id=neighbour(step),
+            device_id_type=MESH_IDS,
+        )
+
+    order = arrivals(reps)
+    copies = {
+        (offset, part): rows_copy(offset, part)
+        for offset in range(reps)
+        for part in (0, 1)
+        if offset or part
+    }
+
+    def pass_on(offset, part):
+        for later, part_of in order:
+            if later and part_of == part and later - link_of(later, part, reps) == offset:
+                copies[later, part].start()
+        copies[offset + 1, part].start()
+
+    gain_copy = side(0, gains.at[here], gains.at[here])
+    gain_copy.start()
+    copies[0, 1].start()
+    pass_on(0, 0)
+    for one in local:
+        one.wait()
+    weight_copy = side(1, weight_ref.at[here], weight_ref.at[here])
+    weight_copy.start()
+
+    written = {}
+    used = [None] * slots
+    tile = 32
+
+    def project(count, offset):
+        slot = count % slots
+        if used[slot] is not None:
+            written[used[slot]].wait()
+        used[slot] = offset
+        gain = jnp.concatenate([gains[0, 0:1], gains[1, 0:1]], axis=1).astype(jnp.float32)
+        for part in range(2):
+
+            def norm_rows(at, unused):
+                cut = pl.ds(pl.multiple_of(at * tile, tile), tile)
+                values = raw[offset, part, cut, :].astype(jnp.float32)
+                scaled = values * rms_scale(values) * gain
+                normed[slot, pl.ds(pl.multiple_of(part * row_count + at * tile, tile), tile), :] = (
+                    scaled.astype(jnp.bfloat16)
+                )
+                return unused
+
+            lax.fori_loop(0, row_count // tile, norm_rows, 0)
+        written[offset] = pltpu.make_async_copy(
+            normed.at[slot], normed_out.at[offset], out_sem.at[offset]
+        )
+        written[offset].start()
+        half = width // 2
+        product = jnp.dot(
+            normed[slot, :, :half], weight_ref[0], preferred_element_type=jnp.float32
+        ) + jnp.dot(normed[slot, :, half:], weight_ref[1], preferred_element_type=jnp.float32)
+        qkv_ref[pl.ds(2 * offset, 2)] = product.astype(jnp.bfloat16).reshape(
+            2, row_count, 3 * LANES
+        )
+
+    ready = []
+    arrived = {(0, 0)}
+    started = False
+    count = 0
+    for offset, part in order:
+        copies[offset, part].wait_recv()
+        pass_on(offset, part)
+        arrived.add((offset, part))
+        if (offset, 1 - part) in arrived:
+            ready.append(offset)
+        if not started and len(ready) >= 1:
+            gain_copy.wait_recv()
+            weight_copy.wait_recv()
+            started = True
+        if started and len(ready) >= 2:
+            base = ready.pop(0)
+            project(count, base)
+            copies[base + 1, 0].wait_recv()
+            copies[base + 1, 1].wait_recv()
+            project(count + 1, base + 1)
+            count += 2
+    for base in ready:
+        project(count, base)
+        copies[base + 1, 0].wait_recv()
+        copies[base + 1, 1].wait_recv()
+        project(count + 1, base + 1)
+        count += 2
+    for offset in used:
+        written[offset].wait()
+    for one in copies.values():
+        one.wait_send()
+    gain_copy.wait_send()
+    weight_copy.wait_send()
+
+
+def gather_heads(tokens, gain, w_query, w_key, w_value):
+    reps = lax.axis_size("rep")
+    _, row_count, width = tokens.shape
+    half = width // 2
+    gain_rows = jnp.broadcast_to(gain[None], (16, half))
+    vmem = pl.BlockSpec(memory_space=pltpu.VMEM)
+    anywhere = pl.BlockSpec(memory_space=pl.ANY)
+    return pl.pallas_call(
+        gather_kernel,
+        out_shape=(
+            jax.ShapeDtypeStruct((reps, 2 * row_count, width), jnp.bfloat16),
+            jax.ShapeDtypeStruct((2 * reps, row_count, 3 * LANES), jnp.bfloat16),
+            jax.ShapeDtypeStruct((2, half, 3 * LANES), jnp.bfloat16),
+        ),
+        in_specs=[vmem, vmem, anywhere, anywhere, anywhere],
+        out_specs=(anywhere, vmem, vmem),
+        scratch_shapes=[
+            pltpu.VMEM((reps, 2, row_count, width), jnp.bfloat16),
+            pltpu.VMEM((4, 2 * row_count, width), jnp.bfloat16),
+            pltpu.VMEM((2, 16, half), jnp.bfloat16),
+            pltpu.SemaphoreType.DMA((3,)),
+            pltpu.SemaphoreType.DMA((reps,)),
+            pltpu.SemaphoreType.DMA((2 * reps,)),
+            pltpu.SemaphoreType.DMA((2 * reps,)),
+            pltpu.SemaphoreType.DMA((2,)),
+            pltpu.SemaphoreType.DMA((2,)),
+        ],
+        compiler_params=pltpu.CompilerParams(
+            vmem_limit_bytes=KERNEL_VMEM, collective_id=0, has_side_effects=True
+        ),
+        cost_estimate=pl.CostEstimate(
+            flops=8 * 10**9, bytes_accessed=250 << 20, transcendentals=0
+        ),
+        name="gather_heads",
+    )(tokens, gain_rows, w_query, w_key, w_value)
+
+
+def scatter_kernel(
+    back_ref,
+    weight_ref,
+    normed_ref,
+    grad_ref,
+    pieces_ref,
+    away,
+    landed,
+    normed,
+    back_t,
+    weight_t,
+    weights_total,
+    half_out,
+    half_in,
+    piece_out,
+    normed_sem,
+    send_sem,
+    recv_sem,
+    side_send,
+    side_recv,
+    piece_send,
+    piece_recv,
+):
+    here, there = lax.axis_index("grp"), lax.axis_index("rep")
+    reps, rows, columns = back_ref.shape
+    row_count = rows // 2
+    width = grad_ref.shape[2]
+    half = width // 2
+    own_rows = half // reps
+    steps = [1 << place for place in range(reps.bit_length() - 1)]
+    across = (1 - here, there)
+
+    def other(offset):
+        index = there
+        for step in steps:
+            if offset & step:
+                index = flipped(index, step)
+        return (here, index)
+
+    barrier = pltpu.get_barrier_semaphore()
+    for target in [across] + [other(offset) for offset in range(1, reps)]:
+        pl.semaphore_signal(barrier, inc=1, device_id=target, device_id_type=MESH_IDS)
+
+    slots = normed.shape[0]
+    fetch = [
+        pltpu.make_async_copy(normed_ref.at[offset], normed.at[offset % slots], normed_sem.at[offset])
+        for offset in range(reps)
+    ]
+    for offset in range(slots):
+        fetch[offset].start()
+
+    for at in range(2):
+        turned = jnp.transpose(weight_ref[at].astype(jnp.float32)).astype(jnp.bfloat16)
+        weight_t[:, pl.ds(at * half, half)] = turned
+    pl.semaphore_wait(barrier, reps)
+
+    def rows_copy(offset, part):
+        if offset == 0:
+            return pltpu.make_async_remote_copy(
+                src_ref=away.at[0, 1],
+                dst_ref=landed.at[0, 1],
+                send_sem=send_sem.at[1],
+                recv_sem=recv_sem.at[1],
+                device_id=across,
+                device_id_type=MESH_IDS,
+            )
+        return pltpu.make_async_remote_copy(
+            src_ref=away.at[offset, part],
+            dst_ref=landed.at[offset, part],
+            send_sem=send_sem.at[2 * offset + part],
+            recv_sem=recv_sem.at[2 * offset + part],
+            device_id=other(link_of(offset, part, reps)),
+            device_id_type=MESH_IDS,
+        )
+
+    copies = {
+        (offset, part): rows_copy(offset, part)
+        for offset in range(reps)
+        for part in (0, 1)
+        if offset or part
+    }
+    tile = 32
+
+    def product(offset, part):
+        return jnp.dot(
+            back_ref[offset, pl.ds(part * row_count, row_count), :],
+            weight_t[...],
+            preferred_element_type=jnp.float32,
+        )
+
+    def send(offset, part):
+        sources = [
+            later
+            for later in range(1, reps)
+            if later - link_of(later, part, reps) == offset
+        ]
+        for later in sources:
+            copies[later, part].wait_recv()
+        total = product(offset, part)
+        for later in sources:
+            total = total + landed[later, part].astype(jnp.float32)
+        if offset == 0 and part == 0:
+            grad_ref[here] = total
+        else:
+            away[offset, part] = total.astype(jnp.bfloat16)
+            copies[offset, part].start()
+
+    def weight_step(offset):
+        fetch[offset].wait()
+        back_t[...] = jnp.transpose(back_ref[offset].astype(jnp.float32)).astype(jnp.bfloat16)
+
+        def columns_at(at, unused):
+            cut = pl.ds(pl.multiple_of(at * 512, 512), 512)
+            term = jnp.dot(
+                back_t[...], normed[offset % slots, :, cut], preferred_element_type=jnp.float32
+            )
+            if offset == 0:
+                weights_total[:, cut] = term
+            else:
+                weights_total[:, cut] += term
+            return unused
+
+        lax.fori_loop(0, width // 512, columns_at, 0)
+        if offset + slots < reps:
+            fetch[offset + slots].start()
+
+    half_copy = pltpu.make_async_remote_copy(
+        src_ref=half_out,
+        dst_ref=half_in,
+        send_sem=side_send,
+        recv_sem=side_recv,
+        device_id=across,
+        device_id_type=MESH_IDS,
+    )
+    piece_copies = [
+        pltpu.make_async_remote_copy(
+            src_ref=piece_out.at[other(offset)[1]],
+            dst_ref=pieces_ref.at[there],
+            send_sem=piece_send.at[offset],
+            recv_sem=piece_recv.at[offset],
+            device_id=other(offset),
+            device_id_type=MESH_IDS,
+        )
+        for offset in range(1, reps)
+    ]
+
+    def cross_weights():
+        cut = pl.ds(pl.multiple_of((1 - here) * half, half), half)
+        half_out[...] = weights_total[:, cut].astype(jnp.bfloat16)
+        half_copy.start()
+
+    def share_weights():
+        half_copy.wait_recv()
+        cut = pl.ds(pl.multiple_of(here * half, half), half)
+        total = jnp.transpose(weights_total[:, cut] + half_in[...].astype(jnp.float32))
+        piece_out[...] = total.astype(jnp.bfloat16).reshape(reps, own_rows, columns)
+        pieces_ref[there] = piece_out[there]
+        for one in piece_copies:
+            one.start()
+
+    far = [step for step in range(reps - 4, 0, -4)]
+    todo = []
+    for base in far + [0]:
+        todo.append((base + 3, 1))
+        todo.append((base + 3, 0))
+        todo.append((base + 1, 1))
+        todo.append((base + 1, 0))
+    first = todo[:2]
+    for offset, part in first:
+        send(offset, part)
+    for offset, part in todo[2:6]:
+        send(offset, part)
+    send(reps - 2, 1)
+    send(reps - 2, 0)
+    for offset, part in todo[6:]:
+        send(offset, part)
+    weights = list(range(reps))
+
+    def weight_steps(count):
+        for _ in range(min(count, len(weights))):
+            weight_step(weights.pop(0))
+
+    last = []
+    order = []
+    for base in sorted(far, key=lambda step: (-bin(step).count("1"), -step)):
+        if base != far[0]:
+            order.append((base + 2, 1))
+            order.append((base + 2, 0))
+    order += [(2, 1), (2, 0)]
+    sums = sorted(far, key=lambda step: (-bin(step).count("1"), -step))
+    for base in sums:
+        last += [(base, 1), (base, 0)]
+    if reps == 16:
+        plan = [
+            (10, 1), (10, 0), 4, (12, 1), (12, 0), 4, (6, 1), (6, 0), 2, (8, 1), 2, (8, 0),
+            (2, 1), (2, 0), 4, "cross", (4, 1), (4, 0), "share", (0, 1), (0, 0),
+        ]
+    else:
+        plan = order + last + [reps, "cross", "share", (0, 1), (0, 0)]
+    for item in plan:
+        if item == "cross":
+            weight_steps(reps)
+            cross_weights()
+        elif item == "share":
+            share_weights()
+        elif isinstance(item, int):
+            weight_steps(item)
+        else:
+            send(*item)
+    copies[0, 1].wait_recv()
+    grad_ref[1 - here] = landed[0, 1].astype(jnp.float32)
+    for one in piece_copies:
+        one.wait()
+    half_copy.wait_send()
+    for one in copies.values():
+        one.wait_send()
+
+
+def scatter_heads(back, weights, normed):
+    reps, rows, columns = back.shape
+    width = normed.shape[2]
+    row_count = rows // 2
+    half = width // 2
+    vmem = pl.BlockSpec(memory_space=pltpu.VMEM)
+    anywhere = pl.BlockSpec(memory_space=pl.ANY)
+    return pl.pallas_call(
+        scatter_kernel,
+        out_shape=(
+            jax.ShapeDtypeStruct((2, row_count, width), jnp.float32),
+            jax.ShapeDtypeStruct((reps, half // reps, columns), jnp.bfloat16),
+        ),
+        in_specs=[vmem, vmem, anywhere],
+        out_specs=(vmem, vmem),
+        scratch_shapes=[
+            pltpu.VMEM((reps, 2, row_count, width), jnp.bfloat16),
+            pltpu.VMEM((reps, 2, row_count, width), jnp.bfloat16),
+            pltpu.VMEM((4, rows, width), jnp.bfloat16),
+            pltpu.VMEM((columns, rows), jnp.bfloat16),
+            pltpu.VMEM((columns, width), jnp.bfloat16),
+            pltpu.VMEM((columns, width), jnp.float32),
+            pltpu.VMEM((columns, half), jnp.bfloat16),
+            pltpu.VMEM((columns, half), jnp.bfloat16),
+            pltpu.VMEM((reps, half // reps, columns), jnp.bfloat16),
+            pltpu.SemaphoreType.DMA((reps,)),
+            pltpu.SemaphoreType.DMA((2 * reps,)),
+            pltpu.SemaphoreType.DMA((2 * reps,)),
+            pltpu.SemaphoreType.DMA,
+            pltpu.SemaphoreType.DMA,
+            pltpu.SemaphoreType.DMA((reps,)),
+            pltpu.SemaphoreType.DMA((reps,)),
+        ],
+        compiler_params=pltpu.CompilerParams(
+            vmem_limit_bytes=KERNEL_VMEM, collective_id=1, has_side_effects=True
+        ),
+        cost_estimate=pl.CostEstimate(
+            flops=14 * 10**9, bytes_accessed=250 << 20, transcendentals=0
+        ),
+        name="scatter_heads",
+    )(back, weights, normed)
+
+
 def heads_body(
     tokens,
     attn_gain,
@@ -885,34 +1395,10 @@
     own_width = hidden_width // (2 * groups)
     stripes = reps // 2
 
+    gathered_rows, qkv, w_heads = gather_heads(tokens, attn_gain, w_query, w_key, w_value)
     gain_one = ordered(here, attn_gain, swap(attn_gain, 1, 0)).astype(jnp.float32)
     gain_two = ordered(here, mlp_gain, swap(mlp_gain, 1, 0)).astype(jnp.float32)
     inputs = tokens.astype(jnp.float32)
-    normed_in = (inputs * rms_scale(inputs) * gain_one).astype(jnp.bfloat16)
-    base = jnp.stack(
-        [pick(normed_in, here, 0), swap(pick(normed_in, 1 - here, 0), 1, 0)], axis=0
-    ).reshape(groups * row_count, width)
-
-    def own_columns(weight):
-        return lax.dynamic_slice_in_dim(weight, there * LANES, LANES, axis=1)
-
-    w_heads = jnp.concatenate(
-        [own_columns(w_query), own_columns(w_key), own_columns(w_value)], axis=1
-    )
-    w_heads = ordered(here, w_heads, swap(w_heads, 1, 0))
-
-    chunks = {0: base}
-    for step in range(reps - 4, 0, -4):
-        chunks[step] = swap(base, 0, step)
-    for step in [0] + list(range(reps - 4, 0, -4)):
-        chunks[step + 2] = swap(chunks[step], 0, 2)
-    for step in [0] + list(range(reps - 4, 0, -4)):
-        for part in (0, 2):
-            chunks[step + part + 1] = swap(chunks[step + part], 0, 1)
-    qkv = jnp.concatenate(
-        [jnp.dot(chunks[step], w_heads, preferred_element_type=jnp.float32).astype(jnp.bfloat16) for step in range(reps)],
-        axis=0,
-    ).reshape(reps * groups, row_count, 3 * LANES)
 
     output_other = swap(
         lax.dynamic_slice_in_dim(w_output, core * (half_width // 2), half_width // 2, axis=0), 1, 0
@@ -1042,38 +1528,14 @@
     output_grad = scatter_stripes(narrow(output_part)[None])[0]
 
     back = attend_back(tables, query, key, value, out_heads, log_sum, grad_heads)
-    back = back.reshape(reps, groups * row_count, 3 * LANES)
-
-    grad_in = None
-    for step in list(range(reps - 4, 0, -4)) + [0]:
-        summed = None
-        for part in (2, 0):
-            away = swap(contract(back[step + part + 1], w_heads, 1, 1, jnp.bfloat16), 0, 1)
-            total = contract(back[step + part], w_heads, 1, 1) + away.astype(jnp.float32)
-            if part == 2:
-                summed = swap(narrow(total), 0, 2).astype(jnp.float32)
-            else:
-                summed = summed + total
-        if step:
-            summed = swap(narrow(summed), 0, step).astype(jnp.float32)
-        grad_in = summed if grad_in is None else grad_in + summed
-    grad_in = grad_in.reshape(groups, row_count, width)
-    grad_in = ordered(here, grad_in[:1], swap(narrow(grad_in[1:]), 1, 0).astype(jnp.float32))
+    grad_in, heads_grad = scatter_heads(
+        back.reshape(reps, groups * row_count, 3 * LANES), w_heads, gathered_rows
+    )
     grad_norm_in, unused_gain = norm_backward(
         inputs.reshape(rows, width), gain_one, grad_in.reshape(rows, width)
     )
     token_grad = (grad_mixed + grad_norm_in).astype(jnp.bfloat16)
 
-    gathered_rows = jnp.concatenate([chunks[step] for step in range(reps)], axis=0)
-    heads_grad = contract(gathered_rows, back.reshape(reps * groups * row_count, 3 * LANES), 0, 0)
-    heads_grad = halve(heads_grad.reshape(groups, half_width, 3 * LANES), 0, here, 1, 0)
-    heads_grad = lax.all_to_all(
-        narrow(heads_grad).reshape(reps, own_rows, 3 * LANES),
-        "rep",
-        split_axis=0,
-        concat_axis=0,
-        tiled=True,
-    )
     heads_grad = (
         heads_grad.reshape(reps, own_rows, 3, LANES)
         .transpose(2, 1, 0, 3)

time: 1110 us -> 994 us (0.90)
  Pallas kernels: 102 us -> 374 us
  waiting for transfers between devices: 517 us -> 349 us
  starting transfers between devices: 129 us -> 29.2 us
  matrix products: 149 us -> 85.3 us
  local copies, waits for them, and re-layouts: 146 us -> 90.8 us
    pallas_call x0 -> x2, Pallas kernels: none -> 252 us  [the longest x1 139 us: gather_heads(): pl.pallas_call(gather_kernel, out_shape=(jax.ShapeDtypeStruct((reps, 2 *...]
    ppermute x63 -> x29, waiting for transfers between devices: 507 us -> 349 us  [swap(): return lax.ppermute(value, BOTH, pairs)]
    ppermute x63 -> x29, starting transfers between devices: 94 us -> 21.3 us  [swap(): return lax.ppermute(value, BOTH, pairs)]
    dot_general x23 -> x6, matrix products: 95.7 us -> 54.7 us  [contract(): lax.dot_general(left_side, right_side, (((left_dim,), (right_dim,)), ((),...]
    all_to_all x1, starting transfers between devices: 27.2 us -> 3.57 us  [heads_body(): lax.all_to_all(attended, BOTH, split_axis=0, concat_axis=0, tiled=True)]
    unnamed x195 -> x74, local copies, waits for them, and re-layouts: 64 us -> 41.6 us
    dot_general x1 -> x0, local copies, waits for them, and re-layouts: 21.4 us -> none  [contract(): lax.dot_general(left_side, right_side, (((left_dim,), (right_dim,)), ((),...]
    dot_general x16 -> x0, matrix products: 16.3 us -> none  [heads_body(): jnp.dot(chunks[step], w_heads, preferred_element_type=jnp.float32)]
  transfers between devices with their start and end apart: 66 -> 31, of which waited for: 24 -> 10; matrix products, arithmetic and copies ran while one was open for 27% -> 18% of each run, Pallas kernels for 9% -> 38%
where the time goes in v2:
time: 994 us; the launch traced here: 987 us
  Pallas kernels  374 us (38%)
  waiting for transfers between devices  349 us (35%)
  local copies, waits for them, and re-layouts  90.8 us (9%)
  matrix products  85.3 us (9%)
  other arithmetic  57.4 us (6%)
  starting transfers between devices  29.2 us (3%)
    ppermute x29, waiting for transfers between devices, swap(): return lax.ppermute(value, BOTH, pairs)  349 us
    pallas_call x1, Pallas kernels, gather_heads(): pl.pallas_call(gather_kernel, out_shape=(jax.ShapeDtypeStruct((reps, 2 *...  139 us
    pallas_call x1, Pallas kernels, scatter_heads(): pl.pallas_call(scatter_kernel, out_shape=(jax.ShapeDtypeStruct((2, row_co...  113 us
    pallas_call x1, Pallas kernels, attend_back(): pl.pallas_call(attend_back_kernel, out_shape=jax.ShapeDtypeStruct((parts,...  63.9 us
    pallas_call x1, Pallas kernels, attend(): pl.pallas_call(attend_kernel, out_shape=(jax.ShapeDtypeStruct((parts, uni...  57.8 us
    dot_general x6, matrix products, contract(): lax.dot_general(left_side, right_side, (((left_dim,), (right_dim,)), ((),...  54.7 us
    unnamed x74, local copies, waits for them, and re-layouts  41.6 us
    ppermute x29, starting transfers between devices, swap(): return lax.ppermute(value, BOTH, pairs)  21.3 us
  transfers between devices with their start and end apart: 31, of which 10 were waited for; matrix products, arithmetic and copies ran while one was open for 18% of the time, Pallas kernels for 38%

profile of v2, /device:TPU:0, one launch (start us, length us, event | category | flops | bytes accessed | tf_op | source)
XLA Modules:
  0.0 986.9 jit_solution(8336040818921656703)
XLA Ops:
  0.7 6.4 copy.73
  8.8 3.0 collective-permute-start
  16.9 138.5 %gather_heads.1 = (bf16[16,256,2048]{2,1,0:T(8,128)(2,1)}, bf16[32,128,384]{2,1,0:T(8,128)(2,1)}, bf16[2,1024,384]{2,1,0:T(8,128)(2,1)}) custom-call(bf16[2,128,2048]{2,1,0:T(8,128)(2,1)} %tokens_ref.1, bf16[16,1024]{1,0:T(8,128)(2,1)} %broadcast_in_dim.16.gain_ref, bf16[1024,2048]{1,0:T(8,128)(2,1)} %w_query.1, bf16[1024,2048]{1,0:T(8,128)(2,1)} %w_key.1, ...), custom_call_target="tpu_custom_call" | custom-call | flops 8000000000 | bytes 262144000 | tf_op jit(solution)/shard_map/gather_heads/pallas_call | solution.py:1083
  156.1 57.8 %attend.1 = (bf16[32,128,128]{2,1,0:T(8,128)(2,1)}, f32[16,128,256]{2,1,0:T(8,128)}, f32[16,8,256]{2,1,0:T(8,128)}, bf16[16,256,128]{2,1,0:T(8,128)(2,1)}, bf16[...) custom-call(s32[32]{0:T(128)} %fusion.38.slot_ref, s32[16]{0:T(128)} %get-tuple-element.42.first_ref, ...), custom_call_target="tpu_custom_call" | custom-call | flops 20000000000 | bytes 16777216 | tf_op jit(solution)/shard_map/attend/pallas_call | solution.py:736
  213.9 3.6 all-to-all-start
  219.4 12.0 %copy.76 = bf16[1024,4096]{0,1:T(8,128)(2,1)} copy(bf16[1024,4096]{1,0:T(8,128)(2,1)} %param.20) | data formatting | bytes 16777216 | tf_op args[8]
  231.4 11.9 %copy.75 = bf16[1024,4096]{0,1:T(8,128)(2,1)} copy(bf16[1024,4096]{1,0:T(8,128)(2,1)} %param.19) | data formatting | bytes 16777216 | tf_op args[7]
  243.4 6.6 constant_dynamic-slice_fusion.6
  250.0 2.4 pad_maximum_fusion.1
  253.3 5.1 maximum_select_fusion.2
  258.6 3.3 multiply_reduce_fusion.3
  265.4 103.2 %collective-permute-done.4 = bf16[256,2048]{1,0:T(8,128)(2,1)} collective-permute-done((bf16[256,2048]{1,0:T(8,128)(2,1)}, bf16[256,2048]{1,0:T(8,128)(2,1)}, u32[]{:S(2)}, u32[]{:S(2)}) %collective-permute-start.4) | collective-permute-done | bytes 1048608 | tf_op jit(solution)/shard_map/ppermute | solution.py:838
  369.6 4.8 constant_dynamic-slice_fusion.3
  374.4 15.6 %collective-permute-done.14 = bf16[1024]{0:T(1024)(128)(2,1)S(1)} collective-permute-done((bf16[1024]{0:T(1024)(128)(2,1)S(1)}, bf16[1024]{0:T(1024)(128)(2,1)S(1)}, u32[]{:S(2)}, u32[]{:S(2)}) %collective-permute-start.14) | collective-permute-done | bytes 2080 | tf_op jit(solution)/shard_map/ppermute | solution.py:838
  391.2 21.0 %fusion.27 = f32[1024,2048]{1,0:T(8,128)} fusion(bf16[256,2048]{1,0:T(8,128)(2,1)} %collective-permute-done.5, bf16[256,2048]{1,0:T(8,128)(2,1)} %collective-permute-done.4, bf16[256,2048]{1,0:T(8,128)(2,1)} %collective-permute-done.3, bf16[256,2048]{1,0:T(8,128)(2,1)} %multiply_convert_fusion.3, bf16[1024,2048]{0,1:T(8,128)(2,1)} %collective-permute-done.6, ...), kind=kOutput, calls=%fused_computation.84 | convolution fusion | flops 8661237760 | bytes 20971520 | tf_op jit(solution)/shard_map/dot_general | solution.py:1442
  412.2 13.1 %multiply_convert_fusion.1 = (bf16[1024,1024]{1,0:T(8,128)(2,1)}, bf16[1024,1024]{1,0:T(8,128)(2,1)}, bf16[1024,1024]{1,0:T(8,128)(2,1)}) fusion(f32[1024,2048]{1,0:T(8,128)} %fusion.27, bf16[1024,2048]{1,0:T(8,128)(2,1)S(1)} %bitcast.237, bf16[256,2048]{1,0:T(8,128)(2,1)S(1)} %collective-permute-done.11, bf16[256,2048]{1,0:T(8,128)(2,1)} %collective-permute-done.10, ...), kind=kOutput, calls=%fused_computation.24 | convolution fusion | flops 4327473152 | bytes 23068672 | tf_op jit(solution)/shard_map/dot_general | solution.py:413
  425.3 18.0 %convolution_convert_fusion.2 = bf16[1024,2048]{1,0:T(8,128)(2,1)} fusion(bf16[1024,1024]{1,0:T(8,128)(2,1)} %get-tuple-element.44, bf16[1024,1024]{1,0:T(8,128)(2,1)} %get-tuple-element.43, bf16[1024,2048]{0,1:T(8,128)(2,1)} %collective-permute-done.6, bf16[1024,1024]{0,1:T(8,128)(2,1)} %bitcast.249, bf16[1024,1024]{0,1:T(8,128)(2,1)} %bitcast.251, ...), kind=kOutput, calls=%fused_computation.28 | convolution fusion | flops 8654946304 | bytes 16777216 | tf_op jit(solution)/shard_map/dot_general | solution.py:413
  443.3 3.4 slice_bitcast_fusion.1
  446.8 6.3 convolution_convert_fusion.4
  455.2 12.3 %convolution_convert_fusion = bf16[2048,2048]{1,0:T(8,128)(2,1)S(1)} fusion(bf16[1024,1024]{1,0:T(8,128)(2,1)} %get-tuple-element.44, bf16[1024,1024]{1,0:T(8,128)(2,1)} %get-tuple-element.43, bf16[256,2048]{1,0:T(8,128)(2,1)} %collective-permute-done.5, bf16[256,2048]{1,0:T(8,128)(2,1)} %collective-permute-done.4, ...), kind=kOutput, calls=%fused_computation.6 | convolution fusion | flops 8619294720 | bytes 16777216 | tf_op jit(solution)/shard_map/dot_general | solution.py:413
  467.5 2.5 dynamic-slice_bitcast_fusion
  470.0 2.6 copy-done.12
  474.2 6.2 convolution_convert_fusion.3
  482.5 2.2 convert_add_fusion.5
  485.6 2.2 convert_add_fusion.6
  489.5 120.8 %collective-permute-done.26 = bf16[1,4,128,2048]{3,2,1,0:T(8,128)(2,1)S(1)} collective-permute-done((bf16[1,4,128,2048]{3,2,1,0:T(8,128)(2,1)S(1)}, bf16[1,4,128,2048]{3,2,1,0:T(8,128)(2,1)S(1)}, u32[]{:S(2)}, u32[]{:S(2)}) %collective-permute-start.26) | collective-permute-done | bytes 2097184 | tf_op jit(solution)/shard_map/ppermute | solution.py:838
  614.4 4.2 multiply_add_fusion
  619.1 2.6 fusion.18
  623.3 4.3 all-to-all-start.1
  627.6 17.3 %collective-permute-done.27 = bf16[1,2,128,2048]{3,2,1,0:T(8,128)(2,1)} collective-permute-done((bf16[1,2,128,2048]{3,2,1,0:T(8,128)(2,1)}, bf16[1,2,128,2048]{3,2,1,0:T(8,128)(2,1)}, u32[]{:S(2)}, u32[]{:S(2)}) %collective-permute-start.27) | collective-permute-done | bytes 1048608 | tf_op jit(solution)/shard_map/ppermute | solution.py:838
  645.0 2.1 fusion.11
  647.1 4.2 collective-permute-start.28
  651.3 2.4 convolution_convert_fusion.1
  653.8 2.5 dynamic-slice_bitcast_fusion.1
  658.3 18.0 %collective-permute-done.28 = bf16[1,1,128,2048]{3,2,1,0:T(8,128)(2,1)S(1)} collective-permute-done((bf16[1,1,128,2048]{3,2,1,0:T(8,128)(2,1)S(1)}, bf16[1,1,128,2048]{3,2,1,0:T(8,128)(2,1)S(1)}, u32[]{:S(2)}, u32[]{:S(2)}) %collective-permute-start.28) | collective-permute-done | bytes 524320 | tf_op jit(solution)/shard_map/ppermute | solution.py:838
  677.4 4.1 fusion
  685.1 63.9 %attend_back.1 = bf16[32,128,384]{2,1,0:T(8,128)(2,1)} custom-call(s32[32]{0:T(128)} %fusion.38.slot_ref, s32[16]{0:T(128)} %get-tuple-element.42.first_ref, s32[16]{0:T(128)} %get-tuple-element.41.plain_ref, f32[128,128]{1,0:T(8,128)} %get-tuple-element.66.cos_unit, f32[128,128]{1,0:T(8,128)} %get-tuple-element.65.sin_unit, ...), custom_call_target="tpu_custom_call" | custom-call | flops 49999998976 | bytes 16777216 | tf_op jit(solution)/shard_map/attend_back/pallas_call | solution.py:768
  748.9 113.4 %scatter_heads.1 = (f32[2,128,2048]{2,1,0:T(8,128)}, bf16[16,64,384]{2,1,0:T(8,128)(2,1)}) custom-call(bf16[16,256,384]{2,1,0:T(8,128)(2,1)} %bitcast.264, bf16[2,1024,384]{2,1,0:T(8,128)(2,1)} %get-tuple-element.29.weight_ref, bf16[16,256,2048]{2,1,0:T(8,128)(2,1)} %get-tuple-element.30.normed_ref), custom_call_target="tpu_custom_call" | custom-call | flops 14000000000 | bytes 262144000 | tf_op jit(solution)/shard_map/scatter_heads/pallas_call | solution.py:1338
  862.4 3.7 reshape.594
  866.1 4.7 fusion.53
  872.0 5.4 fusion.1
  879.6 2.4 fusion.3
  885.9 44.0 %collective-permute-done.22 = bf16[2,1,2,64,2048]{4,3,2,1,0:T(8,128)(2,1)S(1)} collective-permute-done((bf16[2,1,2,64,2048]{4,3,2,1,0:T(8,128)(2,1)S(1)}, bf16[2,1,2,64,2048]{4,3,2,1,0:T(8,128)(2,1)S(1)}, u32[]{:S(2)}, u32[]{:S(2)}) %collective-permute-start.22) | collective-permute-done | bytes 1048608 | tf_op jit(solution)/shard_map/ppermute | solution.py:838
  937.5 6.8 collective-permute-done.24
  946.1 10.6 %collective-permute-done.17 = bf16[1,4,64,2048]{3,2,1,0:T(8,128)(2,1)S(1)} collective-permute-done((bf16[1,4,64,2048]{3,2,1,0:T(8,128)(2,1)S(1)}, bf16[1,4,64,2048]{3,2,1,0:T(8,128)(2,1)S(1)}, u32[]{:S(2)}, u32[]{:S(2)}) %collective-permute-start.17) | collective-permute-done | bytes 1048608 | tf_op jit(solution)/shard_map/ppermute | solution.py:838
  961.2 3.4 copy.90
  968.3 3.0 collective-permute-done.18
  976.3 9.4 collective-permute-done.19
  (191 shorter events, 67.6 us)
Async XLA Ops:
  0.6 11.3 %copy-start = (s32[2,4]{1,0:T(2,128)S(1)}, s32[2,4]{1,0:T(2,128)}, u32[]{:S(2)}) copy-start(s32[2,4]{1,0:T(2,128)} %param.23) | copy-start | bytes 100
  7.1 9.2 copy-start.23
  8.8 146.6 %collective-permute-start = (bf16[512,2048]{0,1:T(8,128)(2,1)S(1)}, bf16[512,2048]{0,1:T(8,128)(2,1)}, u32[]{:S(2)}, u32[]{:S(2)}) collective-permute-start(bf16[512,2048]{0,1:T(8,128)(2,1)S(1)} %constant_dynamic-slice_fusion.8), channel_id=1, source_target_pairs={{0,16},{1,17},{2,18},{3,19},{4,20},{5,21},{6,22},{7,23},{8,24},{9,... | collective-permute-start | bytes 6291464 | tf_op jit(solution)/shard_map/ppermute | solution.py:838
  155.4 97.9 %collective-permute-start.1 = (bf16[512,2048]{0,1:T(8,128)(2,1)}, bf16[512,2048]{0,1:T(8,128)(2,1)}, u32[]{:S(2)}, u32[]{:S(2)}) collective-permute-start(bf16[512,2048]{0,1:T(8,128)(2,1)} %collective-permute-done), channel_id=1, source_target_pairs={{0,1},{1,0},{2,3},{3,2},{4,5},{5,4},{6,7},{7,6},{8,9},{9,8},{10,11... | collective-permute-start | bytes 6291464 | tf_op jit(solution)/shard_map/ppermute | solution.py:838
  156.1 61.3 %copy-start.26 = (bf16[1024]{0:T(1024)(128)(2,1)S(1)}, bf16[1024]{0:T(1024)(128)(2,1)}, u32[]{:S(2)}) copy-start(bf16[1024]{0:T(1024)(128)(2,1)} %param.18) | copy-start | bytes 6148
  213.9 38.7 %all-to-all-start = ((bf16[32,128,128]{2,1,0:T(8,128)(2,1)}), bf16[32,128,128]{2,1,0:T(8,128)(2,1)S(1)}, u32[]{:S(2)}, u32[]{:S(2)}) async-start(bf16[32,128,128]{2,1,0:T(8,128)(2,1)} %get-tuple-element.23), calls=%async_computation | async-start | bytes 2097152 | tf_op jit(solution)/shard_map/all_to_all | solution.py:1433
  217.5 35.1 %collective-permute-start.2 = (bf16[1024]{0:T(1024)(128)(2,1)S(1)}, bf16[1024]{0:T(1024)(128)(2,1)S(1)}, u32[]{:S(2)}, u32[]{:S(2)}) collective-permute-start(bf16[1024]{0:T(1024)(128)(2,1)S(1)} %copy-done.26), channel_id=1, source_target_pairs={{0,16},{1,17},{2,18},{3,19},{4,20},{5,21},{6,22},{7,23},{8,24},{9,... | collective-permute-start | bytes 6152 | tf_op jit(solution)/shard_map/ppermute | solution.py:838
  252.4 138.7 %collective-permute-start.6 = (bf16[1024,2048]{0,1:T(8,128)(2,1)}, bf16[1024,2048]{0,1:T(8,128)(2,1)}, u32[]{:S(2)}, u32[]{:S(2)}) collective-permute-start(bf16[1024,2048]{0,1:T(8,128)(2,1)} %pad_maximum_fusion.1), channel_id=1, source_target_pairs={{0,16},{1,17},{2,18},{3,19},{4,20},{5,21},{6,22},{7,23},{8,24},{9,... | collective-permute-start | bytes 12582920 | tf_op jit(solution)/shard_map/ppermute | solution.py:838
  261.9 351.8 %copy-start.3 = (f32[256,2048]{1,0:T(8,128)}, f32[256,2048]{1,0:T(8,128)S(1)}, u32[]{:S(2)}) copy-start(f32[256,2048]{1,0:T(8,128)S(1)} %get-tuple-element.70) | copy-start | bytes 6291460
  263.4 105.3 %collective-permute-start.4 = (bf16[256,2048]{1,0:T(8,128)(2,1)}, bf16[256,2048]{1,0:T(8,128)(2,1)}, u32[]{:S(2)}, u32[]{:S(2)}) collective-permute-start(bf16[256,2048]{1,0:T(8,128)(2,1)} %multiply_convert_fusion.3), channel_id=1, source_target_pairs={{0,16},{1,17},{2,18},{3,19},{4,20},{5,21},{6,22},{7,23},{8,24},{9,... | collective-permute-start | bytes 3145736 | tf_op jit(solution)/shard_map/ppermute | solution.py:838
  265.2 125.4 %collective-permute-start.10 = (bf16[256,2048]{1,0:T(8,128)(2,1)}, bf16[256,2048]{1,0:T(8,128)(2,1)}, u32[]{:S(2)}, u32[]{:S(2)}) collective-permute-start(bf16[256,2048]{1,0:T(8,128)(2,1)} %bitcast.21), channel_id=1, source_target_pairs={{0,16},{1,17},{2,18},{3,19},{4,20},{5,21},{6,22},{7,23},{8,24},{9,... | collective-permute-start | bytes 3145736 | tf_op jit(solution)/shard_map/ppermute | solution.py:838
  265.4 125.7 %collective-permute-start.3 = (bf16[256,2048]{1,0:T(8,128)(2,1)}, bf16[256,2048]{1,0:T(8,128)(2,1)}, u32[]{:S(2)}, u32[]{:S(2)}) collective-permute-start(bf16[256,2048]{1,0:T(8,128)(2,1)} %multiply_convert_fusion.3), channel_id=1, source_target_pairs={{0,1},{1,0},{2,3},{3,2},{4,5},{5,4},{6,7},{7,6},{8,9},{9,8},{10,11... | collective-permute-start | bytes 3145736 | tf_op jit(solution)/shard_map/ppermute | solution.py:838
  368.6 22.5 %collective-permute-start.5 = (bf16[256,2048]{1,0:T(8,128)(2,1)}, bf16[256,2048]{1,0:T(8,128)(2,1)}, u32[]{:S(2)}, u32[]{:S(2)}) collective-permute-start(bf16[256,2048]{1,0:T(8,128)(2,1)} %collective-permute-done.4), channel_id=1, source_target_pairs={{0,1},{1,0},{2,3},{3,2},{4,5},{5,4},{6,7},{7,6},{8,9},{9,8},{10,11... | collective-permute-start | bytes 3145736 | tf_op jit(solution)/shard_map/ppermute | solution.py:838
  368.6 21.4 %collective-permute-start.14 = (bf16[1024]{0:T(1024)(128)(2,1)S(1)}, bf16[1024]{0:T(1024)(128)(2,1)S(1)}, u32[]{:S(2)}, u32[]{:S(2)}) collective-permute-start(bf16[1024]{0:T(1024)(128)(2,1)S(1)} %copy-done.23), channel_id=1, source_target_pairs={{0,16},{1,17},{2,18},{3,19},{4,20},{5,21},{6,22},{7,23},{8,24},{9,... | collective-permute-start | bytes 6152 | tf_op jit(solution)/shard_map/ppermute | solution.py:838
  390.0 22.2 %collective-permute-start.9 = (bf16[256,2048]{1,0:T(8,128)(2,1)}, bf16[256,2048]{1,0:T(8,128)(2,1)S(1)}, u32[]{:S(2)}, u32[]{:S(2)}) collective-permute-start(bf16[256,2048]{1,0:T(8,128)(2,1)} %bitcast.21), channel_id=1, source_target_pairs={{0,1},{1,0},{2,3},{3,2},{4,5},{5,4},{6,7},{7,6},{8,9},{9,8},{10,11... | collective-permute-start | bytes 3145736 | tf_op jit(solution)/shard_map/ppermute | solution.py:838
  390.6 21.6 %collective-permute-start.11 = (bf16[256,2048]{1,0:T(8,128)(2,1)}, bf16[256,2048]{1,0:T(8,128)(2,1)S(1)}, u32[]{:S(2)}, u32[]{:S(2)}) collective-permute-start(bf16[256,2048]{1,0:T(8,128)(2,1)} %collective-permute-done.10), channel_id=1, source_target_pairs={{0,1},{1,0},{2,3},{3,2},{4,5},{5,4},{6,7},{7,6},{8,9},{9,8},{10,11... | collective-permute-start | bytes 3145736 | tf_op jit(solution)/shard_map/ppermute | solution.py:838
  391.1 21.1 %copy-start.17 = (bf16[8,1,128,2048]{3,2,1,0:T(8,128)(2,1)S(1)}, bf16[8,1,128,2048]{3,2,1,0:T(8,128)(2,1)}, u32[]{:S(2)}) copy-start(bf16[8,1,128,2048]{3,2,1,0:T(8,128)(2,1)} %constant_dynamic-slice_fusion.3) | copy-start | bytes 12582916
  412.2 13.1 %copy-start.27 = (bf16[256,2048]{1,0:T(8,128)(2,1)}, bf16[256,2048]{1,0:T(8,128)(2,1)S(1)}, u32[]{:S(2)}) copy-start(bf16[256,2048]{1,0:T(8,128)(2,1)S(1)} %collective-permute-done.11) | copy-start | bytes 3145732
  446.7 34.4 %collective-permute-start.12 = (bf16[2,256,2048]{2,1,0:T(8,128)(2,1)}, bf16[2,256,2048]{2,1,0:T(8,128)(2,1)}, u32[]{:S(2)}, u32[]{:S(2)}) collective-permute-start(bf16[2,256,2048]{2,1,0:T(8,128)(2,1)} %slice_bitcast_fusion.1), channel_id=1, source_target_pairs={{0,1},{1,0},{2,3},{3,2},{4,5},{5,4},{6,7},{7,6},{8,9},{9,8},{10,11... | collective-permute-start | bytes 6291464 | tf_op jit(solution)/shard_map/ppermute | solution.py:838
  454.7 30.9 %collective-permute-start.7 = (bf16[2,256,2048]{2,1,0:T(8,128)(2,1)}, bf16[2,256,2048]{2,1,0:T(8,128)(2,1)}, u32[]{:S(2)}, u32[]{:S(2)}) collective-permute-start(bf16[2,256,2048]{2,1,0:T(8,128)(2,1)} %slice_bitcast_fusion.4), channel_id=1, source_target_pairs={{0,1},{1,0},{2,3},{3,2},{4,5},{5,4},{6,7},{7,6},{8,9},{9,8},{10,11... | collective-permute-start | bytes 6291464 | tf_op jit(solution)/shard_map/ppermute | solution.py:838
  467.5 6.7 copy-start.28
  467.5 6.7 copy-start.29
  472.7 204.7 %collective-permute-start.20 = (bf16[2,4,2,64,2048]{4,3,2,1,0:T(8,128)(2,1)}, bf16[2,4,2,64,2048]{4,3,2,1,0:T(8,128)(2,1)}, u32[]{:S(2)}, u32[]{:S(2)}) collective-permute-start(bf16[2,4,2,64,2048]{4,3,2,1,0:T(8,128)(2,1)} %dynamic-slice_bitcast_fusion), channel_id=1, source_target_pairs={{0,2},{1,3},{2,0},{3,1},{4,6},{5,7},{6,4},{7,5},{8,10},{9,11},{10,... | collective-permute-start | bytes 12582920 | tf_op jit(solution)/shard_map/ppermute | solution.py:838
  480.5 129.8 %collective-permute-start.26 = (bf16[1,4,128,2048]{3,2,1,0:T(8,128)(2,1)S(1)}, bf16[1,4,128,2048]{3,2,1,0:T(8,128)(2,1)S(1)}, u32[]{:S(2)}, u32[]{:S(2)}) collective-permute-start(bf16[1,4,128,2048]{3,2,1,0:T(8,128)(2,1)S(1)} %dynamic-slice_bitcast_fusion.2), channel_id=1, source_target_pairs={{0,2},{1,3},{2,0},{3,1},{4,6},{5,7},{6,4},{7,5},{8,10},{9,11},{10,... | collective-permute-start | bytes 6291464 | tf_op jit(solution)/shard_map/ppermute | solution.py:838
  484.9 128.8 %collective-permute-start.13 = (bf16[256,2048]{1,0:T(8,128)(2,1)S(1)}, bf16[256,2048]{1,0:T(8,128)(2,1)S(1)}, u32[]{:S(2)}, u32[]{:S(2)}) collective-permute-start(bf16[256,2048]{1,0:T(8,128)(2,1)S(1)} %fusion.20), channel_id=1, source_target_pairs={{0,16},{1,17},{2,18},{3,19},{4,20},{5,21},{6,22},{7,23},{8,24},{9,... | collective-permute-start | bytes 3145736 | tf_op jit(solution)/shard_map/ppermute | solution.py:838
  488.0 126.4 %collective-permute-start.8 = (bf16[256,2048]{1,0:T(8,128)(2,1)S(1)}, bf16[256,2048]{1,0:T(8,128)(2,1)S(1)}, u32[]{:S(2)}, u32[]{:S(2)}) collective-permute-start(bf16[256,2048]{1,0:T(8,128)(2,1)S(1)} %fusion.19), channel_id=1, source_target_pairs={{0,16},{1,17},{2,18},{3,19},{4,20},{5,21},{6,22},{7,23},{8,24},{9,... | collective-permute-start | bytes 3145736 | tf_op jit(solution)/shard_map/ppermute | solution.py:838
  612.3 32.7 %collective-permute-start.27 = (bf16[1,2,128,2048]{3,2,1,0:T(8,128)(2,1)}, bf16[1,2,128,2048]{3,2,1,0:T(8,128)(2,1)}, u32[]{:S(2)}, u32[]{:S(2)}) collective-permute-start(bf16[1,2,128,2048]{3,2,1,0:T(8,128)(2,1)} %dynamic-slice_bitcast_fusion.5), channel_id=1, source_target_pairs={{0,4},{1,5},{2,6},{3,7},{4,0},{5,1},{6,2},{7,3},{8,12},{9,13},{10,... | collective-permute-start | bytes 3145736 | tf_op jit(solution)/shard_map/ppermute | solution.py:838
  622.0 29.3 %copy-start.14 = (bf16[2,16,128,128]{3,1,2,0:T(8,128)(2,1)S(1)}, bf16[2,16,128,128]{3,1,2,0:T(8,128)(2,1)}, u32[]{:S(2)}) copy-start(bf16[2,16,128,128]{3,1,2,0:T(8,128)(2,1)} %copy-done.13) | copy-start | bytes 3145732
  623.3 61.8 %all-to-all-start.1 = ((bf16[32,128,128]{2,1,0:T(8,128)(2,1)}), bf16[32,128,128]{2,1,0:T(8,128)(2,1)}, u32[]{:S(2)}, u32[]{:S(2)}) async-start(bf16[32,128,128]{2,1,0:T(8,128)(2,1)} %bitcast.240), calls=%async_computation.1 | async-start | bytes 2097152 | tf_op jit(solution)/shard_map/all_to_all | solution.py:1463
  645.0 32.4 %slice-start = ((s8[8388608]{0:T(1024)(128)(4,1)}), s8[4194304]{0:T(1024)(128)(4,1)S(1)}, s32[]{:S(2)}) async-start(s8[8388608]{0:T(1024)(128)(4,1)} %bitcast.227), calls=%async_computation.2 | async-start | bytes 8388608
  647.1 30.3 %slice-start.1 = ((s8[8388608]{0:T(1024)(128)(4,1)}), s8[4194304]{0:T(1024)(128)(4,1)S(1)}, s32[]{:S(2)}) async-start(s8[8388608]{0:T(1024)(128)(4,1)} %bitcast.227), calls=%async_computation.3 | async-start | bytes 8388608
  647.1 29.2 %collective-permute-start.28 = (bf16[1,1,128,2048]{3,2,1,0:T(8,128)(2,1)S(1)}, bf16[1,1,128,2048]{3,2,1,0:T(8,128)(2,1)S(1)}, u32[]{:S(2)}, u32[]{:S(2)}) collective-permute-start(bf16[1,1,128,2048]{3,2,1,0:T(8,128)(2,1)S(1)} %constant_dynamic-slice_fusion), channel_id=1, source_target_pairs={{0,8},{1,9},{2,10},{3,11},{4,12},{5,13},{6,14},{7,15},{8,0},{9,1},... | collective-permute-start | bytes 1572872 | tf_op jit(solution)/shard_map/ppermute | solution.py:838
  658.3 213.7 %collective-permute-start.15 = (bf16[2,8,64,2048]{3,2,1,0:T(8,128)(2,1)}, bf16[2,8,64,2048]{3,2,1,0:T(8,128)(2,1)}, u32[]{:S(2)}, u32[]{:S(2)}) collective-permute-start(bf16[2,8,64,2048]{3,2,1,0:T(8,128)(2,1)} %dynamic-slice_bitcast_fusion.1), channel_id=1, source_target_pairs={{0,1},{1,0},{2,3},{3,2},{4,5},{5,4},{6,7},{7,6},{8,9},{9,8},{10,11... | collective-permute-start | bytes 12582920 | tf_op jit(solution)/shard_map/ppermute | solution.py:838
  685.1 192.8 %collective-permute-start.21 = (bf16[2,2,2,64,2048]{4,3,2,1,0:T(8,128)(2,1)}, bf16[2,2,2,64,2048]{4,3,2,1,0:T(8,128)(2,1)}, u32[]{:S(2)}, u32[]{:S(2)}) collective-permute-start(bf16[2,2,2,64,2048]{4,3,2,1,0:T(8,128)(2,1)} %dynamic-slice_bitcast_fusion.3), channel_id=1, source_target_pairs={{0,4},{1,5},{2,6},{3,7},{4,0},{5,1},{6,2},{7,3},{8,12},{9,13},{10,... | collective-permute-start | bytes 6291464 | tf_op jit(solution)/shard_map/ppermute | solution.py:838
  862.4 9.1 copy-start.9
  862.4 9.1 copy-start.22
  862.4 9.1 copy-start.25
  877.7 52.7 %collective-permute-start.16 = (bf16[8,64,2048]{2,1,0:T(8,128)(2,1)S(1)}, bf16[8,64,2048]{2,1,0:T(8,128)(2,1)S(1)}, u32[]{:S(2)}, u32[]{:S(2)}) collective-permute-start(bf16[8,64,2048]{2,1,0:T(8,128)(2,1)S(1)} %dynamic-slice_bitcast_fusion.4), channel_id=1, source_target_pairs={{0,16},{1,17},{2,18},{3,19},{4,20},{5,21},{6,22},{7,23},{8,24},{9,... | collective-permute-start | bytes 6291464 | tf_op jit(solution)/shard_map/ppermute | solution.py:838
  882.1 47.8 %collective-permute-start.22 = (bf16[2,1,2,64,2048]{4,3,2,1,0:T(8,128)(2,1)S(1)}, bf16[2,1,2,64,2048]{4,3,2,1,0:T(8,128)(2,1)S(1)}, u32[]{:S(2)}, u32[]{:S(2)}) collective-permute-start(bf16[2,1,2,64,2048]{4,3,2,1,0:T(8,128)(2,1)S(1)} %constant_dynamic-slice_fusion.1), channel_id=1, source_target_pairs={{0,8},{1,9},{2,10},{3,11},{4,12},{5,13},{6,14},{7,15},{8,0},{9,1},... | collective-permute-start | bytes 3145736 | tf_op jit(solution)/shard_map/ppermute | solution.py:838
  930.4 13.9 %collective-permute-start.24 = (bf16[2,64,2048]{2,1,0:T(8,128)(2,1)S(1)}, bf16[2,64,2048]{2,1,0:T(8,128)(2,1)S(1)}, u32[]{:S(2)}, u32[]{:S(2)}) collective-permute-start(bf16[2,64,2048]{2,1,0:T(8,128)(2,1)S(1)} %dynamic-slice_bitcast_fusion.7), channel_id=1, source_target_pairs={{0,16},{1,17},{2,18},{3,19},{4,20},{5,21},{6,22},{7,23},{8,24},{9,... | collective-permute-start | bytes 1572872 | tf_op jit(solution)/shard_map/ppermute | solution.py:838
  931.5 25.2 %collective-permute-start.17 = (bf16[1,4,64,2048]{3,2,1,0:T(8,128)(2,1)S(1)}, bf16[1,4,64,2048]{3,2,1,0:T(8,128)(2,1)S(1)}, u32[]{:S(2)}, u32[]{:S(2)}) collective-permute-start(bf16[1,4,64,2048]{3,2,1,0:T(8,128)(2,1)S(1)} %dynamic-slice_bitcast_fusion.6), channel_id=1, source_target_pairs={{0,2},{1,3},{2,0},{3,1},{4,6},{5,7},{6,4},{7,5},{8,10},{9,11},{10,... | collective-permute-start | bytes 3145736 | tf_op jit(solution)/shard_map/ppermute | solution.py:838
  937.4 8.3 collective-permute-start.23
  944.4 1.6 collective-permute-start.25
  957.9 13.4 %collective-permute-start.18 = (bf16[1,2,64,2048]{3,2,1,0:T(8,128)(2,1)}, bf16[1,2,64,2048]{3,2,1,0:T(8,128)(2,1)}, u32[]{:S(2)}, u32[]{:S(2)}) collective-permute-start(bf16[1,2,64,2048]{3,2,1,0:T(8,128)(2,1)} %dynamic-slice_bitcast_fusion.8), channel_id=1, source_target_pairs={{0,4},{1,5},{2,6},{3,7},{4,0},{5,1},{6,2},{7,3},{8,12},{9,13},{10,... | collective-permute-start | bytes 1572872 | tf_op jit(solution)/shard_map/ppermute | solution.py:838
  961.2 13.8 %copy-start.19 = (f32[64,4096]{1,0:T(8,128)}, f32[64,4096]{1,0:T(8,128)S(1)}, u32[]{:S(2)}) copy-start(f32[64,4096]{1,0:T(8,128)S(1)} %squeeze.136) | copy-start | bytes 3145732
  961.2 25.3 %copy-start.1 = (s32[2,4]{1,0:T(2,128)S(1)}, s32[2,4]{1,0:T(2,128)}, u32[]{:S(2)}) copy-start(s32[2,4]{1,0:T(2,128)} %param.23) | copy-start | bytes 100
  966.7 19.8 %copy-start.20 = (f32[64,4096]{1,0:T(8,128)}, f32[64,4096]{1,0:T(8,128)S(1)}, u32[]{:S(2)}) copy-start(f32[64,4096]{1,0:T(8,128)S(1)} %squeeze.137) | copy-start | bytes 3145732
  972.6 13.1 %collective-permute-start.19 = (bf16[1,1,64,2048]{3,2,1,0:T(8,128)(2,1)S(1)}, bf16[1,1,64,2048]{3,2,1,0:T(8,128)(2,1)S(1)}, u32[]{:S(2)}, u32[]{:S(2)}) collective-permute-start(bf16[1,1,64,2048]{3,2,1,0:T(8,128)(2,1)S(1)} %constant_dynamic-slice_fusion.2), channel_id=1, source_target_pairs={{0,8},{1,9},{2,10},{3,11},{4,12},{5,13},{6,14},{7,15},{8,0},{9,1},... | collective-permute-start | bytes 786440 | tf_op jit(solution)/shard_map/ppermute | solution.py:838
  (15 other events, 62.9 us)

commit v3 on v2

--- a/solution.py
+++ b/solution.py
@@ -911,9 +911,12 @@
     w_query,
     w_key,
     w_value,
+    w_gate,
+    w_up,
     normed_out,
     qkv_ref,
     weight_ref,
+    in_ref,
     raw,
     normed,
     gains,
@@ -923,8 +926,12 @@
     recv_sem,
     side_send,
     side_recv,
+    stripe_sem,
+    stripe_send,
+    stripe_recv,
 ):
     here, there = lax.axis_index("grp"), lax.axis_index("rep")
+    core = there % 2
     reps = raw.shape[0]
     slots = normed.shape[0]
     row_count, width = raw.shape[2:]
@@ -1003,6 +1010,34 @@
         one.wait()
     weight_copy = side(1, weight_ref.at[here], weight_ref.at[here])
     weight_copy.start()
+
+    stripes = reps // 2
+    own_width = in_ref.shape[2] // 2
+    stripe_copies, stripe_loads = [], []
+    for kind, weight in enumerate((w_gate, w_up)):
+        for at in range(stripes):
+            target_ref = in_ref.at[here, :, pl.ds(kind * own_width + at * LANES, LANES)]
+            number = kind * stripes + at
+
+            def columns_of(grp):
+                first = (grp * stripes + at) * 2 * LANES + core * LANES
+                return weight.at[:, pl.ds(pl.multiple_of(first, LANES), LANES)]
+
+            stripe_loads.append(
+                pltpu.make_async_copy(columns_of(here), target_ref, stripe_sem.at[number])
+            )
+            stripe_copies.append(
+                pltpu.make_async_remote_copy(
+                    src_ref=columns_of(1 - here),
+                    dst_ref=target_ref,
+                    send_sem=stripe_send.at[number],
+                    recv_sem=stripe_recv.at[number],
+                    device_id=across,
+                    device_id_type=MESH_IDS,
+                )
+            )
+    for one in stripe_copies + stripe_loads:
+        one.start()
 
     written = {}
     used = [None] * slots
@@ -1071,9 +1106,11 @@
         one.wait_send()
     gain_copy.wait_send()
     weight_copy.wait_send()
-
-
-def gather_heads(tokens, gain, w_query, w_key, w_value):
+    for one in stripe_copies + stripe_loads:
+        one.wait()
+
+
+def gather_heads(tokens, gain, w_query, w_key, w_value, w_gate, w_up):
     reps = lax.axis_size("rep")
     _, row_count, width = tokens.shape
     half = width // 2
@@ -1086,9 +1123,10 @@
             jax.ShapeDtypeStruct((reps, 2 * row_count, width), jnp.bfloat16),
             jax.ShapeDtypeStruct((2 * reps, row_count, 3 * LANES), jnp.bfloat16),
             jax.ShapeDtypeStruct((2, half, 3 * LANES), jnp.bfloat16),
+            jax.ShapeDtypeStruct((2, half, reps * LANES), jnp.bfloat16),
         ),
-        in_specs=[vmem, vmem, anywhere, anywhere, anywhere],
-        out_specs=(anywhere, vmem, vmem),
+        in_specs=[vmem, vmem] + [anywhere] * 5,
+        out_specs=(anywhere, vmem, vmem, anywhere),
         scratch_shapes=[
             pltpu.VMEM((reps, 2, row_count, width), jnp.bfloat16),
             pltpu.VMEM((4, 2 * row_count, width), jnp.bfloat16),
@@ -1099,6 +1137,9 @@
             pltpu.SemaphoreType.DMA((2 * reps,)),
             pltpu.SemaphoreType.DMA((2,)),
             pltpu.SemaphoreType.DMA((2,)),
+            pltpu.SemaphoreType.DMA((reps,)),
+            pltpu.SemaphoreType.DMA((reps,)),
+            pltpu.SemaphoreType.DMA((reps,)),
         ],
         compiler_params=pltpu.CompilerParams(
             vmem_limit_bytes=KERNEL_VMEM, collective_id=0, has_side_effects=True
@@ -1107,7 +1148,7 @@
             flops=8 * 10**9, bytes_accessed=250 << 20, transcendentals=0
         ),
         name="gather_heads",
-    )(tokens, gain_rows, w_query, w_key, w_value)
+    )(tokens, gain_rows, w_query, w_key, w_value, w_gate, w_up)
 
 
 def scatter_kernel(
@@ -1371,6 +1412,295 @@
     )(back, weights, normed)
 
 
+def mlp_kernel(
+    returned_ref,
+    tokens_ref,
+    gain_ref,
+    out_ref,
+    output_own,
+    output_other,
+    in_ref,
+    down_weight,
+    mixed_ref,
+    mid_ref,
+    hidden_ref,
+    slope_ref,
+    down_ref,
+    grad_ref,
+    branch_ref,
+    att_ref,
+    attended,
+    w_output,
+    w_in,
+    w_out,
+    near_away,
+    near_landed,
+    far_away,
+    far_landed,
+    down_away,
+    down_landed,
+    load_sem,
+    stripe_sem,
+    send_sem,
+    recv_sem,
+):
+    here, there = lax.axis_index("grp"), lax.axis_index("rep")
+    core = there % 2
+    across = (1 - here, there)
+    sibling = (here, flipped(there, 1))
+    groups, heads, row_count, _ = returned_ref.shape
+    rows, width = tokens_ref.shape
+    half = width // 2
+    own_width = w_out.shape[0]
+    stripes = own_width // LANES
+
+    loads = [
+        pltpu.make_async_copy(output_own, w_output.at[here], load_sem.at[0]),
+        pltpu.make_async_copy(output_other, w_output.at[1 - here], load_sem.at[1]),
+        pltpu.make_async_copy(in_ref, w_in, load_sem.at[2]),
+    ]
+    for at in range(stripes):
+        loads.append(
+            pltpu.make_async_copy(
+                down_weight.at[pl.ds(pl.multiple_of((2 * at + core) * LANES, LANES), LANES)],
+                w_out.at[pl.ds(at * LANES, LANES)],
+                stripe_sem.at[at],
+            )
+        )
+    for one in loads:
+        one.start()
+    barrier = pltpu.get_barrier_semaphore()
+    for target in (across, sibling):
+        pl.semaphore_signal(barrier, inc=1, device_id=target, device_id_type=MESH_IDS)
+    pl.semaphore_wait(barrier, 2)
+
+    def copy(at, source, target_ref, target):
+        return pltpu.make_async_remote_copy(
+            src_ref=source,
+            dst_ref=target_ref,
+            send_sem=send_sem.at[at],
+            recv_sem=recv_sem.at[at],
+            device_id=target,
+            device_id_type=MESH_IDS,
+        )
+
+    mid_near = copy(0, mid_ref.at[0], mid_ref.at[1], sibling)
+    mid_far = copy(1, mid_ref.at[0], mid_ref.at[2], across)
+    mid_on = copy(2, mid_ref.at[2], mid_ref.at[3], sibling)
+    grad_near = [copy(3 + at, near_away.at[at], near_landed.at[at], sibling) for at in range(2)]
+    grad_far = copy(5, far_away, far_landed, across)
+    down_near = [copy(6 + at, down_away.at[at], down_landed.at[at], sibling) for at in range(2)]
+
+    for group in range(groups):
+        for head in range(heads):
+            attended[
+                group * row_count : (group + 1) * row_count, head * LANES : (head + 1) * LANES
+            ] = returned_ref[group, head]
+    loads[0].wait()
+    loads[1].wait()
+    wide = 512
+
+    def mix(at, unused):
+        cut = pl.ds(pl.multiple_of(at * wide, wide), wide)
+        mixed_ref[:, cut] = (
+            tokens_ref[:, cut].astype(jnp.float32)
+            + jnp.dot(attended[:, :half], w_output[0, :, cut], preferred_element_type=jnp.float32)
+            + jnp.dot(attended[:, half:], w_output[1, :, cut], preferred_element_type=jnp.float32)
+        )
+        return unused
+
+    lax.fori_loop(0, width // wide, mix, 0)
+    tile = 32
+
+    def norm_rows(at, unused):
+        cut = pl.ds(pl.multiple_of(at * tile, tile), tile)
+        values = mixed_ref[cut, :]
+        mid_ref[0, cut, :] = (values * rms_scale(values) * gain_ref[0:1, :]).astype(jnp.bfloat16)
+        return unused
+
+    lax.fori_loop(0, rows // tile, norm_rows, 0)
+    mid_far.start()
+    mid_near.start()
+    for one in loads[2:]:
+        one.wait()
+    narrow_tile = 256
+
+    def forward(slot):
+        def columns(at, unused):
+            cut = pl.ds(pl.multiple_of(at * narrow_tile, narrow_tile), narrow_tile)
+            up_cut = pl.ds(pl.multiple_of(own_width + at * narrow_tile, narrow_tile), narrow_tile)
+
+            def project(cols):
+                return jnp.dot(
+                    mid_ref[slot, :, :half], w_in[0, :, cols], preferred_element_type=jnp.float32
+                ) + jnp.dot(
+                    mid_ref[slot, :, half:], w_in[1, :, cols], preferred_element_type=jnp.float32
+                )
+
+            gate_pre, up_pre = project(cut), project(up_cut)
+            grad_hidden = contract(out_ref[slot], w_out[cut, :], 1, 1)
+            gate_sig = jax.nn.sigmoid(gate_pre)
+            gate_silu = gate_pre * gate_sig
+            hidden_ref[slot, :, cut] = (gate_silu * up_pre).astype(jnp.bfloat16)
+            slope_ref[slot, :, cut] = (
+                grad_hidden * up_pre * gate_sig * (1.0 + gate_pre * (1.0 - gate_sig))
+            ).astype(jnp.bfloat16)
+            slope_ref[slot, :, up_cut] = (grad_hidden * gate_silu).astype(jnp.bfloat16)
+            return unused
+
+        lax.fori_loop(0, own_width // narrow_tile, columns, 0)
+
+    def backward(slot, finish):
+        for at in range(2):
+
+            def columns(step, unused):
+                cut = pl.ds(pl.multiple_of(step * wide, wide), wide)
+                whole = pl.ds(pl.multiple_of(at * half + step * wide, wide), wide)
+                finish(whole, contract(slope_ref[slot], w_in[at, cut, :], 1, 1))
+                return unused
+
+            lax.fori_loop(0, half // wide, columns, 0)
+
+    def down(slot, finish):
+        def columns(step, unused):
+            cut = pl.ds(pl.multiple_of(step * wide, wide), wide)
+            finish(
+                cut, jnp.dot(hidden_ref[slot], w_out[:, cut], preferred_element_type=jnp.float32)
+            )
+            return unused
+
+        lax.fori_loop(0, width // wide, columns, 0)
+
+    def into(target, at):
+        def finish(cut, values):
+            target[at, :, cut] = values.astype(jnp.bfloat16)
+
+        return finish
+
+    forward(0)
+    mid_near.wait_recv()
+    forward(1)
+    backward(1, into(near_away, 0))
+    grad_near[0].start()
+
+    def keep(cut, values):
+        grad_ref[:, cut] = values
+
+    backward(0, keep)
+    mid_far.wait_recv()
+    mid_on.start()
+    forward(2)
+    mid_on.wait_recv()
+    forward(3)
+    backward(3, into(near_away, 1))
+    grad_near[1].start()
+    grad_near[1].wait_recv()
+
+    def add_near(cut, values):
+        far_away[:, cut] = (values + near_landed[1, :, cut].astype(jnp.float32)).astype(
+            jnp.bfloat16
+        )
+
+    backward(2, add_near)
+    grad_far.start()
+    for at in range(2):
+        down(2 * at + 1, into(down_away, at))
+        down_near[at].start()
+    for at in range(2):
+        down_near[at].wait_recv()
+
+        def add_down(cut, values):
+            down_ref[at, :, cut] = (values + down_landed[at, :, cut].astype(jnp.float32)).astype(
+                jnp.bfloat16
+            )
+
+        down(2 * at, add_down)
+    grad_near[0].wait_recv()
+    grad_far.wait_recv()
+
+    def norm_back(at, unused):
+        cut = pl.ds(pl.multiple_of(at * tile, tile), tile)
+        grad_mid = (
+            grad_ref[cut, :]
+            + near_landed[0, cut, :].astype(jnp.float32)
+            + far_landed[cut, :].astype(jnp.float32)
+        )
+        values = mixed_ref[cut, :]
+        inverse = rms_scale(values)
+        normed = values * inverse
+        weighted = grad_mid * gain_ref[0:1, :]
+        grad = out_ref[0, cut, :].astype(jnp.float32) + inverse * (
+            weighted - normed * jnp.mean(weighted * normed, axis=-1, keepdims=True)
+        )
+        grad_ref[cut, :] = grad
+        branch_ref[cut, :] = grad.astype(jnp.bfloat16)
+        return unused
+
+    lax.fori_loop(0, rows // tile, norm_back, 0)
+    for head in range(0, heads, 4):
+        at = head * LANES // half
+        start = head * LANES - at * half
+        values = contract(
+            branch_ref[...], w_output[at, pl.ds(start, 4 * LANES), :], 1, 1, jnp.bfloat16
+        )
+        for group in range(groups):
+            for step in range(4):
+                att_ref[group, head + step] = values[
+                    group * row_count : (group + 1) * row_count, step * LANES : (step + 1) * LANES
+                ]
+    for one in [mid_near, mid_far, mid_on, grad_far] + grad_near + down_near:
+        one.wait_send()
+
+
+def mlp(returned, tokens, gain, out_quad, output_own, output_other, w_in, w_down):
+    groups, heads, row_count, _ = returned.shape
+    rows, width = tokens.shape
+    half = width // 2
+    hidden_width = w_in.shape[2]
+    own_width = hidden_width // 2
+    vmem = pl.BlockSpec(memory_space=pltpu.VMEM)
+    anywhere = pl.BlockSpec(memory_space=pl.ANY)
+    low, full = jnp.bfloat16, jnp.float32
+    return pl.pallas_call(
+        mlp_kernel,
+        out_shape=(
+            jax.ShapeDtypeStruct((rows, width), full),
+            jax.ShapeDtypeStruct((4, rows, width), low),
+            jax.ShapeDtypeStruct((4, rows, own_width), low),
+            jax.ShapeDtypeStruct((4, rows, hidden_width), low),
+            jax.ShapeDtypeStruct((2, rows, width), low),
+            jax.ShapeDtypeStruct((rows, width), full),
+            jax.ShapeDtypeStruct((rows, width), low),
+            jax.ShapeDtypeStruct((groups, heads, row_count, LANES), low),
+        ),
+        in_specs=[vmem] * 4 + [anywhere] * 4,
+        out_specs=(vmem,) * 8,
+        scratch_shapes=[
+            pltpu.VMEM((rows, width), low),
+            pltpu.VMEM((2, half, width), low),
+            pltpu.VMEM((2, half, hidden_width), low),
+            pltpu.VMEM((own_width, width), low),
+            pltpu.VMEM((2, rows, width), low),
+            pltpu.VMEM((2, rows, width), low),
+            pltpu.VMEM((rows, width), low),
+            pltpu.VMEM((rows, width), low),
+            pltpu.VMEM((2, rows, width), low),
+            pltpu.VMEM((2, rows, width), low),
+            pltpu.SemaphoreType.DMA((3,)),
+            pltpu.SemaphoreType.DMA((own_width // LANES,)),
+            pltpu.SemaphoreType.DMA((8,)),
+            pltpu.SemaphoreType.DMA((8,)),
+        ],
+        compiler_params=pltpu.CompilerParams(
+            vmem_limit_bytes=60 * 1024 * 1024, collective_id=2, has_side_effects=True
+        ),
+        cost_estimate=pl.CostEstimate(
+            flops=36 * 10**9, bytes_accessed=150 << 20, transcendentals=0
+        ),
+        name="mlp",
+    )(returned, tokens, gain, out_quad, output_own, output_other, w_in, w_down)
+
+
 def heads_body(
     tokens,
     attn_gain,
@@ -1395,7 +1725,9 @@
     own_width = hidden_width // (2 * groups)
     stripes = reps // 2
 
-    gathered_rows, qkv, w_heads = gather_heads(tokens, attn_gain, w_query, w_key, w_value)
+    gathered_rows, qkv, w_heads, w_in = gather_heads(
+        tokens, attn_gain, w_query, w_key, w_value, w_gate, w_up
+    )
     gain_one = ordered(here, attn_gain, swap(attn_gain, 1, 0)).astype(jnp.float32)
     gain_two = ordered(here, mlp_gain, swap(mlp_gain, 1, 0)).astype(jnp.float32)
     inputs = tokens.astype(jnp.float32)
@@ -1404,21 +1736,6 @@
         lax.dynamic_slice_in_dim(w_output, core * (half_width // 2), half_width // 2, axis=0), 1, 0
     )
     output_other = ordered(core, output_other, swap(output_other, 0, 1))
-    w_output_full = ordered(here, w_output, output_other)
-
-    def striped(weight):
-        return weight.reshape(half_width, groups, stripes, 2, LANES)
-
-    def own_stripes(weight, grp):
-        cut = pick(pick(striped(weight), grp, 1), core, 2)
-        return cut.reshape(half_width, own_width)
-
-    w_in = jnp.concatenate([own_stripes(w_gate, here), own_stripes(w_up, here)], axis=1)
-    w_in_other = swap(
-        jnp.concatenate([own_stripes(w_gate, 1 - here), own_stripes(w_up, 1 - here)], axis=1), 1, 0
-    )
-    w_in = ordered(here, w_in, w_in_other)
-    w_out = pick(w_down.reshape(stripes, 2, LANES, width), core, 1).reshape(own_width, width)
 
     def gather_quad(value):
         across = swap(value, 1, 0)
@@ -1426,53 +1743,35 @@
 
     out_rows = out_grad.reshape(rows, width)
     out_quad = gather_quad(out_rows)
-    grad_hidden = contract(out_quad, w_out, 1, 1)
 
     tables = attention_tables(lengths, here, there, row_count)
     attended, out_heads, log_sum, query, key, value = attend(tables, qkv)
     returned = lax.all_to_all(attended, BOTH, split_axis=0, concat_axis=0, tiled=True)
-    attn_rows = (
-        returned.reshape(groups, reps, row_count, LANES).transpose(0, 2, 1, 3).reshape(rows, width)
-    )
-    mixed = inputs.reshape(rows, width) + jnp.dot(
-        attn_rows, w_output_full, preferred_element_type=jnp.float32
-    )
-    normed_mid = (mixed * rms_scale(mixed) * gain_two).astype(jnp.bfloat16)
-    mid_quad = gather_quad(normed_mid)
-    gate_up = jnp.dot(mid_quad, w_in, preferred_element_type=jnp.float32)
-    gate_pre, up_pre = gate_up[:, :own_width], gate_up[:, own_width:]
-    gate_sig = jax.nn.sigmoid(gate_pre)
-    gate_silu = gate_pre * gate_sig
-    hidden = (gate_silu * up_pre).astype(jnp.bfloat16)
-    grad_gate = (grad_hidden * up_pre * gate_sig * (1.0 + gate_pre * (1.0 - gate_sig))).astype(
-        jnp.bfloat16
-    )
-    grad_up = (grad_hidden * gate_silu).astype(jnp.bfloat16)
-    grad_in_mlp = jnp.concatenate([grad_gate, grad_up], axis=1)
-
-    def scatter_quad(parts):
-        parts = parts.reshape(2, 2, rows, width)
-        both = parts[:, 0].astype(jnp.float32) + swap(narrow(parts[:, 1]), 0, 1).astype(jnp.float32)
-        return both[0] + swap(narrow(both[1]), 1, 0).astype(jnp.float32)
-
-    grad_mid = scatter_quad(contract(grad_in_mlp, w_in, 1, 1, jnp.bfloat16))
-    grad_norm_mid, unused_gain = norm_backward(mixed, gain_two, grad_mid)
-    grad_mixed = out_rows.astype(jnp.float32) + grad_norm_mid
-    grad_branch = grad_mixed.astype(jnp.bfloat16)
-    grad_att = contract(grad_branch, w_output_full, 1, 1, jnp.bfloat16)
+    returned = returned.reshape(groups, reps, row_count, LANES)
+    attn_rows = returned.transpose(0, 2, 1, 3).reshape(rows, width)
+    mixed, mid_quad, hidden, slopes, down_sums, grad_mixed, grad_branch, grad_att = mlp(
+        returned,
+        tokens.reshape(rows, width),
+        jnp.broadcast_to(gain_two[None], (8, width)),
+        out_quad.reshape(4, rows, width),
+        w_output,
+        output_other,
+        w_in,
+        w_down,
+    )
     grad_heads = lax.all_to_all(
-        grad_att.reshape(groups, row_count, reps, LANES)
-        .transpose(0, 2, 1, 3)
-        .reshape(groups * reps, row_count, LANES),
+        grad_att.reshape(groups * reps, row_count, LANES),
         BOTH,
         split_axis=0,
         concat_axis=0,
         tiled=True,
     )
-
     block_out = (
-        mixed + scatter_quad(jnp.dot(hidden, w_out, preferred_element_type=jnp.float32).astype(jnp.bfloat16))
+        mixed + down_sums[0].astype(jnp.float32) + swap(down_sums[1], 1, 0).astype(jnp.float32)
     ).astype(jnp.bfloat16)
+    mid_quad = mid_quad.reshape(4 * rows, width)
+    hidden = hidden.reshape(4 * rows, own_width)
+    slopes = slopes.reshape(4 * rows, 2 * own_width)
 
     bits = [(there // step) % 2 for step in (1, 2)]
     far = [1 << place for place in range(2, reps.bit_length() - 1)]
@@ -1487,7 +1786,7 @@
             )
         return parts[:, 0]
 
-    mlp_in_grad = contract(mid_quad, grad_in_mlp, 0, 0, jnp.bfloat16)
+    mlp_in_grad = contract(mid_quad, slopes, 0, 0, jnp.bfloat16)
     own_rows = width // (groups * reps)
     mlp_in_part = narrow(
         scatter_stripes(
@@ -1582,7 +1881,7 @@
         and reps % 4 == 0
         and reps & (reps - 1) == 0
         and tokens.shape[1] % UNIT_PAIR == 0
-        and arrays[7].shape[1] % (2 * groups * LANES) == 0
+        and arrays[7].shape[1] == groups * reps * LANES
     )
     return heads_body(*arrays) if fits else ring_body(*arrays)
 

time: 994 us -> 825 us (0.83)
  waiting for transfers between devices: 349 us -> 162 us
  Pallas kernels: 374 us -> 524 us
  matrix products: 85.3 us -> 21.5 us
  local copies, waits for them, and re-layouts: 90.8 us -> 38.9 us
  other arithmetic: 57.4 us -> 46.4 us
    ppermute x29 -> x22, waiting for transfers between devices: 349 us -> 127 us  [swap(): return lax.ppermute(value, BOTH, pairs)]
    pallas_call x0 -> x1, Pallas kernels: none -> 86.4 us  [mlp(): pl.pallas_call(mlp_kernel, out_shape=(jax.ShapeDtypeStruct((rows, width),...]
    pallas_call x1, Pallas kernels: 139 us -> 185 us  [gather_heads(): pl.pallas_call(gather_kernel, out_shape=(jax.ShapeDtypeStruct((reps, 2 *...]
    dot_general x6 -> x3, matrix products: 54.7 us -> 21.5 us  [contract(): lax.dot_general(left_side, right_side, (((left_dim,), (right_dim,)), ((),...]
    unnamed x74 -> x58, local copies, waits for them, and re-layouts: 41.6 us -> 8.54 us
    dot_general x3 -> x0, matrix products: 30.6 us -> none  [the longest x1 21 us: heads_body(): gate_up = jnp.dot(mid_quad, w_in, preferred_element_type=jnp.float32)]
    pallas_call x1, Pallas kernels: 113 us -> 135 us  [scatter_heads(): pl.pallas_call(scatter_kernel, out_shape=(jax.ShapeDtypeStruct((2, row_co...]
    all_to_all x1, waiting for transfers between devices: 0.01 us -> 19.4 us  [heads_body(): lax.all_to_all(attended, BOTH, split_axis=0, concat_axis=0, tiled=True)]
  transfers between devices with their start and end apart: 31 -> 24, of which waited for: 10 -> 12; matrix products, arithmetic and copies ran while one was open for 18% -> 10% of each run, Pallas kernels for 38% -> 53%
where the time goes in v3:
time: 825 us; the launch traced here: 818 us
  Pallas kernels  524 us (64%)
  waiting for transfers between devices  162 us (20%)
  other arithmetic  46.4 us (6%)
  local copies, waits for them, and re-layouts  38.9 us (5%)
  starting transfers between devices  23.4 us (3%)
  matrix products  21.5 us (3%)
    pallas_call x1, Pallas kernels, gather_heads(): pl.pallas_call(gather_kernel, out_shape=(jax.ShapeDtypeStruct((reps, 2 *...  185 us
    pallas_call x1, Pallas kernels, scatter_heads(): pl.pallas_call(scatter_kernel, out_shape=(jax.ShapeDtypeStruct((2, row_co...  135 us
    ppermute x22, waiting for transfers between devices, swap(): return lax.ppermute(value, BOTH, pairs)  127 us
    pallas_call x1, Pallas kernels, mlp(): pl.pallas_call(mlp_kernel, out_shape=(jax.ShapeDtypeStruct((rows, width),...  86.4 us
    pallas_call x1, Pallas kernels, attend_back(): pl.pallas_call(attend_back_kernel, out_shape=jax.ShapeDtypeStruct((parts,...  61.3 us
    pallas_call x1, Pallas kernels, attend(): pl.pallas_call(attend_kernel, out_shape=(jax.ShapeDtypeStruct((parts, uni...  55.2 us
    dot_general x3, matrix products, contract(): lax.dot_general(left_side, right_side, (((left_dim,), (right_dim,)), ((),...  21.5 us
    all_to_all x1, waiting for transfers between devices, heads_body(): lax.all_to_all(attended, BOTH, split_axis=0, concat_axis=0, tiled=True)  19.4 us
  transfers between devices with their start and end apart: 24, of which 12 were waited for; matrix products, arithmetic and copies ran while one was open for 10% of the time, Pallas kernels for 53%

profile of v3, /device:TPU:0, one launch (start us, length us, event | category | flops | bytes accessed | tf_op | source)
XLA Modules:
  0.0 817.7 jit_solution(6529922724517510241)
XLA Ops:
  0.7 3.3 constant_dynamic-slice_fusion.3
  4.0 2.9 collective-permute-start.4
  11.9 185.5 %gather_heads.1 = (bf16[16,256,2048]{2,1,0:T(8,128)(2,1)}, bf16[32,128,384]{2,1,0:T(8,128)(2,1)}, bf16[2,1024,384]{2,1,0:T(8,128)(2,1)}, bf16[2,1024,2048]{2,1,0:T(8,128)(2,1)}) custom-call(bf16[2,128,2048]{2,1,0:T(8,128)(2,1)} %tokens_ref.1, bf16[16,1024]{1,0:T(8,128)(2,1)} %broadcast_in_dim.18.gain_ref, bf16[1024,2048]{1,0:T(8,128)(2,1)} %w_query.1, ...), custom_call_target="tpu_custom_call" | custom-call | flops 8000000000 | bytes 262144000 | tf_op jit(solution)/shard_map/gather_heads/pallas_call | solution.py:1120
  198.1 55.2 %attend.1 = (bf16[32,128,128]{2,1,0:T(8,128)(2,1)}, f32[16,128,256]{2,1,0:T(8,128)}, f32[16,8,256]{2,1,0:T(8,128)}, bf16[16,256,128]{2,1,0:T(8,128)(2,1)}, bf16[...) custom-call(s32[32]{0:T(128)} %fusion.25.slot_ref, s32[16]{0:T(128)} %get-tuple-element.60.first_ref, ...), custom_call_target="tpu_custom_call" | custom-call | flops 20000000000 | bytes 16777216 | tf_op jit(solution)/shard_map/attend/pallas_call | solution.py:736
  253.3 5.2 all-to-all-start
  259.3 1.7 collective-permute-start.7
  262.2 3.4 collective-permute-done
  266.2 19.4 %all-to-all-done = bf16[32,128,128]{2,1,0:T(8,128)(2,1)S(1)} async-done(((bf16[32,128,128]{2,1,0:T(8,128)(2,1)}), bf16[32,128,128]{2,1,0:T(8,128)(2,1)S(1)}, u32[]{:S(2)}, u32[]{:S(2)}) %all-to-all-start) | async-done | bytes 1048608 | tf_op jit(solution)/shard_map/all_to_all | solution.py:1749
  286.3 3.6 pad_maximum_fusion
  290.0 6.3 maximum_select_fusion.output_other
  296.9 86.4 %mlp.1 = (f32[256,2048]{1,0:T(8,128)}, bf16[4,256,2048]{2,1,0:T(8,128)(2,1)}, bf16[4,256,1024]{2,1,0:T(8,128)(2,1)}, bf16[4,256,2048]{2,1,0:T(8,128)(2,1)}, bf16...) custom-call(bf16[2,16,128,128]{3,2,1,0:T(8,128)(2,1)} %bitcast.179, ...), custom_call_target="tpu_custom_call" | custom-call | flops 35999997952 | bytes 157286400 | tf_op jit(solution)/shard_map/mlp/pallas_call | solution.py:1664
  383.3 7.1 convolution_convert_fusion.1
  390.5 2.1 copy-done.7
  392.6 1.6 dynamic-slice_bitcast_fusion.2
  394.1 5.2 all-to-all-start.1
  399.5 1.9 collective-permute-start.6
  401.4 12.0 %bitcast_convert_fusion = bf16[2048,2048]{1,0:T(8,128)(2,1)S(1)} fusion(bf16[4,256,2048]{2,1,0:T(8,128)(2,1)} %get-tuple-element.48, bf16[4,256,2048]{2,1,0:T(8,128)(2,1)} %get-tuple-element.49), kind=kOutput, calls=%fused_computation | convolution fusion | flops 8594128896 | bytes 16777216 | tf_op jit(solution)/shard_map/dot_general | solution.py:413
  413.5 2.5 dynamic-slice_bitcast_fusion
  416.0 2.0 copy-done.6
  418.0 1.5 collective-permute-start.13
  419.5 2.4 convolution_convert_fusion
  421.9 2.7 dynamic-slice_bitcast_fusion.1
  424.6 2.1 copy-done.2
  426.7 9.2 %collective-permute-done.6 = bf16[256,2048]{1,0:T(8,128)(2,1)S(1)} collective-permute-done((bf16[256,2048]{1,0:T(8,128)(2,1)S(1)}, bf16[256,2048]{1,0:T(8,128)(2,1)S(1)}, u32[]{:S(2)}, u32[]{:S(2)}) %collective-permute-start.6) | collective-permute-done | bytes 1048608 | tf_op jit(solution)/shard_map/ppermute | solution.py:838
  436.0 1.5 fusion.8
  437.5 15.9 %all-to-all-done.1.grad_ref = bf16[32,128,128]{2,1,0:T(8,128)(2,1)} async-done(((bf16[32,128,128]{2,1,0:T(8,128)(2,1)}), bf16[32,128,128]{2,1,0:T(8,128)(2,1)}, u32[]{:S(2)}, u32[]{:S(2)}) %all-to-all-start.1) | async-done | bytes 1048608 | tf_op jit(solution)/shard_map/all_to_all | solution.py:1762
  453.4 61.3 %attend_back.1 = bf16[32,128,384]{2,1,0:T(8,128)(2,1)} custom-call(s32[32]{0:T(128)} %fusion.25.slot_ref, s32[16]{0:T(128)} %get-tuple-element.60.first_ref, s32[16]{0:T(128)} %get-tuple-element.59.plain_ref, f32[128,128]{1,0:T(8,128)} %get-tuple-element.75.cos_unit, f32[128,128]{1,0:T(8,128)} %get-tuple-element.74.sin_unit, ...), custom_call_target="tpu_custom_call" | custom-call | flops 49999998976 | bytes 16777216 | tf_op jit(solution)/shard_map/attend_back/pallas_call | solution.py:768
  514.7 135.3 %scatter_heads.1 = (f32[2,128,2048]{2,1,0:T(8,128)}, bf16[16,64,384]{2,1,0:T(8,128)(2,1)}) custom-call(bf16[16,256,384]{2,1,0:T(8,128)(2,1)} %bitcast.198, bf16[2,1024,384]{2,1,0:T(8,128)(2,1)} %get-tuple-element.43.weight_ref, bf16[16,256,2048]{2,1,0:T(8,128)(2,1)} %get-tuple-element.44.normed_ref), custom_call_target="tpu_custom_call" | custom-call | flops 14000000000 | bytes 262144000 | tf_op jit(solution)/shard_map/scatter_heads/pallas_call | solution.py:1379
  650.0 3.8 reshape.531
  653.9 4.7 fusion.33
  660.9 1.6 fusion.13
  662.5 2.6 multiply_reduce_fusion.4
  665.1 5.5 fusion
  671.0 3.7 fusion.1
  676.9 2.4 fusion.2
  679.4 2.1 collective-permute-start.20
  681.5 2.0 multiply_reduce_fusion.6
  684.8 34.6 %collective-permute-done.14 = bf16[2,2,2,64,2048]{4,3,2,1,0:T(8,128)(2,1)S(1)} collective-permute-done((bf16[2,2,2,64,2048]{4,3,2,1,0:T(8,128)(2,1)S(1)}, bf16[2,2,2,64,2048]{4,3,2,1,0:T(8,128)(2,1)S(1)}, u32[]{:S(2)}, u32[]{:S(2)}) %collective-permute-start.14) | collective-permute-done | bytes 2097184 | tf_op jit(solution)/shard_map/ppermute | solution.py:838
  720.6 38.9 %collective-permute-done.20 = bf16[1,2,128,2048]{3,2,1,0:T(8,128)(2,1)S(1)} collective-permute-done((bf16[1,2,128,2048]{3,2,1,0:T(8,128)(2,1)S(1)}, bf16[1,2,128,2048]{3,2,1,0:T(8,128)(2,1)S(1)}, u32[]{:S(2)}, u32[]{:S(2)}) %collective-permute-start.20) | collective-permute-done | bytes 1048608 | tf_op jit(solution)/shard_map/ppermute | solution.py:838
  761.2 20.1 %collective-permute-done.15 = bf16[2,1,2,64,2048]{4,3,2,1,0:T(8,128)(2,1)S(1)} collective-permute-done((bf16[2,1,2,64,2048]{4,3,2,1,0:T(8,128)(2,1)S(1)}, bf16[2,1,2,64,2048]{4,3,2,1,0:T(8,128)(2,1)S(1)}, u32[]{:S(2)}, u32[]{:S(2)}) %collective-permute-start.15) | collective-permute-done | bytes 1048608 | tf_op jit(solution)/shard_map/ppermute | solution.py:838
  782.3 2.9 collective-permute-done.10
  786.1 4.0 collective-permute-done.21
  791.4 4.9 collective-permute-done.17
  796.4 4.8 collective-permute-done.11
  805.2 2.4 copy.57
  808.5 1.9 multiply_reduce_fusion.2
  811.7 3.7 collective-permute-done.12
  815.4 1.9 add_bitcast_fusion.1
  (143 shorter events, 27.9 us)
Async XLA Ops:
  0.6 6.9 copy-start
  0.7 6.3 copy-start.17
  0.7 10.7 %copy-start.20 = (bf16[1024]{0:T(1024)(128)(2,1)S(1)}, bf16[1024]{0:T(1024)(128)(2,1)}, u32[]{:S(2)}) copy-start(bf16[1024]{0:T(1024)(128)(2,1)} %param.13) | copy-start | bytes 6148
  4.0 254.5 %collective-permute-start.4 = (bf16[512,2048]{1,0:T(8,128)(2,1)}, bf16[512,2048]{1,0:T(8,128)(2,1)}, u32[]{:S(2)}, u32[]{:S(2)}) collective-permute-start(bf16[512,2048]{1,0:T(8,128)(2,1)} %constant_dynamic-slice_fusion.3), channel_id=1, source_target_pairs={{0,16},{1,17},{2,18},{3,19},{4,20},{5,21},{6,22},{7,23},{8,24},{9,... | collective-permute-start | bytes 6291464 | tf_op jit(solution)/shard_map/ppermute | solution.py:838
  6.9 252.1 %collective-permute-start.2 = (bf16[256,2048]{1,0:T(8,128)(2,1)S(1)}, bf16[256,2048]{1,0:T(8,128)(2,1)}, u32[]{:S(2)}, u32[]{:S(2)}) collective-permute-start(bf16[256,2048]{1,0:T(8,128)(2,1)S(1)} %bitcast.192), channel_id=1, source_target_pairs={{0,16},{1,17},{2,18},{3,19},{4,20},{5,21},{6,22},{7,23},{8,24},{9,... | collective-permute-start | bytes 3145736 | tf_op jit(solution)/shard_map/ppermute | solution.py:838
  198.1 62.9 %copy-start.23 = (bf16[1024]{0:T(1024)(128)(2,1)S(1)}, bf16[1024]{0:T(1024)(128)(2,1)}, u32[]{:S(2)}) copy-start(bf16[1024]{0:T(1024)(128)(2,1)} %param.18) | copy-start | bytes 6148
  198.1 63.2 %copy-start.3 = (bf16[2,128,2048]{2,1,0:T(8,128)(2,1)S(1)}, bf16[2,128,2048]{2,1,0:T(8,128)(2,1)}, u32[]{:S(2)}) copy-start(bf16[2,128,2048]{2,1,0:T(8,128)(2,1)} %tokens_ref.1) | copy-start | bytes 3145732
  253.3 32.4 %all-to-all-start = ((bf16[32,128,128]{2,1,0:T(8,128)(2,1)}), bf16[32,128,128]{2,1,0:T(8,128)(2,1)S(1)}, u32[]{:S(2)}, u32[]{:S(2)}) async-start(bf16[32,128,128]{2,1,0:T(8,128)(2,1)} %get-tuple-element.32), calls=%async_computation | async-start | bytes 2097152 | tf_op jit(solution)/shard_map/all_to_all | solution.py:1749
  258.4 31.5 %collective-permute-start.5 = (bf16[512,2048]{1,0:T(8,128)(2,1)}, bf16[512,2048]{1,0:T(8,128)(2,1)}, u32[]{:S(2)}, u32[]{:S(2)}) collective-permute-start(bf16[512,2048]{1,0:T(8,128)(2,1)} %collective-permute-done.4), channel_id=1, source_target_pairs={{0,1},{1,0},{2,3},{3,2},{4,5},{5,4},{6,7},{7,6},{8,9},{9,8},{10,11... | collective-permute-start | bytes 6291464 | tf_op jit(solution)/shard_map/ppermute | solution.py:838
  258.8 27.5 %collective-permute-start.1 = (bf16[256,2048]{1,0:T(8,128)(2,1)S(1)}, bf16[256,2048]{1,0:T(8,128)(2,1)}, u32[]{:S(2)}, u32[]{:S(2)}) collective-permute-start(bf16[256,2048]{1,0:T(8,128)(2,1)S(1)} %bitcast.193), channel_id=1, source_target_pairs={{0,1},{1,0},{2,3},{3,2},{4,5},{5,4},{6,7},{7,6},{8,9},{9,8},{10,11... | collective-permute-start | bytes 3145736 | tf_op jit(solution)/shard_map/ppermute | solution.py:838
  259.0 27.3 %collective-permute-start.3 = (bf16[256,2048]{1,0:T(8,128)(2,1)}, bf16[256,2048]{1,0:T(8,128)(2,1)}, u32[]{:S(2)}, u32[]{:S(2)}) collective-permute-start(bf16[256,2048]{1,0:T(8,128)(2,1)} %collective-permute-done.2), channel_id=1, source_target_pairs={{0,1},{1,0},{2,3},{3,2},{4,5},{5,4},{6,7},{7,6},{8,9},{9,8},{10,11... | collective-permute-start | bytes 3145736 | tf_op jit(solution)/shard_map/ppermute | solution.py:838
  259.3 6.3 collective-permute-start.7
  261.0 4.6 collective-permute-start
  285.6 4.4 copy-start.9
  390.4 9.0 %copy-start.13 = (bf16[2,256,2048]{2,1,0:T(8,128)(2,1)S(1)}, bf16[2,256,2048]{2,1,0:T(8,128)(2,1)}, u32[]{:S(2)}) copy-start(bf16[2,256,2048]{2,1,0:T(8,128)(2,1)} %get-tuple-element.35) | copy-start | bytes 6291460
  394.1 281.4 %collective-permute-start.19 = (bf16[1,4,128,2048]{3,2,1,0:T(8,128)(2,1)}, bf16[1,4,128,2048]{3,2,1,0:T(8,128)(2,1)}, u32[]{:S(2)}, u32[]{:S(2)}) collective-permute-start(bf16[1,4,128,2048]{3,2,1,0:T(8,128)(2,1)} %dynamic-slice_bitcast_fusion.2), channel_id=1, source_target_pairs={{0,2},{1,3},{2,0},{3,1},{4,6},{5,7},{6,4},{7,5},{8,10},{9,11},{10,... | collective-permute-start | bytes 6291464 | tf_op jit(solution)/shard_map/ppermute | solution.py:838
  394.1 59.3 %all-to-all-start.1 = ((bf16[32,128,128]{2,1,0:T(8,128)(2,1)}), bf16[32,128,128]{2,1,0:T(8,128)(2,1)}, u32[]{:S(2)}, u32[]{:S(2)}) async-start(bf16[32,128,128]{2,1,0:T(8,128)(2,1)} %bitcast.186), calls=%async_computation.1 | async-start | bytes 2097152 | tf_op jit(solution)/shard_map/all_to_all | solution.py:1762
  399.5 36.5 %collective-permute-start.6 = (bf16[256,2048]{1,0:T(8,128)(2,1)S(1)}, bf16[256,2048]{1,0:T(8,128)(2,1)S(1)}, u32[]{:S(2)}, u32[]{:S(2)}) collective-permute-start(bf16[256,2048]{1,0:T(8,128)(2,1)S(1)} %slice_bitcast_fusion), channel_id=1, source_target_pairs={{0,16},{1,17},{2,18},{3,19},{4,20},{5,21},{6,22},{7,23},{8,24},{9,... | collective-permute-start | bytes 3145736 | tf_op jit(solution)/shard_map/ppermute | solution.py:838
  413.4 4.5 copy-start.6
  413.5 6.0 copy-start.18
  418.0 247.1 %collective-permute-start.13 = (bf16[2,4,2,64,2048]{4,3,2,1,0:T(8,128)(2,1)}, bf16[2,4,2,64,2048]{4,3,2,1,0:T(8,128)(2,1)}, u32[]{:S(2)}, u32[]{:S(2)}) collective-permute-start(bf16[2,4,2,64,2048]{4,3,2,1,0:T(8,128)(2,1)} %dynamic-slice_bitcast_fusion), channel_id=1, source_target_pairs={{0,2},{1,3},{2,0},{3,1},{4,6},{5,7},{6,4},{7,5},{8,10},{9,11},{10,... | collective-permute-start | bytes 12582920 | tf_op jit(solution)/shard_map/ppermute | solution.py:838
  421.9 4.8 copy-start.2
  421.9 14.1 %copy-start.14 = (f32[256,2048]{1,0:T(8,128)S(1)}, f32[256,2048]{1,0:T(8,128)}, u32[]{:S(2)}) copy-start(f32[256,2048]{1,0:T(8,128)} %get-tuple-element.34) | copy-start | bytes 6291460
  426.7 244.3 %collective-permute-start.8 = (bf16[2,8,64,2048]{3,2,1,0:T(8,128)(2,1)}, bf16[2,8,64,2048]{3,2,1,0:T(8,128)(2,1)}, u32[]{:S(2)}, u32[]{:S(2)}) collective-permute-start(bf16[2,8,64,2048]{3,2,1,0:T(8,128)(2,1)} %dynamic-slice_bitcast_fusion.1), channel_id=1, source_target_pairs={{0,1},{1,0},{2,3},{3,2},{4,5},{5,4},{6,7},{7,6},{8,9},{9,8},{10,11... | collective-permute-start | bytes 12582920 | tf_op jit(solution)/shard_map/ppermute | solution.py:838
  650.0 10.3 %copy-start.4 = (bf16[2,128,2048]{2,1,0:T(8,128)(2,1)S(1)}, bf16[2,128,2048]{2,1,0:T(8,128)(2,1)}, u32[]{:S(2)}) copy-start(bf16[2,128,2048]{2,1,0:T(8,128)(2,1)} %tokens_ref.1) | copy-start | bytes 3145732
  650.0 10.3 %copy-start.5 = (f32[2,128,2048]{2,1,0:T(8,128)S(1)}, f32[2,128,2048]{2,1,0:T(8,128)}, u32[]{:S(2)}) copy-start(f32[2,128,2048]{2,1,0:T(8,128)} %get-tuple-element.45) | copy-start | bytes 6291460
  650.0 10.3 %copy-start.19 = (f32[2048]{0:T(1024)S(1)}, f32[2048]{0:T(1024)}, u32[]{:S(2)}) copy-start(f32[2048]{0:T(1024)} %fusion.22) | copy-start | bytes 24580
  650.0 10.3 %copy-start.22 = (f32[2,128]{1,0:T(2,128)S(1)}, f32[2,128]{1,0:T(2,128)}, u32[]{:S(2)}) copy-start(f32[2,128]{1,0:T(2,128)} %get-tuple-element.71) | copy-start | bytes 3076
  653.9 7.0 copy-start.12
  653.9 7.0 copy-start.21
  660.9 10.1 %slice-start = ((s8[8388608]{0:T(1024)(128)(4,1)}), s8[4194304]{0:T(1024)(128)(4,1)S(1)}, s32[]{:S(2)}) async-start(s8[8388608]{0:T(1024)(128)(4,1)} %bitcast.161), calls=%async_computation.2 | async-start | bytes 8388608
  665.1 5.9 slice-start.1
  670.9 48.5 %collective-permute-start.14 = (bf16[2,2,2,64,2048]{4,3,2,1,0:T(8,128)(2,1)S(1)}, bf16[2,2,2,64,2048]{4,3,2,1,0:T(8,128)(2,1)S(1)}, u32[]{:S(2)}, u32[]{:S(2)}) collective-permute-start(bf16[2,2,2,64,2048]{4,3,2,1,0:T(8,128)(2,1)S(1)} %dynamic-slice_bitcast_fusion.3), channel_id=1, source_target_pairs={{0,4},{1,5},{2,6},{3,7},{4,0},{5,1},{6,2},{7,3},{8,12},{9,13},{10,... | collective-permute-start | bytes 6291464 | tf_op jit(solution)/shard_map/ppermute | solution.py:838
  674.7 2.2 copy-start.8
  675.0 6.5 copy-start.15
  675.0 84.9 %collective-permute-start.9 = (bf16[8,64,2048]{2,1,0:T(8,128)(2,1)S(1)}, bf16[8,64,2048]{2,1,0:T(8,128)(2,1)S(1)}, u32[]{:S(2)}, u32[]{:S(2)}) collective-permute-start(bf16[8,64,2048]{2,1,0:T(8,128)(2,1)S(1)} %dynamic-slice_bitcast_fusion.4), channel_id=1, source_target_pairs={{0,16},{1,17},{2,18},{3,19},{4,20},{5,21},{6,22},{7,23},{8,24},{9,... | collective-permute-start | bytes 6291464 | tf_op jit(solution)/shard_map/ppermute | solution.py:838
  679.4 80.1 %collective-permute-start.20 = (bf16[1,2,128,2048]{3,2,1,0:T(8,128)(2,1)S(1)}, bf16[1,2,128,2048]{3,2,1,0:T(8,128)(2,1)S(1)}, u32[]{:S(2)}, u32[]{:S(2)}) collective-permute-start(bf16[1,2,128,2048]{3,2,1,0:T(8,128)(2,1)S(1)} %dynamic-slice_bitcast_fusion.5), channel_id=1, source_target_pairs={{0,4},{1,5},{2,6},{3,7},{4,0},{5,1},{6,2},{7,3},{8,12},{9,13},{10,... | collective-permute-start | bytes 3145736 | tf_op jit(solution)/shard_map/ppermute | solution.py:838
  720.5 60.8 %collective-permute-start.15 = (bf16[2,1,2,64,2048]{4,3,2,1,0:T(8,128)(2,1)S(1)}, bf16[2,1,2,64,2048]{4,3,2,1,0:T(8,128)(2,1)S(1)}, u32[]{:S(2)}, u32[]{:S(2)}) collective-permute-start(bf16[2,1,2,64,2048]{4,3,2,1,0:T(8,128)(2,1)S(1)} %constant_dynamic-slice_fusion.1), channel_id=1, source_target_pairs={{0,8},{1,9},{2,10},{3,11},{4,12},{5,13},{6,14},{7,15},{8,0},{9,1},... | collective-permute-start | bytes 3145736 | tf_op jit(solution)/shard_map/ppermute | solution.py:838
  760.8 24.4 %collective-permute-start.10 = (bf16[1,4,64,2048]{3,2,1,0:T(8,128)(2,1)S(1)}, bf16[1,4,64,2048]{3,2,1,0:T(8,128)(2,1)S(1)}, u32[]{:S(2)}, u32[]{:S(2)}) collective-permute-start(bf16[1,4,64,2048]{3,2,1,0:T(8,128)(2,1)S(1)} %dynamic-slice_bitcast_fusion.6), channel_id=1, source_target_pairs={{0,2},{1,3},{2,0},{3,1},{4,6},{5,7},{6,4},{7,5},{8,10},{9,11},{10,... | collective-permute-start | bytes 3145736 | tf_op jit(solution)/shard_map/ppermute | solution.py:838
  761.0 29.1 %collective-permute-start.21 = (bf16[1,1,128,2048]{3,2,1,0:T(8,128)(2,1)S(1)}, bf16[1,1,128,2048]{3,2,1,0:T(8,128)(2,1)S(1)}, u32[]{:S(2)}, u32[]{:S(2)}) collective-permute-start(bf16[1,1,128,2048]{3,2,1,0:T(8,128)(2,1)S(1)} %constant_dynamic-slice_fusion), channel_id=1, source_target_pairs={{0,8},{1,9},{2,10},{3,11},{4,12},{5,13},{6,14},{7,15},{8,0},{9,1},... | collective-permute-start | bytes 1572872 | tf_op jit(solution)/shard_map/ppermute | solution.py:838
  781.7 9.5 %collective-permute-start.16 = (bf16[64,2048]{1,0:T(8,128)(2,1)S(1)}, bf16[64,2048]{1,0:T(8,128)(2,1)S(1)}, u32[]{:S(2)}, u32[]{:S(2)}) collective-permute-start(bf16[64,2048]{1,0:T(8,128)(2,1)S(1)} %get-tuple-element.67), channel_id=1, source_target_pairs={{0,1},{1,0},{2,3},{3,2},{4,5},{5,4},{6,7},{7,6},{8,9},{9,8},{10,11... | collective-permute-start | bytes 786440 | tf_op jit(solution)/shard_map/ppermute | solution.py:838
  781.9 14.4 %collective-permute-start.17 = (bf16[2,64,2048]{2,1,0:T(8,128)(2,1)S(1)}, bf16[2,64,2048]{2,1,0:T(8,128)(2,1)S(1)}, u32[]{:S(2)}, u32[]{:S(2)}) collective-permute-start(bf16[2,64,2048]{2,1,0:T(8,128)(2,1)S(1)} %dynamic-slice_bitcast_fusion.7), channel_id=1, source_target_pairs={{0,16},{1,17},{2,18},{3,19},{4,20},{5,21},{6,22},{7,23},{8,24},{9,... | collective-permute-start | bytes 1572872 | tf_op jit(solution)/shard_map/ppermute | solution.py:838
  786.0 15.2 %collective-permute-start.11 = (bf16[1,2,64,2048]{3,2,1,0:T(8,128)(2,1)S(1)}, bf16[1,2,64,2048]{3,2,1,0:T(8,128)(2,1)S(1)}, u32[]{:S(2)}, u32[]{:S(2)}) collective-permute-start(bf16[1,2,64,2048]{3,2,1,0:T(8,128)(2,1)S(1)} %dynamic-slice_bitcast_fusion.8), channel_id=1, source_target_pairs={{0,4},{1,5},{2,6},{3,7},{4,0},{5,1},{6,2},{7,3},{8,12},{9,13},{10,... | collective-permute-start | bytes 1572872 | tf_op jit(solution)/shard_map/ppermute | solution.py:838
  796.3 5.2 collective-permute-start.18
  801.4 14.0 %collective-permute-start.12 = (bf16[1,1,64,2048]{3,2,1,0:T(8,128)(2,1)S(1)}, bf16[1,1,64,2048]{3,2,1,0:T(8,128)(2,1)}, u32[]{:S(2)}, u32[]{:S(2)}) collective-permute-start(bf16[1,1,64,2048]{3,2,1,0:T(8,128)(2,1)S(1)} %constant_dynamic-slice_fusion.2), channel_id=1, source_target_pairs={{0,8},{1,9},{2,10},{3,11},{4,12},{5,13},{6,14},{7,15},{8,0},{9,1},... | collective-permute-start | bytes 786440 | tf_op jit(solution)/shard_map/ppermute | solution.py:838
  805.2 12.1 %copy-start.10 = (f32[64,4096]{1,0:T(8,128)}, f32[64,4096]{1,0:T(8,128)S(1)}, u32[]{:S(2)}) copy-start(f32[64,4096]{1,0:T(8,128)S(1)} %squeeze.109) | copy-start | bytes 3145732
  805.2 12.1 %copy-start.1 = (s32[2,4]{1,0:T(2,128)S(1)}, s32[2,4]{1,0:T(2,128)}, u32[]{:S(2)}) copy-start(s32[2,4]{1,0:T(2,128)} %param.23) | copy-start | bytes 100
  808.5 8.8 %copy-start.11 = (f32[64,4096]{1,0:T(8,128)}, f32[64,4096]{1,0:T(8,128)S(1)}, u32[]{:S(2)}) copy-start(f32[64,4096]{1,0:T(8,128)S(1)} %squeeze.110) | copy-start | bytes 3145732
  (2 other events, 2.9 us)

commit v4 on v3

--- a/solution.py
+++ b/solution.py
@@ -20,6 +20,7 @@
 UNIT_BLOCK = 8
 UNIT_PAIR = 16
 KERNEL_VMEM = 56 * 1024 * 1024
+SCATTER_REFS = 18
 
 
 def from_behind(value, axis, steps):
@@ -913,13 +914,20 @@
     w_value,
     w_gate,
     w_up,
+    w_down,
+    w_output,
+    out_rows,
     normed_out,
     qkv_ref,
     weight_ref,
-    in_ref,
+    gate_ref,
+    up_ref,
+    down_ref,
+    output_ref,
+    out_away,
+    gains,
     raw,
     normed,
-    gains,
     weight_sem,
     out_sem,
     send_sem,
@@ -927,8 +935,6 @@
     side_send,
     side_recv,
     stripe_sem,
-    stripe_send,
-    stripe_recv,
 ):
     here, there = lax.axis_index("grp"), lax.axis_index("rep")
     core = there % 2
@@ -1011,33 +1017,47 @@
     weight_copy = side(1, weight_ref.at[here], weight_ref.at[here])
     weight_copy.start()
 
-    stripes = reps // 2
-    own_width = in_ref.shape[2] // 2
-    stripe_copies, stripe_loads = [], []
-    for kind, weight in enumerate((w_gate, w_up)):
-        for at in range(stripes):
-            target_ref = in_ref.at[here, :, pl.ds(kind * own_width + at * LANES, LANES)]
-            number = kind * stripes + at
-
-            def columns_of(grp):
-                first = (grp * stripes + at) * 2 * LANES + core * LANES
-                return weight.at[:, pl.ds(pl.multiple_of(first, LANES), LANES)]
-
-            stripe_loads.append(
-                pltpu.make_async_copy(columns_of(here), target_ref, stripe_sem.at[number])
-            )
-            stripe_copies.append(
-                pltpu.make_async_remote_copy(
-                    src_ref=columns_of(1 - here),
-                    dst_ref=target_ref,
-                    send_sem=stripe_send.at[number],
-                    recv_sem=stripe_recv.at[number],
-                    device_id=across,
-                    device_id_type=MESH_IDS,
-                )
-            )
-    for one in stripe_copies + stripe_loads:
+    stripes = [
+        (grp, high, low)
+        for grp in range(2)
+        for high in range(reps // 8)
+        for low in range(2)
+    ]
+    place = 4 * ((there // 4) % 2) + there % 2
+    stripe_loads = []
+
+    def load(source, target_ref):
+        stripe_loads.append(
+            pltpu.make_async_copy(source, target_ref, stripe_sem.at[len(stripe_loads)])
+        )
+
+    def columns_of(weight, grp, high, low):
+        first = (grp * reps + 8 * high + 2 * low + place) * LANES
+        return weight.at[:, pl.ds(pl.multiple_of(first, LANES), LANES)]
+
+    for weight, target_ref in ((w_gate, gate_ref.at[here]), (w_up, up_ref)):
+        for at, stripe in enumerate(stripes):
+            load(columns_of(weight, *stripe), target_ref.at[:, pl.ds(at * LANES, LANES)])
+    for at, (grp, high, low) in enumerate(stripes[: len(stripes) // 2]):
+        first = (8 * high + 2 * low + place) * LANES
+        load(
+            w_down.at[pl.ds(pl.multiple_of(first, LANES), LANES)],
+            down_ref.at[pl.ds(at * LANES, LANES)],
+        )
+    load(out_rows, out_away)
+    for one in stripe_loads:
         one.start()
+    quarter = output_ref.shape[0]
+    output_copy = side(
+        2,
+        w_output.at[pl.ds(pl.multiple_of((there % 4) * quarter, quarter), quarter)],
+        output_ref,
+    )
+    output_copy.start()
+    gate_copy = side(3, gate_ref.at[here], gate_ref.at[here])
+    for one in stripe_loads[: len(stripes)]:
+        one.wait()
+    gate_copy.start()
 
     written = {}
     used = [None] * slots
@@ -1106,15 +1126,22 @@
         one.wait_send()
     gain_copy.wait_send()
     weight_copy.wait_send()
-    for one in stripe_copies + stripe_loads:
+    for one in stripe_loads[len(stripes) :]:
         one.wait()
-
-
-def gather_heads(tokens, gain, w_query, w_key, w_value, w_gate, w_up):
+    gate_copy.wait()
+    output_copy.wait()
+
+
+def gather_heads(
+    tokens, gains, w_query, w_key, w_value, w_gate, w_up, w_down, w_output, out_rows
+):
     reps = lax.axis_size("rep")
     _, row_count, width = tokens.shape
     half = width // 2
-    gain_rows = jnp.broadcast_to(gain[None], (16, half))
+    own_width = reps // 2 * LANES
+    gain_rows = jnp.concatenate(
+        [gains[0][None], gains[1][None], jnp.zeros((14, half), jnp.bfloat16)], axis=0
+    )
     vmem = pl.BlockSpec(memory_space=pltpu.VMEM)
     anywhere = pl.BlockSpec(memory_space=pl.ANY)
     return pl.pallas_call(
@@ -1123,23 +1150,25 @@
             jax.ShapeDtypeStruct((reps, 2 * row_count, width), jnp.bfloat16),
             jax.ShapeDtypeStruct((2 * reps, row_count, 3 * LANES), jnp.bfloat16),
             jax.ShapeDtypeStruct((2, half, 3 * LANES), jnp.bfloat16),
-            jax.ShapeDtypeStruct((2, half, reps * LANES), jnp.bfloat16),
-        ),
-        in_specs=[vmem, vmem] + [anywhere] * 5,
-        out_specs=(anywhere, vmem, vmem, anywhere),
+            jax.ShapeDtypeStruct((2, half, own_width), jnp.bfloat16),
+            jax.ShapeDtypeStruct((half, own_width), jnp.bfloat16),
+            jax.ShapeDtypeStruct((own_width // 2, width), jnp.bfloat16),
+            jax.ShapeDtypeStruct((half // 4, width), jnp.bfloat16),
+            jax.ShapeDtypeStruct(out_rows.shape, jnp.bfloat16),
+            jax.ShapeDtypeStruct((2, 16, half), jnp.bfloat16),
+        ),
+        in_specs=[vmem, vmem] + [anywhere] * 8,
+        out_specs=(anywhere,) + (vmem,) * 8,
         scratch_shapes=[
             pltpu.VMEM((reps, 2, row_count, width), jnp.bfloat16),
             pltpu.VMEM((4, 2 * row_count, width), jnp.bfloat16),
-            pltpu.VMEM((2, 16, half), jnp.bfloat16),
             pltpu.SemaphoreType.DMA((3,)),
             pltpu.SemaphoreType.DMA((reps,)),
             pltpu.SemaphoreType.DMA((2 * reps,)),
             pltpu.SemaphoreType.DMA((2 * reps,)),
-            pltpu.SemaphoreType.DMA((2,)),
-            pltpu.SemaphoreType.DMA((2,)),
-            pltpu.SemaphoreType.DMA((reps,)),
-            pltpu.SemaphoreType.DMA((reps,)),
-            pltpu.SemaphoreType.DMA((reps,)),
+            pltpu.SemaphoreType.DMA((4,)),
+            pltpu.SemaphoreType.DMA((4,)),
+            pltpu.SemaphoreType.DMA((reps // 2 * 5 // 2 + 1,)),
         ],
         compiler_params=pltpu.CompilerParams(
             vmem_limit_bytes=KERNEL_VMEM, collective_id=0, has_side_effects=True
@@ -1148,10 +1177,19 @@
             flops=8 * 10**9, bytes_accessed=250 << 20, transcendentals=0
         ),
         name="gather_heads",
-    )(tokens, gain_rows, w_query, w_key, w_value, w_gate, w_up)
+    )(tokens, gain_rows, w_query, w_key, w_value, w_gate, w_up, w_down, w_output, out_rows)
 
 
 def scatter_kernel(
+    back_ref,
+    weight_ref,
+    normed_ref,
+    *refs,
+):
+    scatter_rows(back_ref, weight_ref, normed_ref, *refs[-SCATTER_REFS:])
+
+
+def scatter_rows(
     back_ref,
     weight_ref,
     normed_ref,
@@ -1369,7 +1407,7 @@
         one.wait_send()
 
 
-def scatter_heads(back, weights, normed):
+def scatter_heads(back, weights, normed, ahead):
     reps, rows, columns = back.shape
     width = normed.shape[2]
     row_count = rows // 2
@@ -1382,7 +1420,7 @@
             jax.ShapeDtypeStruct((2, row_count, width), jnp.float32),
             jax.ShapeDtypeStruct((reps, half // reps, columns), jnp.bfloat16),
         ),
-        in_specs=[vmem, vmem, anywhere],
+        in_specs=[vmem, vmem, anywhere] + [anywhere] * len(ahead),
         out_specs=(vmem, vmem),
         scratch_shapes=[
             pltpu.VMEM((reps, 2, row_count, width), jnp.bfloat16),
@@ -1409,27 +1447,37 @@
             flops=14 * 10**9, bytes_accessed=250 << 20, transcendentals=0
         ),
         name="scatter_heads",
-    )(back, weights, normed)
+    )(back, weights, normed, *ahead)
 
 
 def mlp_kernel(
-    returned_ref,
+    heads_ref,
     tokens_ref,
     gain_ref,
     out_ref,
     output_own,
-    output_other,
-    in_ref,
-    down_weight,
+    output_a,
+    output_b,
+    output_c,
+    output_d,
+    gate_in,
+    up_own,
+    up_other,
+    down_own,
+    down_other,
     mixed_ref,
+    attended,
+    down_ref,
+    grad_ref,
+    branch_ref,
+    back_ref,
+    gate_ref,
+    up_ref,
+    down_grad_ref,
+    returned,
     mid_ref,
     hidden_ref,
     slope_ref,
-    down_ref,
-    grad_ref,
-    branch_ref,
-    att_ref,
-    attended,
     w_output,
     w_in,
     w_out,
@@ -1437,42 +1485,111 @@
     near_landed,
     far_away,
     far_landed,
-    down_away,
     down_landed,
     load_sem,
-    stripe_sem,
+    part_sem,
     send_sem,
     recv_sem,
+    heads_send,
+    heads_recv,
+    back_send,
+    back_recv,
 ):
     here, there = lax.axis_index("grp"), lax.axis_index("rep")
-    core = there % 2
-    across = (1 - here, there)
+    across = (here, flipped(there, 4))
     sibling = (here, flipped(there, 1))
-    groups, heads, row_count, _ = returned_ref.shape
+    groups, heads, row_count, _ = returned.shape
     rows, width = tokens_ref.shape
     half = width // 2
+    quarter = half // 4
     own_width = w_out.shape[0]
-    stripes = own_width // LANES
 
     loads = [
         pltpu.make_async_copy(output_own, w_output.at[here], load_sem.at[0]),
-        pltpu.make_async_copy(output_other, w_output.at[1 - here], load_sem.at[1]),
-        pltpu.make_async_copy(in_ref, w_in, load_sem.at[2]),
+        pltpu.make_async_copy(gate_in, w_in.at[:, :, pl.ds(0, own_width)], load_sem.at[1]),
+        pltpu.make_async_copy(
+            up_own, w_in.at[here, :, pl.ds(own_width, own_width)], load_sem.at[2]
+        ),
+        pltpu.make_async_copy(
+            up_other, w_in.at[1 - here, :, pl.ds(own_width, own_width)], load_sem.at[3]
+        ),
     ]
-    for at in range(stripes):
-        loads.append(
+    own_part = own_width // 2
+    loads += [
+        pltpu.make_async_copy(
+            down_own,
+            w_out.at[pl.ds(pl.multiple_of(here * own_part, own_part), own_part)],
+            load_sem.at[4],
+        ),
+        pltpu.make_async_copy(
+            down_other,
+            w_out.at[pl.ds(pl.multiple_of((1 - here) * own_part, own_part), own_part)],
+            load_sem.at[5],
+        ),
+    ]
+    place = there % 4
+    rest = []
+    for at, (piece, part) in enumerate(
+        (
+            (output_a, place),
+            (output_b, flipped(place, 2)),
+            (output_c, flipped(place, 1)),
+            (output_d, 3 - place),
+        )
+    ):
+        rest.append(
             pltpu.make_async_copy(
-                down_weight.at[pl.ds(pl.multiple_of((2 * at + core) * LANES, LANES), LANES)],
-                w_out.at[pl.ds(at * LANES, LANES)],
-                stripe_sem.at[at],
+                piece,
+                w_output.at[1 - here, pl.ds(pl.multiple_of(part * quarter, quarter), quarter)],
+                part_sem.at[at],
             )
         )
+    loads = loads[:1] + rest + loads[1:]
     for one in loads:
         one.start()
+    steps = [1 << place for place in range(heads.bit_length() - 1)]
+
+    def other(crossing, offset):
+        index = there
+        for step in steps:
+            if offset & step:
+                index = flipped(index, step)
+        return (1 - here if crossing else here, index)
+
+    others = [
+        (crossing, offset) for offset in range(heads) for crossing in (0, 1) if offset or crossing
+    ]
     barrier = pltpu.get_barrier_semaphore()
-    for target in (across, sibling):
-        pl.semaphore_signal(barrier, inc=1, device_id=target, device_id_type=MESH_IDS)
-    pl.semaphore_wait(barrier, 2)
+    for key in others:
+        pl.semaphore_signal(barrier, inc=1, device_id=other(*key), device_id_type=MESH_IDS)
+    pl.semaphore_wait(barrier, len(others))
+
+    heads_copies, back_copies = [], []
+    for at, key in enumerate(others):
+        target = other(*key)
+        heads_copies.append(
+            pltpu.make_async_remote_copy(
+                src_ref=heads_ref.at[target[0] * heads + target[1]],
+                dst_ref=returned.at[here, there],
+                send_sem=heads_send.at[at],
+                recv_sem=heads_recv.at[at],
+                device_id=target,
+                device_id_type=MESH_IDS,
+            )
+        )
+        back_copies.append(
+            pltpu.make_async_remote_copy(
+                src_ref=returned.at[target[0], target[1]],
+                dst_ref=back_ref.at[here * heads + there],
+                send_sem=back_send.at[at],
+                recv_sem=back_recv.at[at],
+                device_id=target,
+                device_id_type=MESH_IDS,
+            )
+        )
+    for one in heads_copies[::-1]:
+        one.start()
+    returned[here, there] = heads_ref[here * heads + there]
 
     def copy(at, source, target_ref, target):
         return pltpu.make_async_remote_copy(
@@ -1489,15 +1606,24 @@
     mid_on = copy(2, mid_ref.at[2], mid_ref.at[3], sibling)
     grad_near = [copy(3 + at, near_away.at[at], near_landed.at[at], sibling) for at in range(2)]
     grad_far = copy(5, far_away, far_landed, across)
-    down_near = [copy(6 + at, down_away.at[at], down_landed.at[at], sibling) for at in range(2)]
-
+    down_near = [copy(6 + at, near_away.at[at], down_landed.at[at], sibling) for at in range(2)]
+    gate_cross = copy(
+        8, w_in.at[1 - here, :, pl.ds(0, own_width)], gate_ref, (1 - here, there)
+    )
+    up_out = pltpu.make_async_copy(
+        w_in.at[:, :, pl.ds(own_width, own_width)], up_ref, load_sem.at[0]
+    )
+    down_out = pltpu.make_async_copy(w_out, down_grad_ref, load_sem.at[1])
+
+    for one in heads_copies:
+        one.wait()
     for group in range(groups):
         for head in range(heads):
             attended[
                 group * row_count : (group + 1) * row_count, head * LANES : (head + 1) * LANES
-            ] = returned_ref[group, head]
-    loads[0].wait()
-    loads[1].wait()
+            ] = returned[group, head]
+    for one in loads[:5]:
+        one.wait()
     wide = 512
 
     def mix(at, unused):
@@ -1521,7 +1647,7 @@
     lax.fori_loop(0, rows // tile, norm_rows, 0)
     mid_far.start()
     mid_near.start()
-    for one in loads[2:]:
+    for one in loads[5:]:
         one.wait()
     narrow_tile = 256
 
@@ -1603,9 +1729,37 @@
 
     backward(2, add_near)
     grad_far.start()
+
+    def turned(values):
+        flat = values.reshape(4 * rows, values.shape[2]).astype(jnp.float32)
+        return jnp.transpose(flat).astype(jnp.bfloat16)
+
+    def in_grads(at):
+        def some_rows(step, unused):
+            cut = pl.ds(pl.multiple_of(step * narrow_tile, narrow_tile), narrow_tile)
+            source = pl.ds(pl.multiple_of(at * half + step * narrow_tile, narrow_tile), narrow_tile)
+            left = turned(mid_ref[:, :, source])
+
+            def columns(place_at, unused):
+                cols = pl.ds(pl.multiple_of(place_at * wide, wide), wide)
+                right = slope_ref[:, :, cols].reshape(4 * rows, wide)
+                w_in[at, cut, cols] = jnp.dot(
+                    left, right, preferred_element_type=jnp.float32
+                ).astype(jnp.bfloat16)
+                return unused
+
+            return lax.fori_loop(0, 2 * own_width // wide, columns, unused)
+
+        lax.fori_loop(0, half // narrow_tile, some_rows, 0)
+
+    in_grads(1 - here)
+    gate_cross.start()
     for at in range(2):
-        down(2 * at + 1, into(down_away, at))
+        grad_near[at].wait_send()
+        down(2 * at + 1, into(near_away, at))
         down_near[at].start()
+    in_grads(here)
+    up_out.start()
     for at in range(2):
         down_near[at].wait_recv()
 
@@ -1615,6 +1769,23 @@
             )
 
         down(2 * at, add_down)
+
+    def down_rows(step, unused):
+        cut = pl.ds(pl.multiple_of(step * narrow_tile, narrow_tile), narrow_tile)
+        left = turned(hidden_ref[:, :, cut])
+
+        def columns(place_at, unused):
+            cols = pl.ds(pl.multiple_of(place_at * wide, wide), wide)
+            right = out_ref[:, :, cols].reshape(4 * rows, wide)
+            w_out[cut, cols] = jnp.dot(left, right, preferred_element_type=jnp.float32).astype(
+                jnp.bfloat16
+            )
+            return unused
+
+        return lax.fori_loop(0, width // wide, columns, unused)
+
+    lax.fori_loop(0, own_width // narrow_tile, down_rows, 0)
+    down_out.start()
     grad_near[0].wait_recv()
     grad_far.wait_recv()
 
@@ -1645,60 +1816,102 @@
         )
         for group in range(groups):
             for step in range(4):
-                att_ref[group, head + step] = values[
+                returned[group, head + step] = values[
                     group * row_count : (group + 1) * row_count, step * LANES : (step + 1) * LANES
                 ]
-    for one in [mid_near, mid_far, mid_on, grad_far] + grad_near + down_near:
+    for one in back_copies[::-1]:
+        one.start()
+    back_ref[here * heads + there] = returned[here, there]
+    gate_cross.wait()
+
+    def add_gate(at, unused):
+        cut = pl.ds(pl.multiple_of(at * tile, tile), tile)
+        gate_ref[cut, :] = (
+            gate_ref[cut, :].astype(jnp.float32)
+            + w_in[here, cut, pl.ds(0, own_width)].astype(jnp.float32)
+        ).astype(jnp.bfloat16)
+        return unused
+
+    lax.fori_loop(0, half // tile, add_gate, 0)
+    up_out.wait()
+    down_out.wait()
+    for one in back_copies:
+        one.wait()
+    for one in [mid_near, mid_far, mid_on, grad_far] + down_near:
         one.wait_send()
 
 
-def mlp(returned, tokens, gain, out_quad, output_own, output_other, w_in, w_down):
-    groups, heads, row_count, _ = returned.shape
+def mlp(heads, tokens, gain, out_quad, output_parts, in_parts, down_parts):
+    count, row_count, _ = heads.shape
+    groups = lax.axis_size("grp")
     rows, width = tokens.shape
     half = width // 2
-    hidden_width = w_in.shape[2]
-    own_width = hidden_width // 2
+    own_width = in_parts[0].shape[2]
     vmem = pl.BlockSpec(memory_space=pltpu.VMEM)
     anywhere = pl.BlockSpec(memory_space=pl.ANY)
     low, full = jnp.bfloat16, jnp.float32
+    others = pltpu.SemaphoreType.DMA((count - 1,))
     return pl.pallas_call(
         mlp_kernel,
         out_shape=(
             jax.ShapeDtypeStruct((rows, width), full),
-            jax.ShapeDtypeStruct((4, rows, width), low),
-            jax.ShapeDtypeStruct((4, rows, own_width), low),
-            jax.ShapeDtypeStruct((4, rows, hidden_width), low),
+            jax.ShapeDtypeStruct((rows, width), low),
             jax.ShapeDtypeStruct((2, rows, width), low),
             jax.ShapeDtypeStruct((rows, width), full),
             jax.ShapeDtypeStruct((rows, width), low),
-            jax.ShapeDtypeStruct((groups, heads, row_count, LANES), low),
-        ),
-        in_specs=[vmem] * 4 + [anywhere] * 4,
-        out_specs=(vmem,) * 8,
+            jax.ShapeDtypeStruct((count, row_count, LANES), low),
+            jax.ShapeDtypeStruct((half, own_width), low),
+            jax.ShapeDtypeStruct((2, half, own_width), low),
+            jax.ShapeDtypeStruct((own_width, width), low),
+        ),
+        in_specs=[vmem] * 4 + [anywhere] * 10,
+        out_specs=(vmem,) * 7 + (anywhere,) * 2,
         scratch_shapes=[
-            pltpu.VMEM((rows, width), low),
+            pltpu.VMEM((groups, count // groups, row_count, LANES), low),
+            pltpu.VMEM((4, rows, width), low),
+            pltpu.VMEM((4, rows, own_width), low),
+            pltpu.VMEM((4, rows, 2 * own_width), low),
             pltpu.VMEM((2, half, width), low),
-            pltpu.VMEM((2, half, hidden_width), low),
+            pltpu.VMEM((2, half, 2 * own_width), low),
             pltpu.VMEM((own_width, width), low),
             pltpu.VMEM((2, rows, width), low),
             pltpu.VMEM((2, rows, width), low),
             pltpu.VMEM((rows, width), low),
             pltpu.VMEM((rows, width), low),
             pltpu.VMEM((2, rows, width), low),
-            pltpu.VMEM((2, rows, width), low),
-            pltpu.SemaphoreType.DMA((3,)),
-            pltpu.SemaphoreType.DMA((own_width // LANES,)),
-            pltpu.SemaphoreType.DMA((8,)),
-            pltpu.SemaphoreType.DMA((8,)),
+            pltpu.SemaphoreType.DMA((6,)),
+            pltpu.SemaphoreType.DMA((4,)),
+            pltpu.SemaphoreType.DMA((9,)),
+            pltpu.SemaphoreType.DMA((9,)),
+            others,
+            others,
+            others,
+            others,
         ],
         compiler_params=pltpu.CompilerParams(
-            vmem_limit_bytes=60 * 1024 * 1024, collective_id=2, has_side_effects=True
+            vmem_limit_bytes=62 * 1024 * 1024, collective_id=2, has_side_effects=True
         ),
         cost_estimate=pl.CostEstimate(
-            flops=36 * 10**9, bytes_accessed=150 << 20, transcendentals=0
+            flops=150 * 10**9, bytes_accessed=150 << 20, transcendentals=0
         ),
         name="mlp",
-    )(returned, tokens, gain, out_quad, output_own, output_other, w_in, w_down)
+    )(heads, tokens, gain, out_quad, *output_parts, *in_parts, *down_parts)
+
+
+def after_kernel(*refs):
+    pass
+
+
+def after(values, ahead):
+    anywhere = pl.BlockSpec(memory_space=pl.ANY)
+    return pl.pallas_call(
+        after_kernel,
+        out_shape=tuple(jax.ShapeDtypeStruct(one.shape, one.dtype) for one in values),
+        in_specs=[anywhere] * (len(values) + 1),
+        out_specs=(anywhere,) * len(values),
+        input_output_aliases={at: at for at in range(len(values))},
+        name="after",
+    )(*values, ahead)
 
 
 def heads_body(
@@ -1717,119 +1930,151 @@
 ):
     groups, reps = lax.axis_size("grp"), lax.axis_size("rep")
     here, there = lax.axis_index("grp"), lax.axis_index("rep")
-    core = there % 2
     micro_count, row_count, width = tokens.shape
     rows = micro_count * row_count
     hidden_width = w_gate.shape[1]
-    half_width = width // groups
     own_width = hidden_width // (2 * groups)
-    stripes = reps // 2
-
-    gathered_rows, qkv, w_heads, w_in = gather_heads(
-        tokens, attn_gain, w_query, w_key, w_value, w_gate, w_up
-    )
-    gain_one = ordered(here, attn_gain, swap(attn_gain, 1, 0)).astype(jnp.float32)
-    gain_two = ordered(here, mlp_gain, swap(mlp_gain, 1, 0)).astype(jnp.float32)
+
+    out_rows = out_grad.reshape(rows, width)
+    (
+        gathered_rows,
+        qkv,
+        w_heads,
+        gate_in,
+        up_own,
+        down_own,
+        output_part,
+        out_own,
+        gains,
+    ) = gather_heads(
+        tokens,
+        (attn_gain, mlp_gain),
+        w_query,
+        w_key,
+        w_value,
+        w_gate,
+        w_up,
+        w_down,
+        w_output,
+        out_rows,
+    )
+    gain_one = gains[:, 0].reshape(width).astype(jnp.float32)
+    gain_two = gains[:, 1].reshape(width).astype(jnp.float32)
     inputs = tokens.astype(jnp.float32)
 
-    output_other = swap(
-        lax.dynamic_slice_in_dim(w_output, core * (half_width // 2), half_width // 2, axis=0), 1, 0
-    )
-    output_other = ordered(core, output_other, swap(output_other, 0, 1))
-
-    def gather_quad(value):
-        across = swap(value, 1, 0)
-        return jnp.concatenate([value, swap(value, 0, 1), across, swap(across, 0, 1)], axis=0)
-
-    out_rows = out_grad.reshape(rows, width)
-    out_quad = gather_quad(out_rows)
+    output_beside = swap(output_part, 0, 2)
+    output_parts = (
+        w_output,
+        output_part,
+        output_beside,
+        swap(output_part, 0, 1),
+        swap(output_beside, 0, 1),
+    )
+    in_parts = (gate_in, up_own, swap(up_own, 1, 0))
+    down_parts = (down_own, swap(down_own, 1, 0))
+    out_far = swap(out_own, 0, 4)
+    out_quad = jnp.stack([out_rows, swap(out_own, 0, 1), out_far, swap(out_far, 0, 1)], axis=0)
 
     tables = attention_tables(lengths, here, there, row_count)
     attended, out_heads, log_sum, query, key, value = attend(tables, qkv)
-    returned = lax.all_to_all(attended, BOTH, split_axis=0, concat_axis=0, tiled=True)
-    returned = returned.reshape(groups, reps, row_count, LANES)
-    attn_rows = returned.transpose(0, 2, 1, 3).reshape(rows, width)
-    mixed, mid_quad, hidden, slopes, down_sums, grad_mixed, grad_branch, grad_att = mlp(
-        returned,
+    (
+        mixed,
+        attn_rows,
+        down_sums,
+        grad_mixed,
+        grad_branch,
+        grad_heads,
+        gate_part,
+        up_part,
+        down_part,
+    ) = mlp(
+        attended,
         tokens.reshape(rows, width),
         jnp.broadcast_to(gain_two[None], (8, width)),
-        out_quad.reshape(4, rows, width),
-        w_output,
-        output_other,
-        w_in,
-        w_down,
-    )
-    grad_heads = lax.all_to_all(
-        grad_att.reshape(groups * reps, row_count, LANES),
-        BOTH,
-        split_axis=0,
-        concat_axis=0,
-        tiled=True,
-    )
+        out_quad,
+        output_parts,
+        in_parts,
+        down_parts,
+    )
+
+    own_rows = width // (groups * reps)
+    high = reps // 8
+    high_steps = [step for step in (8 << place for place in range(8)) if step < reps]
+    bit = {step: (there // step) % 2 for step in [1, 2, 4] + high_steps}
+
+    def send(parts, axis, step):
+        flag, grp_step, rep_step = (here, 1, 0) if step == 0 else (bit[step], 0, step)
+        return pick(parts, flag, axis), swap(pick(parts, 1 - flag, axis), grp_step, rep_step)
+
+    def add(kept, arrived):
+        return narrow(kept.astype(jnp.float32) + arrived.astype(jnp.float32))
+
+    def over(parts, axis, step):
+        return add(*send(parts, axis, step))
+
+    def over_high(parts, axis):
+        for step in high_steps:
+            shape = parts.shape
+            count = shape[axis] // 2
+            parts = parts.reshape(shape[:axis] + (count, 2) + shape[axis + 1 :])
+            parts = over(parts, axis + 1, step)
+        return parts.reshape(parts.shape[:axis] + parts.shape[axis + 1 :])
+
+    by_owner = (groups, high, 2, 2, 2, own_rows)
+    up_kept, up_sent = send(up_part.reshape(by_owner + (own_width,)), 0, 0)
+    down_kept, down_sent = send(down_part.reshape(groups, high, 2, LANES, width), 2, 2)
+    output_grad = contract(attn_rows, grad_branch, 0, 0, jnp.bfloat16)
+    output_grad = over(output_grad.reshape(by_owner + (width,)), 4, 1)
+    output_kept, output_sent = send(output_grad, 2, 4)
+    sums_sent = swap(down_sums[1], 0, 4)
+
+    back = attend_back(tables, query, key, value, out_heads, log_sum, grad_heads)
+
+    up_sent, down_sent, output_sent, sums_sent = after(
+        (up_sent, down_sent, output_sent, sums_sent), back
+    )
+    up_part = add(up_kept, up_sent)
+    down_part = add(down_kept, down_sent)
+    output_grad = add(output_kept, output_sent)
+    early = (up_part, down_part, output_grad)
+    gate_kept, gate_sent = send(gate_part.reshape(by_owner[1:] + (own_width,)), 2, 2)
+    up_kept, up_sent = send(up_part, 0, 8)
+    down_kept, down_sent = send(down_part, 0, 0)
+    output_kept, output_sent = send(output_grad, 0, 0)
+    grad_in, heads_grad = scatter_heads(
+        back.reshape(reps, groups * row_count, 3 * LANES), w_heads, gathered_rows, early
+    )
+    gate_sent, up_sent, down_sent, output_sent = after(
+        (gate_sent, up_sent, down_sent, output_sent), grad_in
+    )
+    gate_part = over_high(add(gate_kept, gate_sent), 0)
+    up_part = over(add(up_kept, up_sent), 1, 2)
+    down_grad = over_high(add(down_kept, down_sent), 0).astype(jnp.float32)
+    output_grad = over_high(over(add(output_kept, output_sent), 1, 2), 0).astype(jnp.float32)
     block_out = (
-        mixed + down_sums[0].astype(jnp.float32) + swap(down_sums[1], 1, 0).astype(jnp.float32)
+        mixed + down_sums[0].astype(jnp.float32) + sums_sent.astype(jnp.float32)
     ).astype(jnp.bfloat16)
-    mid_quad = mid_quad.reshape(4 * rows, width)
-    hidden = hidden.reshape(4 * rows, own_width)
-    slopes = slopes.reshape(4 * rows, 2 * own_width)
-
-    bits = [(there // step) % 2 for step in (1, 2)]
-    far = [1 << place for place in range(2, reps.bit_length() - 1)]
-
-    def scatter_stripes(parts):
-        lead, rest = parts.shape[0], parts.shape[2:]
-        parts = halve(parts.reshape((lead, stripes // 2, 2) + rest), 2, bits[1], 0, 2)
-        for step in far:
-            count = parts.shape[1]
-            parts = halve(
-                narrow(parts).reshape((lead, count // 2, 2) + rest), 2, (there // step) % 2, 0, step
-            )
-        return parts[:, 0]
-
-    mlp_in_grad = contract(mid_quad, slopes, 0, 0, jnp.bfloat16)
-    own_rows = width // (groups * reps)
-    mlp_in_part = narrow(
-        scatter_stripes(
-            mlp_in_grad.reshape(groups, stripes, 2, own_rows, 2 * own_width)
-        )
-    )
-    down_grad = scatter_stripes(
-        contract(hidden, out_quad, 0, 0, jnp.bfloat16).reshape(1, stripes, LANES, width)
-    )[0]
-
-    kept = pick(mlp_in_part, here, 0)
-    crossed = swap(pick(mlp_in_part, 1 - here, 0), 1, 0)
+
+    quad_part = jnp.concatenate([gate_part, up_part], axis=-1)
+    kept = pick(quad_part, bit[4], 0)
+    crossed = swap(pick(quad_part, 1 - bit[4], 0), 0, 4)
     columns = []
     for part in (kept, crossed):
-        columns.append(pick(part, core, 0))
-        columns.append(swap(pick(part, 1 - core, 0), 0, 1))
-    by_grp = [
-        jnp.where(
-            core == 0,
-            jnp.stack([columns[2 * at], columns[2 * at + 1]], axis=1),
-            jnp.stack([columns[2 * at + 1], columns[2 * at]], axis=1),
-        )
-        for at in range(2)
-    ]
-    pieces = jnp.where(
-        here == 0,
-        jnp.stack([by_grp[0], by_grp[1]], axis=1),
-        jnp.stack([by_grp[1], by_grp[0]], axis=1),
-    )
-    pieces = pieces.reshape(own_rows, groups, 2, 2, stripes, LANES).transpose(3, 0, 1, 4, 2, 5)
-    pieces = pieces.reshape(2, own_rows, hidden_width).astype(jnp.float32)
-    gate_grad, up_grad = pieces[0], pieces[1]
-
-    output_part = contract(attn_rows, grad_branch, 0, 0, jnp.bfloat16)
-    output_part = output_part.reshape(groups, stripes, 2, own_rows, width)
-    output_part = halve(output_part, 2, core, 0, 1)
-    output_part = halve(narrow(output_part), 0, here, 1, 0)
-    output_grad = scatter_stripes(narrow(output_part)[None])[0]
-
-    back = attend_back(tables, query, key, value, out_heads, log_sum, grad_heads)
-    grad_in, heads_grad = scatter_heads(
-        back.reshape(reps, groups * row_count, 3 * LANES), w_heads, gathered_rows
-    )
+        columns.append(pick(part, bit[1], 0))
+        columns.append(swap(pick(part, 1 - bit[1], 0), 0, 1))
+
+    def by_bit(flag, own, other):
+        return jnp.where(
+            flag == 0, jnp.stack([own, other], axis=1), jnp.stack([other, own], axis=1)
+        )
+
+    pieces = by_bit(
+        bit[4], by_bit(bit[1], columns[0], columns[1]), by_bit(bit[1], columns[2], columns[3])
+    )
+    pieces = pieces.reshape(own_rows, 2, 2, 2, groups, high, 2, LANES)
+    pieces = pieces.transpose(3, 0, 4, 5, 1, 6, 2, 7).reshape(2, own_rows, hidden_width)
+    gate_grad, up_grad = pieces[0].astype(jnp.float32), pieces[1].astype(jnp.float32)
+
     grad_norm_in, unused_gain = norm_backward(
         inputs.reshape(rows, width), gain_one, grad_in.reshape(rows, width)
     )
@@ -1878,7 +2123,7 @@
         groups == 2
         and tokens.shape[0] == groups
         and tokens.shape[2] == reps * LANES
-        and reps % 4 == 0
+        and reps == 16
         and reps & (reps - 1) == 0
         and tokens.shape[1] % UNIT_PAIR == 0
         and arrays[7].shape[1] == groups * reps * LANES

time: 825 us -> 701 us (0.85)
  waiting for transfers between devices: 162 us -> 84.8 us
  Pallas kernels: 524 us -> 498 us
  matrix products: 21.5 us -> 3.92 us
    pallas_call x1, Pallas kernels: 185 us -> 110 us  [gather_heads(): pl.pallas_call(gather_kernel, out_shape=(jax.ShapeDtypeStruct((reps, 2 *...]
    pallas_call x1, Pallas kernels: 86.4 us -> 144 us  [mlp(): pl.pallas_call(mlp_kernel, out_shape=(jax.ShapeDtypeStruct((rows, width),...]
    ppermute x22 -> x25, waiting for transfers between devices: 127 us -> 84.8 us  [swap(): return lax.ppermute(value, BOTH, pairs)]
    all_to_all x2 -> x0, waiting for transfers between devices: 35.3 us -> none  [the longest x1 19.4 us: heads_body(): lax.all_to_all(attended, BOTH, split_axis=0, concat_axis=0, tiled=True)]
    dot_general x3 -> x1, matrix products: 21.5 us -> 3.92 us  [contract(): lax.dot_general(left_side, right_side, (((left_dim,), (right_dim,)), ((),...]
    all_to_all x2 -> x0, starting transfers between devices: 10.4 us -> none  [the longest x1 5.24 us: heads_body(): lax.all_to_all(grad_att.reshape(groups * reps, row_count, LANES), BOTH, s...]
    ppermute x22 -> x25, starting transfers between devices: 13 us -> 22.4 us  [swap(): return lax.ppermute(value, BOTH, pairs)]
    convert_element_type x9 -> x10, other arithmetic: 15 us -> 18.1 us  [narrow(): return value.astype(jnp.bfloat16)]
  transfers between devices with their start and end apart: 24 -> 25, of which waited for: 12 -> 8; matrix products, arithmetic and copies ran while one was open for 10% -> 8% of each run, Pallas kernels for 53% -> 35%
where the time goes in v4:
time: 701 us; the launch traced here: 692 us
  Pallas kernels  498 us (71%)
  waiting for transfers between devices  84.8 us (12%)
  other arithmetic  43.3 us (6%)
  local copies, waits for them, and re-layouts  37.6 us (5%)
  starting transfers between devices  22.4 us (3%)
    pallas_call x1, Pallas kernels, mlp(): pl.pallas_call(mlp_kernel, out_shape=(jax.ShapeDtypeStruct((rows, width),...  144 us
    pallas_call x1, Pallas kernels, scatter_heads(): pl.pallas_call(scatter_kernel, out_shape=(jax.ShapeDtypeStruct((2, row_co...  134 us
    pallas_call x1, Pallas kernels, gather_heads(): pl.pallas_call(gather_kernel, out_shape=(jax.ShapeDtypeStruct((reps, 2 *...  110 us
    ppermute x25, waiting for transfers between devices, swap(): return lax.ppermute(value, BOTH, pairs)  84.8 us
    pallas_call x1, Pallas kernels, attend_back(): pl.pallas_call(attend_back_kernel, out_shape=jax.ShapeDtypeStruct((parts,...  58.4 us
    pallas_call x1, Pallas kernels, attend(): pl.pallas_call(attend_kernel, out_shape=(jax.ShapeDtypeStruct((parts, uni...  52.5 us
    ppermute x25, starting transfers between devices, swap(): return lax.ppermute(value, BOTH, pairs)  22.4 us
    convert_element_type x10, other arithmetic, narrow(): return value.astype(jnp.bfloat16)  18.1 us
  transfers between devices with their start and end apart: 25, of which 8 were waited for; matrix products, arithmetic and copies ran while one was open for 8% of the time, Pallas kernels for 35%

profile of v4, /device:TPU:0, one launch (start us, length us, event | category | flops | bytes accessed | tf_op | source)
XLA Modules:
  0.0 691.6 jit_solution(2698984926607019751)
XLA Ops:
  2.8 109.7 %gather_heads.1 = (bf16[16,256,2048]{2,1,0:T(8,128)(2,1)}, bf16[32,128,384]{2,1,0:T(8,128)(2,1)}, bf16[2,1024,384]{2,1,0:T(8,128)(2,1)}, bf16[2,1024,1024]{2,1,0...) custom-call(bf16[2,128,2048]{2,1,0:T(8,128)(2,1)} %tokens_ref.1, ...), custom_call_target="tpu_custom_call" | custom-call | flops 8000000000 | bytes 262144000 | tf_op jit(solution)/shard_map/gather_heads/pallas_call | solution.py:1147
  112.5 1.6 collective-permute-start.1
  114.1 1.5 collective-permute-start.3
  120.8 16.0 %collective-permute-done.1 = bf16[256,2048]{1,0:T(8,128)(2,1)S(1)} collective-permute-done((bf16[256,2048]{1,0:T(8,128)(2,1)}, bf16[256,2048]{1,0:T(8,128)(2,1)S(1)}, u32[]{:S(2)}, u32[]{:S(2)}) %collective-permute-start.1) | collective-permute-done | bytes 1048608 | tf_op jit(solution)/shard_map/ppermute | solution.py:839
  137.3 2.7 collective-permute-done.3.output_b
  140.7 52.5 %attend.1 = (bf16[32,128,128]{2,1,0:T(8,128)(2,1)}, f32[16,128,256]{2,1,0:T(8,128)}, f32[16,8,256]{2,1,0:T(8,128)}, bf16[16,256,128]{2,1,0:T(8,128)(2,1)}, bf16[...) custom-call(s32[32]{0:T(128)} %fusion.34.slot_ref, s32[16]{0:T(128)} %get-tuple-element.88.first_ref, ...), custom_call_target="tpu_custom_call" | custom-call | flops 20000000000 | bytes 16777216 | tf_op jit(solution)/shard_map/attend/pallas_call | solution.py:737
  193.2 1.4 slice_convert_fusion.2
  194.7 3.3 pad_maximum_fusion.out_ref
  198.0 11.0 %collective-permute-done.7.down_other = bf16[512,2048]{1,0:T(8,128)(2,1)} collective-permute-done((bf16[512,2048]{1,0:T(8,128)(2,1)}, bf16[512,2048]{1,0:T(8,128)(2,1)}, u32[]{:S(2)}, u32[]{:S(2)}) %collective-permute-start.7) | collective-permute-done | bytes 2097184 | tf_op jit(solution)/shard_map/ppermute | solution.py:839
  209.6 143.6 %mlp.1 = (f32[256,2048]{1,0:T(8,128)}, bf16[256,2048]{1,0:T(8,128)(2,1)}, bf16[2,256,2048]{2,1,0:T(8,128)(2,1)}, f32[256,2048]{1,0:T(8,128)}, bf16[256,2048]{1,0...) custom-call(bf16[32,128,128]{2,1,0:T(8,128)(2,1)} %get-tuple-element, ...), custom_call_target="tpu_custom_call" | custom-call | flops 149999992832 | bytes 157286400 | tf_op jit(solution)/shard_map/mlp/pallas_call | solution.py:1854
  353.2 3.9 convolution_convert_fusion
  357.1 4.2 constant_dynamic-slice_fusion.5
  361.3 4.8 copy.101
  366.7 3.3 dynamic-slice_bitcast_fusion.1
  370.1 1.3 collective-permute-start.9
  371.3 1.5 dynamic-slice_bitcast_fusion.2
  373.8 3.4 collective-permute-start.12
  379.0 3.7 fusion
  382.9 1.9 copy-done.3
  385.5 58.4 %attend_back.1.refs_4_ = bf16[32,128,384]{2,1,0:T(8,128)(2,1)} custom-call(s32[32]{0:T(128)} %fusion.34.slot_ref, s32[16]{0:T(128)} %get-tuple-element.88.first_ref, s32[16]{0:T(128)} %get-tuple-element.87.plain_ref, f32[128,128]{1,0:T(8,128)} %get-tuple-element.107.cos_unit, f32[128,128]{1,0:T(8,128)} %get-tuple-element.106.sin_unit, ...), custom_call_target="tpu_custom_call" | custom-call | flops 49999998976 | bytes 16777216 | tf_op jit(solution)/shard_map/attend_back/pallas_call | solution.py:769
  446.3 3.3 fusion.1.refs_2_
  449.7 3.2 fusion.3.refs_0_
  453.0 1.1 dynamic-slice_bitcast_fusion.5
  454.0 1.3 collective-permute-start.14
  455.3 1.1 dynamic-slice_bitcast_fusion.3
  458.4 1.1 dynamic-slice_bitcast_fusion.4
  460.5 133.9 %scatter_heads.1 = (f32[2,128,2048]{2,1,0:T(8,128)}, bf16[16,64,384]{2,1,0:T(8,128)(2,1)}) custom-call(bf16[16,256,384]{2,1,0:T(8,128)(2,1)} %bitcast.157, bf16[2,1024,384]{2,1,0:T(8,128)(2,1)} %get-tuple-element.67.weight_ref, bf16[16,256,2048]{2,1,0:T(8,128)(2,1)} %get-tuple-element.68.normed_ref, bf16[2,2,2,2,64,1024]{5,4,3,2,1,0:T(8,128)(2,1)} %copy-done.6, ...), custom_call_target="tpu_custom_call" | custom-call | flops 14000000000 | bytes 262144000 | tf_op jit(solution)/shard_map/scatter_heads/pallas_call | solution.py:1417
  594.4 2.6 reshape.432
  597.0 1.6 fusion.41
  600.7 2.2 multiply_reduce_fusion.6
  602.9 2.6 multiply_reduce_fusion.4
  605.5 1.3 convert_divide_fusion.1
  606.8 1.5 fusion.9
  608.6 1.6 fusion.14
  610.3 1.5 copy-done.9
  611.8 1.8 fusion.4
  613.8 1.7 fusion.5
  615.5 2.0 collective-permute-start.20
  617.5 1.7 fusion.6
  619.2 3.0 collective-permute-start.19
  622.2 1.5 fusion.7
  623.9 6.3 collective-permute-done.20
  630.5 31.7 %collective-permute-done.19 = bf16[1,2,2,64,1024]{4,3,2,1,0:T(8,128)(2,1)S(1)} collective-permute-done((bf16[1,2,2,64,1024]{4,3,2,1,0:T(8,128)(2,1)S(1)}, bf16[1,2,2,64,1024]{4,3,2,1,0:T(8,128)(2,1)S(1)}, u32[]{:S(2)}, u32[]{:S(2)}) %collective-permute-start.19) | collective-permute-done | bytes 524320 | tf_op jit(solution)/shard_map/ppermute | solution.py:839
  662.9 2.1 collective-permute-start.18
  665.0 1.1 fusion.20
  666.3 16.3 %collective-permute-done.22 = bf16[2,64,2048]{2,1,0:T(8,128)(2,1)S(1)} collective-permute-done((bf16[2,64,2048]{2,1,0:T(8,128)(2,1)S(1)}, bf16[2,64,2048]{2,1,0:T(8,128)(2,1)S(1)}, u32[]{:S(2)}, u32[]{:S(2)}) %collective-permute-start.22) | collective-permute-done | bytes 524320 | tf_op jit(solution)/shard_map/ppermute | solution.py:839
  688.2 1.9 multiply_reduce_fusion.2
  690.2 1.3 convert_divide_fusion
  (159 shorter events, 28.2 us)
Async XLA Ops:
  0.6 115.8 %copy-start = (s32[2,4]{1,0:T(2,128)S(1)}, s32[2,4]{1,0:T(2,128)}, u32[]{:S(2)}) copy-start(s32[2,4]{1,0:T(2,128)} %param.23) | copy-start | bytes 100
  112.5 24.3 %collective-permute-start.1 = (bf16[256,2048]{1,0:T(8,128)(2,1)}, bf16[256,2048]{1,0:T(8,128)(2,1)S(1)}, u32[]{:S(2)}, u32[]{:S(2)}) collective-permute-start(bf16[256,2048]{1,0:T(8,128)(2,1)} %get-tuple-element.48), channel_id=1, source_target_pairs={{0,4},{1,5},{2,6},{3,7},{4,0},{5,1},{6,2},{7,3},{8,12},{9,13},{10,... | collective-permute-start | bytes 3145736 | tf_op jit(solution)/shard_map/ppermute | solution.py:839
  114.1 23.2 %collective-permute-start = (bf16[256,2048]{1,0:T(8,128)(2,1)}, bf16[256,2048]{1,0:T(8,128)(2,1)S(1)}, u32[]{:S(2)}, u32[]{:S(2)}) collective-permute-start(bf16[256,2048]{1,0:T(8,128)(2,1)} %get-tuple-element.48), channel_id=1, source_target_pairs={{0,1},{1,0},{2,3},{3,2},{4,5},{5,4},{6,7},{7,6},{8,9},{9,8},{10,11... | collective-permute-start | bytes 3145736 | tf_op jit(solution)/shard_map/ppermute | solution.py:839
  114.1 25.9 %collective-permute-start.3 = (bf16[256,2048]{1,0:T(8,128)(2,1)}, bf16[256,2048]{1,0:T(8,128)(2,1)}, u32[]{:S(2)}, u32[]{:S(2)}) collective-permute-start(bf16[256,2048]{1,0:T(8,128)(2,1)} %get-tuple-element.49.output_a), channel_id=1, source_target_pairs={{0,2},{1,3},{2,0},{3,1},{4,6},{5,7},{6,4},{7,5},{8,10},{9,11},{10,... | collective-permute-start | bytes 3145736 | tf_op jit(solution)/shard_map/ppermute | solution.py:839
  115.6 82.3 %collective-permute-start.4 = (bf16[256,2048]{1,0:T(8,128)(2,1)}, bf16[256,2048]{1,0:T(8,128)(2,1)}, u32[]{:S(2)}, u32[]{:S(2)}) collective-permute-start(bf16[256,2048]{1,0:T(8,128)(2,1)} %get-tuple-element.49.output_a), channel_id=1, source_target_pairs={{0,1},{1,0},{2,3},{3,2},{4,5},{5,4},{6,7},{7,6},{8,9},{9,8},{10,11... | collective-permute-start | bytes 3145736 | tf_op jit(solution)/shard_map/ppermute | solution.py:839
  115.9 82.1 %collective-permute-start.6 = (bf16[1024,1024]{1,0:T(8,128)(2,1)}, bf16[1024,1024]{1,0:T(8,128)(2,1)}, u32[]{:S(2)}, u32[]{:S(2)}) collective-permute-start(bf16[1024,1024]{1,0:T(8,128)(2,1)} %get-tuple-element.51.up_own), channel_id=1, source_target_pairs={{0,16},{1,17},{2,18},{3,19},{4,20},{5,21},{6,22},{7,23},{8,24},{9,... | collective-permute-start | bytes 6291464 | tf_op jit(solution)/shard_map/ppermute | solution.py:839
  136.8 72.2 %collective-permute-start.7 = (bf16[512,2048]{1,0:T(8,128)(2,1)}, bf16[512,2048]{1,0:T(8,128)(2,1)}, u32[]{:S(2)}, u32[]{:S(2)}) collective-permute-start(bf16[512,2048]{1,0:T(8,128)(2,1)} %get-tuple-element.52.down_own), channel_id=1, source_target_pairs={{0,16},{1,17},{2,18},{3,19},{4,20},{5,21},{6,22},{7,23},{8,24},{9,... | collective-permute-start | bytes 6291464 | tf_op jit(solution)/shard_map/ppermute | solution.py:839
  137.3 57.3 %collective-permute-start.2 = (bf16[256,2048]{1,0:T(8,128)(2,1)S(1)}, bf16[256,2048]{1,0:T(8,128)(2,1)}, u32[]{:S(2)}, u32[]{:S(2)}) collective-permute-start(bf16[256,2048]{1,0:T(8,128)(2,1)S(1)} %collective-permute-done.1), channel_id=1, source_target_pairs={{0,1},{1,0},{2,3},{3,2},{4,5},{5,4},{6,7},{7,6},{8,9},{9,8},{10,11... | collective-permute-start | bytes 3145736 | tf_op jit(solution)/shard_map/ppermute | solution.py:839
  140.0 58.0 %collective-permute-start.5 = (bf16[256,2048]{1,0:T(8,128)(2,1)}, bf16[256,2048]{1,0:T(8,128)(2,1)}, u32[]{:S(2)}, u32[]{:S(2)}) collective-permute-start(bf16[256,2048]{1,0:T(8,128)(2,1)} %collective-permute-done.3.output_b), channel_id=1, source_target_pairs={{0,1},{1,0},{2,3},{3,2},{4,5},{5,4},{6,7},{7,6},{8,9},{9,8},{10,11... | collective-permute-start | bytes 3145736 | tf_op jit(solution)/shard_map/ppermute | solution.py:839
  140.7 54.0 %copy-start.21 = (bf16[2,128,2048]{2,1,0:T(8,128)(2,1)S(1)}, bf16[2,128,2048]{2,1,0:T(8,128)(2,1)}, u32[]{:S(2)}) copy-start(bf16[2,128,2048]{2,1,0:T(8,128)(2,1)} %param.22) | copy-start | bytes 3145732
  361.3 5.1 copy-start.5
  366.2 12.9 %collective-permute-start.10 = (bf16[2,2,2,2,64,2048]{5,4,3,1,0,2:T(8,128)(2,1)}, bf16[2,2,2,2,64,2048]{5,4,3,1,0,2:T(8,128)(2,1)}, u32[]{:S(2)}, u32[]{:S(2)}) collective-permute-start(bf16[2,2,2,2,64,2048]{5,4,3,1,0,2:T(8,128)(2,1)} %bitcast.147), channel_id=1, source_target_pairs={{0,1},{1,0},{2,3},{3,2},{4,5},{5,4},{6,7},{7,6},{8,9},{9,8},{10,11... | collective-permute-start | bytes 12582920 | tf_op jit(solution)/shard_map/ppermute | solution.py:839
  366.7 4.6 copy-start.17
  370.1 73.9 %collective-permute-start.9 = (bf16[2,2,128,2048]{3,2,1,0:T(8,128)(2,1)}, bf16[2,2,128,2048]{3,2,1,0:T(8,128)(2,1)S(1)}, u32[]{:S(2)}, u32[]{:S(2)}) collective-permute-start(bf16[2,2,128,2048]{3,2,1,0:T(8,128)(2,1)} %dynamic-slice_bitcast_fusion.1), channel_id=1, source_target_pairs={{0,2},{1,3},{2,0},{3,1},{4,6},{5,7},{6,4},{7,5},{8,10},{9,11},{10,... | collective-permute-start | bytes 6291464 | tf_op jit(solution)/shard_map/ppermute | solution.py:839
  371.3 2.3 copy-start.23
  371.3 5.9 copy-start.25
  372.8 72.1 %collective-permute-start.8 = (bf16[2,2,2,2,64,1024]{5,4,3,2,1,0:T(8,128)(2,1)}, bf16[2,2,2,2,64,1024]{5,4,3,2,1,0:T(8,128)(2,1)}, u32[]{:S(2)}, u32[]{:S(2)}) collective-permute-start(bf16[2,2,2,2,64,1024]{5,4,3,2,1,0:T(8,128)(2,1)} %dynamic-slice_bitcast_fusion.2), channel_id=1, source_target_pairs={{0,16},{1,17},{2,18},{3,19},{4,20},{5,21},{6,22},{7,23},{8,24},{9,... | collective-permute-start | bytes 6291464 | tf_op jit(solution)/shard_map/ppermute | solution.py:839
  373.7 5.3 copy-start.4
  373.8 70.2 %collective-permute-start.12 = (bf16[256,2048]{1,0:T(8,128)(2,1)S(1)}, bf16[256,2048]{1,0:T(8,128)(2,1)S(1)}, u32[]{:S(2)}, u32[]{:S(2)}) collective-permute-start(bf16[256,2048]{1,0:T(8,128)(2,1)S(1)} %slice_bitcast_fusion), channel_id=1, source_target_pairs={{0,4},{1,5},{2,6},{3,7},{4,0},{5,1},{6,2},{7,3},{8,12},{9,13},{10,... | collective-permute-start | bytes 3145736 | tf_op jit(solution)/shard_map/ppermute | solution.py:839
  378.3 232.0 %collective-permute-start.13 = (bf16[2,2,2,64,1024]{4,3,2,1,0:T(8,128)(2,1)}, bf16[2,2,2,64,1024]{4,3,2,1,0:T(8,128)(2,1)}, u32[]{:S(2)}, u32[]{:S(2)}) collective-permute-start(bf16[2,2,2,64,1024]{4,3,2,1,0:T(8,128)(2,1)} %dynamic-slice_bitcast_fusion.6), channel_id=1, source_target_pairs={{0,2},{1,3},{2,0},{3,1},{4,6},{5,7},{6,4},{7,5},{8,10},{9,11},{10,... | collective-permute-start | bytes 3145736 | tf_op jit(solution)/shard_map/ppermute | solution.py:839
  382.7 2.0 copy-start.3
  384.7 60.9 %collective-permute-start.11 = (bf16[2,2,2,64,2048]{4,3,2,1,0:T(8,128)(2,1)S(1)}, bf16[2,2,2,64,2048]{4,3,2,1,0:T(8,128)(2,1)}, u32[]{:S(2)}, u32[]{:S(2)}) collective-permute-start(bf16[2,2,2,64,2048]{4,3,2,1,0:T(8,128)(2,1)S(1)} %dynamic-slice_bitcast_fusion), channel_id=1, source_target_pairs={{0,4},{1,5},{2,6},{3,7},{4,0},{5,1},{6,2},{7,3},{8,12},{9,13},{10,... | collective-permute-start | bytes 6291464 | tf_op jit(solution)/shard_map/ppermute | solution.py:839
  446.3 3.4 copy-start.18
  449.6 5.8 copy-start.12
  449.7 7.7 %copy-start.16 = (bf16[1024,2048]{1,0:T(8,128)(2,1)S(1)}, bf16[1024,2048]{1,0:T(8,128)(2,1)}, u32[]{:S(2)}) copy-start(bf16[1024,2048]{1,0:T(8,128)(2,1)} %get-tuple-element.56) | copy-start | bytes 12582916
  452.9 3.5 copy-start.6
  452.9 4.5 copy-start.11
  454.0 156.2 %collective-permute-start.14 = (bf16[2,2,2,64,1024]{4,3,2,1,0:T(8,128)(2,1)}, bf16[2,2,2,64,1024]{4,3,2,1,0:T(8,128)(2,1)}, u32[]{:S(2)}, u32[]{:S(2)}) collective-permute-start(bf16[2,2,2,64,1024]{4,3,2,1,0:T(8,128)(2,1)} %dynamic-slice_bitcast_fusion.5), channel_id=1, source_target_pairs={{0,8},{1,9},{2,10},{3,11},{4,12},{5,13},{6,14},{7,15},{8,0},{9,1},... | collective-permute-start | bytes 3145736 | tf_op jit(solution)/shard_map/ppermute | solution.py:839
  456.4 153.8 %collective-permute-start.16 = (bf16[2,2,64,2048]{3,2,1,0:T(8,128)(2,1)}, bf16[2,2,64,2048]{3,2,1,0:T(8,128)(2,1)}, u32[]{:S(2)}, u32[]{:S(2)}) collective-permute-start(bf16[2,2,64,2048]{3,2,1,0:T(8,128)(2,1)} %dynamic-slice_bitcast_fusion.3), channel_id=1, source_target_pairs={{0,16},{1,17},{2,18},{3,19},{4,20},{5,21},{6,22},{7,23},{8,24},{9,... | collective-permute-start | bytes 3145736 | tf_op jit(solution)/shard_map/ppermute | solution.py:839
  458.4 2.1 copy-start.8
  459.5 150.7 %collective-permute-start.15 = (bf16[2,128,2048]{2,1,0:T(8,128)(2,1)}, bf16[2,128,2048]{2,1,0:T(8,128)(2,1)}, u32[]{:S(2)}, u32[]{:S(2)}) collective-permute-start(bf16[2,128,2048]{2,1,0:T(8,128)(2,1)} %dynamic-slice_bitcast_fusion.4), channel_id=1, source_target_pairs={{0,16},{1,17},{2,18},{3,19},{4,20},{5,21},{6,22},{7,23},{8,24},{9,... | collective-permute-start | bytes 3145736 | tf_op jit(solution)/shard_map/ppermute | solution.py:839
  600.2 6.6 copy-start.27
  600.7 6.1 copy-start.15
  600.7 6.1 copy-start.24
  606.8 1.8 copy-start.22
  611.8 1.9 copy-start.7
  613.7 51.3 %collective-permute-start.24 = (bf16[1,128,2048]{2,1,0:T(8,128)(2,1)S(1)}, bf16[1,128,2048]{2,1,0:T(8,128)(2,1)S(1)}, u32[]{:S(2)}, u32[]{:S(2)}) collective-permute-start(bf16[1,128,2048]{2,1,0:T(8,128)(2,1)S(1)} %constant_dynamic-slice_fusion), channel_id=1, source_target_pairs={{0,8},{1,9},{2,10},{3,11},{4,12},{5,13},{6,14},{7,15},{8,0},{9,1},... | collective-permute-start | bytes 1572872 | tf_op jit(solution)/shard_map/ppermute | solution.py:839
  613.7 3.7 copy-start.26
  615.5 14.8 %collective-permute-start.20 = (bf16[2,2,64,1024]{3,2,1,0:T(8,128)(2,1)S(1)}, bf16[2,2,64,1024]{3,2,1,0:T(8,128)(2,1)S(1)}, u32[]{:S(2)}, u32[]{:S(2)}) collective-permute-start(bf16[2,2,64,1024]{3,2,1,0:T(8,128)(2,1)S(1)} %dynamic-slice_bitcast_fusion.7), channel_id=1, source_target_pairs={{0,2},{1,3},{2,0},{3,1},{4,6},{5,7},{6,4},{7,5},{8,10},{9,11},{10,... | collective-permute-start | bytes 1572872 | tf_op jit(solution)/shard_map/ppermute | solution.py:839
  617.5 4.7 copy-start.13
  619.2 43.0 %collective-permute-start.19 = (bf16[1,2,2,64,1024]{4,3,2,1,0:T(8,128)(2,1)S(1)}, bf16[1,2,2,64,1024]{4,3,2,1,0:T(8,128)(2,1)S(1)}, u32[]{:S(2)}, u32[]{:S(2)}) collective-permute-start(bf16[1,2,2,64,1024]{4,3,2,1,0:T(8,128)(2,1)S(1)} %constant_dynamic-slice_fusion.2), channel_id=1, source_target_pairs={{0,8},{1,9},{2,10},{3,11},{4,12},{5,13},{6,14},{7,15},{8,0},{9,1},... | collective-permute-start | bytes 1572872 | tf_op jit(solution)/shard_map/ppermute | solution.py:839
  623.7 39.0 %collective-permute-start.17 = (bf16[2,64,2048]{2,1,0:T(8,128)(2,1)S(1)}, bf16[2,64,2048]{2,1,0:T(8,128)(2,1)S(1)}, u32[]{:S(2)}, u32[]{:S(2)}) collective-permute-start(bf16[2,64,2048]{2,1,0:T(8,128)(2,1)S(1)} %dynamic-slice_bitcast_fusion.8), channel_id=1, source_target_pairs={{0,2},{1,3},{2,0},{3,1},{4,6},{5,7},{6,4},{7,5},{8,10},{9,11},{10,... | collective-permute-start | bytes 1572872 | tf_op jit(solution)/shard_map/ppermute | solution.py:839
  662.5 21.1 %collective-permute-start.21 = (bf16[64,2048]{1,0:T(8,128)(2,1)S(1)}, bf16[64,2048]{1,0:T(8,128)(2,1)S(1)}, u32[]{:S(2)}, u32[]{:S(2)}) collective-permute-start(bf16[64,2048]{1,0:T(8,128)(2,1)S(1)} %get-tuple-element.97), channel_id=1, source_target_pairs={{0,1},{1,0},{2,3},{3,2},{4,5},{5,4},{6,7},{7,6},{8,9},{9,8},{10,11... | collective-permute-start | bytes 786440 | tf_op jit(solution)/shard_map/ppermute | solution.py:839
  662.6 20.0 %collective-permute-start.22 = (bf16[2,64,2048]{2,1,0:T(8,128)(2,1)S(1)}, bf16[2,64,2048]{2,1,0:T(8,128)(2,1)S(1)}, u32[]{:S(2)}, u32[]{:S(2)}) collective-permute-start(bf16[2,64,2048]{2,1,0:T(8,128)(2,1)S(1)} %fusion.22), channel_id=1, source_target_pairs={{0,4},{1,5},{2,6},{3,7},{4,0},{5,1},{6,2},{7,3},{8,12},{9,13},{10,... | collective-permute-start | bytes 1572872 | tf_op jit(solution)/shard_map/ppermute | solution.py:839
  662.9 19.8 %collective-permute-start.18 = (bf16[1,64,2048]{2,1,0:T(8,128)(2,1)S(1)}, bf16[1,64,2048]{2,1,0:T(8,128)(2,1)S(1)}, u32[]{:S(2)}, u32[]{:S(2)}) collective-permute-start(bf16[1,64,2048]{2,1,0:T(8,128)(2,1)S(1)} %constant_dynamic-slice_fusion.3), channel_id=1, source_target_pairs={{0,8},{1,9},{2,10},{3,11},{4,12},{5,13},{6,14},{7,15},{8,0},{9,1},... | collective-permute-start | bytes 786440 | tf_op jit(solution)/shard_map/ppermute | solution.py:839
  682.6 1.6 collective-permute-start.23
  687.3 4.1 copy-start.1
  688.2 3.2 copy-start.20
  (6 other events, 8.8 us)

commit v5 on v4

--- a/solution.py
+++ b/solution.py
@@ -922,7 +922,8 @@
     weight_ref,
     gate_ref,
     up_ref,
-    down_ref,
+    down_first,
+    down_second,
     output_ref,
     out_away,
     gains,
@@ -1040,9 +1041,10 @@
             load(columns_of(weight, *stripe), target_ref.at[:, pl.ds(at * LANES, LANES)])
     for at, (grp, high, low) in enumerate(stripes[: len(stripes) // 2]):
         first = (8 * high + 2 * low + place) * LANES
+        target_ref = (down_first, down_second)[at // 2]
         load(
             w_down.at[pl.ds(pl.multiple_of(first, LANES), LANES)],
-            down_ref.at[pl.ds(at * LANES, LANES)],
+            target_ref.at[pl.ds(at % 2 * LANES, LANES)],
         )
     load(out_rows, out_away)
     for one in stripe_loads:
@@ -1152,13 +1154,14 @@
             jax.ShapeDtypeStruct((2, half, 3 * LANES), jnp.bfloat16),
             jax.ShapeDtypeStruct((2, half, own_width), jnp.bfloat16),
             jax.ShapeDtypeStruct((half, own_width), jnp.bfloat16),
-            jax.ShapeDtypeStruct((own_width // 2, width), jnp.bfloat16),
+            jax.ShapeDtypeStruct((2 * LANES, width), jnp.bfloat16),
+            jax.ShapeDtypeStruct((own_width // 2 - 2 * LANES, width), jnp.bfloat16),
             jax.ShapeDtypeStruct((half // 4, width), jnp.bfloat16),
             jax.ShapeDtypeStruct(out_rows.shape, jnp.bfloat16),
             jax.ShapeDtypeStruct((2, 16, half), jnp.bfloat16),
         ),
         in_specs=[vmem, vmem] + [anywhere] * 8,
-        out_specs=(anywhere,) + (vmem,) * 8,
+        out_specs=(anywhere,) + (vmem,) * 9,
         scratch_shapes=[
             pltpu.VMEM((reps, 2, row_count, width), jnp.bfloat16),
             pltpu.VMEM((4, 2 * row_count, width), jnp.bfloat16),
@@ -1454,27 +1457,32 @@
     heads_ref,
     tokens_ref,
     gain_ref,
-    out_ref,
+    out_rows,
+    out_across,
     output_own,
-    output_a,
-    output_b,
-    output_c,
-    output_d,
+    output_part,
+    output_beside,
     gate_in,
     up_own,
     up_other,
-    down_own,
+    down_first,
+    down_second,
     down_other,
     mixed_ref,
-    attended,
     down_ref,
     grad_ref,
-    branch_ref,
     back_ref,
     gate_ref,
-    up_ref,
-    down_grad_ref,
+    up_kept,
+    up_sent,
+    down_kept,
+    down_sent,
+    output_kept,
+    output_sent,
+    attended,
+    branch_ref,
     returned,
+    out_ref,
     mid_ref,
     hidden_ref,
     slope_ref,
@@ -1494,6 +1502,11 @@
     heads_recv,
     back_send,
     back_recv,
+    piece_sem,
+    place_sem,
+    core_send,
+    core_recv,
+    free_sem,
 ):
     here, there = lax.axis_index("grp"), lax.axis_index("rep")
     across = (here, flipped(there, 4))
@@ -1515,35 +1528,36 @@
         ),
     ]
     own_part = own_width // 2
+    early_rows = down_first.shape[0]
+
+    def down_cut(grp, first, count):
+        return pl.ds(pl.multiple_of(grp * own_part + first, LANES), count)
+
+    late_rows = own_part - early_rows
     loads += [
         pltpu.make_async_copy(
-            down_own,
-            w_out.at[pl.ds(pl.multiple_of(here * own_part, own_part), own_part)],
-            load_sem.at[4],
+            down_first, w_out.at[down_cut(here, 0, early_rows)], load_sem.at[4]
         ),
         pltpu.make_async_copy(
-            down_other,
-            w_out.at[pl.ds(pl.multiple_of((1 - here) * own_part, own_part), own_part)],
-            load_sem.at[5],
-        ),
+            down_second, w_out.at[down_cut(here, early_rows, late_rows)], load_sem.at[5]
+        ),
+        pltpu.make_async_copy(
+            down_other, w_out.at[down_cut(1 - here, 0, early_rows)], load_sem.at[6]
+        ),
+        pltpu.make_async_copy(out_rows, out_ref.at[0], load_sem.at[7]),
+        pltpu.make_async_copy(out_across, out_ref.at[2], load_sem.at[8]),
     ]
     place = there % 4
-    rest = []
-    for at, (piece, part) in enumerate(
-        (
-            (output_a, place),
-            (output_b, flipped(place, 2)),
-            (output_c, flipped(place, 1)),
-            (output_d, 3 - place),
-        )
-    ):
-        rest.append(
-            pltpu.make_async_copy(
-                piece,
-                w_output.at[1 - here, pl.ds(pl.multiple_of(part * quarter, quarter), quarter)],
-                part_sem.at[at],
-            )
-        )
+    core = there % 2
+
+    def output_cut(part):
+        return w_output.at[1 - here, pl.ds(pl.multiple_of(part * quarter, quarter), quarter)]
+
+    output_pieces = ((output_part, place), (output_beside, flipped(place, 2)))
+    rest = [
+        pltpu.make_async_copy(piece, output_cut(part), part_sem.at[at])
+        for at, (piece, part) in enumerate(output_pieces)
+    ]
     loads = loads[:1] + rest + loads[1:]
     for one in loads:
         one.start()
@@ -1563,6 +1577,18 @@
     for key in others:
         pl.semaphore_signal(barrier, inc=1, device_id=other(*key), device_id_type=MESH_IDS)
     pl.semaphore_wait(barrier, len(others))
+
+    facing = (1 - here, there)
+
+    def copy(at, source, target_ref, target):
+        return pltpu.make_async_remote_copy(
+            src_ref=source,
+            dst_ref=target_ref,
+            send_sem=send_sem.at[at],
+            recv_sem=recv_sem.at[at],
+            device_id=target,
+            device_id_type=MESH_IDS,
+        )
 
     heads_copies, back_copies = [], []
     for at, key in enumerate(others):
@@ -1589,17 +1615,16 @@
         )
     for one in heads_copies[::-1]:
         one.start()
+    output_near = [
+        copy(at, piece, output_cut(part), sibling)
+        for at, (piece, part) in enumerate(output_pieces, 9)
+    ]
+    down_far = copy(11, down_second, w_out.at[down_cut(here, early_rows, late_rows)], facing)
+    out_near = copy(12, out_rows, out_ref.at[1], sibling)
+    out_on = copy(13, out_across, out_ref.at[3], sibling)
+    for one in output_near + [out_near, out_on, down_far]:
+        one.start()
     returned[here, there] = heads_ref[here * heads + there]
-
-    def copy(at, source, target_ref, target):
-        return pltpu.make_async_remote_copy(
-            src_ref=source,
-            dst_ref=target_ref,
-            send_sem=send_sem.at[at],
-            recv_sem=recv_sem.at[at],
-            device_id=target,
-            device_id_type=MESH_IDS,
-        )
 
     mid_near = copy(0, mid_ref.at[0], mid_ref.at[1], sibling)
     mid_far = copy(1, mid_ref.at[0], mid_ref.at[2], across)
@@ -1608,12 +1633,21 @@
     grad_far = copy(5, far_away, far_landed, across)
     down_near = [copy(6 + at, near_away.at[at], down_landed.at[at], sibling) for at in range(2)]
     gate_cross = copy(
-        8, w_in.at[1 - here, :, pl.ds(0, own_width)], gate_ref, (1 - here, there)
-    )
-    up_out = pltpu.make_async_copy(
-        w_in.at[:, :, pl.ds(own_width, own_width)], up_ref, load_sem.at[0]
-    )
-    down_out = pltpu.make_async_copy(w_out, down_grad_ref, load_sem.at[1])
+        8, w_in.at[1 - here, :, pl.ds(0, own_width)], gate_ref, facing
+    )
+    up_cut = pl.ds(own_width, own_width)
+    up_outs = [
+        pltpu.make_async_copy(w_in.at[here, :, up_cut], up_kept, load_sem.at[0]),
+        pltpu.make_async_copy(w_in.at[1 - here, :, up_cut], up_sent, load_sem.at[1]),
+    ]
+    low = (there // 2) % 2
+    down_outs = []
+    for at in range(own_width // (2 * LANES)):
+        for kind, (target_ref, bit) in enumerate(((down_kept, low), (down_sent, 1 - low))):
+            cut = pl.ds(pl.multiple_of((2 * at + bit) * LANES, LANES), LANES)
+            down_outs.append(
+                pltpu.make_async_copy(w_out.at[cut], target_ref.at[at], piece_sem.at[2 * at + kind])
+            )
 
     for one in heads_copies:
         one.wait()
@@ -1622,8 +1656,10 @@
             attended[
                 group * row_count : (group + 1) * row_count, head * LANES : (head + 1) * LANES
             ] = returned[group, head]
-    for one in loads[:5]:
+    for one in loads[:3]:
         one.wait()
+    for one in output_near:
+        one.wait_recv()
     wide = 512
 
     def mix(at, unused):
@@ -1647,8 +1683,9 @@
     lax.fori_loop(0, rows // tile, norm_rows, 0)
     mid_far.start()
     mid_near.start()
-    for one in loads[5:]:
+    for one in loads[3:]:
         one.wait()
+    down_far.wait_recv()
     narrow_tile = 256
 
     def forward(slot):
@@ -1705,6 +1742,7 @@
 
     forward(0)
     mid_near.wait_recv()
+    out_near.wait_recv()
     forward(1)
     backward(1, into(near_away, 0))
     grad_near[0].start()
@@ -1717,6 +1755,7 @@
     mid_on.start()
     forward(2)
     mid_on.wait_recv()
+    out_on.wait_recv()
     forward(3)
     backward(3, into(near_away, 1))
     grad_near[1].start()
@@ -1759,7 +1798,11 @@
         down(2 * at + 1, into(near_away, at))
         down_near[at].start()
     in_grads(here)
-    up_out.start()
+    for one in up_outs:
+        one.start()
+    for one in (mid_near, mid_far, mid_on):
+        one.wait_send()
+    pl.semaphore_signal(free_sem, inc=1, device_id=sibling, device_id_type=MESH_IDS)
     for at in range(2):
         down_near[at].wait_recv()
 
@@ -1785,7 +1828,8 @@
         return lax.fori_loop(0, width // wide, columns, unused)
 
     lax.fori_loop(0, own_width // narrow_tile, down_rows, 0)
-    down_out.start()
+    for one in down_outs:
+        one.start()
     grad_near[0].wait_recv()
     grad_far.wait_recv()
 
@@ -1822,6 +1866,51 @@
     for one in back_copies[::-1]:
         one.start()
     back_ref[here * heads + there] = returned[here, there]
+
+    for at in range(2):
+
+        def output_rows(step, unused):
+            cut = pl.ds(pl.multiple_of(step * narrow_tile, narrow_tile), narrow_tile)
+            source = pl.ds(pl.multiple_of(at * half + step * narrow_tile, narrow_tile), narrow_tile)
+            left = jnp.transpose(attended[:, source].astype(jnp.float32)).astype(jnp.bfloat16)
+
+            def columns(place_at, unused):
+                cols = pl.ds(pl.multiple_of(place_at * wide, wide), wide)
+                w_output[at, cut, cols] = jnp.dot(
+                    left, branch_ref[:, cols], preferred_element_type=jnp.float32
+                ).astype(jnp.bfloat16)
+                return unused
+
+            return lax.fori_loop(0, width // wide, columns, unused)
+
+        lax.fori_loop(0, half // narrow_tile, output_rows, 0)
+
+    own_rows = half // heads
+    stripes = heads // 2
+    pl.semaphore_wait(free_sem, 1)
+
+    def stripe_of(at, bit):
+        first = (at % stripes * 2 + bit) * own_rows
+        return pl.ds(pl.multiple_of(first, own_rows), own_rows)
+
+    def landed_at(at):
+        per_slot = rows // own_rows
+        return at // per_slot, pl.ds(at % per_slot * own_rows, own_rows)
+
+    core_copies = []
+    for at in range(2 * stripes):
+        slot, cut = landed_at(at)
+        core_copies.append(
+            pltpu.make_async_remote_copy(
+                src_ref=w_output.at[at // stripes, stripe_of(at, 1 - core)],
+                dst_ref=mid_ref.at[slot, cut],
+                send_sem=core_send.at[at],
+                recv_sem=core_recv.at[at],
+                device_id=sibling,
+                device_id_type=MESH_IDS,
+            )
+        )
+        core_copies[-1].start()
     gate_cross.wait()
 
     def add_gate(at, unused):
@@ -1833,17 +1922,42 @@
         return unused
 
     lax.fori_loop(0, half // tile, add_gate, 0)
-    up_out.wait()
-    down_out.wait()
+    far_bit = (there // 4) % 2
+    output_outs = []
+    for at in range(2 * stripes):
+        core_copies[at].wait_recv()
+        slot, cut = landed_at(at)
+        own = stripe_of(at, core)
+        w_output[at // stripes, own, :] = (
+            w_output[at // stripes, own, :].astype(jnp.float32)
+            + mid_ref[slot, cut, :].astype(jnp.float32)
+        ).astype(jnp.bfloat16)
+    for at in range(stripes):
+        grp, high, low_bit = at // (stripes // 2), at // 2 % (stripes // 4), at % 2
+        for kind, (target_ref, bit) in enumerate(
+            ((output_kept, far_bit), (output_sent, 1 - far_bit))
+        ):
+            first = ((high * 4 + bit * 2 + low_bit) * 2 + core) * own_rows
+            cut = pl.ds(pl.multiple_of(first, own_rows), own_rows)
+            output_outs.append(
+                pltpu.make_async_copy(
+                    w_output.at[grp, cut], target_ref.at[at], place_sem.at[2 * at + kind]
+                )
+            )
+            output_outs[-1].start()
+    for one in up_outs + down_outs + output_outs:
+        one.wait()
     for one in back_copies:
         one.wait()
-    for one in [mid_near, mid_far, mid_on, grad_far] + down_near:
+    for one in [grad_far, out_near, out_on, down_far]:
         one.wait_send()
-
-
-def mlp(heads, tokens, gain, out_quad, output_parts, in_parts, down_parts):
+    for one in down_near + output_near + core_copies:
+        one.wait_send()
+
+
+def mlp(heads, tokens, gain, out_rows, out_across, output_parts, in_parts, down_parts):
     count, row_count, _ = heads.shape
-    groups = lax.axis_size("grp")
+    groups, reps = lax.axis_size("grp"), lax.axis_size("rep")
     rows, width = tokens.shape
     half = width // 2
     own_width = in_parts[0].shape[2]
@@ -1855,19 +1969,24 @@
         mlp_kernel,
         out_shape=(
             jax.ShapeDtypeStruct((rows, width), full),
-            jax.ShapeDtypeStruct((rows, width), low),
             jax.ShapeDtypeStruct((2, rows, width), low),
             jax.ShapeDtypeStruct((rows, width), full),
-            jax.ShapeDtypeStruct((rows, width), low),
             jax.ShapeDtypeStruct((count, row_count, LANES), low),
             jax.ShapeDtypeStruct((half, own_width), low),
-            jax.ShapeDtypeStruct((2, half, own_width), low),
-            jax.ShapeDtypeStruct((own_width, width), low),
-        ),
-        in_specs=[vmem] * 4 + [anywhere] * 10,
-        out_specs=(vmem,) * 7 + (anywhere,) * 2,
+            jax.ShapeDtypeStruct((half, own_width), low),
+            jax.ShapeDtypeStruct((half, own_width), low),
+            jax.ShapeDtypeStruct((own_width // (2 * LANES), LANES, width), low),
+            jax.ShapeDtypeStruct((own_width // (2 * LANES), LANES, width), low),
+            jax.ShapeDtypeStruct((reps // 2, half // reps, width), low),
+            jax.ShapeDtypeStruct((reps // 2, half // reps, width), low),
+        ),
+        in_specs=[vmem] * 3 + [anywhere] * 11,
+        out_specs=(vmem,) * 5 + (anywhere,) * 6,
         scratch_shapes=[
-            pltpu.VMEM((groups, count // groups, row_count, LANES), low),
+            pltpu.VMEM((rows, width), low),
+            pltpu.VMEM((rows, width), low),
+            pltpu.VMEM((groups, reps, row_count, LANES), low),
+            pltpu.VMEM((4, rows, width), low),
             pltpu.VMEM((4, rows, width), low),
             pltpu.VMEM((4, rows, own_width), low),
             pltpu.VMEM((4, rows, 2 * own_width), low),
@@ -1879,14 +1998,19 @@
             pltpu.VMEM((rows, width), low),
             pltpu.VMEM((rows, width), low),
             pltpu.VMEM((2, rows, width), low),
-            pltpu.SemaphoreType.DMA((6,)),
-            pltpu.SemaphoreType.DMA((4,)),
             pltpu.SemaphoreType.DMA((9,)),
-            pltpu.SemaphoreType.DMA((9,)),
+            pltpu.SemaphoreType.DMA((2,)),
+            pltpu.SemaphoreType.DMA((14,)),
+            pltpu.SemaphoreType.DMA((14,)),
             others,
             others,
             others,
             others,
+            pltpu.SemaphoreType.DMA((own_width // LANES,)),
+            pltpu.SemaphoreType.DMA((reps,)),
+            pltpu.SemaphoreType.DMA((reps,)),
+            pltpu.SemaphoreType.DMA((reps,)),
+            pltpu.SemaphoreType.REGULAR,
         ],
         compiler_params=pltpu.CompilerParams(
             vmem_limit_bytes=62 * 1024 * 1024, collective_id=2, has_side_effects=True
@@ -1895,7 +2019,7 @@
             flops=150 * 10**9, bytes_accessed=150 << 20, transcendentals=0
         ),
         name="mlp",
-    )(heads, tokens, gain, out_quad, *output_parts, *in_parts, *down_parts)
+    )(heads, tokens, gain, out_rows, out_across, *output_parts, *in_parts, *down_parts)
 
 
 def after_kernel(*refs):
@@ -1942,7 +2066,8 @@
         w_heads,
         gate_in,
         up_own,
-        down_own,
+        down_first,
+        down_second,
         output_part,
         out_own,
         gains,
@@ -1962,36 +2087,30 @@
     gain_two = gains[:, 1].reshape(width).astype(jnp.float32)
     inputs = tokens.astype(jnp.float32)
 
-    output_beside = swap(output_part, 0, 2)
-    output_parts = (
-        w_output,
-        output_part,
-        output_beside,
-        swap(output_part, 0, 1),
-        swap(output_beside, 0, 1),
-    )
+    output_parts = (w_output, output_part, swap(output_part, 0, 2))
     in_parts = (gate_in, up_own, swap(up_own, 1, 0))
-    down_parts = (down_own, swap(down_own, 1, 0))
-    out_far = swap(out_own, 0, 4)
-    out_quad = jnp.stack([out_rows, swap(out_own, 0, 1), out_far, swap(out_far, 0, 1)], axis=0)
+    down_parts = (down_first, down_second, swap(down_first, 1, 0))
 
     tables = attention_tables(lengths, here, there, row_count)
     attended, out_heads, log_sum, query, key, value = attend(tables, qkv)
     (
         mixed,
-        attn_rows,
         down_sums,
         grad_mixed,
-        grad_branch,
         grad_heads,
         gate_part,
-        up_part,
-        down_part,
+        up_kept,
+        up_sent,
+        down_kept,
+        down_sent,
+        output_kept,
+        output_sent,
     ) = mlp(
         attended,
         tokens.reshape(rows, width),
         jnp.broadcast_to(gain_two[None], (8, width)),
-        out_quad,
+        out_rows,
+        swap(out_own, 0, 4),
         output_parts,
         in_parts,
         down_parts,
@@ -2021,11 +2140,9 @@
         return parts.reshape(parts.shape[:axis] + parts.shape[axis + 1 :])
 
     by_owner = (groups, high, 2, 2, 2, own_rows)
-    up_kept, up_sent = send(up_part.reshape(by_owner + (own_width,)), 0, 0)
-    down_kept, down_sent = send(down_part.reshape(groups, high, 2, LANES, width), 2, 2)
-    output_grad = contract(attn_rows, grad_branch, 0, 0, jnp.bfloat16)
-    output_grad = over(output_grad.reshape(by_owner + (width,)), 4, 1)
-    output_kept, output_sent = send(output_grad, 2, 4)
+    up_sent = swap(up_sent, 1, 0)
+    down_sent = swap(down_sent, 0, 2)
+    output_sent = swap(output_sent, 0, 4)
     sums_sent = swap(down_sums[1], 0, 4)
 
     back = attend_back(tables, query, key, value, out_heads, log_sum, grad_heads)
@@ -2033,9 +2150,9 @@
     up_sent, down_sent, output_sent, sums_sent = after(
         (up_sent, down_sent, output_sent, sums_sent), back
     )
-    up_part = add(up_kept, up_sent)
-    down_part = add(down_kept, down_sent)
-    output_grad = add(output_kept, output_sent)
+    up_part = add(up_kept, up_sent).reshape(by_owner[1:] + (own_width,))
+    down_part = add(down_kept, down_sent).reshape(groups, high, LANES, width)
+    output_grad = add(output_kept, output_sent).reshape(groups, high, 2, own_rows, width)
     early = (up_part, down_part, output_grad)
     gate_kept, gate_sent = send(gate_part.reshape(by_owner[1:] + (own_width,)), 2, 2)
     up_kept, up_sent = send(up_part, 0, 8)

time: 701 us -> 664 us (0.947)
  waiting for transfers between devices: 84.8 us -> 71 us
  local copies, waits for them, and re-layouts: 37.6 us -> 24.4 us
  Pallas kernels: 498 us -> 506 us
  other arithmetic: 43.3 us -> 36.1 us
    pallas_call x1, Pallas kernels: 144 us -> 158 us  [mlp(): pl.pallas_call(mlp_kernel, out_shape=(jax.ShapeDtypeStruct((rows, width),...]
    ppermute x25 -> x20, waiting for transfers between devices: 84.8 us -> 71 us  [swap(): return lax.ppermute(value, BOTH, pairs)]
    dynamic_slice x3 -> x1, local copies, waits for them, and re-layouts: 9.05 us -> 0.04 us  [pick(): return lax.dynamic_index_in_dim(value, index, axis, keepdims=False)]
    convert_element_type x10 -> x9, other arithmetic: 18.1 us -> 13.7 us  [narrow(): return value.astype(jnp.bfloat16)]
    ppermute x25 -> x20, starting transfers between devices: 22.4 us -> 21.7 us  [swap(): return lax.ppermute(value, BOTH, pairs)]
  transfers between devices with their start and end apart: 25 -> 20, of which waited for: 8 -> 6; matrix products, arithmetic and copies ran while one was open for 8% -> 6% of each run, Pallas kernels for 35% -> 36%
where the time goes in v5:
time: 664 us; the launch traced here: 660 us
  Pallas kernels  506 us (76%)
  waiting for transfers between devices  71 us (11%)
  other arithmetic  36.1 us (5%)
  local copies, waits for them, and re-layouts  24.4 us (4%)
  starting transfers between devices  21.7 us (3%)
    pallas_call x1, Pallas kernels, mlp(): pl.pallas_call(mlp_kernel, out_shape=(jax.ShapeDtypeStruct((rows, width),...  158 us
    pallas_call x1, Pallas kernels, scatter_heads(): pl.pallas_call(scatter_kernel, out_shape=(jax.ShapeDtypeStruct((2, row_co...  134 us
    pallas_call x1, Pallas kernels, gather_heads(): pl.pallas_call(gather_kernel, out_shape=(jax.ShapeDtypeStruct((reps, 2 *...  110 us
    ppermute x20, waiting for transfers between devices, swap(): return lax.ppermute(value, BOTH, pairs)  71 us
    pallas_call x1, Pallas kernels, attend_back(): pl.pallas_call(attend_back_kernel, out_shape=jax.ShapeDtypeStruct((parts,...  54.8 us
    pallas_call x1, Pallas kernels, attend(): pl.pallas_call(attend_kernel, out_shape=(jax.ShapeDtypeStruct((parts, uni...  49.2 us
    ppermute x20, starting transfers between devices, swap(): return lax.ppermute(value, BOTH, pairs)  21.7 us
    convert_element_type x9, other arithmetic, narrow(): return value.astype(jnp.bfloat16)  13.7 us
  transfers between devices with their start and end apart: 20, of which 6 were waited for; matrix products, arithmetic and copies ran while one was open for 6% of the time, Pallas kernels for 36%

profile of v5, /device:TPU:0, one launch (start us, length us, event | category | flops | bytes accessed | tf_op | source)
XLA Modules:
  0.0 660.4 jit_solution(12523765052141639045)
XLA Ops:
  2.8 109.7 %gather_heads.1 = (bf16[16,256,2048]{2,1,0:T(8,128)(2,1)}, bf16[32,128,384]{2,1,0:T(8,128)(2,1)}, bf16[2,1024,384]{2,1,0:T(8,128)(2,1)}, bf16[2,1024,1024]{2,1,0...) custom-call(bf16[2,128,2048]{2,1,0:T(8,128)(2,1)} %tokens_ref.1, ...), custom_call_target="tpu_custom_call" | custom-call | flops 8000000000 | bytes 262144000 | tf_op jit(solution)/shard_map/gather_heads/pallas_call | solution.py:1149
  113.1 1.5 collective-permute-start.1
  114.6 1.5 collective-permute-start.3
  116.1 1.6 collective-permute-start
  119.8 1.0 multiply_sine_fusion
  122.7 49.2 %attend.1 = (bf16[32,128,128]{2,1,0:T(8,128)(2,1)}, f32[16,128,256]{2,1,0:T(8,128)}, f32[16,8,256]{2,1,0:T(8,128)}, bf16[16,256,128]{2,1,0:T(8,128)(2,1)}, bf16[...) custom-call(s32[32]{0:T(128)} %fusion.30.slot_ref, s32[16]{0:T(128)} %get-tuple-element.94.first_ref, ...), custom_call_target="tpu_custom_call" | custom-call | flops 20000000000 | bytes 16777216 | tf_op jit(solution)/shard_map/attend/pallas_call | solution.py:737
  172.8 1.4 slice_convert_fusion.2
  174.2 7.6 %collective-permute-done.3.down_other = bf16[256,2048]{1,0:T(8,128)(2,1)} collective-permute-done((bf16[256,2048]{1,0:T(8,128)(2,1)}, bf16[256,2048]{1,0:T(8,128)(2,1)}, u32[]{:S(2)}, u32[]{:S(2)}) %collective-permute-start.3) | collective-permute-done | bytes 1048608 | tf_op jit(solution)/shard_map/ppermute | solution.py:839
  183.2 157.8 %mlp.1 = (f32[256,2048]{1,0:T(8,128)}, bf16[2,256,2048]{2,1,0:T(8,128)(2,1)}, f32[256,2048]{1,0:T(8,128)}, bf16[32,128,128]{2,1,0:T(8,128)(2,1)}, bf16[1024,1024...) custom-call(bf16[32,128,128]{2,1,0:T(8,128)(2,1)} %get-tuple-element, ...), custom_call_target="tpu_custom_call" | custom-call | flops 149999992832 | bytes 157286400 | tf_op jit(solution)/shard_map/mlp/pallas_call | solution.py:1968
  341.0 1.5 slice_bitcast_fusion
  342.7 1.3 collective-permute-start.4
  344.7 1.9 collective-permute-start.6
  346.6 1.1 dynamic-slice_bitcast_fusion.3
  347.7 1.4 collective-permute-start.8
  349.1 54.8 %attend_back.1.refs_4_ = bf16[32,128,384]{2,1,0:T(8,128)(2,1)} custom-call(s32[32]{0:T(128)} %fusion.30.slot_ref, s32[16]{0:T(128)} %get-tuple-element.94.first_ref, s32[16]{0:T(128)} %get-tuple-element.93.plain_ref, f32[128,128]{1,0:T(8,128)} %get-tuple-element.111.cos_unit, f32[128,128]{1,0:T(8,128)} %get-tuple-element.110.sin_unit, ...), custom_call_target="tpu_custom_call" | custom-call | flops 49999998976 | bytes 16777216 | tf_op jit(solution)/shard_map/attend_back/pallas_call | solution.py:769
  404.0 8.7 %collective-permute-done.6.refs_2_ = bf16[8,64,2048]{2,1,0:T(8,128)(2,1)} collective-permute-done((bf16[8,64,2048]{2,1,0:T(8,128)(2,1)}, bf16[8,64,2048]{2,1,0:T(8,128)(2,1)}, u32[]{:S(2)}, u32[]{:S(2)}) %collective-permute-start.6) | collective-permute-done | bytes 2097184 | tf_op jit(solution)/shard_map/ppermute | solution.py:839
  412.7 3.2 add_convert_fusion.2
  415.9 1.1 dynamic-slice_bitcast_fusion.2
  417.6 1.0 copy-done.20
  418.6 2.4 add_convert_fusion
  421.0 1.2 dynamic-slice_bitcast_fusion
  422.2 1.5 collective-permute-start.11
  423.7 2.4 add_convert_fusion.1
  426.1 1.2 dynamic-slice_bitcast_fusion.1
  427.4 1.5 collective-permute-start.10
  428.8 134.3 %scatter_heads.1 = (f32[2,128,2048]{2,1,0:T(8,128)}, bf16[16,64,384]{2,1,0:T(8,128)(2,1)}) custom-call(bf16[16,256,384]{2,1,0:T(8,128)(2,1)} %bitcast.128, bf16[2,1024,384]{2,1,0:T(8,128)(2,1)} %get-tuple-element.70.weight_ref, bf16[16,256,2048]{2,1,0:T(8,128)(2,1)} %get-tuple-element.71.normed_ref, bf16[2,2,2,2,64,1024]{5,4,3,2,1,0:T(8,128)(2,1)} %bitcast.119, ...), custom_call_target="tpu_custom_call" | custom-call | flops 14000000000 | bytes 262144000 | tf_op jit(solution)/shard_map/scatter_heads/pallas_call | solution.py:1420
  563.1 2.6 reshape.420
  565.7 1.6 fusion.37
  569.7 2.2 multiply_reduce_fusion.6
  571.9 2.6 multiply_reduce_fusion.4
  574.5 1.3 convert_divide_fusion.1
  575.8 1.5 fusion.5
  577.5 1.6 fusion.10
  579.2 0.9 copy-done.16
  580.1 1.0 copy-done.8
  581.1 1.8 fusion
  584.9 1.7 fusion.2
  586.6 2.7 collective-permute-start.14
  589.3 1.5 fusion.3
  590.9 1.1 collective-permute-start.12
  592.0 6.6 %collective-permute-done.15 = bf16[2,2,64,1024]{3,2,1,0:T(8,128)(2,1)S(1)} collective-permute-done((bf16[2,2,64,1024]{3,2,1,0:T(8,128)(2,1)S(1)}, bf16[2,2,64,1024]{3,2,1,0:T(8,128)(2,1)S(1)}, u32[]{:S(2)}, u32[]{:S(2)}) %collective-permute-start.15) | collective-permute-done | bytes 524320 | tf_op jit(solution)/shard_map/ppermute | solution.py:839
  598.8 32.2 %collective-permute-done.14 = bf16[1,2,2,64,1024]{4,3,2,1,0:T(8,128)(2,1)S(1)} collective-permute-done((bf16[1,2,2,64,1024]{4,3,2,1,0:T(8,128)(2,1)S(1)}, bf16[1,2,2,64,1024]{4,3,2,1,0:T(8,128)(2,1)S(1)}, u32[]{:S(2)}, u32[]{:S(2)}) %collective-permute-start.14) | collective-permute-done | bytes 524320 | tf_op jit(solution)/shard_map/ppermute | solution.py:839
  631.7 2.6 collective-permute-start.13
  634.3 1.1 fusion.16
  635.6 15.8 %collective-permute-done.17 = bf16[2,64,2048]{2,1,0:T(8,128)(2,1)S(1)} collective-permute-done((bf16[2,64,2048]{2,1,0:T(8,128)(2,1)S(1)}, bf16[2,64,2048]{2,1,0:T(8,128)(2,1)S(1)}, u32[]{:S(2)}, u32[]{:S(2)}) %collective-permute-start.17) | collective-permute-done | bytes 524320 | tf_op jit(solution)/shard_map/ppermute | solution.py:839
  651.5 0.9 fusion.20
  657.0 1.9 multiply_reduce_fusion.2
  659.0 1.3 convert_divide_fusion
  (141 shorter events, 21.1 us)
Async XLA Ops:
  0.6 117.1 %copy-start = (s32[2,4]{1,0:T(2,128)S(1)}, s32[2,4]{1,0:T(2,128)}, u32[]{:S(2)}) copy-start(s32[2,4]{1,0:T(2,128)} %param.23) | copy-start | bytes 100
  112.5 69.4 %collective-permute-start.2 = (bf16[1024,1024]{1,0:T(8,128)(2,1)}, bf16[1024,1024]{1,0:T(8,128)(2,1)S(1)}, u32[]{:S(2)}, u32[]{:S(2)}) collective-permute-start(bf16[1024,1024]{1,0:T(8,128)(2,1)} %get-tuple-element.54.up_own), channel_id=1, source_target_pairs={{0,16},{1,17},{2,18},{3,19},{4,20},{5,21},{6,22},{7,23},{8,24},{9,... | collective-permute-start | bytes 6291464 | tf_op jit(solution)/shard_map/ppermute | solution.py:839
  113.1 61.2 %collective-permute-start.1 = (bf16[256,2048]{1,0:T(8,128)(2,1)}, bf16[256,2048]{1,0:T(8,128)(2,1)}, u32[]{:S(2)}, u32[]{:S(2)}) collective-permute-start(bf16[256,2048]{1,0:T(8,128)(2,1)} %get-tuple-element.52.output_part), channel_id=1, source_target_pairs={{0,2},{1,3},{2,0},{3,1},{4,6},{5,7},{6,4},{7,5},{8,10},{9,11},{10,... | collective-permute-start | bytes 3145736 | tf_op jit(solution)/shard_map/ppermute | solution.py:839
  114.6 67.2 %collective-permute-start.3 = (bf16[256,2048]{1,0:T(8,128)(2,1)}, bf16[256,2048]{1,0:T(8,128)(2,1)}, u32[]{:S(2)}, u32[]{:S(2)}) collective-permute-start(bf16[256,2048]{1,0:T(8,128)(2,1)} %get-tuple-element.55.down_first), channel_id=1, source_target_pairs={{0,16},{1,17},{2,18},{3,19},{4,20},{5,21},{6,22},{7,23},{8,24},{9,... | collective-permute-start | bytes 3145736 | tf_op jit(solution)/shard_map/ppermute | solution.py:839
  116.1 65.7 %collective-permute-start = (bf16[256,2048]{1,0:T(8,128)(2,1)}, bf16[256,2048]{1,0:T(8,128)(2,1)}, u32[]{:S(2)}, u32[]{:S(2)}) collective-permute-start(bf16[256,2048]{1,0:T(8,128)(2,1)} %get-tuple-element.51), channel_id=1, source_target_pairs={{0,4},{1,5},{2,6},{3,7},{4,0},{5,1},{6,2},{7,3},{8,12},{9,13},{10,... | collective-permute-start | bytes 3145736 | tf_op jit(solution)/shard_map/ppermute | solution.py:839
  122.7 49.2 %copy-start.3 = (bf16[2,128,2048]{2,1,0:T(8,128)(2,1)S(1)}, bf16[2,128,2048]{2,1,0:T(8,128)(2,1)}, u32[]{:S(2)}) copy-start(bf16[2,128,2048]{2,1,0:T(8,128)(2,1)} %tokens_ref.1) | copy-start | bytes 3145732
  181.8 1.4 copy-start.28
  341.0 5.6 copy-start.22
  342.5 61.4 %collective-permute-start.7 = (bf16[256,2048]{1,0:T(8,128)(2,1)S(1)}, bf16[256,2048]{1,0:T(8,128)(2,1)S(1)}, u32[]{:S(2)}, u32[]{:S(2)}) collective-permute-start(bf16[256,2048]{1,0:T(8,128)(2,1)S(1)} %slice_bitcast_fusion), channel_id=1, source_target_pairs={{0,4},{1,5},{2,6},{3,7},{4,0},{5,1},{6,2},{7,3},{8,12},{9,13},{10,... | collective-permute-start | bytes 3145736 | tf_op jit(solution)/shard_map/ppermute | solution.py:839
  342.7 61.2 %collective-permute-start.4 = (bf16[1024,1024]{1,0:T(8,128)(2,1)}, bf16[1024,1024]{1,0:T(8,128)(2,1)S(1)}, u32[]{:S(2)}, u32[]{:S(2)}) collective-permute-start(bf16[1024,1024]{1,0:T(8,128)(2,1)} %get-tuple-element.59), channel_id=1, source_target_pairs={{0,16},{1,17},{2,18},{3,19},{4,20},{5,21},{6,22},{7,23},{8,24},{9,... | collective-permute-start | bytes 6291464 | tf_op jit(solution)/shard_map/ppermute | solution.py:839
  344.1 59.9 %collective-permute-start.5 = (bf16[4,128,2048]{2,1,0:T(8,128)(2,1)}, bf16[4,128,2048]{2,1,0:T(8,128)(2,1)}, u32[]{:S(2)}, u32[]{:S(2)}) collective-permute-start(bf16[4,128,2048]{2,1,0:T(8,128)(2,1)} %get-tuple-element.60), channel_id=1, source_target_pairs={{0,2},{1,3},{2,0},{3,1},{4,6},{5,7},{6,4},{7,5},{8,10},{9,11},{10,... | collective-permute-start | bytes 6291464 | tf_op jit(solution)/shard_map/ppermute | solution.py:839
  344.7 68.0 %collective-permute-start.6 = (bf16[8,64,2048]{2,1,0:T(8,128)(2,1)}, bf16[8,64,2048]{2,1,0:T(8,128)(2,1)}, u32[]{:S(2)}, u32[]{:S(2)}) collective-permute-start(bf16[8,64,2048]{2,1,0:T(8,128)(2,1)} %get-tuple-element.61), channel_id=1, source_target_pairs={{0,4},{1,5},{2,6},{3,7},{4,0},{5,1},{6,2},{7,3},{8,12},{9,13},{10,... | collective-permute-start | bytes 6291464 | tf_op jit(solution)/shard_map/ppermute | solution.py:839
  347.7 231.4 %collective-permute-start.8 = (bf16[2,2,2,64,1024]{4,3,2,1,0:T(8,128)(2,1)}, bf16[2,2,2,64,1024]{4,3,2,1,0:T(8,128)(2,1)}, u32[]{:S(2)}, u32[]{:S(2)}) collective-permute-start(bf16[2,2,2,64,1024]{4,3,2,1,0:T(8,128)(2,1)} %dynamic-slice_bitcast_fusion.3), channel_id=1, source_target_pairs={{0,2},{1,3},{2,0},{3,1},{4,6},{5,7},{6,4},{7,5},{8,10},{9,11},{10,... | collective-permute-start | bytes 3145736 | tf_op jit(solution)/shard_map/ppermute | solution.py:839
  403.9 8.7 %copy-start.12 = (bf16[256,2048]{1,0:T(8,128)(2,1)}, bf16[256,2048]{1,0:T(8,128)(2,1)S(1)}, u32[]{:S(2)}) copy-start(bf16[256,2048]{1,0:T(8,128)(2,1)S(1)} %collective-permute-done.7.refs_3_) | copy-start | bytes 3145732
  403.9 8.7 %copy-start.9 = (bf16[1024,1024]{1,0:T(8,128)(2,1)}, bf16[1024,1024]{1,0:T(8,128)(2,1)S(1)}, u32[]{:S(2)}) copy-start(bf16[1024,1024]{1,0:T(8,128)(2,1)S(1)} %collective-permute-done.4.refs_0_) | copy-start | bytes 6291460
  415.9 5.1 copy-start.5
  415.9 2.7 copy-start.20
  417.0 162.2 %collective-permute-start.9 = (bf16[2,2,2,64,1024]{4,3,2,1,0:T(8,128)(2,1)}, bf16[2,2,2,64,1024]{4,3,2,1,0:T(8,128)(2,1)S(1)}, u32[]{:S(2)}, u32[]{:S(2)}) collective-permute-start(bf16[2,2,2,64,1024]{4,3,2,1,0:T(8,128)(2,1)} %dynamic-slice_bitcast_fusion.2), channel_id=1, source_target_pairs={{0,8},{1,9},{2,10},{3,11},{4,12},{5,13},{6,14},{7,15},{8,0},{9,1},... | collective-permute-start | bytes 3145736 | tf_op jit(solution)/shard_map/ppermute | solution.py:839
  421.0 5.1 copy-start.10
  421.0 2.7 copy-start.19
  422.2 157.0 %collective-permute-start.11 = (bf16[2,2,64,2048]{3,2,1,0:T(8,128)(2,1)}, bf16[2,2,64,2048]{3,2,1,0:T(8,128)(2,1)}, u32[]{:S(2)}, u32[]{:S(2)}) collective-permute-start(bf16[2,2,64,2048]{3,2,1,0:T(8,128)(2,1)} %dynamic-slice_bitcast_fusion), channel_id=1, source_target_pairs={{0,16},{1,17},{2,18},{3,19},{4,20},{5,21},{6,22},{7,23},{8,24},{9,... | collective-permute-start | bytes 3145736 | tf_op jit(solution)/shard_map/ppermute | solution.py:839
  426.1 2.7 copy-start.7
  427.4 151.8 %collective-permute-start.10 = (bf16[2,128,2048]{2,1,0:T(8,128)(2,1)}, bf16[2,128,2048]{2,1,0:T(8,128)(2,1)}, u32[]{:S(2)}, u32[]{:S(2)}) collective-permute-start(bf16[2,128,2048]{2,1,0:T(8,128)(2,1)} %dynamic-slice_bitcast_fusion.1), channel_id=1, source_target_pairs={{0,16},{1,17},{2,18},{3,19},{4,20},{5,21},{6,22},{7,23},{8,24},{9,... | collective-permute-start | bytes 3145736 | tf_op jit(solution)/shard_map/ppermute | solution.py:839
  567.3 1.6 copy-start.2
  567.3 1.8 copy-start.4
  567.3 1.8 copy-start.25
  567.3 1.8 copy-start.27
  569.2 6.6 copy-start.24
  569.7 6.1 copy-start.13
  569.7 6.1 copy-start.21
  575.7 1.8 copy-start.18
  575.8 1.8 copy-start.26
  579.1 2.0 copy-start.8
  581.1 1.9 copy-start.6
  581.1 2.2 copy-start.17
  582.9 51.3 %collective-permute-start.19 = (bf16[1,128,2048]{2,1,0:T(8,128)(2,1)S(1)}, bf16[1,128,2048]{2,1,0:T(8,128)(2,1)S(1)}, u32[]{:S(2)}, u32[]{:S(2)}) collective-permute-start(bf16[1,128,2048]{2,1,0:T(8,128)(2,1)S(1)} %constant_dynamic-slice_fusion), channel_id=1, source_target_pairs={{0,8},{1,9},{2,10},{3,11},{4,12},{5,13},{6,14},{7,15},{8,0},{9,1},... | collective-permute-start | bytes 1572872 | tf_op jit(solution)/shard_map/ppermute | solution.py:839
  583.3 1.6 copy-start.23
  583.8 14.8 %collective-permute-start.15 = (bf16[2,2,64,1024]{3,2,1,0:T(8,128)(2,1)S(1)}, bf16[2,2,64,1024]{3,2,1,0:T(8,128)(2,1)S(1)}, u32[]{:S(2)}, u32[]{:S(2)}) collective-permute-start(bf16[2,2,64,1024]{3,2,1,0:T(8,128)(2,1)S(1)} %dynamic-slice_bitcast_fusion.4), channel_id=1, source_target_pairs={{0,2},{1,3},{2,0},{3,1},{4,6},{5,7},{6,4},{7,5},{8,10},{9,11},{10,... | collective-permute-start | bytes 1572872 | tf_op jit(solution)/shard_map/ppermute | solution.py:839
  584.9 4.5 copy-start.11
  586.6 44.4 %collective-permute-start.14 = (bf16[1,2,2,64,1024]{4,3,2,1,0:T(8,128)(2,1)S(1)}, bf16[1,2,2,64,1024]{4,3,2,1,0:T(8,128)(2,1)S(1)}, u32[]{:S(2)}, u32[]{:S(2)}) collective-permute-start(bf16[1,2,2,64,1024]{4,3,2,1,0:T(8,128)(2,1)S(1)} %constant_dynamic-slice_fusion.2), channel_id=1, source_target_pairs={{0,8},{1,9},{2,10},{3,11},{4,12},{5,13},{6,14},{7,15},{8,0},{9,1},... | collective-permute-start | bytes 1572872 | tf_op jit(solution)/shard_map/ppermute | solution.py:839
  590.9 40.6 %collective-permute-start.12 = (bf16[2,64,2048]{2,1,0:T(8,128)(2,1)S(1)}, bf16[2,64,2048]{2,1,0:T(8,128)(2,1)S(1)}, u32[]{:S(2)}, u32[]{:S(2)}) collective-permute-start(bf16[2,64,2048]{2,1,0:T(8,128)(2,1)S(1)} %dynamic-slice_bitcast_fusion.5), channel_id=1, source_target_pairs={{0,2},{1,3},{2,0},{3,1},{4,6},{5,7},{6,4},{7,5},{8,10},{9,11},{10,... | collective-permute-start | bytes 1572872 | tf_op jit(solution)/shard_map/ppermute | solution.py:839
  631.3 21.1 %collective-permute-start.16 = (bf16[64,2048]{1,0:T(8,128)(2,1)S(1)}, bf16[64,2048]{1,0:T(8,128)(2,1)S(1)}, u32[]{:S(2)}, u32[]{:S(2)}) collective-permute-start(bf16[64,2048]{1,0:T(8,128)(2,1)S(1)} %get-tuple-element.101), channel_id=1, source_target_pairs={{0,1},{1,0},{2,3},{3,2},{4,5},{5,4},{6,7},{7,6},{8,9},{9,8},{10,11... | collective-permute-start | bytes 786440 | tf_op jit(solution)/shard_map/ppermute | solution.py:839
  631.4 20.0 %collective-permute-start.17 = (bf16[2,64,2048]{2,1,0:T(8,128)(2,1)S(1)}, bf16[2,64,2048]{2,1,0:T(8,128)(2,1)S(1)}, u32[]{:S(2)}, u32[]{:S(2)}) collective-permute-start(bf16[2,64,2048]{2,1,0:T(8,128)(2,1)S(1)} %fusion.18), channel_id=1, source_target_pairs={{0,4},{1,5},{2,6},{3,7},{4,0},{5,1},{6,2},{7,3},{8,12},{9,13},{10,... | collective-permute-start | bytes 1572872 | tf_op jit(solution)/shard_map/ppermute | solution.py:839
  631.7 19.8 %collective-permute-start.13 = (bf16[1,64,2048]{2,1,0:T(8,128)(2,1)S(1)}, bf16[1,64,2048]{2,1,0:T(8,128)(2,1)S(1)}, u32[]{:S(2)}, u32[]{:S(2)}) collective-permute-start(bf16[1,64,2048]{2,1,0:T(8,128)(2,1)S(1)} %constant_dynamic-slice_fusion.3), channel_id=1, source_target_pairs={{0,8},{1,9},{2,10},{3,11},{4,12},{5,13},{6,14},{7,15},{8,0},{9,1},... | collective-permute-start | bytes 786440 | tf_op jit(solution)/shard_map/ppermute | solution.py:839
  651.4 1.6 collective-permute-start.18
  655.3 1.7 copy-start.14
  656.1 4.1 copy-start.1
  657.0 3.2 copy-start.15
  (1 other events, 1.0 us)

commit v6 on v5

--- a/solution.py
+++ b/solution.py
@@ -426,6 +426,65 @@
     return jnp.where(lane % HD < HD // 2, -ahead, behind)
 
 
+def fill_tables(lengths_ref, begin_at, cos_unit, sin_unit, cos_part, sin_part):
+    parts, units = cos_part.shape[0], cos_unit.shape[0]
+    here = lax.axis_index("grp")
+
+    def frequency(shape):
+        lane = lax.broadcasted_iota(jnp.int32, shape, 1) % (HD // 2)
+        return jnp.exp(lane.astype(jnp.float32) * (-2.0 * math.log(rope_base) / HD))
+
+    unit = lax.broadcasted_iota(jnp.int32, (units, LANES), 0)
+    begin = jnp.zeros((units, LANES), jnp.int32)
+    end = 0
+    for seq in range(lengths_ref.shape[1]):
+        end = end + lengths_ref[here, seq]
+        begin = jnp.where(unit >= end, end, begin)
+    begin_at[...] = begin
+    angle = ((unit - begin) * parts).astype(jnp.float32) * frequency((units, LANES))
+    cos_unit[...] = jnp.cos(angle)
+    sin_unit[...] = jnp.sin(angle)
+    part = lax.broadcasted_iota(jnp.int32, (parts, LANES), 0).astype(jnp.float32)
+    angle = part * frequency((parts, LANES))
+    cos_part[...] = jnp.cos(angle)
+    sin_part[...] = jnp.sin(angle)
+
+
+def begin_of(lengths_ref, unit):
+    here = lax.axis_index("grp")
+    begin, end = 0, 0
+    for seq in range(lengths_ref.shape[1]):
+        end = end + lengths_ref[here, seq]
+        begin = jnp.where(unit >= end, end, begin)
+    return begin
+
+
+def key_range(lengths_ref, at, parts, block):
+    first_unit = at * UNIT_BLOCK
+    last_unit = first_unit + UNIT_BLOCK - 1
+    least = jnp.maximum(begin_of(lengths_ref, first_unit) * parts, at * block - (WINDOW - 1))
+    most = jnp.maximum(
+        begin_of(lengths_ref, last_unit) * parts, (at + 1) * block - 1 - (WINDOW - 1)
+    )
+    first = jnp.maximum(least, 0) // block
+    return first, jnp.minimum(jnp.maximum((most + block - 1) // block, first), at)
+
+
+def low_of(begin_at, at, parts):
+    begin = begin_at[pl.ds(pl.multiple_of(at * UNIT_BLOCK, UNIT_BLOCK), UNIT_BLOCK), :] * parts
+    shape = (parts, UNIT_BLOCK, LANES)
+    part = lax.broadcasted_iota(jnp.int32, shape, 0)
+    unit = lax.broadcasted_iota(jnp.int32, shape, 1) + at * UNIT_BLOCK
+    low = jnp.maximum(begin[None], unit * parts + part - (WINDOW - 1))
+    return low.reshape(parts * UNIT_BLOCK, LANES).astype(jnp.float32)
+
+
+def slot_of(part):
+    groups, reps = lax.axis_size("grp"), lax.axis_size("rep")
+    offset = (part % reps) ^ lax.axis_index("rep")
+    return offset * groups + ((part // reps) ^ lax.axis_index("grp"))
+
+
 def pair_angles(unit_at, cos_unit, sin_unit, cos_part, sin_part):
     unit_cos = cos_unit[pl.ds(unit_at, UNIT_PAIR), :][None]
     unit_sin = sin_unit[pl.ds(unit_at, UNIT_PAIR), :][None]
@@ -447,14 +506,7 @@
 
 
 def attend_kernel(
-    slot_ref,
-    first_ref,
-    plain_ref,
-    cos_unit,
-    sin_unit,
-    cos_part,
-    sin_part,
-    low_ref,
+    lengths_ref,
     qkv_ref,
     att_ref,
     out_ref,
@@ -462,22 +514,33 @@
     query_ref,
     key_ref,
     value_ref,
-    query_t,
-    value_t,
+    query_heads,
+    key_t,
+    tops,
+    sums,
+    totals,
+    lows,
+    causal_at,
     key_at,
-    causal_at,
+    begin_at,
+    cos_unit,
+    sin_unit,
+    cos_part,
+    sin_part,
 ):
     parts, units, _ = qkv_ref.shape
     block = parts * UNIT_BLOCK
     pairs = units // UNIT_PAIR
-    key_at[...] = key_offsets(block)
-    causal_at[...] = jnp.where(key_offsets(block) <= query_offsets(block), 0.0, masked_score)
-    extra = value_t.shape[2] - HD
+    halves = UNIT_PAIR // UNIT_BLOCK
+    wide = block // LANES
+    fill_tables(lengths_ref, begin_at, cos_unit, sin_unit, cos_part, sin_part)
+    key_at[...] = query_offsets(block).astype(jnp.float32)
+    causal_at[...] = jnp.where(query_offsets(block) <= key_offsets(block), 0.0, masked_score)
 
     def lay_out(pair, unused):
         unit_at = pl.multiple_of(pair * UNIT_PAIR, UNIT_PAIR)
         rows = jnp.stack(
-            [qkv_ref[slot_ref[part], pl.ds(unit_at, UNIT_PAIR), :] for part in range(parts)]
+            [qkv_ref[slot_of(part), pl.ds(unit_at, UNIT_PAIR), :] for part in range(parts)]
         )
         cosine, sine = pair_angles(unit_at, cos_unit, sin_unit, cos_part, sin_part)
         flat = (parts * UNIT_PAIR, LANES)
@@ -492,79 +555,105 @@
         query = rotated(rows[:, :, :LANES]) * (1.0 / math.sqrt(HD))
         key = rotated(rows[:, :, LANES : 2 * LANES])
         value = rows[:, :, 2 * LANES :].astype(jnp.float32)
-        for half in range(UNIT_PAIR // UNIT_BLOCK):
-            at = pair * (UNIT_PAIR // UNIT_BLOCK) + half
+        for half in range(halves):
+            at = pair * halves + half
             cut = slice(half * UNIT_BLOCK, (half + 1) * UNIT_BLOCK)
             query_rows = query[:, cut].reshape(block, LANES)
-            value_rows = value[:, cut].reshape(block, LANES)
+            key_rows = key[:, cut].reshape(block, LANES)
             query_ref[at] = query_rows.astype(jnp.bfloat16)
-            key_ref[at] = key[:, cut].reshape(block, LANES).astype(jnp.bfloat16)
-            value_ref[at] = value_rows.astype(jnp.bfloat16)
-            turned = jnp.transpose(query_rows)
-            row = lax.broadcasted_iota(jnp.int32, turned.shape, 0)
-            query_t[0, at] = jnp.where(row < HD, turned, 0.0).astype(jnp.bfloat16)
-            query_t[1, at] = jnp.where(row < HD, 0.0, turned).astype(jnp.bfloat16)
-            turned = jnp.transpose(value_rows).astype(jnp.bfloat16)
+            key_ref[at] = key_rows.astype(jnp.bfloat16)
+            value_ref[at] = value[:, cut].reshape(block, LANES).astype(jnp.bfloat16)
+            lane = lax.broadcasted_iota(jnp.int32, query_rows.shape, 1)
+            query_heads[at, 0] = jnp.where(lane < HD, query_rows, 0.0).astype(jnp.bfloat16)
+            query_heads[at, 1] = jnp.where(lane < HD, 0.0, query_rows).astype(jnp.bfloat16)
+            key_t[at] = jnp.transpose(key_rows).astype(jnp.bfloat16)
+        return unused
+
+    lax.fori_loop(0, pairs, lay_out, 0)
+
+    def query_pair(pair, unused):
+        ids = [pair * halves + half for half in range(halves)]
+        for half, at in enumerate(ids):
+            lows[half] = low_of(begin_at, at, parts)
+        first, _ = key_range(lengths_ref, ids[0], parts, block)
+        _, plain = key_range(lengths_ref, ids[-1], parts, block)
+        plain = jnp.minimum(plain, ids[0])
+
+        def wider(value):
+            return jnp.concatenate([value] * wide, axis=1)
+
+        def scores_of(half, head, key_block, causal, bounded):
+            scores = jnp.dot(
+                query_heads[ids[half], head], key_t[key_block], preferred_element_type=jnp.float32
+            )
+            if causal:
+                scores = scores + causal_at[...]
+            if bounded:
+                bound = wider(lows[half] - (key_block * block).astype(jnp.float32))
+                scores = jnp.where(key_at[...] >= bound, scores, masked_score)
+            return scores
+
+        def folded(combine, values):
+            result = values[:, :LANES]
+            for at in range(1, wide):
+                result = combine(result, values[:, at * LANES : (at + 1) * LANES])
+            return result
+
+        def top_step(half, head, key_block, causal, bounded, fresh):
+            high = folded(jnp.maximum, scores_of(half, head, key_block, causal, bounded))
+            tops[half, head] = high if fresh else jnp.maximum(tops[half, head], high)
+
+        def sum_step(half, head, key_block, causal, bounded, fresh):
+            scores = scores_of(half, head, key_block, causal, bounded)
+            weights = jnp.exp(scores - wider(tops[half, head]))
+            part = folded(jnp.add, weights)
+            product = jnp.dot(
+                weights.astype(jnp.bfloat16),
+                value_ref[key_block],
+                preferred_element_type=jnp.float32,
+            )
+            sums[half, head] = part if fresh else sums[half, head] + part
+            totals[half, head] = product if fresh else totals[half, head] + product
+
+        def over_keys(step):
+            for half, at in enumerate(ids):
+                for head in range(2):
+                    step(half, head, at, True, True, True)
+                    for earlier in ids[:half]:
+                        step(half, head, earlier, False, True, False)
+
+            def all_steps(bounded):
+                def go(key_block, unused):
+                    for half in range(halves):
+                        for head in range(2):
+                            step(half, head, key_block, False, bounded, False)
+                    return unused
+
+                return go
+
+            lax.fori_loop(first, plain, all_steps(True), 0)
+            lax.fori_loop(plain, ids[0], all_steps(False), 0)
+
+        over_keys(top_step)
+        for half in range(halves):
             for head in range(2):
-                value_t[head, at, pl.ds(0, HD), :] = turned[head * HD : (head + 1) * HD]
-                value_t[head, at, pl.ds(HD, extra), :] = jnp.ones((extra, block), jnp.bfloat16)
-        return unused
-
-    lax.fori_loop(0, pairs, lay_out, 0)
-
-    def query_block(at):
-        low = low_ref[at, 0:1, :]
-
-        def step(key_block, carried, causal, bounded):
-            new = []
+                high = jnp.max(tops[half, head], axis=1, keepdims=True)
+                tops[half, head] = jnp.broadcast_to(high, (block, LANES))
+        over_keys(sum_step)
+        done = []
+        for half, at in enumerate(ids):
+            rows = []
             for head in range(2):
-                top, total = carried[2 * head : 2 * head + 2]
-                scores = jnp.dot(
-                    key_ref[key_block], query_t[head, at], preferred_element_type=jnp.float32
+                total = jnp.broadcast_to(
+                    jnp.sum(sums[half, head], axis=1, keepdims=True), (block, LANES)
                 )
-                if causal:
-                    scores = scores + causal_at[...]
-                if bounded:
-                    scores = jnp.where(
-                        key_at[...] >= low - key_block * block, scores, masked_score
-                    )
-                high = jnp.maximum(top, jnp.max(scores, axis=0, keepdims=True))
-                weights = jnp.exp(scores - high).astype(jnp.bfloat16)
-                total = total * jnp.exp(top - high) + jnp.dot(
-                    value_t[head, key_block], weights, preferred_element_type=jnp.float32
-                )
-                new += [high, total]
-            return tuple(new)
-
-        empty = (
-            jnp.full((1, block), masked_score, jnp.float32),
-            jnp.zeros((HD + extra, block), jnp.float32),
-        )
-        carried = step(at, empty * 2, True, True)
-        carried = lax.fori_loop(
-            first_ref[at],
-            plain_ref[at],
-            lambda key_block, held: step(key_block, held, False, True),
-            carried,
-        )
-        carried = lax.fori_loop(
-            plain_ref[at],
-            at,
-            lambda key_block, held: step(key_block, held, False, False),
-            carried,
-        )
-        heads = []
-        for head in range(2):
-            top, total = carried[2 * head : 2 * head + 2]
-            heads.append(total[:HD] / total[HD : HD + 1])
-            log_ref[at, head : head + 1, :] = top + jnp.log(total[HD : HD + 1])
-        both = jnp.concatenate(heads, axis=0)
-        out_ref[at] = both
-        return jnp.transpose(both).reshape(parts, UNIT_BLOCK, LANES)
-
-    def query_pair(pair, unused):
-        halves = UNIT_PAIR // UNIT_BLOCK
-        done = [query_block(pair * halves + half) for half in range(halves)]
+                rows.append(totals[half, head] / total)
+                log = jnp.transpose(tops[half, head] + jnp.log(total))
+                log_ref[at, head : head + 1, :] = log[0:1]
+            lane = lax.broadcasted_iota(jnp.int32, (block, LANES), 1)
+            both = jnp.where(lane < HD, rows[0], rows[1])
+            out_ref[at] = jnp.transpose(both)
+            done.append(both.reshape(parts, UNIT_BLOCK, LANES))
         unit_at = pl.multiple_of(pair * UNIT_PAIR, UNIT_PAIR)
         att_ref[:, pl.ds(unit_at, UNIT_PAIR), :] = jnp.concatenate(done, axis=1).astype(
             jnp.bfloat16
@@ -575,14 +664,7 @@
 
 
 def attend_back_kernel(
-    slot_ref,
-    first_ref,
-    plain_ref,
-    cos_unit,
-    sin_unit,
-    cos_part,
-    sin_part,
-    low_ref,
+    lengths_ref,
     query_ref,
     key_ref,
     value_ref,
@@ -595,12 +677,18 @@
     value_total,
     key_at,
     causal_at,
+    begin_at,
+    cos_unit,
+    sin_unit,
+    cos_part,
+    sin_part,
 ):
     parts, units, _ = grad_ref.shape
     block = parts * UNIT_BLOCK
     pairs = units // UNIT_PAIR
     halves = UNIT_PAIR // UNIT_BLOCK
-    key_at[...] = key_offsets(block)
+    fill_tables(lengths_ref, begin_at, cos_unit, sin_unit, cos_part, sin_part)
+    key_at[...] = key_offsets(block).astype(jnp.float32)
     causal_at[...] = jnp.where(key_offsets(block) <= query_offsets(block), 0.0, masked_score)
 
     def lay_out(at, unused):
@@ -619,70 +707,100 @@
             jnp.where(place < HD, zero, values).astype(jnp.bfloat16),
         ]
 
-    def query_block(at, grad_rows):
-        low = low_ref[at, 0:1, :]
+    def prepare(at, grad_rows):
         query_rows = query_ref[at].astype(jnp.float32)
-        query_heads = jnp.concatenate(split_heads(query_rows, 1), axis=0)
-        grad_heads = jnp.concatenate(split_heads(grad_rows, 1), axis=0)
-        query_t = split_heads(jnp.transpose(query_rows), 0)
         grad_turned = jnp.transpose(grad_rows)
-        grad_t = split_heads(grad_turned, 0)
         product = grad_turned * out_ref[at]
-        inner = [
-            jnp.sum(product[head * HD : (head + 1) * HD], axis=0, keepdims=True)
-            for head in range(2)
+        return dict(
+            low=jnp.transpose(low_of(begin_at, at, parts))[0:1],
+            query=jnp.concatenate(split_heads(query_rows, 1), axis=0),
+            grad=jnp.concatenate(split_heads(grad_rows, 1), axis=0),
+            query_t=split_heads(jnp.transpose(query_rows), 0),
+            grad_t=split_heads(grad_turned, 0),
+            inner=[
+                jnp.sum(product[head * HD : (head + 1) * HD], axis=0, keepdims=True)
+                for head in range(2)
+            ],
+            logs=[log_ref[at, head : head + 1, :] for head in range(2)],
+        )
+
+    def step(held, key_block, carried, causal, bounded):
+        probs, slopes, new = [], [], []
+        for head in range(2):
+            scores = jnp.dot(
+                key_ref[key_block], held["query_t"][head], preferred_element_type=jnp.float32
+            )
+            if causal:
+                scores = scores + causal_at[...]
+            if bounded:
+                scores = jnp.where(
+                    key_at[...] >= held["low"] - (key_block * block).astype(jnp.float32), scores, masked_score
+                )
+            soft = jnp.exp(scores - held["logs"][head])
+            grad_probs = jnp.dot(
+                value_ref[key_block], held["grad_t"][head], preferred_element_type=jnp.float32
+            )
+            slope = (soft * (grad_probs - held["inner"][head])).astype(jnp.bfloat16)
+            probs.append(soft.astype(jnp.bfloat16))
+            slopes.append(slope)
+            new.append(
+                carried[head]
+                + jnp.dot(
+                    key_t[key_block, pl.ds(head * HD, HD), :],
+                    slope,
+                    preferred_element_type=jnp.float32,
+                )
+            )
+        return tuple(new), probs, slopes
+
+    def add_key(key_block, held, probs, slopes):
+        value_total[key_block] += jnp.dot(
+            jnp.concatenate(probs, axis=1),
+            jnp.concatenate([one["grad"] for one in held], axis=0),
+            preferred_element_type=jnp.float32,
+        )
+        key_total[key_block] += jnp.dot(
+            jnp.concatenate(slopes, axis=1),
+            jnp.concatenate([one["query"] for one in held], axis=0),
+            preferred_element_type=jnp.float32,
+        )
+
+    def query_blocks(pair, grads):
+        ids = [pair * halves + half for half in range(halves)]
+        held = [prepare(at, rows) for at, rows in zip(ids, grads)]
+        states = []
+        for half, at in enumerate(ids):
+            state, probs, slopes = step(
+                held[half], at, (jnp.zeros((HD, block), jnp.float32),) * 2, True, True
+            )
+            add_key(at, held[half : half + 1], probs, slopes)
+            for earlier in ids[:half]:
+                state, probs, slopes = step(held[half], earlier, state, False, True)
+                add_key(earlier, held[half : half + 1], probs, slopes)
+            states.append(state)
+
+        def all_steps(bounded):
+            def run(key_block, carried):
+                new, probs, slopes = [], [], []
+                for half in range(halves):
+                    state, prob, slope = step(held[half], key_block, carried[half], False, bounded)
+                    new.append(state)
+                    probs += prob
+                    slopes += slope
+                add_key(key_block, held, probs, slopes)
+                return tuple(new)
+
+            return run
+
+        first, _ = key_range(lengths_ref, ids[0], parts, block)
+        _, plain = key_range(lengths_ref, ids[-1], parts, block)
+        plain = jnp.minimum(plain, ids[0])
+        states = lax.fori_loop(first, plain, all_steps(True), tuple(states))
+        states = lax.fori_loop(plain, ids[0], all_steps(False), states)
+        return [
+            jnp.transpose(jnp.concatenate(state, axis=0)) * (1.0 / math.sqrt(HD))
+            for state in states
         ]
-        logs = [log_ref[at, head : head + 1, :] for head in range(2)]
-
-        def step(key_block, carried, causal, bounded):
-            probs, slopes, new = [], [], []
-            for head in range(2):
-                scores = jnp.dot(
-                    key_ref[key_block], query_t[head], preferred_element_type=jnp.float32
-                )
-                if causal:
-                    scores = scores + causal_at[...]
-                if bounded:
-                    scores = jnp.where(
-                        key_at[...] >= low - key_block * block, scores, masked_score
-                    )
-                soft = jnp.exp(scores - logs[head])
-                grad_probs = jnp.dot(
-                    value_ref[key_block], grad_t[head], preferred_element_type=jnp.float32
-                )
-                slope = (soft * (grad_probs - inner[head])).astype(jnp.bfloat16)
-                probs.append(soft.astype(jnp.bfloat16))
-                slopes.append(slope)
-                new.append(
-                    carried[head]
-                    + jnp.dot(
-                        key_t[key_block, pl.ds(head * HD, HD), :],
-                        slope,
-                        preferred_element_type=jnp.float32,
-                    )
-                )
-            value_total[key_block] += jnp.dot(
-                jnp.concatenate(probs, axis=1), grad_heads, preferred_element_type=jnp.float32
-            )
-            key_total[key_block] += jnp.dot(
-                jnp.concatenate(slopes, axis=1), query_heads, preferred_element_type=jnp.float32
-            )
-            return tuple(new)
-
-        carried = step(at, (jnp.zeros((HD, block), jnp.float32),) * 2, True, True)
-        carried = lax.fori_loop(
-            first_ref[at],
-            plain_ref[at],
-            lambda key_block, held: step(key_block, held, False, True),
-            carried,
-        )
-        carried = lax.fori_loop(
-            plain_ref[at],
-            at,
-            lambda key_block, held: step(key_block, held, False, False),
-            carried,
-        )
-        return jnp.transpose(jnp.concatenate(carried, axis=0)) * (1.0 / math.sqrt(HD))
 
     def turn_back(rows, cosine, sine):
         flat = (parts * UNIT_PAIR, LANES)
@@ -694,18 +812,18 @@
 
     def put(values, unit_at, lane_at):
         for part in range(parts):
-            back_ref[slot_ref[part], pl.ds(unit_at, UNIT_PAIR), pl.ds(lane_at, LANES)] = values[part]
+            back_ref[slot_of(part), pl.ds(unit_at, UNIT_PAIR), pl.ds(lane_at, LANES)] = values[part]
 
     def query_pair(pair, unused):
         unit_at = pl.multiple_of(pair * UNIT_PAIR, UNIT_PAIR)
         grads = grad_ref[:, pl.ds(unit_at, UNIT_PAIR), :].astype(jnp.float32)
-        done = [
-            query_block(
-                pair * halves + half,
-                grads[:, half * UNIT_BLOCK : (half + 1) * UNIT_BLOCK].reshape(block, LANES),
-            )
-            for half in range(halves)
-        ]
+        done = query_blocks(
+            pair,
+            [
+                grads[:, half * UNIT_BLOCK : (half + 1) * UNIT_BLOCK].reshape(block, LANES)
+                for half in range(halves)
+            ],
+        )
         cosine, sine = pair_angles(unit_at, cos_unit, sin_unit, cos_part, sin_part)
         put(turn_back(done, cosine, sine), unit_at, 0)
         return unused
@@ -726,14 +844,21 @@
     lax.fori_loop(0, pairs, key_pair, 0)
 
 
-def attend(tables, qkv):
+def table_shapes(parts, units):
+    table = pltpu.VMEM((units, LANES), jnp.float32)
+    row = pltpu.VMEM((parts, LANES), jnp.float32)
+    return [pltpu.VMEM((units, LANES), jnp.int32), table, table, row, row]
+
+
+def attend(lengths, qkv):
     parts, units, _ = qkv.shape
     block = parts * UNIT_BLOCK
     blocks = units // UNIT_BLOCK
     smem = pl.BlockSpec(memory_space=pltpu.SMEM)
     vmem = pl.BlockSpec(memory_space=pltpu.VMEM)
     rows = jax.ShapeDtypeStruct((blocks, block, LANES), jnp.bfloat16)
-    extra = UNIT_PAIR
+    halves = UNIT_PAIR // UNIT_BLOCK
+    held = pltpu.VMEM((halves, 2, block, LANES), jnp.float32)
     return pl.pallas_call(
         attend_kernel,
         out_shape=(
@@ -744,23 +869,28 @@
             rows,
             rows,
         ),
-        in_specs=[smem] * 3 + [vmem] * 6,
+        in_specs=[smem, vmem],
         out_specs=(vmem,) * 6,
         scratch_shapes=[
-            pltpu.VMEM((2, blocks, LANES, block), jnp.bfloat16),
-            pltpu.VMEM((2, blocks, HD + extra, block), jnp.bfloat16),
-            pltpu.VMEM((block, block), jnp.int32),
+            pltpu.VMEM((blocks, 2, block, LANES), jnp.bfloat16),
+            pltpu.VMEM((blocks, LANES, block), jnp.bfloat16),
+            held,
+            held,
+            held,
+            pltpu.VMEM((halves, block, LANES), jnp.float32),
             pltpu.VMEM((block, block), jnp.float32),
-        ],
+            pltpu.VMEM((block, block), jnp.float32),
+        ]
+        + table_shapes(parts, units),
         compiler_params=pltpu.CompilerParams(vmem_limit_bytes=KERNEL_VMEM),
         cost_estimate=pl.CostEstimate(
             flops=20 * 10**9, bytes_accessed=16 << 20, transcendentals=20 * 10**6
         ),
         name="attend",
-    )(*tables, qkv)
-
-
-def attend_back(tables, query, key, value, out, log, grad):
+    )(lengths, qkv)
+
+
+def attend_back(lengths, query, key, value, out, log, grad):
     parts, units, _ = grad.shape
     block = parts * UNIT_BLOCK
     blocks = units // UNIT_BLOCK
@@ -769,64 +899,22 @@
     return pl.pallas_call(
         attend_back_kernel,
         out_shape=jax.ShapeDtypeStruct((parts, units, 3 * LANES), jnp.bfloat16),
-        in_specs=[smem] * 3 + [vmem] * 11,
+        in_specs=[smem] + [vmem] * 6,
         out_specs=vmem,
         scratch_shapes=[
             pltpu.VMEM((blocks, LANES, block), jnp.bfloat16),
             pltpu.VMEM((blocks, block, LANES), jnp.float32),
             pltpu.VMEM((blocks, block, LANES), jnp.float32),
-            pltpu.VMEM((block, block), jnp.int32),
             pltpu.VMEM((block, block), jnp.float32),
-        ],
+            pltpu.VMEM((block, block), jnp.float32),
+        ]
+        + table_shapes(parts, units),
         compiler_params=pltpu.CompilerParams(vmem_limit_bytes=KERNEL_VMEM),
         cost_estimate=pl.CostEstimate(
             flops=50 * 10**9, bytes_accessed=16 << 20, transcendentals=20 * 10**6
         ),
         name="attend_back",
-    )(*tables, query, key, value, out, log, grad)
-
-
-def attention_tables(lengths, grp_here, rep_here, units):
-    reps = lax.axis_size("rep")
-    parts = lax.axis_size("grp") * reps
-    block = parts * UNIT_BLOCK
-    blocks = units // UNIT_BLOCK
-    own = lax.dynamic_index_in_dim(lengths, grp_here, 0, keepdims=False)
-    ends = jnp.cumsum(own)
-    unit_ids = jnp.arange(units, dtype=jnp.int32)
-    begin = jnp.max(
-        jnp.where(ends[None, :] <= unit_ids[:, None], ends[None, :], 0), axis=1
-    ).astype(jnp.int32)
-    part_ids = jnp.arange(parts, dtype=jnp.int32)
-    offset = part_ids % reps ^ rep_here
-    slot = offset * lax.axis_size("grp") + (part_ids // reps ^ grp_here)
-    frequency = jnp.power(
-        rope_base, -2.0 * (jnp.arange(LANES) % (HD // 2)).astype(jnp.float32) / HD
-    )
-    unit_angle = ((unit_ids - begin) * parts).astype(jnp.float32)[:, None] * frequency[None, :]
-    part_angle = part_ids.astype(jnp.float32)[:, None] * frequency[None, :]
-    low = jnp.maximum(
-        (begin * parts)[:, None], unit_ids[:, None] * parts + part_ids[None, :] - (WINDOW - 1)
-    )
-    low = low.reshape(blocks, UNIT_BLOCK, parts)
-    least = jnp.min(low, axis=(1, 2))
-    most = jnp.max(low, axis=(1, 2))
-    block_ids = jnp.arange(blocks, dtype=jnp.int32)
-    first = jnp.maximum(least, 0) // block
-    plain = jnp.clip((most + block - 1) // block, first, block_ids)
-    low_rows = jnp.broadcast_to(
-        low.transpose(0, 2, 1).reshape(blocks, 1, block), (blocks, 8, block)
-    )
-    return (
-        slot,
-        first,
-        plain,
-        jnp.cos(unit_angle),
-        jnp.sin(unit_angle),
-        jnp.cos(part_angle),
-        jnp.sin(part_angle),
-        low_rows,
-    )
+    )(lengths, query, key, value, out, log, grad)
 
 
 def swap(value, grp_step, rep_step):
@@ -900,8 +988,8 @@
     return order + rest
 
 
-def link_of(offset, part, reps):
-    if reps > 8 and offset == reps - 2 and part == 1:
+def link_of(offset, part, reps, turned=1):
+    if offset == reps - 2 and part == turned:
         return 4
     return lowest(offset)
 
@@ -922,8 +1010,7 @@
     weight_ref,
     gate_ref,
     up_ref,
-    down_first,
-    down_second,
+    down_ref,
     output_ref,
     out_away,
     gains,
@@ -1041,10 +1128,9 @@
             load(columns_of(weight, *stripe), target_ref.at[:, pl.ds(at * LANES, LANES)])
     for at, (grp, high, low) in enumerate(stripes[: len(stripes) // 2]):
         first = (8 * high + 2 * low + place) * LANES
-        target_ref = (down_first, down_second)[at // 2]
         load(
             w_down.at[pl.ds(pl.multiple_of(first, LANES), LANES)],
-            target_ref.at[pl.ds(at % 2 * LANES, LANES)],
+            down_ref.at[pl.ds(at * LANES, LANES)],
         )
     load(out_rows, out_away)
     for one in stripe_loads:
@@ -1154,14 +1240,13 @@
             jax.ShapeDtypeStruct((2, half, 3 * LANES), jnp.bfloat16),
             jax.ShapeDtypeStruct((2, half, own_width), jnp.bfloat16),
             jax.ShapeDtypeStruct((half, own_width), jnp.bfloat16),
-            jax.ShapeDtypeStruct((2 * LANES, width), jnp.bfloat16),
-            jax.ShapeDtypeStruct((own_width // 2 - 2 * LANES, width), jnp.bfloat16),
+            jax.ShapeDtypeStruct((own_width // 2, width), jnp.bfloat16),
             jax.ShapeDtypeStruct((half // 4, width), jnp.bfloat16),
             jax.ShapeDtypeStruct(out_rows.shape, jnp.bfloat16),
             jax.ShapeDtypeStruct((2, 16, half), jnp.bfloat16),
         ),
         in_specs=[vmem, vmem] + [anywhere] * 8,
-        out_specs=(anywhere,) + (vmem,) * 9,
+        out_specs=(anywhere,) + (vmem,) * 8,
         scratch_shapes=[
             pltpu.VMEM((reps, 2, row_count, width), jnp.bfloat16),
             pltpu.VMEM((4, 2 * row_count, width), jnp.bfloat16),
@@ -1183,23 +1268,44 @@
     )(tokens, gain_rows, w_query, w_key, w_value, w_gate, w_up, w_down, w_output, out_rows)
 
 
+SCATTER_PLAN = (
+    ("first", "up"), ("rows", 13, 0), ("rows", 15, 0), ("weights", 1), ("rows", 1, 0),
+    ("rows", 15, 1), ("weights", 2), ("rows", 5, 0), ("first", "down"), ("rows", 14, 0),
+    ("first", "gate"), ("rows", 12, 0), ("rows", 13, 1), ("weights", 1), ("rows", 14, 1),
+    ("rows", 9, 1), ("weights", 1), ("sum", "up"), ("weights", 1), ("rows", 11, 0),
+    ("rows", 11, 1), ("rows", 1, 1), ("rows", 10, 0), ("rows", 7, 0), ("first", "out"),
+    ("weights", 1), ("sum", "down"), ("weights", 4), ("rows", 3, 1), ("rows", 10, 1),
+    ("weights", 1), ("sum", "gate"), ("rows", 7, 1), ("rows", 3, 0), ("rows", 9, 0),
+    ("rows", 2, 1), ("rows", 12, 1), ("weights", 3), ("sum", "quad"), ("weights", 1),
+    ("weights over",), ("rows", 6, 1), ("rows", 8, 0), ("rows", 8, 1), ("rows", 5, 1),
+    ("sum", "out"), ("rows", 4, 1), ("sum", "out next"), ("rows", 6, 0), ("weights out",),
+    ("rows", 2, 0), ("rows", 0, 1), ("rows", 4, 0), ("rows", 0, 0), ("sum", "quad next"),
+)
+
+
 def scatter_kernel(
     back_ref,
     weight_ref,
+    tokens_ref,
+    mixed_grad,
+    gain_ref,
     normed_ref,
-    *refs,
-):
-    scatter_rows(back_ref, weight_ref, normed_ref, *refs[-SCATTER_REFS:])
-
-
-def scatter_rows(
-    back_ref,
-    weight_ref,
-    normed_ref,
-    grad_ref,
+    gate_kept,
+    gate_met,
+    up_kept,
+    up_met,
+    down_kept,
+    down_met,
+    output_kept,
+    output_met,
+    token_ref,
     pieces_ref,
+    quad_ref,
+    down_ref,
+    output_ref,
     away,
     landed,
+    grad_in,
     normed,
     back_t,
     weight_t,
@@ -1207,6 +1313,21 @@
     half_out,
     half_in,
     piece_out,
+    gate_away,
+    gate_landed,
+    up_away,
+    up_landed,
+    up_last,
+    down_away,
+    down_landed,
+    down_last,
+    output_away,
+    output_landed,
+    output_next,
+    output_last,
+    narrow_stage,
+    wide_stage,
+    crossed,
     normed_sem,
     send_sem,
     recv_sem,
@@ -1214,14 +1335,18 @@
     side_recv,
     piece_send,
     piece_recv,
+    stage_sem,
+    sum_send,
+    sum_recv,
 ):
     here, there = lax.axis_index("grp"), lax.axis_index("rep")
     reps, rows, columns = back_ref.shape
     row_count = rows // 2
-    width = grad_ref.shape[2]
+    width = token_ref.shape[1]
     half = width // 2
     own_rows = half // reps
     steps = [1 << place for place in range(reps.bit_length() - 1)]
+    bit = {step: (there // step) % 2 for step in steps}
     across = (1 - here, there)
 
     def other(offset):
@@ -1243,10 +1368,167 @@
     for offset in range(slots):
         fetch[offset].start()
 
+    def part_of(ref, axis, index):
+        return ref.at[(slice(None),) * axis + (index,)]
+
+    def load(at, source, target_ref):
+        copy = pltpu.make_async_copy(source, target_ref, stage_sem.at[at])
+        copy.start()
+        return copy
+
+    def open_half(at, kept, met, axis, flag, stage, target_ref):
+        return (
+            load(2 * at, part_of(kept, axis, flag), stage),
+            load(2 * at + 1, part_of(met, axis, flag), target_ref),
+        )
+
+    firsts = [
+        open_half(0, down_kept, down_met, 0, 1 - here, wide_stage.at[0], down_away),
+        open_half(1, output_kept, output_met, 0, 1 - here, wide_stage.at[1], output_away),
+        open_half(2, gate_kept, gate_met, 1, 1 - bit[2], narrow_stage.at[1, 0], gate_away),
+        open_half(3, up_kept, up_met, 2, 1 - bit[2], narrow_stage.at[0], up_away),
+    ]
+
     for at in range(2):
         turned = jnp.transpose(weight_ref[at].astype(jnp.float32)).astype(jnp.bfloat16)
         weight_t[:, pl.ds(at * half, half)] = turned
     pl.semaphore_wait(barrier, reps)
+
+    def add_to(target_ref, *sources):
+        lead = target_ref.shape[:-2]
+        count = 1
+        for size in lead:
+            count *= size
+        for at in range(count):
+            index, rest = [], at
+            for size in lead[::-1]:
+                index.insert(0, rest % size)
+                rest //= size
+
+            def some_rows(step, unused):
+                place = tuple(index) + (pl.ds(pl.multiple_of(step * 16, 16), 16),)
+                total = target_ref[place].astype(jnp.float32)
+                for source in sources:
+                    total = total + source[place].astype(jnp.float32)
+                target_ref[place] = total.astype(target_ref.dtype)
+                return unused
+
+            lax.fori_loop(0, target_ref.shape[-2] // 16, some_rows, 0)
+
+    def sum_copy(at, source, target_ref, target):
+        return pltpu.make_async_remote_copy(
+            src_ref=source,
+            dst_ref=target_ref,
+            send_sem=sum_send.at[at],
+            recv_sem=sum_recv.at[at],
+            device_id=target,
+            device_id_type=MESH_IDS,
+        )
+
+    down_cross = sum_copy(0, down_away, down_landed, across)
+    output_cross = sum_copy(1, output_away, output_landed, across)
+    gate_low = sum_copy(2, gate_away, gate_landed, other(2))
+    up_low = sum_copy(3, up_away, up_landed, other(2))
+    down_high = sum_copy(4, down_landed.at[1 - bit[8]], down_last, other(8))
+    up_high = sum_copy(5, up_landed.at[1 - bit[8]], up_last, other(8))
+    output_low = sum_copy(6, output_landed.at[:, 1 - bit[2]], output_next, other(2))
+    output_high = sum_copy(7, output_next.at[1 - bit[8]], output_last, other(8))
+    quad_far = [
+        sum_copy(8, gate_landed.at[1 - bit[4]], crossed.at[0], other(4)),
+        sum_copy(9, up_last.at[1 - bit[4]], crossed.at[1], other(4)),
+    ]
+    quad_near = [
+        sum_copy(10, gate_landed.at[bit[4], 1 - bit[1]], quad_ref.at[bit[4], bit[1], 0], other(1)),
+        sum_copy(11, up_last.at[bit[4], 1 - bit[1]], quad_ref.at[bit[4], bit[1], 1], other(1)),
+        sum_copy(12, crossed.at[0, 1 - bit[1]], quad_ref.at[1 - bit[4], bit[1], 0], other(1)),
+        sum_copy(13, crossed.at[1, 1 - bit[1]], quad_ref.at[1 - bit[4], bit[1], 1], other(1)),
+    ]
+    sum_copies = (
+        [down_cross, output_cross, gate_low, up_low, down_high, up_high, output_low, output_high]
+        + quad_far
+        + quad_near
+    )
+
+    def first_send(at, target_ref, stage, copy):
+        for one in firsts[at]:
+            one.wait()
+        add_to(target_ref, stage)
+        copy.start()
+
+    def own_half(at, kept, met, axis, flag, stage_a, stage_b, copy, target_ref):
+        loads = (
+            load(2 * at, part_of(kept, axis, flag), stage_a),
+            load(2 * at + 1, part_of(met, axis, flag), stage_b),
+        )
+        for one in loads:
+            one.wait()
+        copy.wait_recv()
+        add_to(target_ref, stage_a, stage_b)
+
+    def down_sum():
+        own_half(
+            0, down_kept, down_met, 0, here, wide_stage.at[0], wide_stage.at[1], down_cross,
+            down_landed,
+        )
+        down_high.start()
+
+    def output_sum():
+        own_half(
+            1, output_kept, output_met, 0, here, wide_stage.at[0], wide_stage.at[1], output_cross,
+            output_landed,
+        )
+        output_low.start()
+
+    def gate_sum():
+        own_half(
+            2, gate_kept, gate_met, 1, bit[2], narrow_stage.at[0, 0], narrow_stage.at[1, 0],
+            gate_low, gate_landed,
+        )
+
+    def up_sum():
+        own_half(
+            3, up_kept, up_met, 2, bit[2], narrow_stage.at[0], narrow_stage.at[1], up_low,
+            up_landed,
+        )
+        up_high.start()
+
+    def output_next_sum():
+        output_low.wait_recv()
+        add_to(output_next, output_landed.at[:, bit[2]])
+        output_high.start()
+
+    def quad_send():
+        up_high.wait_recv()
+        add_to(up_last, up_landed.at[bit[8]])
+        for one in quad_far + quad_near[:2]:
+            one.start()
+        quad_ref[bit[4], bit[1], 0] = gate_landed[bit[4], bit[1]]
+        quad_ref[bit[4], bit[1], 1] = up_last[bit[4], bit[1]]
+
+    def quad_pass():
+        for one in quad_far:
+            one.wait_recv()
+        for one in quad_near[2:]:
+            one.start()
+        for kind in range(2):
+            quad_ref[1 - bit[4], bit[1], kind] = crossed[kind, bit[1]]
+
+    def last_sums():
+        down_high.wait_recv()
+        output_high.wait_recv()
+
+        def down_rows(step, unused):
+            cut = pl.ds(pl.multiple_of(step * 16, 16), 16)
+            for at in range(down_last.shape[0]):
+                down_ref[at, cut] = down_last[at, cut].astype(jnp.float32) + down_landed[
+                    bit[8], at, cut
+                ].astype(jnp.float32)
+            output_ref[cut] = output_last[cut].astype(jnp.float32) + output_next[
+                bit[8], cut
+            ].astype(jnp.float32)
+            return unused
+
+        lax.fori_loop(0, own_rows // 16, down_rows, 0)
 
     def rows_copy(offset, part):
         if offset == 0:
@@ -1259,11 +1541,11 @@
                 device_id_type=MESH_IDS,
             )
         return pltpu.make_async_remote_copy(
-            src_ref=away.at[offset, part],
+            src_ref=away.at[offset // 2, part],
             dst_ref=landed.at[offset, part],
             send_sem=send_sem.at[2 * offset + part],
             recv_sem=recv_sem.at[2 * offset + part],
-            device_id=other(link_of(offset, part, reps)),
+            device_id=other(link_of(offset, part, reps, 0)),
             device_id_type=MESH_IDS,
         )
 
@@ -1273,30 +1555,28 @@
         for part in (0, 1)
         if offset or part
     }
-    tile = 32
-
-    def product(offset, part):
-        return jnp.dot(
-            back_ref[offset, pl.ds(part * row_count, row_count), :],
-            weight_t[...],
-            preferred_element_type=jnp.float32,
-        )
 
     def send(offset, part):
         sources = [
             later
             for later in range(1, reps)
-            if later - link_of(later, part, reps) == offset
+            if later - link_of(later, part, reps, 0) == offset
         ]
         for later in sources:
             copies[later, part].wait_recv()
-        total = product(offset, part)
+        total = jnp.dot(
+            back_ref[offset, pl.ds(part * row_count, row_count), :],
+            weight_t[...],
+            preferred_element_type=jnp.float32,
+        )
         for later in sources:
             total = total + landed[later, part].astype(jnp.float32)
         if offset == 0 and part == 0:
-            grad_ref[here] = total
+            grad_in[...] = total
         else:
-            away[offset, part] = total.astype(jnp.bfloat16)
+            if offset % 2 == 0:
+                copies[offset + 1, part].wait_send()
+            away[offset // 2, part] = total.astype(jnp.bfloat16)
             copies[offset, part].start()
 
     def weight_step(offset):
@@ -1352,89 +1632,124 @@
         for one in piece_copies:
             one.start()
 
-    far = [step for step in range(reps - 4, 0, -4)]
-    todo = []
-    for base in far + [0]:
-        todo.append((base + 3, 1))
-        todo.append((base + 3, 0))
-        todo.append((base + 1, 1))
-        todo.append((base + 1, 0))
-    first = todo[:2]
-    for offset, part in first:
-        send(offset, part)
-    for offset, part in todo[2:6]:
-        send(offset, part)
-    send(reps - 2, 1)
-    send(reps - 2, 0)
-    for offset, part in todo[6:]:
-        send(offset, part)
     weights = list(range(reps))
 
     def weight_steps(count):
         for _ in range(min(count, len(weights))):
             weight_step(weights.pop(0))
 
-    last = []
-    order = []
-    for base in sorted(far, key=lambda step: (-bin(step).count("1"), -step)):
-        if base != far[0]:
-            order.append((base + 2, 1))
-            order.append((base + 2, 0))
-    order += [(2, 1), (2, 0)]
-    sums = sorted(far, key=lambda step: (-bin(step).count("1"), -step))
-    for base in sums:
-        last += [(base, 1), (base, 0)]
-    if reps == 16:
-        plan = [
-            (10, 1), (10, 0), 4, (12, 1), (12, 0), 4, (6, 1), (6, 0), 2, (8, 1), 2, (8, 0),
-            (2, 1), (2, 0), 4, "cross", (4, 1), (4, 0), "share", (0, 1), (0, 0),
-        ]
-    else:
-        plan = order + last + [reps, "cross", "share", (0, 1), (0, 0)]
-    for item in plan:
-        if item == "cross":
-            weight_steps(reps)
+    firsts_by = {
+        "down": lambda: first_send(0, down_away, wide_stage.at[0], down_cross),
+        "out": lambda: first_send(1, output_away, wide_stage.at[1], output_cross),
+        "gate": lambda: first_send(2, gate_away, narrow_stage.at[1, 0], gate_low),
+        "up": lambda: first_send(3, up_away, narrow_stage.at[0], up_low),
+    }
+    sums_by = {
+        "down": down_sum,
+        "out": output_sum,
+        "gate": gate_sum,
+        "up": up_sum,
+        "out next": output_next_sum,
+        "quad": quad_send,
+        "quad next": quad_pass,
+    }
+    for kind, *what in SCATTER_PLAN:
+        if kind == "rows":
+            send(*what)
+        elif kind == "weights":
+            weight_steps(*what)
+        elif kind == "first":
+            firsts_by[what[0]]()
+        elif kind == "sum":
+            sums_by[what[0]]()
+        elif kind == "weights over":
             cross_weights()
-        elif item == "share":
+        else:
             share_weights()
-        elif isinstance(item, int):
-            weight_steps(item)
-        else:
-            send(*item)
+    last_sums()
     copies[0, 1].wait_recv()
-    grad_ref[1 - here] = landed[0, 1].astype(jnp.float32)
+
+    tile = 32
+
+    def norm_rows(grp, step, grad_rows):
+        place = pl.ds(pl.multiple_of(grp * row_count + step * tile, tile), tile)
+        values = tokens_ref[place, :].astype(jnp.float32)
+        inverse = rms_scale(values)
+        normed_rows = values * inverse
+        weighted = grad_rows * gain_ref[0:1, :]
+        token_ref[place, :] = (
+            mixed_grad[place, :]
+            + inverse
+            * (weighted - normed_rows * jnp.mean(weighted * normed_rows, axis=-1, keepdims=True))
+        ).astype(jnp.bfloat16)
+
+    def norm_back(step, unused):
+        cut = pl.ds(pl.multiple_of(step * tile, tile), tile)
+        norm_rows(here, step, grad_in[cut, :])
+        norm_rows(1 - here, step, landed[0, 1, cut, :].astype(jnp.float32))
+        return unused
+
+    lax.fori_loop(0, row_count // tile, norm_back, 0)
     for one in piece_copies:
         one.wait()
-    half_copy.wait_send()
-    for one in copies.values():
+    for one in quad_near:
+        one.wait_recv()
+    for one in [half_copy] + sum_copies:
         one.wait_send()
-
-
-def scatter_heads(back, weights, normed, ahead):
+    for (offset, part), one in copies.items():
+        if offset % 2 == 0 or (offset == 1 and part == 0):
+            one.wait_send()
+
+
+def scatter_heads(back, weights, tokens, mixed_grad, gain, normed, sums):
     reps, rows, columns = back.shape
     width = normed.shape[2]
     row_count = rows // 2
     half = width // 2
+    own_rows = half // reps
+    own_width = width // 2
     vmem = pl.BlockSpec(memory_space=pltpu.VMEM)
     anywhere = pl.BlockSpec(memory_space=pl.ANY)
+    low, full = jnp.bfloat16, jnp.float32
+    wide = (2, 2, own_rows, width)
+    slim = (2, 2, 2, own_rows, own_width)
     return pl.pallas_call(
         scatter_kernel,
         out_shape=(
-            jax.ShapeDtypeStruct((2, row_count, width), jnp.float32),
-            jax.ShapeDtypeStruct((reps, half // reps, columns), jnp.bfloat16),
+            jax.ShapeDtypeStruct((rows, width), low),
+            jax.ShapeDtypeStruct((reps, own_rows, columns), low),
+            jax.ShapeDtypeStruct(slim, low),
+            jax.ShapeDtypeStruct(wide[1:], full),
+            jax.ShapeDtypeStruct(wide[2:], full),
         ),
-        in_specs=[vmem, vmem, anywhere] + [anywhere] * len(ahead),
-        out_specs=(vmem, vmem),
+        in_specs=[vmem] * 5 + [anywhere] * 9,
+        out_specs=(vmem,) * 5,
         scratch_shapes=[
-            pltpu.VMEM((reps, 2, row_count, width), jnp.bfloat16),
-            pltpu.VMEM((reps, 2, row_count, width), jnp.bfloat16),
-            pltpu.VMEM((4, rows, width), jnp.bfloat16),
-            pltpu.VMEM((columns, rows), jnp.bfloat16),
-            pltpu.VMEM((columns, width), jnp.bfloat16),
-            pltpu.VMEM((columns, width), jnp.float32),
-            pltpu.VMEM((columns, half), jnp.bfloat16),
-            pltpu.VMEM((columns, half), jnp.bfloat16),
-            pltpu.VMEM((reps, half // reps, columns), jnp.bfloat16),
+            pltpu.VMEM((reps // 2, 2, row_count, width), low),
+            pltpu.VMEM((reps, 2, row_count, width), low),
+            pltpu.VMEM((row_count, width), full),
+            pltpu.VMEM((2, rows, width), low),
+            pltpu.VMEM((columns, rows), low),
+            pltpu.VMEM((columns, width), low),
+            pltpu.VMEM((columns, width), full),
+            pltpu.VMEM((columns, half), low),
+            pltpu.VMEM((columns, half), low),
+            pltpu.VMEM((reps, own_rows, columns), low),
+            pltpu.VMEM(slim[1:], low),
+            pltpu.VMEM(slim[1:], low),
+            pltpu.VMEM(slim, low),
+            pltpu.VMEM(slim, low),
+            pltpu.VMEM(slim[1:], low),
+            pltpu.VMEM(wide, low),
+            pltpu.VMEM(wide, low),
+            pltpu.VMEM(wide[1:], low),
+            pltpu.VMEM(wide, low),
+            pltpu.VMEM(wide, low),
+            pltpu.VMEM(wide[1:], low),
+            pltpu.VMEM(wide[2:], low),
+            pltpu.VMEM((2,) + slim, low),
+            pltpu.VMEM((2,) + wide, low),
+            pltpu.VMEM(slim[1:], low),
             pltpu.SemaphoreType.DMA((reps,)),
             pltpu.SemaphoreType.DMA((2 * reps,)),
             pltpu.SemaphoreType.DMA((2 * reps,)),
@@ -1442,15 +1757,18 @@
             pltpu.SemaphoreType.DMA,
             pltpu.SemaphoreType.DMA((reps,)),
             pltpu.SemaphoreType.DMA((reps,)),
+            pltpu.SemaphoreType.DMA((8,)),
+            pltpu.SemaphoreType.DMA((14,)),
+            pltpu.SemaphoreType.DMA((14,)),
         ],
         compiler_params=pltpu.CompilerParams(
-            vmem_limit_bytes=KERNEL_VMEM, collective_id=1, has_side_effects=True
+            vmem_limit_bytes=62 * 1024 * 1024, collective_id=1, has_side_effects=True
         ),
         cost_estimate=pl.CostEstimate(
             flops=14 * 10**9, bytes_accessed=250 << 20, transcendentals=0
         ),
         name="scatter_heads",
-    )(back, weights, normed, *ahead)
+    )(back, weights, tokens, mixed_grad, gain, normed, *sums)
 
 
 def mlp_kernel(
@@ -1465,11 +1783,8 @@
     gate_in,
     up_own,
     up_other,
-    down_first,
-    down_second,
-    down_other,
-    mixed_ref,
-    down_ref,
+    down_own,
+    block_ref,
     grad_ref,
     back_ref,
     gate_ref,
@@ -1479,6 +1794,9 @@
     down_sent,
     output_kept,
     output_sent,
+    mixed_ref,
+    down_own_ref,
+    down_far_landed,
     attended,
     branch_ref,
     returned,
@@ -1528,24 +1846,20 @@
         ),
     ]
     own_part = own_width // 2
-    early_rows = down_first.shape[0]
-
-    def down_cut(grp, first, count):
-        return pl.ds(pl.multiple_of(grp * own_part + first, LANES), count)
-
-    late_rows = own_part - early_rows
+
+    def down_cut(grp):
+        return pl.ds(pl.multiple_of(grp * own_part, own_part), own_part)
+
     loads += [
+        pltpu.make_async_copy(down_own, w_out.at[down_cut(here)], load_sem.at[4]),
+        pltpu.make_async_copy(out_rows.at[pl.ds(0, row_count)], out_ref.at[0, 0], load_sem.at[5]),
         pltpu.make_async_copy(
-            down_first, w_out.at[down_cut(here, 0, early_rows)], load_sem.at[4]
+            out_rows.at[pl.ds(row_count, row_count)], out_ref.at[1, 0], load_sem.at[6]
         ),
+        pltpu.make_async_copy(out_across.at[pl.ds(0, row_count)], out_ref.at[0, 2], load_sem.at[7]),
         pltpu.make_async_copy(
-            down_second, w_out.at[down_cut(here, early_rows, late_rows)], load_sem.at[5]
+            out_across.at[pl.ds(row_count, row_count)], out_ref.at[1, 2], load_sem.at[8]
         ),
-        pltpu.make_async_copy(
-            down_other, w_out.at[down_cut(1 - here, 0, early_rows)], load_sem.at[6]
-        ),
-        pltpu.make_async_copy(out_rows, out_ref.at[0], load_sem.at[7]),
-        pltpu.make_async_copy(out_across, out_ref.at[2], load_sem.at[8]),
     ]
     place = there % 4
     core = there % 2
@@ -1615,26 +1929,47 @@
         )
     for one in heads_copies[::-1]:
         one.start()
+    parts = range(groups)
+
+    def rows_of(part):
+        return pl.ds(part * row_count, row_count)
+
     output_near = [
-        copy(at, piece, output_cut(part), sibling)
-        for at, (piece, part) in enumerate(output_pieces, 9)
+        copy(at, piece, output_cut(part), sibling) for at, (piece, part) in enumerate(output_pieces)
     ]
-    down_far = copy(11, down_second, w_out.at[down_cut(here, early_rows, late_rows)], facing)
-    out_near = copy(12, out_rows, out_ref.at[1], sibling)
-    out_on = copy(13, out_across, out_ref.at[3], sibling)
-    for one in output_near + [out_near, out_on, down_far]:
+    down_far = copy(2, down_own, w_out.at[down_cut(here)], facing)
+    out_near = [
+        copy(3 + part, out_rows.at[rows_of(part)], out_ref.at[part, 1], sibling) for part in parts
+    ]
+    out_on = [
+        copy(5 + part, out_across.at[rows_of(part)], out_ref.at[part, 3], sibling) for part in parts
+    ]
+    for one in output_near + out_near + out_on + [down_far]:
         one.start()
     returned[here, there] = heads_ref[here * heads + there]
 
-    mid_near = copy(0, mid_ref.at[0], mid_ref.at[1], sibling)
-    mid_far = copy(1, mid_ref.at[0], mid_ref.at[2], across)
-    mid_on = copy(2, mid_ref.at[2], mid_ref.at[3], sibling)
-    grad_near = [copy(3 + at, near_away.at[at], near_landed.at[at], sibling) for at in range(2)]
-    grad_far = copy(5, far_away, far_landed, across)
-    down_near = [copy(6 + at, near_away.at[at], down_landed.at[at], sibling) for at in range(2)]
-    gate_cross = copy(
-        8, w_in.at[1 - here, :, pl.ds(0, own_width)], gate_ref, facing
-    )
+    mid_near = [copy(7 + at, mid_ref.at[at, 0], mid_ref.at[at, 1], sibling) for at in parts]
+    mid_far = [copy(9 + at, mid_ref.at[at, 0], mid_ref.at[at, 2], across) for at in parts]
+    mid_on = [copy(11 + at, mid_ref.at[at, 2], mid_ref.at[at, 3], sibling) for at in parts]
+    grad_near = {
+        (side, at): copy(
+            13 + 2 * side + at, near_away.at[side, at], near_landed.at[side, at], sibling
+        )
+        for side in range(2)
+        for at in parts
+    }
+    grad_far = [copy(17 + at, far_away.at[at], far_landed.at[at], across) for at in parts]
+    down_near = {
+        (side, at): copy(
+            19 + 2 * side + at, near_away.at[side, at], down_landed.at[side, at], sibling
+        )
+        for side in range(2)
+        for at in parts
+    }
+    down_over = [
+        copy(23 + at, down_own_ref.at[1, at], down_far_landed.at[at], across) for at in parts
+    ]
+    gate_cross = copy(25, w_in.at[1 - here, :, pl.ds(0, own_width)], gate_ref, facing)
     up_cut = pl.ds(own_width, own_width)
     up_outs = [
         pltpu.make_async_copy(w_in.at[here, :, up_cut], up_kept, load_sem.at[0]),
@@ -1673,115 +2008,158 @@
 
     lax.fori_loop(0, width // wide, mix, 0)
     tile = 32
-
-    def norm_rows(at, unused):
-        cut = pl.ds(pl.multiple_of(at * tile, tile), tile)
-        values = mixed_ref[cut, :]
-        mid_ref[0, cut, :] = (values * rms_scale(values) * gain_ref[0:1, :]).astype(jnp.bfloat16)
-        return unused
-
-    lax.fori_loop(0, rows // tile, norm_rows, 0)
-    mid_far.start()
-    mid_near.start()
+    for part in parts:
+
+        def norm_rows(at, unused):
+            cut = pl.ds(pl.multiple_of(at * tile, tile), tile)
+            values = mixed_ref[pl.ds(pl.multiple_of(part * row_count + at * tile, tile), tile), :]
+            mid_ref[part, 0, cut, :] = (
+                values * rms_scale(values) * gain_ref[0:1, :]
+            ).astype(jnp.bfloat16)
+            return unused
+
+        lax.fori_loop(0, row_count // tile, norm_rows, 0)
+        mid_far[part].start()
+        mid_near[part].start()
     for one in loads[3:]:
         one.wait()
-    down_far.wait_recv()
     narrow_tile = 256
-
-    def forward(slot):
-        def columns(at, unused):
+    per_half = own_part // narrow_tile
+    every = (0, 1)
+
+    def pair_rows(ref, side, part, cols):
+        values = ref[part, pl.ds(2 * side, 2), :, cols]
+        return values.reshape(rows, values.shape[2])
+
+    def forward(side, part, halves):
+        def columns(step, unused):
+            at = jnp.where(step < per_half, halves[0] * per_half, halves[-1] * per_half - per_half)
+            at = at + step
             cut = pl.ds(pl.multiple_of(at * narrow_tile, narrow_tile), narrow_tile)
             up_cut = pl.ds(pl.multiple_of(own_width + at * narrow_tile, narrow_tile), narrow_tile)
+            low_rows = pair_rows(mid_ref, side, part, slice(0, half))
+            high_rows = pair_rows(mid_ref, side, part, slice(half, width))
 
             def project(cols):
                 return jnp.dot(
-                    mid_ref[slot, :, :half], w_in[0, :, cols], preferred_element_type=jnp.float32
-                ) + jnp.dot(
-                    mid_ref[slot, :, half:], w_in[1, :, cols], preferred_element_type=jnp.float32
-                )
+                    low_rows, w_in[0, :, cols], preferred_element_type=jnp.float32
+                ) + jnp.dot(high_rows, w_in[1, :, cols], preferred_element_type=jnp.float32)
 
             gate_pre, up_pre = project(cut), project(up_cut)
-            grad_hidden = contract(out_ref[slot], w_out[cut, :], 1, 1)
+            grad_hidden = contract(
+                pair_rows(out_ref, side, part, slice(0, width)), w_out[cut, :], 1, 1
+            )
             gate_sig = jax.nn.sigmoid(gate_pre)
             gate_silu = gate_pre * gate_sig
-            hidden_ref[slot, :, cut] = (gate_silu * up_pre).astype(jnp.bfloat16)
-            slope_ref[slot, :, cut] = (
-                grad_hidden * up_pre * gate_sig * (1.0 + gate_pre * (1.0 - gate_sig))
-            ).astype(jnp.bfloat16)
-            slope_ref[slot, :, up_cut] = (grad_hidden * gate_silu).astype(jnp.bfloat16)
+
+            def put(ref, cols, values):
+                ref[part, pl.ds(2 * side, 2), :, cols] = values.astype(jnp.bfloat16).reshape(
+                    2, row_count, narrow_tile
+                )
+
+            put(hidden_ref, cut, gate_silu * up_pre)
+            put(
+                slope_ref,
+                cut,
+                grad_hidden * up_pre * gate_sig * (1.0 + gate_pre * (1.0 - gate_sig)),
+            )
+            put(slope_ref, up_cut, grad_hidden * gate_silu)
             return unused
 
-        lax.fori_loop(0, own_width // narrow_tile, columns, 0)
-
-    def backward(slot, finish):
+        lax.fori_loop(0, len(halves) * per_half, columns, 0)
+
+    def backward(side, part):
         for at in range(2):
 
             def columns(step, unused):
                 cut = pl.ds(pl.multiple_of(step * wide, wide), wide)
                 whole = pl.ds(pl.multiple_of(at * half + step * wide, wide), wide)
-                finish(whole, contract(slope_ref[slot], w_in[at, cut, :], 1, 1))
+                values = contract(
+                    pair_rows(slope_ref, side, part, slice(0, 2 * own_width)),
+                    w_in[at, cut, :],
+                    1,
+                    1,
+                )
+                near_away[side, part, :, whole] = values[row_count:].astype(jnp.bfloat16)
+                if side == 0:
+                    grad_ref[rows_of(part), whole] = values[:row_count]
+                else:
+                    far_away[part, :, whole] = values[:row_count].astype(jnp.bfloat16)
                 return unused
 
             lax.fori_loop(0, half // wide, columns, 0)
-
-    def down(slot, finish):
+        grad_near[side, part].start()
+
+    def add_rows(target_ref, source_ref):
+        def some_rows(at, unused):
+            cut = pl.ds(pl.multiple_of(at * tile, tile), tile)
+            target_ref[cut, :] = (
+                target_ref[cut, :].astype(jnp.float32) + source_ref[cut, :].astype(jnp.float32)
+            ).astype(target_ref.dtype)
+            return unused
+
+        lax.fori_loop(0, row_count // tile, some_rows, 0)
+
+    def far_send(part):
+        grad_near[1, part].wait_recv()
+        add_rows(far_away.at[part], near_landed.at[1, part])
+        grad_far[part].start()
+
+    def down(side, part):
+        grad_near[side, part].wait_send()
+
         def columns(step, unused):
             cut = pl.ds(pl.multiple_of(step * wide, wide), wide)
-            finish(
-                cut, jnp.dot(hidden_ref[slot], w_out[:, cut], preferred_element_type=jnp.float32)
-            )
+            values = jnp.dot(
+                pair_rows(hidden_ref, side, part, slice(0, own_width)),
+                w_out[:, cut],
+                preferred_element_type=jnp.float32,
+            ).astype(jnp.bfloat16)
+            near_away[side, part, :, cut] = values[row_count:]
+            down_own_ref[side, part, :, cut] = values[:row_count]
             return unused
 
         lax.fori_loop(0, width // wide, columns, 0)
-
-    def into(target, at):
-        def finish(cut, values):
-            target[at, :, cut] = values.astype(jnp.bfloat16)
-
-        return finish
-
-    forward(0)
-    mid_near.wait_recv()
-    out_near.wait_recv()
-    forward(1)
-    backward(1, into(near_away, 0))
-    grad_near[0].start()
-
-    def keep(cut, values):
-        grad_ref[:, cut] = values
-
-    backward(0, keep)
-    mid_far.wait_recv()
-    mid_on.start()
-    forward(2)
-    mid_on.wait_recv()
-    out_on.wait_recv()
-    forward(3)
-    backward(3, into(near_away, 1))
-    grad_near[1].start()
-    grad_near[1].wait_recv()
-
-    def add_near(cut, values):
-        far_away[:, cut] = (values + near_landed[1, :, cut].astype(jnp.float32)).astype(
-            jnp.bfloat16
-        )
-
-    backward(2, add_near)
-    grad_far.start()
+        down_near[side, part].start()
+
+    def down_meet(side, part):
+        down_near[side, part].wait_recv()
+        add_rows(down_own_ref.at[side, part], down_landed.at[side, part])
+
+    for part in parts:
+        mid_near[part].wait_recv()
+        out_near[part].wait_recv()
+        forward(0, part, (here,))
+    for part in parts:
+        mid_far[part].wait_recv()
+        mid_on[part].start()
+        if part == 0:
+            down_far.wait_recv()
+        else:
+            forward(0, 0, (1 - here,))
+            far_send(0)
+        mid_on[part].wait_recv()
+        out_on[part].wait_recv()
+        forward(1, part, every)
+        backward(1, part)
+    forward(0, 1, (1 - here,))
+    far_send(1)
+    for part in parts:
+        backward(0, part)
 
     def turned(values):
-        flat = values.reshape(4 * rows, values.shape[2]).astype(jnp.float32)
+        flat = values.reshape(4 * rows, values.shape[3]).astype(jnp.float32)
         return jnp.transpose(flat).astype(jnp.bfloat16)
 
     def in_grads(at):
         def some_rows(step, unused):
             cut = pl.ds(pl.multiple_of(step * narrow_tile, narrow_tile), narrow_tile)
             source = pl.ds(pl.multiple_of(at * half + step * narrow_tile, narrow_tile), narrow_tile)
-            left = turned(mid_ref[:, :, source])
+            left = turned(mid_ref[:, :, :, source])
 
             def columns(place_at, unused):
                 cols = pl.ds(pl.multiple_of(place_at * wide, wide), wide)
-                right = slope_ref[:, :, cols].reshape(4 * rows, wide)
+                right = slope_ref[:, :, :, cols].reshape(4 * rows, wide)
                 w_in[at, cut, cols] = jnp.dot(
                     left, right, preferred_element_type=jnp.float32
                 ).astype(jnp.bfloat16)
@@ -1791,35 +2169,13 @@
 
         lax.fori_loop(0, half // narrow_tile, some_rows, 0)
 
-    in_grads(1 - here)
-    gate_cross.start()
-    for at in range(2):
-        grad_near[at].wait_send()
-        down(2 * at + 1, into(near_away, at))
-        down_near[at].start()
-    in_grads(here)
-    for one in up_outs:
-        one.start()
-    for one in (mid_near, mid_far, mid_on):
-        one.wait_send()
-    pl.semaphore_signal(free_sem, inc=1, device_id=sibling, device_id_type=MESH_IDS)
-    for at in range(2):
-        down_near[at].wait_recv()
-
-        def add_down(cut, values):
-            down_ref[at, :, cut] = (values + down_landed[at, :, cut].astype(jnp.float32)).astype(
-                jnp.bfloat16
-            )
-
-        down(2 * at, add_down)
-
     def down_rows(step, unused):
         cut = pl.ds(pl.multiple_of(step * narrow_tile, narrow_tile), narrow_tile)
-        left = turned(hidden_ref[:, :, cut])
+        left = turned(hidden_ref[:, :, :, cut])
 
         def columns(place_at, unused):
             cols = pl.ds(pl.multiple_of(place_at * wide, wide), wide)
-            right = out_ref[:, :, cols].reshape(4 * rows, wide)
+            right = out_ref[:, :, :, cols].reshape(4 * rows, wide)
             w_out[cut, cols] = jnp.dot(left, right, preferred_element_type=jnp.float32).astype(
                 jnp.bfloat16
             )
@@ -1827,45 +2183,69 @@
 
         return lax.fori_loop(0, width // wide, columns, unused)
 
+    def finish(part):
+        grad_near[0, part].wait_recv()
+        grad_far[part].wait_recv()
+
+        def norm_back(at, unused):
+            cut = pl.ds(pl.multiple_of(at * tile, tile), tile)
+            place = pl.ds(pl.multiple_of(part * row_count + at * tile, tile), tile)
+            grad_mid = (
+                grad_ref[place, :]
+                + near_landed[0, part, cut, :].astype(jnp.float32)
+                + far_landed[part, cut, :].astype(jnp.float32)
+            )
+            values = mixed_ref[place, :]
+            inverse = rms_scale(values)
+            normed = values * inverse
+            weighted = grad_mid * gain_ref[0:1, :]
+            grad = out_ref[part, 0, cut, :].astype(jnp.float32) + inverse * (
+                weighted - normed * jnp.mean(weighted * normed, axis=-1, keepdims=True)
+            )
+            grad_ref[place, :] = grad
+            branch_ref[place, :] = grad.astype(jnp.bfloat16)
+            return unused
+
+        lax.fori_loop(0, row_count // tile, norm_back, 0)
+        for head in range(0, heads, 4):
+            at = head * LANES // half
+            start = head * LANES - at * half
+            values = contract(
+                branch_ref[rows_of(part), :],
+                w_output[at, pl.ds(start, 4 * LANES), :],
+                1,
+                1,
+                jnp.bfloat16,
+            )
+            for step in range(4):
+                returned[part, head + step] = values[:, step * LANES : (step + 1) * LANES]
+        for at, (crossing, _) in enumerate(others):
+
+            @pl.when(jnp.where(crossing, 1 - here, here) == part)
+            def _():
+                back_copies[at].start()
+
+    in_grads(1 - here)
+    gate_cross.start()
+    down(1, 0)
+    finish(0)
+    down(1, 1)
+    finish(1)
+    back_ref[here * heads + there] = returned[here, there]
+    for part in parts:
+        down_meet(1, part)
+        down_over[part].start()
+    in_grads(here)
+    for one in up_outs:
+        one.start()
+    for one in mid_near + mid_far + mid_on:
+        one.wait_send()
+    pl.semaphore_signal(free_sem, inc=1, device_id=sibling, device_id_type=MESH_IDS)
+    for part in parts:
+        down(0, part)
     lax.fori_loop(0, own_width // narrow_tile, down_rows, 0)
     for one in down_outs:
         one.start()
-    grad_near[0].wait_recv()
-    grad_far.wait_recv()
-
-    def norm_back(at, unused):
-        cut = pl.ds(pl.multiple_of(at * tile, tile), tile)
-        grad_mid = (
-            grad_ref[cut, :]
-            + near_landed[0, cut, :].astype(jnp.float32)
-            + far_landed[cut, :].astype(jnp.float32)
-        )
-        values = mixed_ref[cut, :]
-        inverse = rms_scale(values)
-        normed = values * inverse
-        weighted = grad_mid * gain_ref[0:1, :]
-        grad = out_ref[0, cut, :].astype(jnp.float32) + inverse * (
-            weighted - normed * jnp.mean(weighted * normed, axis=-1, keepdims=True)
-        )
-        grad_ref[cut, :] = grad
-        branch_ref[cut, :] = grad.astype(jnp.bfloat16)
-        return unused
-
-    lax.fori_loop(0, rows // tile, norm_back, 0)
-    for head in range(0, heads, 4):
-        at = head * LANES // half
-        start = head * LANES - at * half
-        values = contract(
-            branch_ref[...], w_output[at, pl.ds(start, 4 * LANES), :], 1, 1, jnp.bfloat16
-        )
-        for group in range(groups):
-            for step in range(4):
-                returned[group, head + step] = values[
-                    group * row_count : (group + 1) * row_count, step * LANES : (step + 1) * LANES
-                ]
-    for one in back_copies[::-1]:
-        one.start()
-    back_ref[here * heads + there] = returned[here, there]
 
     for at in range(2):
 
@@ -1894,16 +2274,16 @@
         return pl.ds(pl.multiple_of(first, own_rows), own_rows)
 
     def landed_at(at):
-        per_slot = rows // own_rows
-        return at // per_slot, pl.ds(at % per_slot * own_rows, own_rows)
+        per_slot = row_count // own_rows
+        slot = at // per_slot
+        return (slot // 4, slot % 4, pl.ds(at % per_slot * own_rows, own_rows))
 
     core_copies = []
     for at in range(2 * stripes):
-        slot, cut = landed_at(at)
         core_copies.append(
             pltpu.make_async_remote_copy(
                 src_ref=w_output.at[at // stripes, stripe_of(at, 1 - core)],
-                dst_ref=mid_ref.at[slot, cut],
+                dst_ref=mid_ref.at[landed_at(at)],
                 send_sem=core_send.at[at],
                 recv_sem=core_recv.at[at],
                 device_id=sibling,
@@ -1926,11 +2306,10 @@
     output_outs = []
     for at in range(2 * stripes):
         core_copies[at].wait_recv()
-        slot, cut = landed_at(at)
         own = stripe_of(at, core)
         w_output[at // stripes, own, :] = (
             w_output[at // stripes, own, :].astype(jnp.float32)
-            + mid_ref[slot, cut, :].astype(jnp.float32)
+            + mid_ref[landed_at(at)].astype(jnp.float32)
         ).astype(jnp.bfloat16)
     for at in range(stripes):
         grp, high, low_bit = at // (stripes // 2), at // 2 % (stripes // 4), at % 2
@@ -1945,17 +2324,32 @@
                 )
             )
             output_outs[-1].start()
+    for part in parts:
+        down_meet(0, part)
+        down_over[part].wait_recv()
+
+        def block_rows(at, unused):
+            cut = pl.ds(pl.multiple_of(at * tile, tile), tile)
+            place = pl.ds(pl.multiple_of(part * row_count + at * tile, tile), tile)
+            block_ref[place, :] = (
+                mixed_ref[place, :]
+                + down_own_ref[0, part, cut, :].astype(jnp.float32)
+                + down_far_landed[part, cut, :].astype(jnp.float32)
+            ).astype(jnp.bfloat16)
+            return unused
+
+        lax.fori_loop(0, row_count // tile, block_rows, 0)
     for one in up_outs + down_outs + output_outs:
         one.wait()
     for one in back_copies:
         one.wait()
-    for one in [grad_far, out_near, out_on, down_far]:
+    for one in grad_far + out_near + out_on + down_over + [down_far]:
         one.wait_send()
-    for one in down_near + output_near + core_copies:
+    for one in list(down_near.values()) + output_near + core_copies:
         one.wait_send()
 
 
-def mlp(heads, tokens, gain, out_rows, out_across, output_parts, in_parts, down_parts):
+def mlp(heads, tokens, gain, out_rows, out_across, output_parts, in_parts, down_own):
     count, row_count, _ = heads.shape
     groups, reps = lax.axis_size("grp"), lax.axis_size("rep")
     rows, width = tokens.shape
@@ -1968,8 +2362,7 @@
     return pl.pallas_call(
         mlp_kernel,
         out_shape=(
-            jax.ShapeDtypeStruct((rows, width), full),
-            jax.ShapeDtypeStruct((2, rows, width), low),
+            jax.ShapeDtypeStruct((rows, width), low),
             jax.ShapeDtypeStruct((rows, width), full),
             jax.ShapeDtypeStruct((count, row_count, LANES), low),
             jax.ShapeDtypeStruct((half, own_width), low),
@@ -1980,28 +2373,31 @@
             jax.ShapeDtypeStruct((reps // 2, half // reps, width), low),
             jax.ShapeDtypeStruct((reps // 2, half // reps, width), low),
         ),
-        in_specs=[vmem] * 3 + [anywhere] * 11,
-        out_specs=(vmem,) * 5 + (anywhere,) * 6,
+        in_specs=[vmem] * 3 + [anywhere] * 9,
+        out_specs=(vmem,) * 4 + (anywhere,) * 6,
         scratch_shapes=[
+            pltpu.VMEM((rows, width), full),
+            pltpu.VMEM((2, 2, row_count, width), low),
+            pltpu.VMEM((2, row_count, width), low),
             pltpu.VMEM((rows, width), low),
             pltpu.VMEM((rows, width), low),
             pltpu.VMEM((groups, reps, row_count, LANES), low),
-            pltpu.VMEM((4, rows, width), low),
-            pltpu.VMEM((4, rows, width), low),
-            pltpu.VMEM((4, rows, own_width), low),
-            pltpu.VMEM((4, rows, 2 * own_width), low),
+            pltpu.VMEM((groups, 4, row_count, width), low),
+            pltpu.VMEM((groups, 4, row_count, width), low),
+            pltpu.VMEM((groups, 4, row_count, own_width), low),
+            pltpu.VMEM((groups, 4, row_count, 2 * own_width), low),
             pltpu.VMEM((2, half, width), low),
             pltpu.VMEM((2, half, 2 * own_width), low),
             pltpu.VMEM((own_width, width), low),
-            pltpu.VMEM((2, rows, width), low),
-            pltpu.VMEM((2, rows, width), low),
-            pltpu.VMEM((rows, width), low),
-            pltpu.VMEM((rows, width), low),
-            pltpu.VMEM((2, rows, width), low),
+            pltpu.VMEM((2, 2, row_count, width), low),
+            pltpu.VMEM((2, 2, row_count, width), low),
+            pltpu.VMEM((2, row_count, width), low),
+            pltpu.VMEM((2, row_count, width), low),
+            pltpu.VMEM((2, 2, row_count, width), low),
             pltpu.SemaphoreType.DMA((9,)),
             pltpu.SemaphoreType.DMA((2,)),
-            pltpu.SemaphoreType.DMA((14,)),
-            pltpu.SemaphoreType.DMA((14,)),
+            pltpu.SemaphoreType.DMA((26,)),
+            pltpu.SemaphoreType.DMA((26,)),
             others,
             others,
             others,
@@ -2019,7 +2415,7 @@
             flops=150 * 10**9, bytes_accessed=150 << 20, transcendentals=0
         ),
         name="mlp",
-    )(heads, tokens, gain, out_rows, out_across, *output_parts, *in_parts, *down_parts)
+    )(heads, tokens, gain, out_rows, out_across, *output_parts, *in_parts, down_own)
 
 
 def after_kernel(*refs):
@@ -2066,8 +2462,7 @@
         w_heads,
         gate_in,
         up_own,
-        down_first,
-        down_second,
+        down_own,
         output_part,
         out_own,
         gains,
@@ -2085,17 +2480,13 @@
     )
     gain_one = gains[:, 0].reshape(width).astype(jnp.float32)
     gain_two = gains[:, 1].reshape(width).astype(jnp.float32)
-    inputs = tokens.astype(jnp.float32)
 
     output_parts = (w_output, output_part, swap(output_part, 0, 2))
     in_parts = (gate_in, up_own, swap(up_own, 1, 0))
-    down_parts = (down_first, down_second, swap(down_first, 1, 0))
-
-    tables = attention_tables(lengths, here, there, row_count)
-    attended, out_heads, log_sum, query, key, value = attend(tables, qkv)
+
+    attended, out_heads, log_sum, query, key, value = attend(lengths, qkv)
     (
-        mixed,
-        down_sums,
+        block_out,
         grad_mixed,
         grad_heads,
         gate_part,
@@ -2113,90 +2504,43 @@
         swap(out_own, 0, 4),
         output_parts,
         in_parts,
-        down_parts,
+        down_own,
     )
 
     own_rows = width // (groups * reps)
-    high = reps // 8
-    high_steps = [step for step in (8 << place for place in range(8)) if step < reps]
-    bit = {step: (there // step) % 2 for step in [1, 2, 4] + high_steps}
-
-    def send(parts, axis, step):
-        flag, grp_step, rep_step = (here, 1, 0) if step == 0 else (bit[step], 0, step)
-        return pick(parts, flag, axis), swap(pick(parts, 1 - flag, axis), grp_step, rep_step)
-
-    def add(kept, arrived):
-        return narrow(kept.astype(jnp.float32) + arrived.astype(jnp.float32))
-
-    def over(parts, axis, step):
-        return add(*send(parts, axis, step))
-
-    def over_high(parts, axis):
-        for step in high_steps:
-            shape = parts.shape
-            count = shape[axis] // 2
-            parts = parts.reshape(shape[:axis] + (count, 2) + shape[axis + 1 :])
-            parts = over(parts, axis + 1, step)
-        return parts.reshape(parts.shape[:axis] + parts.shape[axis + 1 :])
-
-    by_owner = (groups, high, 2, 2, 2, own_rows)
-    up_sent = swap(up_sent, 1, 0)
-    down_sent = swap(down_sent, 0, 2)
-    output_sent = swap(output_sent, 0, 4)
-    sums_sent = swap(down_sums[1], 0, 4)
-
-    back = attend_back(tables, query, key, value, out_heads, log_sum, grad_heads)
-
-    up_sent, down_sent, output_sent, sums_sent = after(
-        (up_sent, down_sent, output_sent, sums_sent), back
-    )
-    up_part = add(up_kept, up_sent).reshape(by_owner[1:] + (own_width,))
-    down_part = add(down_kept, down_sent).reshape(groups, high, LANES, width)
-    output_grad = add(output_kept, output_sent).reshape(groups, high, 2, own_rows, width)
-    early = (up_part, down_part, output_grad)
-    gate_kept, gate_sent = send(gate_part.reshape(by_owner[1:] + (own_width,)), 2, 2)
-    up_kept, up_sent = send(up_part, 0, 8)
-    down_kept, down_sent = send(down_part, 0, 0)
-    output_kept, output_sent = send(output_grad, 0, 0)
-    grad_in, heads_grad = scatter_heads(
-        back.reshape(reps, groups * row_count, 3 * LANES), w_heads, gathered_rows, early
-    )
-    gate_sent, up_sent, down_sent, output_sent = after(
-        (gate_sent, up_sent, down_sent, output_sent), grad_in
-    )
-    gate_part = over_high(add(gate_kept, gate_sent), 0)
-    up_part = over(add(up_kept, up_sent), 1, 2)
-    down_grad = over_high(add(down_kept, down_sent), 0).astype(jnp.float32)
-    output_grad = over_high(over(add(output_kept, output_sent), 1, 2), 0).astype(jnp.float32)
-    block_out = (
-        mixed + down_sums[0].astype(jnp.float32) + sums_sent.astype(jnp.float32)
-    ).astype(jnp.bfloat16)
-
-    quad_part = jnp.concatenate([gate_part, up_part], axis=-1)
-    kept = pick(quad_part, bit[4], 0)
-    crossed = swap(pick(quad_part, 1 - bit[4], 0), 0, 4)
-    columns = []
-    for part in (kept, crossed):
-        columns.append(pick(part, bit[1], 0))
-        columns.append(swap(pick(part, 1 - bit[1], 0), 0, 1))
-
-    def by_bit(flag, own, other):
-        return jnp.where(
-            flag == 0, jnp.stack([own, other], axis=1), jnp.stack([other, own], axis=1)
-        )
-
-    pieces = by_bit(
-        bit[4], by_bit(bit[1], columns[0], columns[1]), by_bit(bit[1], columns[2], columns[3])
-    )
-    pieces = pieces.reshape(own_rows, 2, 2, 2, groups, high, 2, LANES)
-    pieces = pieces.transpose(3, 0, 4, 5, 1, 6, 2, 7).reshape(2, own_rows, hidden_width)
+    by_owner = (2, 2, 2, 2, own_rows, own_width)
+    gate_part = gate_part.reshape(by_owner)
+    high_bit = there // 8 % 2
+    gate_kept = pick(gate_part, high_bit, 0)
+    sums = (
+        swap(pick(gate_part, 1 - high_bit, 0), 0, 8),
+        swap(up_sent, 1, 0),
+        swap(down_sent, 0, 2),
+        swap(output_sent, 0, 4),
+    )
+    back = attend_back(lengths, query, key, value, out_heads, log_sum, grad_heads)
+    gate_met, up_met, down_met, output_met = after(sums, back)
+    token_grad, heads_grad, quad_grad, down_grad, output_grad = scatter_heads(
+        back.reshape(reps, groups * row_count, 3 * LANES),
+        w_heads,
+        tokens.reshape(rows, width),
+        grad_mixed,
+        jnp.broadcast_to(gain_one[None], (8, width)),
+        gathered_rows,
+        (
+            gate_kept,
+            gate_met,
+            up_kept.reshape(by_owner),
+            up_met.reshape(by_owner),
+            down_kept.reshape(2, 2, 2, own_rows, width),
+            down_met.reshape(2, 2, 2, own_rows, width),
+            output_kept.reshape(2, 2, 2, own_rows, width),
+            output_met.reshape(2, 2, 2, own_rows, width),
+        ),
+    )
+    pieces = quad_grad.reshape(2, 2, 2, own_rows, groups, 2, 2, LANES)
+    pieces = pieces.transpose(2, 3, 4, 5, 0, 6, 1, 7).reshape(2, own_rows, hidden_width)
     gate_grad, up_grad = pieces[0].astype(jnp.float32), pieces[1].astype(jnp.float32)
-
-    grad_norm_in, unused_gain = norm_backward(
-        inputs.reshape(rows, width), gain_one, grad_in.reshape(rows, width)
-    )
-    token_grad = (grad_mixed + grad_norm_in).astype(jnp.bfloat16)
-
     heads_grad = (
         heads_grad.reshape(reps, own_rows, 3, LANES)
         .transpose(2, 1, 0, 3)
@@ -2229,7 +2573,7 @@
         mlp_gain_grad,
         gate_grad,
         up_grad,
-        down_grad,
+        down_grad.reshape(2 * own_rows, width),
     )
 
 

time: 664 us -> 598 us (0.901)
  waiting for transfers between devices: 71 us -> 23.2 us
  other arithmetic: 36.1 us -> 12 us
  Pallas kernels: 506 us -> 521 us
  starting transfers between devices: 21.7 us -> 9.23 us
    ppermute x20 -> x7, waiting for transfers between devices: 71 us -> 23.2 us  [swap(): return lax.ppermute(value, BOTH, pairs)]
    pallas_call x1, Pallas kernels: 134 us -> 163 us  [scatter_heads(): pl.pallas_call(scatter_kernel, out_shape=(jax.ShapeDtypeStruct((rows, wid...]
    convert_element_type x15 -> x0, other arithmetic: 18.8 us -> none  [the longest x9 13.7 us: narrow(): return value.astype(jnp.bfloat16)]
    ppermute x20 -> x7, starting transfers between devices: 21.7 us -> 9.23 us  [swap(): return lax.ppermute(value, BOTH, pairs)]
    pallas_call x1, Pallas kernels: 49.2 us -> 36.7 us  [attend(): pl.pallas_call(attend_kernel, out_shape=(jax.ShapeDtypeStruct((parts, uni...]
  transfers between devices with their start and end apart: 20 -> 7, of which waited for: 6 -> 2; matrix products, arithmetic and copies ran while one was open for 6% -> 0% of each run, Pallas kernels for 36% -> 15%
where the time goes in v6:
time: 598 us; the launch traced here: 589 us
  Pallas kernels  521 us (87%)
  waiting for transfers between devices  23.2 us (4%)
  local copies, waits for them, and re-layouts  21.8 us (4%)
  other arithmetic  12 us (2%)
  starting transfers between devices  9.23 us (2%)
    pallas_call x1, Pallas kernels, scatter_heads(): pl.pallas_call(scatter_kernel, out_shape=(jax.ShapeDtypeStruct((rows, wid...  163 us
    pallas_call x1, Pallas kernels, mlp(): pl.pallas_call(mlp_kernel, out_shape=(jax.ShapeDtypeStruct((rows, width),...  160 us
    pallas_call x1, Pallas kernels, gather_heads(): pl.pallas_call(gather_kernel, out_shape=(jax.ShapeDtypeStruct((reps, 2 *...  110 us
    pallas_call x1, Pallas kernels, attend_back(): pl.pallas_call(attend_back_kernel, out_shape=jax.ShapeDtypeStruct((parts,...  51.1 us
    pallas_call x1, Pallas kernels, attend(): pl.pallas_call(attend_kernel, out_shape=(jax.ShapeDtypeStruct((parts, uni...  36.7 us
    ppermute x7, waiting for transfers between devices, swap(): return lax.ppermute(value, BOTH, pairs)  23.2 us
  transfers between devices with their start and end apart: 7, of which 2 were waited for; matrix products, arithmetic and copies ran while one was open for 0% of the time, Pallas kernels for 15%

profile of v6, /device:TPU:0, one launch (start us, length us, event | category | flops | bytes accessed | tf_op | source)
XLA Modules:
  0.0 588.7 jit_solution(916007418925799520)
XLA Ops:
  0.6 0.7 broadcast_in_dim.22
  1.3 0.7 broadcast_in_dim.10
  2.0 0.1 pad.2.clone
  2.1 0.7 maximum_maximum_fusion.gain_ref
  2.8 109.8 %gather_heads.1 = (bf16[16,256,2048]{2,1,0:T(8,128)(2,1)}, bf16[32,128,384]{2,1,0:T(8,128)(2,1)}, bf16[2,1024,384]{2,1,0:T(8,128)(2,1)}, bf16[2,1024,1024]{2,1,0...) custom-call(bf16[2,128,2048]{2,1,0:T(8,128)(2,1)} %tokens_ref.1, ...), custom_call_target="tpu_custom_call" | custom-call | flops 8000000000 | bytes 262144000 | tf_op jit(solution)/shard_map/gather_heads/pallas_call | solution.py:1235
  112.6 1.6 collective-permute-start
  114.2 1.5 collective-permute-start.1
  115.7 0.5 collective-permute-start.2
  116.3 36.7 %attend.1 = (bf16[32,128,128]{2,1,0:T(8,128)(2,1)}, f32[16,128,256]{2,1,0:T(8,128)}, f32[16,8,256]{2,1,0:T(8,128)}, bf16[16,256,128]{2,1,0:T(8,128)(2,1)}, bf16[...) custom-call(s32[2,4]{1,0:T(2,128)} %lengths_ref.3, bf16[32,128,384]{2,1,0:T(8,128)(2,1)} %get-tuple-element.45.qkv_ref), custom_call_target="tpu_custom_call" | custom-call | flops 20000000000 | bytes 16777216 | tf_op jit(solution)/shard_map/attend/pallas_call | solution.py:862
  153.0 1.4 slice_convert_fusion.2
  154.4 0.0 collective-permute-done.out_across
  154.4 0.0 collective-permute-done.1.output_beside
  154.4 7.4 %collective-permute-done.2.up_other = bf16[1024,1024]{1,0:T(8,128)(2,1)S(1)} collective-permute-done((bf16[1024,1024]{1,0:T(8,128)(2,1)}, bf16[1024,1024]{1,0:T(8,128)(2,1)S(1)}, u32[]{:S(2)}, u32[]{:S(2)}) %collective-permute-start.2) | collective-permute-done | bytes 2097184 | tf_op jit(solution)/shard_map/ppermute | solution.py:927
  161.9 0.7 broadcast_in_dim.24.gain_ref
  162.5 0.7 copy-done.10
  163.3 160.5 %mlp.1 = (bf16[256,2048]{1,0:T(8,128)(2,1)}, f32[256,2048]{1,0:T(8,128)}, bf16[32,128,128]{2,1,0:T(8,128)(2,1)}, bf16[1024,1024]{1,0:T(8,128)(2,1)}, bf16[1024,1...) custom-call(bf16[32,128,128]{2,1,0:T(8,128)(2,1)} %get-tuple-element, ...), custom_call_target="tpu_custom_call" | custom-call | flops 149999992832 | bytes 157286400 | tf_op jit(solution)/shard_map/mlp/pallas_call | solution.py:2362
  323.8 2.9 dynamic-slice_bitcast_fusion
  326.7 0.6 collective-permute-start.3
  327.2 1.3 collective-permute-start.4
  328.5 1.5 collective-permute-start.5
  330.0 2.2 collective-permute-start.6
  332.2 51.1 %attend_back.1.refs_4_ = bf16[32,128,384]{2,1,0:T(8,128)(2,1)} custom-call(s32[2,4]{1,0:T(2,128)} %lengths_ref.3, bf16[16,256,128]{2,1,0:T(8,128)(2,1)} %get-tuple-element.54.query_ref, bf16[16,256,128]{2,1,0:T(8,128)(2,1)} %get-tuple-element.55.key_ref, bf16[16,256,128]{2,1,0:T(8,128)(2,1)} %get-tuple-element.56.value_ref, ...), custom_call_target="tpu_custom_call" | custom-call | flops 49999998976 | bytes 16777216 | tf_op jit(solution)/shard_map/attend_back/pallas_call | solution.py:899
  383.4 15.7 %collective-permute-done.6.refs_3_ = bf16[8,64,2048]{2,1,0:T(8,128)(2,1)} collective-permute-done((bf16[8,64,2048]{2,1,0:T(8,128)(2,1)S(1)}, bf16[8,64,2048]{2,1,0:T(8,128)(2,1)}, u32[]{:S(2)}, u32[]{:S(2)}) %collective-permute-start.6) | collective-permute-done | bytes 2097184 | tf_op jit(solution)/shard_map/ppermute | solution.py:927
  399.1 0.6 broadcast_in_dim.25.gain_ref
  399.8 163.2 %scatter_heads.1 = (bf16[256,2048]{1,0:T(8,128)(2,1)}, bf16[16,64,384]{2,1,0:T(8,128)(2,1)}, bf16[2,2,2,64,1024]{4,3,2,1,0:T(8,128)(2,1)}, f32[2,64,2048]{2,1,0:T(8,128)}, f32[64,2048]{1,0:T(8,128)}) custom-call(bf16[16,256,384]{2,1,0:T(8,128)(2,1)} %bitcast.42, bf16[2,1024,384]{2,1,0:T(8,128)(2,1)} %get-tuple-element.60.weight_ref, ...), custom_call_target="tpu_custom_call" | custom-call | flops 14000000000 | bytes 262144000 | tf_op jit(solution)/shard_map/scatter_heads/pallas_call | solution.py:1716
  563.0 2.4 reshape.117
  565.4 1.6 fusion
  567.0 1.1 copy.45
  568.1 1.1 copy.44
  569.2 1.1 copy.43
  570.3 0.7 reshape.111
  571.0 0.3 copy.59
  571.3 0.2 slice_convert_fusion
  571.5 0.8 copy.48
  572.3 0.8 reshape.116
  573.2 0.0 copy-start
  573.2 0.8 copy.47
  574.0 0.8 reshape.115
  574.8 0.0 copy-start.1
  574.8 2.6 multiply_reduce_fusion.4
  577.4 2.9 multiply_reduce_fusion.2
  580.4 1.7 multiply_reduce_fusion
  582.0 1.3 convert_divide_fusion
  583.3 1.3 convert_divide_fusion.1
  584.6 1.0 copy.68
  585.5 1.0 copy.69
  586.5 0.8 copy.70
  587.3 1.0 copy.71
  (28 shorter events, 0.1 us)
Async XLA Ops:
  112.6 41.9 %collective-permute-start = (bf16[256,2048]{1,0:T(8,128)(2,1)}, bf16[256,2048]{1,0:T(8,128)(2,1)S(1)}, u32[]{:S(2)}, u32[]{:S(2)}) collective-permute-start(bf16[256,2048]{1,0:T(8,128)(2,1)} %get-tuple-element.48), channel_id=1, source_target_pairs={{0,4},{1,5},{2,6},{3,7},{4,0},{5,1},{6,2},{7,3},{8,12},{9,13},{10,... | collective-permute-start | bytes 3145736 | tf_op jit(solution)/shard_map/ppermute | solution.py:927
  114.2 40.2 %collective-permute-start.1 = (bf16[256,2048]{1,0:T(8,128)(2,1)}, bf16[256,2048]{1,0:T(8,128)(2,1)}, u32[]{:S(2)}, u32[]{:S(2)}) collective-permute-start(bf16[256,2048]{1,0:T(8,128)(2,1)} %get-tuple-element.49.output_part), channel_id=1, source_target_pairs={{0,2},{1,3},{2,0},{3,1},{4,6},{5,7},{6,4},{7,5},{8,10},{9,11},{10,... | collective-permute-start | bytes 3145736 | tf_op jit(solution)/shard_map/ppermute | solution.py:927
  115.7 46.1 %collective-permute-start.2 = (bf16[1024,1024]{1,0:T(8,128)(2,1)}, bf16[1024,1024]{1,0:T(8,128)(2,1)S(1)}, u32[]{:S(2)}, u32[]{:S(2)}) collective-permute-start(bf16[1024,1024]{1,0:T(8,128)(2,1)} %get-tuple-element.51.up_own), channel_id=1, source_target_pairs={{0,16},{1,17},{2,18},{3,19},{4,20},{5,21},{6,22},{7,23},{8,24},{9,... | collective-permute-start | bytes 6291464 | tf_op jit(solution)/shard_map/ppermute | solution.py:927
  154.4 8.9 %copy-start.12 = (bf16[256,2048]{1,0:T(8,128)(2,1)}, bf16[256,2048]{1,0:T(8,128)(2,1)S(1)}, u32[]{:S(2)}) copy-start(bf16[256,2048]{1,0:T(8,128)(2,1)S(1)} %collective-permute-done.out_across) | copy-start | bytes 3145732
  161.9 1.4 copy-start.10
  323.8 6.2 %copy-start.11 = (bf16[8,64,2048]{2,1,0:T(8,128)(2,1)S(1)}, bf16[8,64,2048]{2,1,0:T(8,128)(2,1)}, u32[]{:S(2)}) copy-start(bf16[8,64,2048]{2,1,0:T(8,128)(2,1)} %get-tuple-element.66) | copy-start | bytes 6291460
  326.7 56.7 %collective-permute-start.3 = (bf16[2,2,2,64,1024]{4,3,2,1,0:T(8,128)(2,1)S(1)}, bf16[2,2,2,64,1024]{4,3,2,1,0:T(8,128)(2,1)S(1)}, u32[]{:S(2)}, u32[]{:S(2)}) collective-permute-start(bf16[2,2,2,64,1024]{4,3,2,1,0:T(8,128)(2,1)S(1)} %get-tuple-element.88), channel_id=1, source_target_pairs={{0,8},{1,9},{2,10},{3,11},{4,12},{5,13},{6,14},{7,15},{8,0},{9,1},... | collective-permute-start | bytes 3145736 | tf_op jit(solution)/shard_map/ppermute | solution.py:927
  327.2 56.1 %collective-permute-start.4 = (bf16[1024,1024]{1,0:T(8,128)(2,1)}, bf16[1024,1024]{1,0:T(8,128)(2,1)S(1)}, u32[]{:S(2)}, u32[]{:S(2)}) collective-permute-start(bf16[1024,1024]{1,0:T(8,128)(2,1)} %get-tuple-element.64), channel_id=1, source_target_pairs={{0,16},{1,17},{2,18},{3,19},{4,20},{5,21},{6,22},{7,23},{8,24},{9,... | collective-permute-start | bytes 6291464 | tf_op jit(solution)/shard_map/ppermute | solution.py:927
  328.5 54.9 %collective-permute-start.5 = (bf16[4,128,2048]{2,1,0:T(8,128)(2,1)}, bf16[4,128,2048]{2,1,0:T(8,128)(2,1)}, u32[]{:S(2)}, u32[]{:S(2)}) collective-permute-start(bf16[4,128,2048]{2,1,0:T(8,128)(2,1)} %get-tuple-element.65), channel_id=1, source_target_pairs={{0,2},{1,3},{2,0},{3,1},{4,6},{5,7},{6,4},{7,5},{8,10},{9,11},{10,... | collective-permute-start | bytes 6291464 | tf_op jit(solution)/shard_map/ppermute | solution.py:927
  330.0 69.1 %collective-permute-start.6 = (bf16[8,64,2048]{2,1,0:T(8,128)(2,1)S(1)}, bf16[8,64,2048]{2,1,0:T(8,128)(2,1)}, u32[]{:S(2)}, u32[]{:S(2)}) collective-permute-start(bf16[8,64,2048]{2,1,0:T(8,128)(2,1)S(1)} %copy-done.11), channel_id=1, source_target_pairs={{0,4},{1,5},{2,6},{3,7},{4,0},{5,1},{6,2},{7,3},{8,12},{9,13},{10,... | collective-permute-start | bytes 6291464 | tf_op jit(solution)/shard_map/ppermute | solution.py:927
  383.3 15.8 %copy-start.9 = (f32[2,1,1024]{2,1,0:T(1,128)S(1)}, f32[2,1,1024]{2,1,0:T(1,128)}, u32[]{:S(2)}) copy-start(f32[2,1,1024]{2,1,0:T(1,128)} %get-tuple-element.92) | copy-start | bytes 24580
  383.3 15.8 %copy-start.3 = (bf16[2,2,2,64,1024]{4,3,2,1,0:T(8,128)(2,1)}, bf16[2,2,2,64,1024]{4,3,2,1,0:T(8,128)(2,1)S(1)}, u32[]{:S(2)}) copy-start(bf16[2,2,2,64,1024]{4,3,2,1,0:T(8,128)(2,1)S(1)} %collective-permute-done.3.refs_0_) | copy-start | bytes 3145732
  383.4 15.8 %copy-start.2 = (bf16[1024,1024]{1,0:T(8,128)(2,1)}, bf16[1024,1024]{1,0:T(8,128)(2,1)S(1)}, u32[]{:S(2)}) copy-start(bf16[1024,1024]{1,0:T(8,128)(2,1)S(1)} %collective-permute-done.4.refs_1_) | copy-start | bytes 6291460
  567.0 3.3 copy-start.7
  573.2 7.2 %copy-start = (f32[64,4096]{1,0:T(8,128)}, f32[64,4096]{1,0:T(8,128)S(1)}, u32[]{:S(2)}) copy-start(f32[64,4096]{1,0:T(8,128)S(1)} %reshape.116) | copy-start | bytes 3145732
  574.8 7.2 %copy-start.1 = (f32[64,4096]{1,0:T(8,128)}, f32[64,4096]{1,0:T(8,128)S(1)}, u32[]{:S(2)}) copy-start(f32[64,4096]{1,0:T(8,128)S(1)} %reshape.115) | copy-start | bytes 3145732
  580.3 4.2 copy-start.4
  580.3 5.2 copy-start.6
  584.6 1.9 copy-start.8
  584.6 2.7 copy-start.5

commit v7 on v6

--- a/solution.py
+++ b/solution.py
@@ -961,37 +961,20 @@
     return offset & -offset
 
 
-def arrivals(reps):
-    far = [step for step in range(4, reps, 4)]
-    far.sort(key=lambda step: (bin(step).count("1"), step))
-    order = [(2, 0), (0, 1)]
-    for at, step in enumerate(far):
-        if bin(step).count("1") == 1:
-            order.append((step, 0))
-    order.append((2, 1))
-    for step in far:
-        if bin(step).count("1") == 1:
-            order.append((step, 1))
-    single = [step for step in far if bin(step).count("1") == 1]
-    double = [step for step in far if bin(step).count("1") > 1]
-    rest = []
-    for step in single[:1]:
-        rest.append((step + 2, 0))
-    for step in double:
-        rest.append((step, 0))
-    for step in single[:1]:
-        rest.append((step + 2, 1))
-    for step in double:
-        rest.append((step, 1))
-    for step in single[1:] + double:
-        rest += [(step + 2, 0), (step + 2, 1)]
-    return order + rest
-
-
-def link_of(offset, part, reps, turned=1):
-    if offset == reps - 2 and part == turned:
-        return 4
-    return lowest(offset)
+def link_of(offset, part, turned):
+    return turned.get((offset, part), lowest(offset))
+
+
+GATHER_LINKS = {(14, 0): 4}
+GATHER_PLAN = (
+    ("rows", 4, 0), ("rows", 0, 1), ("rows", 4, 1), ("rows", 8, 0), ("rows", 8, 1),
+    ("rows", 6, 0), ("rows", 2, 0), ("rows", 6, 1), ("project", 5), ("project", 0),
+    ("project", 9), ("project", 4), ("rows", 10, 0), ("project", 6), ("project", 8),
+    ("project", 1), ("rows", 12, 1), ("rows", 2, 1), ("project", 2), ("project", 7),
+    ("rows", 12, 0), ("rows", 10, 1), ("project", 10), ("project", 3), ("project", 12),
+    ("rows", 14, 0), ("project", 13), ("rows", 14, 1), ("project", 14), ("project", 11),
+    ("project", 15),
+)
 
 
 def gather_kernel(
@@ -1008,9 +991,12 @@
     normed_out,
     qkv_ref,
     weight_ref,
-    gate_ref,
+    gate_own,
+    gate_met,
     up_ref,
-    down_ref,
+    up_piece,
+    down_first,
+    down_second,
     output_ref,
     out_away,
     gains,
@@ -1072,7 +1058,7 @@
                 device_id=across,
                 device_id_type=MESH_IDS,
             )
-        step = link_of(offset, part, reps)
+        step = link_of(offset, part, GATHER_LINKS)
         return pltpu.make_async_remote_copy(
             src_ref=raw.at[offset - step, part],
             dst_ref=raw.at[offset, part],
@@ -1082,7 +1068,7 @@
             device_id_type=MESH_IDS,
         )
 
-    order = arrivals(reps)
+    order = [tuple(what) for kind, *what in GATHER_PLAN if kind == "rows"]
     copies = {
         (offset, part): rows_copy(offset, part)
         for offset in range(reps)
@@ -1092,7 +1078,7 @@
 
     def pass_on(offset, part):
         for later, part_of in order:
-            if later and part_of == part and later - link_of(later, part, reps) == offset:
+            if later and part_of == part and later - link_of(later, part, GATHER_LINKS) == offset:
                 copies[later, part].start()
         copies[offset + 1, part].start()
 
@@ -1123,14 +1109,23 @@
         first = (grp * reps + 8 * high + 2 * low + place) * LANES
         return weight.at[:, pl.ds(pl.multiple_of(first, LANES), LANES)]
 
-    for weight, target_ref in ((w_gate, gate_ref.at[here]), (w_up, up_ref)):
+    for weight, target_ref in ((w_gate, gate_own), (w_up, up_ref)):
         for at, stripe in enumerate(stripes):
             load(columns_of(weight, *stripe), target_ref.at[:, pl.ds(at * LANES, LANES)])
     for at, (grp, high, low) in enumerate(stripes[: len(stripes) // 2]):
         first = (8 * high + 2 * low + place) * LANES
         load(
             w_down.at[pl.ds(pl.multiple_of(first, LANES), LANES)],
-            down_ref.at[pl.ds(at * LANES, LANES)],
+            (down_first, down_second)[at // 2].at[pl.ds(at % 2 * LANES, LANES)],
+        )
+    piece_rows = up_piece.shape[0]
+    low = (there // 2) % 2
+    for at, stripe in enumerate(stripes):
+        load(
+            columns_of(w_up, *stripe).at[
+                pl.ds(pl.multiple_of(low * piece_rows, piece_rows), piece_rows)
+            ],
+            up_piece.at[:, pl.ds(at * LANES, LANES)],
         )
     load(out_rows, out_away)
     for one in stripe_loads:
@@ -1142,7 +1137,9 @@
         output_ref,
     )
     output_copy.start()
-    gate_copy = side(3, gate_ref.at[here], gate_ref.at[here])
+    gate_copy = side(
+        3, gate_own.at[pl.ds(pl.multiple_of(low * piece_rows, piece_rows), piece_rows)], gate_met
+    )
     for one in stripe_loads[: len(stripes)]:
         one.wait()
     gate_copy.start()
@@ -1181,33 +1178,20 @@
             2, row_count, 3 * LANES
         )
 
-    ready = []
-    arrived = {(0, 0)}
-    started = False
     count = 0
-    for offset, part in order:
-        copies[offset, part].wait_recv()
-        pass_on(offset, part)
-        arrived.add((offset, part))
-        if (offset, 1 - part) in arrived:
-            ready.append(offset)
-        if not started and len(ready) >= 1:
+    for kind, *what in GATHER_PLAN:
+        if kind == "rows":
+            copies[tuple(what)].wait_recv()
+            pass_on(*what)
+            continue
+        if count == 0:
             gain_copy.wait_recv()
             weight_copy.wait_recv()
-            started = True
-        if started and len(ready) >= 2:
-            base = ready.pop(0)
-            project(count, base)
-            copies[base + 1, 0].wait_recv()
-            copies[base + 1, 1].wait_recv()
-            project(count + 1, base + 1)
-            count += 2
-    for base in ready:
-        project(count, base)
-        copies[base + 1, 0].wait_recv()
-        copies[base + 1, 1].wait_recv()
-        project(count + 1, base + 1)
-        count += 2
+        if what[0] % 2:
+            for part in (0, 1):
+                copies[what[0], part].wait_recv()
+        project(count, what[0])
+        count += 1
     for offset in used:
         written[offset].wait()
     for one in copies.values():
@@ -1238,15 +1222,18 @@
             jax.ShapeDtypeStruct((reps, 2 * row_count, width), jnp.bfloat16),
             jax.ShapeDtypeStruct((2 * reps, row_count, 3 * LANES), jnp.bfloat16),
             jax.ShapeDtypeStruct((2, half, 3 * LANES), jnp.bfloat16),
-            jax.ShapeDtypeStruct((2, half, own_width), jnp.bfloat16),
             jax.ShapeDtypeStruct((half, own_width), jnp.bfloat16),
-            jax.ShapeDtypeStruct((own_width // 2, width), jnp.bfloat16),
+            jax.ShapeDtypeStruct((half // 2, own_width), jnp.bfloat16),
+            jax.ShapeDtypeStruct((half, own_width), jnp.bfloat16),
+            jax.ShapeDtypeStruct((half // 2, own_width), jnp.bfloat16),
+            jax.ShapeDtypeStruct((own_width // 4, width), jnp.bfloat16),
+            jax.ShapeDtypeStruct((own_width // 4, width), jnp.bfloat16),
             jax.ShapeDtypeStruct((half // 4, width), jnp.bfloat16),
             jax.ShapeDtypeStruct(out_rows.shape, jnp.bfloat16),
             jax.ShapeDtypeStruct((2, 16, half), jnp.bfloat16),
         ),
         in_specs=[vmem, vmem] + [anywhere] * 8,
-        out_specs=(anywhere,) + (vmem,) * 8,
+        out_specs=(anywhere,) + (vmem,) * 11,
         scratch_shapes=[
             pltpu.VMEM((reps, 2, row_count, width), jnp.bfloat16),
             pltpu.VMEM((4, 2 * row_count, width), jnp.bfloat16),
@@ -1256,7 +1243,7 @@
             pltpu.SemaphoreType.DMA((2 * reps,)),
             pltpu.SemaphoreType.DMA((4,)),
             pltpu.SemaphoreType.DMA((4,)),
-            pltpu.SemaphoreType.DMA((reps // 2 * 5 // 2 + 1,)),
+            pltpu.SemaphoreType.DMA((reps // 2 * 7 // 2 + 1,)),
         ],
         compiler_params=pltpu.CompilerParams(
             vmem_limit_bytes=KERNEL_VMEM, collective_id=0, has_side_effects=True
@@ -1269,18 +1256,20 @@
 
 
 SCATTER_PLAN = (
-    ("first", "up"), ("rows", 13, 0), ("rows", 15, 0), ("weights", 1), ("rows", 1, 0),
-    ("rows", 15, 1), ("weights", 2), ("rows", 5, 0), ("first", "down"), ("rows", 14, 0),
-    ("first", "gate"), ("rows", 12, 0), ("rows", 13, 1), ("weights", 1), ("rows", 14, 1),
-    ("rows", 9, 1), ("weights", 1), ("sum", "up"), ("weights", 1), ("rows", 11, 0),
-    ("rows", 11, 1), ("rows", 1, 1), ("rows", 10, 0), ("rows", 7, 0), ("first", "out"),
-    ("weights", 1), ("sum", "down"), ("weights", 4), ("rows", 3, 1), ("rows", 10, 1),
-    ("weights", 1), ("sum", "gate"), ("rows", 7, 1), ("rows", 3, 0), ("rows", 9, 0),
-    ("rows", 2, 1), ("rows", 12, 1), ("weights", 3), ("sum", "quad"), ("weights", 1),
-    ("weights over",), ("rows", 6, 1), ("rows", 8, 0), ("rows", 8, 1), ("rows", 5, 1),
-    ("sum", "out"), ("rows", 4, 1), ("sum", "out next"), ("rows", 6, 0), ("weights out",),
-    ("rows", 2, 0), ("rows", 0, 1), ("rows", 4, 0), ("rows", 0, 0), ("sum", "quad next"),
+    ("first", "down"), ("first", "up"), ("rows", 5, 0), ("rows", 4, 0), ("rows", 15, 0),
+    ("rows", 15, 1), ("weights", 1), ("first", "gate"), ("rows", 14, 1), ("weights", 1),
+    ("rows", 7, 0), ("first", "out"), ("sum", "down"), ("rows", 3, 1), ("rows", 13, 1),
+    ("rows", 11, 0), ("rows", 6, 0), ("rows", 11, 1), ("rows", 5, 1), ("rows", 10, 1),
+    ("sum", "up"), ("weights", 2), ("rows", 9, 1), ("rows", 1, 1), ("weights", 1),
+    ("rows", 14, 0), ("weights", 1), ("rows", 12, 1), ("weights", 1), ("sum", "gate"),
+    ("weights", 2), ("rows", 10, 0), ("weights", 1), ("rows", 7, 1), ("sum", "out"),
+    ("rows", 13, 0), ("rows", 6, 1), ("weights", 1), ("rows", 3, 0), ("rows", 12, 0),
+    ("rows", 1, 0), ("rows", 9, 0), ("weights", 3), ("rows", 8, 1), ("sum", "quad"),
+    ("rows", 2, 1), ("rows", 2, 0), ("weights", 2), ("sum", "out next"), ("rows", 8, 0),
+    ("weights over",), ("rows", 4, 1), ("sum", "quad next"), ("weights out",), ("rows", 0, 1),
+    ("rows", 0, 0),
 )
+SCATTER_LINKS = {(6, 0): 4}
 
 
 def scatter_kernel(
@@ -1325,9 +1314,11 @@
     output_landed,
     output_next,
     output_last,
-    narrow_stage,
+    gate_stage,
+    up_stage,
     wide_stage,
-    crossed,
+    gate_crossed,
+    up_crossed,
     normed_sem,
     send_sem,
     recv_sem,
@@ -1377,16 +1368,16 @@
         return copy
 
     def open_half(at, kept, met, axis, flag, stage, target_ref):
-        return (
-            load(2 * at, part_of(kept, axis, flag), stage),
-            load(2 * at + 1, part_of(met, axis, flag), target_ref),
-        )
+        loads = [load(2 * at + 1, part_of(met, axis, flag), target_ref)]
+        if stage is not None:
+            loads.append(load(2 * at, part_of(kept, axis, flag), stage))
+        return loads
 
     firsts = [
-        open_half(0, down_kept, down_met, 0, 1 - here, wide_stage.at[0], down_away),
-        open_half(1, output_kept, output_met, 0, 1 - here, wide_stage.at[1], output_away),
-        open_half(2, gate_kept, gate_met, 1, 1 - bit[2], narrow_stage.at[1, 0], gate_away),
-        open_half(3, up_kept, up_met, 2, 1 - bit[2], narrow_stage.at[0], up_away),
+        open_half(0, down_kept, down_met, 1, 1 - bit[2], wide_stage, down_away),
+        open_half(1, output_kept, output_met, 0, 1 - here, None, output_away),
+        open_half(2, gate_kept, gate_met, 1, 1 - bit[2], gate_stage.at[0], gate_away),
+        open_half(3, up_kept, up_met, 0, 1 - here, up_stage, up_away),
     ]
 
     for at in range(2):
@@ -1425,36 +1416,41 @@
             device_id_type=MESH_IDS,
         )
 
-    down_cross = sum_copy(0, down_away, down_landed, across)
+    down_cross = sum_copy(0, down_away, down_landed, other(2))
     output_cross = sum_copy(1, output_away, output_landed, across)
     gate_low = sum_copy(2, gate_away, gate_landed, other(2))
-    up_low = sum_copy(3, up_away, up_landed, other(2))
+    up_low = sum_copy(3, up_away, up_landed, across)
     down_high = sum_copy(4, down_landed.at[1 - bit[8]], down_last, other(8))
     up_high = sum_copy(5, up_landed.at[1 - bit[8]], up_last, other(8))
     output_low = sum_copy(6, output_landed.at[:, 1 - bit[2]], output_next, other(2))
     output_high = sum_copy(7, output_next.at[1 - bit[8]], output_last, other(8))
     quad_far = [
-        sum_copy(8, gate_landed.at[1 - bit[4]], crossed.at[0], other(4)),
-        sum_copy(9, up_last.at[1 - bit[4]], crossed.at[1], other(4)),
+        sum_copy(8, gate_landed.at[1 - bit[4]], gate_crossed, other(4)),
+        sum_copy(9, up_last.at[1 - bit[4]], up_crossed, other(4)),
     ]
+    early_width = gate_crossed.shape[2]
+    early = pl.ds(0, early_width)
+    late = pl.ds(early_width, quad_ref.shape[3] - early_width)
+    beside = 1 - bit[1]
     quad_near = [
-        sum_copy(10, gate_landed.at[bit[4], 1 - bit[1]], quad_ref.at[bit[4], bit[1], 0], other(1)),
-        sum_copy(11, up_last.at[bit[4], 1 - bit[1]], quad_ref.at[bit[4], bit[1], 1], other(1)),
-        sum_copy(12, crossed.at[0, 1 - bit[1]], quad_ref.at[1 - bit[4], bit[1], 0], other(1)),
-        sum_copy(13, crossed.at[1, 1 - bit[1]], quad_ref.at[1 - bit[4], bit[1], 1], other(1)),
+        sum_copy(at, source, quad_ref.at[far, bit[1], :, cols], other(1))
+        for at, source, far, cols in (
+            (10, gate_landed.at[bit[4], beside], bit[4], early),
+            (11, up_last.at[bit[4], beside], bit[4], late),
+            (12, gate_crossed.at[beside], 1 - bit[4], early),
+            (13, up_crossed.at[beside], 1 - bit[4], late),
+        )
     ]
-    sum_copies = (
-        [down_cross, output_cross, gate_low, up_low, down_high, up_high, output_low, output_high]
-        + quad_far
-        + quad_near
-    )
-
     def first_send(at, target_ref, stage, copy):
         for one in firsts[at]:
             one.wait()
         add_to(target_ref, stage)
         copy.start()
 
+    def down_first():
+        first_send(0, down_away, wide_stage, down_cross)
+        firsts[1].append(load(2, part_of(output_kept, 0, 1 - here), wide_stage))
+
     def own_half(at, kept, met, axis, flag, stage_a, stage_b, copy, target_ref):
         loads = (
             load(2 * at, part_of(kept, axis, flag), stage_a),
@@ -1466,28 +1462,30 @@
         add_to(target_ref, stage_a, stage_b)
 
     def down_sum():
+        down_cross.wait_send()
         own_half(
-            0, down_kept, down_met, 0, here, wide_stage.at[0], wide_stage.at[1], down_cross,
-            down_landed,
+            0, down_kept, down_met, 1, bit[2], wide_stage, down_away, down_cross, down_landed
         )
         down_high.start()
 
     def output_sum():
+        output_cross.wait_send()
         own_half(
-            1, output_kept, output_met, 0, here, wide_stage.at[0], wide_stage.at[1], output_cross,
+            1, output_kept, output_met, 0, here, wide_stage, output_away, output_cross,
             output_landed,
         )
         output_low.start()
 
     def gate_sum():
         own_half(
-            2, gate_kept, gate_met, 1, bit[2], narrow_stage.at[0, 0], narrow_stage.at[1, 0],
+            2, gate_kept, gate_met, 1, bit[2], gate_stage.at[0], gate_stage.at[1],
             gate_low, gate_landed,
         )
 
     def up_sum():
+        up_low.wait_send()
         own_half(
-            3, up_kept, up_met, 2, bit[2], narrow_stage.at[0], narrow_stage.at[1], up_low,
+            3, up_kept, up_met, 0, here, up_stage, up_away, up_low,
             up_landed,
         )
         up_high.start()
@@ -1502,16 +1500,16 @@
         add_to(up_last, up_landed.at[bit[8]])
         for one in quad_far + quad_near[:2]:
             one.start()
-        quad_ref[bit[4], bit[1], 0] = gate_landed[bit[4], bit[1]]
-        quad_ref[bit[4], bit[1], 1] = up_last[bit[4], bit[1]]
+        quad_ref[bit[4], bit[1], :, early] = gate_landed[bit[4], bit[1]]
+        quad_ref[bit[4], bit[1], :, late] = up_last[bit[4], bit[1]]
 
     def quad_pass():
         for one in quad_far:
             one.wait_recv()
         for one in quad_near[2:]:
             one.start()
-        for kind in range(2):
-            quad_ref[1 - bit[4], bit[1], kind] = crossed[kind, bit[1]]
+        quad_ref[1 - bit[4], bit[1], :, early] = gate_crossed[bit[1]]
+        quad_ref[1 - bit[4], bit[1], :, late] = up_crossed[bit[1]]
 
     def last_sums():
         down_high.wait_recv()
@@ -1545,7 +1543,7 @@
             dst_ref=landed.at[offset, part],
             send_sem=send_sem.at[2 * offset + part],
             recv_sem=recv_sem.at[2 * offset + part],
-            device_id=other(link_of(offset, part, reps, 0)),
+            device_id=other(link_of(offset, part, SCATTER_LINKS)),
             device_id_type=MESH_IDS,
         )
 
@@ -1560,7 +1558,7 @@
         sources = [
             later
             for later in range(1, reps)
-            if later - link_of(later, part, reps, 0) == offset
+            if later - link_of(later, part, SCATTER_LINKS) == offset
         ]
         for later in sources:
             copies[later, part].wait_recv()
@@ -1639,10 +1637,10 @@
             weight_step(weights.pop(0))
 
     firsts_by = {
-        "down": lambda: first_send(0, down_away, wide_stage.at[0], down_cross),
-        "out": lambda: first_send(1, output_away, wide_stage.at[1], output_cross),
-        "gate": lambda: first_send(2, gate_away, narrow_stage.at[1, 0], gate_low),
-        "up": lambda: first_send(3, up_away, narrow_stage.at[0], up_low),
+        "down": down_first,
+        "out": lambda: first_send(1, output_away, wide_stage, output_cross),
+        "gate": lambda: first_send(2, gate_away, gate_stage.at[0], gate_low),
+        "up": lambda: first_send(3, up_away, up_stage, up_low),
     }
     sums_by = {
         "down": down_sum,
@@ -1694,7 +1692,8 @@
         one.wait()
     for one in quad_near:
         one.wait_recv()
-    for one in [half_copy] + sum_copies:
+    half_copy.wait_send()
+    for one in [gate_low, down_high, up_high, output_low, output_high] + quad_far + quad_near:
         one.wait_send()
     for (offset, part), one in copies.items():
         if offset % 2 == 0 or (offset == 1 and part == 0):
@@ -1707,18 +1706,18 @@
     row_count = rows // 2
     half = width // 2
     own_rows = half // reps
-    own_width = width // 2
     vmem = pl.BlockSpec(memory_space=pltpu.VMEM)
     anywhere = pl.BlockSpec(memory_space=pl.ANY)
     low, full = jnp.bfloat16, jnp.float32
     wide = (2, 2, own_rows, width)
-    slim = (2, 2, 2, own_rows, own_width)
+    thin = (2, 2, own_rows, sums[0].shape[-1])
+    slim = (2, 2, 2, own_rows, sums[2].shape[-1])
     return pl.pallas_call(
         scatter_kernel,
         out_shape=(
             jax.ShapeDtypeStruct((rows, width), low),
             jax.ShapeDtypeStruct((reps, own_rows, columns), low),
-            jax.ShapeDtypeStruct(slim, low),
+            jax.ShapeDtypeStruct((2, 2, own_rows, width), low),
             jax.ShapeDtypeStruct(wide[1:], full),
             jax.ShapeDtypeStruct(wide[2:], full),
         ),
@@ -1735,8 +1734,8 @@
             pltpu.VMEM((columns, half), low),
             pltpu.VMEM((columns, half), low),
             pltpu.VMEM((reps, own_rows, columns), low),
-            pltpu.VMEM(slim[1:], low),
-            pltpu.VMEM(slim[1:], low),
+            pltpu.VMEM(thin, low),
+            pltpu.VMEM(thin, low),
             pltpu.VMEM(slim, low),
             pltpu.VMEM(slim, low),
             pltpu.VMEM(slim[1:], low),
@@ -1747,9 +1746,11 @@
             pltpu.VMEM(wide, low),
             pltpu.VMEM(wide[1:], low),
             pltpu.VMEM(wide[2:], low),
-            pltpu.VMEM((2,) + slim, low),
-            pltpu.VMEM((2,) + wide, low),
-            pltpu.VMEM(slim[1:], low),
+            pltpu.VMEM((2,) + thin, low),
+            pltpu.VMEM(slim, low),
+            pltpu.VMEM(wide, low),
+            pltpu.VMEM(thin[1:], low),
+            pltpu.VMEM(slim[2:], low),
             pltpu.SemaphoreType.DMA((reps,)),
             pltpu.SemaphoreType.DMA((2 * reps,)),
             pltpu.SemaphoreType.DMA((2 * reps,)),
@@ -1780,16 +1781,20 @@
     output_own,
     output_part,
     output_beside,
-    gate_in,
+    gate_own,
+    gate_met,
+    gate_beside,
     up_own,
     up_other,
-    down_own,
+    down_first,
+    down_second,
+    down_other,
     block_ref,
     grad_ref,
     back_ref,
     gate_ref,
-    up_kept,
-    up_sent,
+    late_kept,
+    late_sent,
     down_kept,
     down_sent,
     output_kept,
@@ -1821,6 +1826,7 @@
     back_send,
     back_recv,
     piece_sem,
+    late_sem,
     place_sem,
     core_send,
     core_recv,
@@ -1835,23 +1841,35 @@
     quarter = half // 4
     own_width = w_out.shape[0]
 
+    low = (there // 2) % 2
+    up_rows = up_other.shape[0]
+
+    def in_cut(part, first):
+        cut = pl.ds(pl.multiple_of(part * up_rows, up_rows), up_rows)
+        return w_in.at[1 - here, cut, pl.ds(first, own_width)]
+
     loads = [
         pltpu.make_async_copy(output_own, w_output.at[here], load_sem.at[0]),
-        pltpu.make_async_copy(gate_in, w_in.at[:, :, pl.ds(0, own_width)], load_sem.at[1]),
+        pltpu.make_async_copy(gate_own, w_in.at[here, :, pl.ds(0, own_width)], load_sem.at[1]),
+        pltpu.make_async_copy(gate_met, in_cut(low, 0), load_sem.at[11]),
+        pltpu.make_async_copy(gate_beside, in_cut(1 - low, 0), load_sem.at[12]),
         pltpu.make_async_copy(
             up_own, w_in.at[here, :, pl.ds(own_width, own_width)], load_sem.at[2]
         ),
-        pltpu.make_async_copy(
-            up_other, w_in.at[1 - here, :, pl.ds(own_width, own_width)], load_sem.at[3]
-        ),
+        pltpu.make_async_copy(up_other, in_cut(low, own_width), load_sem.at[3]),
     ]
     own_part = own_width // 2
 
-    def down_cut(grp):
-        return pl.ds(pl.multiple_of(grp * own_part, own_part), own_part)
+    early_rows = down_first.shape[0]
+    late_rows = own_part - early_rows
+
+    def down_cut(grp, first, count):
+        return w_out.at[pl.ds(pl.multiple_of(grp * own_part + first, LANES), count)]
 
     loads += [
-        pltpu.make_async_copy(down_own, w_out.at[down_cut(here)], load_sem.at[4]),
+        pltpu.make_async_copy(down_first, down_cut(here, 0, early_rows), load_sem.at[4]),
+        pltpu.make_async_copy(down_second, down_cut(here, early_rows, late_rows), load_sem.at[9]),
+        pltpu.make_async_copy(down_other, down_cut(1 - here, 0, early_rows), load_sem.at[10]),
         pltpu.make_async_copy(out_rows.at[pl.ds(0, row_count)], out_ref.at[0, 0], load_sem.at[5]),
         pltpu.make_async_copy(
             out_rows.at[pl.ds(row_count, row_count)], out_ref.at[1, 0], load_sem.at[6]
@@ -1937,17 +1955,19 @@
     output_near = [
         copy(at, piece, output_cut(part), sibling) for at, (piece, part) in enumerate(output_pieces)
     ]
-    down_far = copy(2, down_own, w_out.at[down_cut(here)], facing)
+    down_far = copy(2, down_second, down_cut(here, early_rows, late_rows), facing)
+    up_beside = copy(26, up_other, in_cut(low, own_width), (here, flipped(there, 2)))
     out_near = [
         copy(3 + part, out_rows.at[rows_of(part)], out_ref.at[part, 1], sibling) for part in parts
     ]
     out_on = [
         copy(5 + part, out_across.at[rows_of(part)], out_ref.at[part, 3], sibling) for part in parts
     ]
-    for one in output_near + out_near + out_on + [down_far]:
+    for one in output_near + out_near + out_on + [down_far, up_beside]:
         one.start()
     returned[here, there] = heads_ref[here * heads + there]
 
+    early_width = gate_ref.shape[1]
     mid_near = [copy(7 + at, mid_ref.at[at, 0], mid_ref.at[at, 1], sibling) for at in parts]
     mid_far = [copy(9 + at, mid_ref.at[at, 0], mid_ref.at[at, 2], across) for at in parts]
     mid_on = [copy(11 + at, mid_ref.at[at, 2], mid_ref.at[at, 3], sibling) for at in parts]
@@ -1969,20 +1989,28 @@
     down_over = [
         copy(23 + at, down_own_ref.at[1, at], down_far_landed.at[at], across) for at in parts
     ]
-    gate_cross = copy(25, w_in.at[1 - here, :, pl.ds(0, own_width)], gate_ref, facing)
-    up_cut = pl.ds(own_width, own_width)
+    gate_cross = copy(25, w_in.at[1 - here, :, pl.ds(0, early_width)], gate_ref, facing)
+    late_cut = pl.ds(early_width, 2 * own_width - early_width)
+    late_block = late_kept.shape[1]
+
+    def late_rows_of(at, bit):
+        return pl.ds(pl.multiple_of((2 * at + bit) * late_block, late_block), late_block)
+
     up_outs = [
-        pltpu.make_async_copy(w_in.at[here, :, up_cut], up_kept, load_sem.at[0]),
-        pltpu.make_async_copy(w_in.at[1 - here, :, up_cut], up_sent, load_sem.at[1]),
+        pltpu.make_async_copy(
+            w_in.at[at // 4, late_rows_of(at % 4, bit), late_cut], target_ref.at[at], late_sem.at[2 * at + kind]
+        )
+        for at in range(8)
+        for kind, (target_ref, bit) in enumerate(((late_kept, low), (late_sent, 1 - low)))
     ]
-    low = (there // 2) % 2
-    down_outs = []
-    for at in range(own_width // (2 * LANES)):
-        for kind, (target_ref, bit) in enumerate(((down_kept, low), (down_sent, 1 - low))):
-            cut = pl.ds(pl.multiple_of((2 * at + bit) * LANES, LANES), LANES)
-            down_outs.append(
-                pltpu.make_async_copy(w_out.at[cut], target_ref.at[at], piece_sem.at[2 * at + kind])
-            )
+    down_outs = [
+        pltpu.make_async_copy(
+            w_out.at[pl.ds(pl.multiple_of(grp * own_part, own_part), own_part)],
+            target_ref,
+            piece_sem.at[kind],
+        )
+        for kind, (target_ref, grp) in enumerate(((down_kept, here), (down_sent, 1 - here)))
+    ]
 
     for one in heads_copies:
         one.wait()
@@ -2023,6 +2051,7 @@
         mid_near[part].start()
     for one in loads[3:]:
         one.wait()
+    up_beside.wait_recv()
     narrow_tile = 256
     per_half = own_part // narrow_tile
     every = (0, 1)
@@ -2229,23 +2258,14 @@
     gate_cross.start()
     down(1, 0)
     finish(0)
-    down(1, 1)
-    finish(1)
-    back_ref[here * heads + there] = returned[here, there]
-    for part in parts:
-        down_meet(1, part)
-        down_over[part].start()
     in_grads(here)
     for one in up_outs:
         one.start()
     for one in mid_near + mid_far + mid_on:
         one.wait_send()
     pl.semaphore_signal(free_sem, inc=1, device_id=sibling, device_id_type=MESH_IDS)
-    for part in parts:
-        down(0, part)
-    lax.fori_loop(0, own_width // narrow_tile, down_rows, 0)
-    for one in down_outs:
-        one.start()
+    finish(1)
+    back_ref[here * heads + there] = returned[here, there]
 
     for at in range(2):
 
@@ -2291,13 +2311,22 @@
             )
         )
         core_copies[-1].start()
+    down(1, 1)
+    for part in parts:
+        down_meet(1, part)
+        down_over[part].start()
+    for part in parts:
+        down(0, part)
+    lax.fori_loop(0, own_width // narrow_tile, down_rows, 0)
+    for one in down_outs:
+        one.start()
     gate_cross.wait()
 
     def add_gate(at, unused):
         cut = pl.ds(pl.multiple_of(at * tile, tile), tile)
         gate_ref[cut, :] = (
             gate_ref[cut, :].astype(jnp.float32)
-            + w_in[here, cut, pl.ds(0, own_width)].astype(jnp.float32)
+            + w_in[here, cut, pl.ds(0, early_width)].astype(jnp.float32)
         ).astype(jnp.bfloat16)
         return unused
 
@@ -2343,18 +2372,19 @@
         one.wait()
     for one in back_copies:
         one.wait()
-    for one in grad_far + out_near + out_on + down_over + [down_far]:
+    for one in grad_far + out_near + out_on + down_over + [down_far, up_beside]:
         one.wait_send()
     for one in list(down_near.values()) + output_near + core_copies:
         one.wait_send()
 
 
-def mlp(heads, tokens, gain, out_rows, out_across, output_parts, in_parts, down_own):
+def mlp(heads, tokens, gain, out_rows, out_across, output_parts, in_parts, down_parts):
     count, row_count, _ = heads.shape
     groups, reps = lax.axis_size("grp"), lax.axis_size("rep")
     rows, width = tokens.shape
     half = width // 2
-    own_width = in_parts[0].shape[2]
+    own_width = in_parts[0].shape[1]
+    early_width = own_width // 2
     vmem = pl.BlockSpec(memory_space=pltpu.VMEM)
     anywhere = pl.BlockSpec(memory_space=pl.ANY)
     low, full = jnp.bfloat16, jnp.float32
@@ -2365,15 +2395,15 @@
             jax.ShapeDtypeStruct((rows, width), low),
             jax.ShapeDtypeStruct((rows, width), full),
             jax.ShapeDtypeStruct((count, row_count, LANES), low),
-            jax.ShapeDtypeStruct((half, own_width), low),
-            jax.ShapeDtypeStruct((half, own_width), low),
-            jax.ShapeDtypeStruct((half, own_width), low),
-            jax.ShapeDtypeStruct((own_width // (2 * LANES), LANES, width), low),
-            jax.ShapeDtypeStruct((own_width // (2 * LANES), LANES, width), low),
+            jax.ShapeDtypeStruct((half, early_width), low),
+            jax.ShapeDtypeStruct((8, half // 8, 2 * own_width - early_width), low),
+            jax.ShapeDtypeStruct((8, half // 8, 2 * own_width - early_width), low),
+            jax.ShapeDtypeStruct((own_width // 2, width), low),
+            jax.ShapeDtypeStruct((own_width // 2, width), low),
             jax.ShapeDtypeStruct((reps // 2, half // reps, width), low),
             jax.ShapeDtypeStruct((reps // 2, half // reps, width), low),
         ),
-        in_specs=[vmem] * 3 + [anywhere] * 9,
+        in_specs=[vmem] * 3 + [anywhere] * 13,
         out_specs=(vmem,) * 4 + (anywhere,) * 6,
         scratch_shapes=[
             pltpu.VMEM((rows, width), full),
@@ -2394,15 +2424,16 @@
             pltpu.VMEM((2, row_count, width), low),
             pltpu.VMEM((2, row_count, width), low),
             pltpu.VMEM((2, 2, row_count, width), low),
-            pltpu.SemaphoreType.DMA((9,)),
+            pltpu.SemaphoreType.DMA((13,)),
             pltpu.SemaphoreType.DMA((2,)),
-            pltpu.SemaphoreType.DMA((26,)),
-            pltpu.SemaphoreType.DMA((26,)),
+            pltpu.SemaphoreType.DMA((27,)),
+            pltpu.SemaphoreType.DMA((27,)),
             others,
             others,
             others,
             others,
-            pltpu.SemaphoreType.DMA((own_width // LANES,)),
+            pltpu.SemaphoreType.DMA((2,)),
+            pltpu.SemaphoreType.DMA((16,)),
             pltpu.SemaphoreType.DMA((reps,)),
             pltpu.SemaphoreType.DMA((reps,)),
             pltpu.SemaphoreType.DMA((reps,)),
@@ -2415,7 +2446,7 @@
             flops=150 * 10**9, bytes_accessed=150 << 20, transcendentals=0
         ),
         name="mlp",
-    )(heads, tokens, gain, out_rows, out_across, *output_parts, *in_parts, down_own)
+    )(heads, tokens, gain, out_rows, out_across, *output_parts, *in_parts, *down_parts)
 
 
 def after_kernel(*refs):
@@ -2460,9 +2491,12 @@
         gathered_rows,
         qkv,
         w_heads,
-        gate_in,
+        gate_own,
+        gate_met,
         up_own,
-        down_own,
+        up_piece,
+        down_first,
+        down_second,
         output_part,
         out_own,
         gains,
@@ -2482,7 +2516,8 @@
     gain_two = gains[:, 1].reshape(width).astype(jnp.float32)
 
     output_parts = (w_output, output_part, swap(output_part, 0, 2))
-    in_parts = (gate_in, up_own, swap(up_own, 1, 0))
+    in_parts = (gate_own, gate_met, swap(gate_met, 0, 2), up_own, swap(up_piece, 1, 0))
+    down_parts = (down_first, down_second, swap(down_first, 1, 0))
 
     attended, out_heads, log_sum, query, key, value = attend(lengths, qkv)
     (
@@ -2490,8 +2525,8 @@
         grad_mixed,
         grad_heads,
         gate_part,
-        up_kept,
-        up_sent,
+        late_kept,
+        late_sent,
         down_kept,
         down_sent,
         output_kept,
@@ -2504,22 +2539,22 @@
         swap(out_own, 0, 4),
         output_parts,
         in_parts,
-        down_own,
+        down_parts,
     )
 
     own_rows = width // (groups * reps)
-    by_owner = (2, 2, 2, 2, own_rows, own_width)
+    by_owner = (2, 2, 2, 2, own_rows, -1)
     gate_part = gate_part.reshape(by_owner)
     high_bit = there // 8 % 2
     gate_kept = pick(gate_part, high_bit, 0)
     sums = (
         swap(pick(gate_part, 1 - high_bit, 0), 0, 8),
-        swap(up_sent, 1, 0),
-        swap(down_sent, 0, 2),
+        swap(late_sent, 0, 2),
+        swap(down_sent, 1, 0),
         swap(output_sent, 0, 4),
     )
     back = attend_back(lengths, query, key, value, out_heads, log_sum, grad_heads)
-    gate_met, up_met, down_met, output_met = after(sums, back)
+    gate_met, late_met, down_met, output_met = after(sums, back)
     token_grad, heads_grad, quad_grad, down_grad, output_grad = scatter_heads(
         back.reshape(reps, groups * row_count, 3 * LANES),
         w_heads,
@@ -2530,16 +2565,16 @@
         (
             gate_kept,
             gate_met,
-            up_kept.reshape(by_owner),
-            up_met.reshape(by_owner),
+            late_kept.reshape(by_owner),
+            late_met.reshape(by_owner),
             down_kept.reshape(2, 2, 2, own_rows, width),
             down_met.reshape(2, 2, 2, own_rows, width),
             output_kept.reshape(2, 2, 2, own_rows, width),
             output_met.reshape(2, 2, 2, own_rows, width),
         ),
     )
-    pieces = quad_grad.reshape(2, 2, 2, own_rows, groups, 2, 2, LANES)
-    pieces = pieces.transpose(2, 3, 4, 5, 0, 6, 1, 7).reshape(2, own_rows, hidden_width)
+    pieces = quad_grad.reshape(2, 2, own_rows, 2, groups, 2, 2, LANES)
+    pieces = pieces.transpose(3, 2, 4, 5, 0, 6, 1, 7).reshape(2, own_rows, hidden_width)
     gate_grad, up_grad = pieces[0].astype(jnp.float32), pieces[1].astype(jnp.float32)
     heads_grad = (
         heads_grad.reshape(reps, own_rows, 3, LANES)

time: 598 us -> 585 us (0.978)
  Pallas kernels: 521 us -> 511 us
    pallas_call x1, Pallas kernels: 160 us -> 141 us  [mlp(): pl.pallas_call(mlp_kernel, out_shape=(jax.ShapeDtypeStruct((rows, width),...]
    pallas_call x1, Pallas kernels: 163 us -> 170 us  [scatter_heads(): pl.pallas_call(scatter_kernel, out_shape=(jax.ShapeDtypeStruct((rows, wid...]
    ppermute x7 -> x9, waiting for transfers between devices: 23.2 us -> 19.1 us  [swap(): return lax.ppermute(value, BOTH, pairs)]
  transfers between devices with their start and end apart: 7 -> 9, of which waited for: 2 -> 4; matrix products, arithmetic and copies ran while one was open for 0% -> 0% of each run, Pallas kernels for 15% -> 15%
where the time goes in v7:
time: 585 us; the launch traced here: 576 us
  Pallas kernels  511 us (87%)
  local copies, waits for them, and re-layouts  24.5 us (4%)
  waiting for transfers between devices  19.1 us (3%)
  other arithmetic  12.1 us (2%)
  starting transfers between devices  7.24 us (1%)
    pallas_call x1, Pallas kernels, scatter_heads(): pl.pallas_call(scatter_kernel, out_shape=(jax.ShapeDtypeStruct((rows, wid...  170 us
    pallas_call x1, Pallas kernels, mlp(): pl.pallas_call(mlp_kernel, out_shape=(jax.ShapeDtypeStruct((rows, width),...  141 us
    pallas_call x1, Pallas kernels, gather_heads(): pl.pallas_call(gather_kernel, out_shape=(jax.ShapeDtypeStruct((reps, 2 *...  112 us
    pallas_call x1, Pallas kernels, attend_back(): pl.pallas_call(attend_back_kernel, out_shape=jax.ShapeDtypeStruct((parts,...  51.2 us
    pallas_call x1, Pallas kernels, attend(): pl.pallas_call(attend_kernel, out_shape=(jax.ShapeDtypeStruct((parts, uni...  36.8 us
    ppermute x9, waiting for transfers between devices, swap(): return lax.ppermute(value, BOTH, pairs)  19.1 us
  transfers between devices with their start and end apart: 9, of which 4 were waited for; matrix products, arithmetic and copies ran while one was open for 0% of the time, Pallas kernels for 15%

profile of v7, /device:TPU:0, one launch (start us, length us, event | category | flops | bytes accessed | tf_op | source)
XLA Modules:
  0.0 575.7 jit_solution(8965245870342050525)
XLA Ops:
  0.6 0.7 broadcast_in_dim.22
  1.3 0.7 broadcast_in_dim.10
  2.0 0.1 pad.2.clone
  2.1 0.7 maximum_maximum_fusion.gain_ref
  2.8 112.1 %gather_heads.1 = (bf16[16,256,2048]{2,1,0:T(8,128)(2,1)}, bf16[32,128,384]{2,1,0:T(8,128)(2,1)}, bf16[2,1024,384]{2,1,0:T(8,128)(2,1)}, bf16[1024,1024]{1,0:T(8...) custom-call(bf16[2,128,2048]{2,1,0:T(8,128)(2,1)} %tokens_ref.1, ...), custom_call_target="tpu_custom_call" | custom-call | flops 8000000000 | bytes 262144000 | tf_op jit(solution)/shard_map/gather_heads/pallas_call | solution.py:1219
  115.0 0.6 collective-permute-start.1
  115.5 1.5 collective-permute-start.2
  117.0 1.5 collective-permute-start.3
  118.5 0.6 collective-permute-start.4
  119.1 36.8 %attend.1 = (bf16[32,128,128]{2,1,0:T(8,128)(2,1)}, f32[16,128,256]{2,1,0:T(8,128)}, f32[16,8,256]{2,1,0:T(8,128)}, bf16[16,256,128]{2,1,0:T(8,128)(2,1)}, bf16[...) custom-call(s32[2,4]{1,0:T(2,128)} %lengths_ref.3, bf16[32,128,384]{2,1,0:T(8,128)(2,1)} %get-tuple-element.48.qkv_ref), custom_call_target="tpu_custom_call" | custom-call | flops 20000000000 | bytes 16777216 | tf_op jit(solution)/shard_map/attend/pallas_call | solution.py:862
  155.9 1.4 slice_convert_fusion.2
  157.3 5.1 collective-permute-done.2.gate_beside
  162.4 1.5 collective-permute-done.4.down_other
  163.9 0.6 broadcast_in_dim.24.gain_ref
  164.5 141.1 %mlp.1 = (bf16[256,2048]{1,0:T(8,128)(2,1)}, f32[256,2048]{1,0:T(8,128)}, bf16[32,128,128]{2,1,0:T(8,128)(2,1)}, bf16[1024,512]{1,0:T(8,128)(2,1)}, bf16[8,128,1...) custom-call(bf16[32,128,128]{2,1,0:T(8,128)(2,1)} %get-tuple-element, ...), custom_call_target="tpu_custom_call" | custom-call | flops 149999992832 | bytes 157286400 | tf_op jit(solution)/shard_map/mlp/pallas_call | solution.py:2392
  305.6 2.1 dynamic-slice_bitcast_fusion
  307.7 0.9 collective-permute-start.6
  308.6 0.4 collective-permute-start.7
  309.1 1.7 collective-permute-start.8
  310.8 51.2 %attend_back.1.refs_4_ = bf16[32,128,384]{2,1,0:T(8,128)(2,1)} custom-call(s32[2,4]{1,0:T(2,128)} %lengths_ref.3, bf16[16,256,128]{2,1,0:T(8,128)(2,1)} %get-tuple-element.60.query_ref, bf16[16,256,128]{2,1,0:T(8,128)(2,1)} %get-tuple-element.61.key_ref, bf16[16,256,128]{2,1,0:T(8,128)(2,1)} %get-tuple-element.62.value_ref, ...), custom_call_target="tpu_custom_call" | custom-call | flops 49999998976 | bytes 16777216 | tf_op jit(solution)/shard_map/attend_back/pallas_call | solution.py:899
  362.0 1.3 copy-done.3
  363.3 3.4 collective-permute-done.8.refs_3_
  366.7 1.3 copy-done.4
  368.0 9.2 %collective-permute-done.6.refs_1_ = bf16[8,128,1536]{2,1,0:T(8,128)(2,1)S(1)} collective-permute-done((bf16[8,128,1536]{2,1,0:T(8,128)(2,1)}, bf16[8,128,1536]{2,1,0:T(8,128)(2,1)S(1)}, u32[]{:S(2)}, u32[]{:S(2)}) %collective-permute-start.6) | collective-permute-done | bytes 3145760 | tf_op jit(solution)/shard_map/ppermute | solution.py:927
  377.2 1.7 copy-done.2
  378.9 0.6 broadcast_in_dim.25.gain_ref
  379.5 170.2 %scatter_heads.1 = (bf16[256,2048]{1,0:T(8,128)(2,1)}, bf16[16,64,384]{2,1,0:T(8,128)(2,1)}, bf16[2,2,64,2048]{3,2,1,0:T(8,128)(2,1)}, f32[2,64,2048]{2,1,0:T(8,128)}, f32[64,2048]{1,0:T(8,128)}) custom-call(bf16[16,256,384]{2,1,0:T(8,128)(2,1)} %bitcast.42, bf16[2,1024,384]{2,1,0:T(8,128)(2,1)} %get-tuple-element.66.weight_ref, bf16[256,2048]{1,0:T(8,128)(2,1)} %bitcast.52, ...), custom_call_target="tpu_custom_call" | custom-call | flops 14000000000 | bytes 262144000 | tf_op jit(solution)/shard_map/scatter_heads/pallas_call | solution.py:1715
  549.7 2.4 reshape.117
  552.2 1.6 fusion
  553.8 1.1 copy.45
  554.9 1.1 copy.44
  556.0 1.1 copy.43
  557.1 0.7 reshape.111
  557.8 0.3 copy.59
  558.1 0.2 slice_convert_fusion
  558.3 0.8 copy.48
  559.1 0.8 reshape.116
  560.0 0.8 copy.47
  560.8 0.8 reshape.115
  561.6 2.6 multiply_reduce_fusion.4
  564.2 3.0 multiply_reduce_fusion.2
  567.2 1.6 multiply_reduce_fusion
  568.9 1.4 convert_divide_fusion
  570.3 1.3 convert_divide_fusion.1
  571.5 1.0 copy.68
  572.5 1.0 copy.69
  573.5 0.8 copy.70
  574.3 1.0 copy.71
  (32 shorter events, 0.1 us)
Async XLA Ops:
  114.9 42.4 %collective-permute-start = (bf16[256,2048]{1,0:T(8,128)(2,1)}, bf16[256,2048]{1,0:T(8,128)(2,1)S(1)}, u32[]{:S(2)}, u32[]{:S(2)}) collective-permute-start(bf16[256,2048]{1,0:T(8,128)(2,1)} %get-tuple-element.51), channel_id=1, source_target_pairs={{0,4},{1,5},{2,6},{3,7},{4,0},{5,1},{6,2},{7,3},{8,12},{9,13},{10,... | collective-permute-start | bytes 3145736 | tf_op jit(solution)/shard_map/ppermute | solution.py:927
  115.0 42.3 %collective-permute-start.1 = (bf16[256,2048]{1,0:T(8,128)(2,1)}, bf16[256,2048]{1,0:T(8,128)(2,1)S(1)}, u32[]{:S(2)}, u32[]{:S(2)}) collective-permute-start(bf16[256,2048]{1,0:T(8,128)(2,1)} %get-tuple-element.52.output_part), channel_id=1, source_target_pairs={{0,2},{1,3},{2,0},{3,1},{4,6},{5,7},{6,4},{7,5},{8,10},{9,11},{10,... | collective-permute-start | bytes 3145736 | tf_op jit(solution)/shard_map/ppermute | solution.py:927
  115.5 46.8 %collective-permute-start.2 = (bf16[512,1024]{1,0:T(8,128)(2,1)}, bf16[512,1024]{1,0:T(8,128)(2,1)}, u32[]{:S(2)}, u32[]{:S(2)}) collective-permute-start(bf16[512,1024]{1,0:T(8,128)(2,1)} %get-tuple-element.54.gate_met), channel_id=1, source_target_pairs={{0,2},{1,3},{2,0},{3,1},{4,6},{5,7},{6,4},{7,5},{8,10},{9,11},{10,... | collective-permute-start | bytes 3145736 | tf_op jit(solution)/shard_map/ppermute | solution.py:927
  117.0 45.3 %collective-permute-start.3 = (bf16[512,1024]{1,0:T(8,128)(2,1)}, bf16[512,1024]{1,0:T(8,128)(2,1)}, u32[]{:S(2)}, u32[]{:S(2)}) collective-permute-start(bf16[512,1024]{1,0:T(8,128)(2,1)} %get-tuple-element.56), channel_id=1, source_target_pairs={{0,16},{1,17},{2,18},{3,19},{4,20},{5,21},{6,22},{7,23},{8,24},{9,... | collective-permute-start | bytes 3145736 | tf_op jit(solution)/shard_map/ppermute | solution.py:927
  118.5 45.4 %collective-permute-start.4 = (bf16[256,2048]{1,0:T(8,128)(2,1)}, bf16[256,2048]{1,0:T(8,128)(2,1)}, u32[]{:S(2)}, u32[]{:S(2)}) collective-permute-start(bf16[256,2048]{1,0:T(8,128)(2,1)} %get-tuple-element.57.down_first), channel_id=1, source_target_pairs={{0,16},{1,17},{2,18},{3,19},{4,20},{5,21},{6,22},{7,23},{8,24},{9,... | collective-permute-start | bytes 3145736 | tf_op jit(solution)/shard_map/ppermute | solution.py:927
  157.3 7.2 %copy-start.11 = (bf16[256,2048]{1,0:T(8,128)(2,1)}, bf16[256,2048]{1,0:T(8,128)(2,1)S(1)}, u32[]{:S(2)}) copy-start(bf16[256,2048]{1,0:T(8,128)(2,1)S(1)} %collective-permute-done.out_across) | copy-start | bytes 3145732
  157.3 7.2 %copy-start.12 = (bf16[256,2048]{1,0:T(8,128)(2,1)}, bf16[256,2048]{1,0:T(8,128)(2,1)S(1)}, u32[]{:S(2)}) copy-start(bf16[256,2048]{1,0:T(8,128)(2,1)S(1)} %collective-permute-done.1.output_beside) | copy-start | bytes 3145732
  307.7 54.3 %collective-permute-start.5 = (bf16[2,2,2,64,512]{4,3,2,1,0:T(8,128)(2,1)S(1)}, bf16[2,2,2,64,512]{4,3,2,1,0:T(8,128)(2,1)}, u32[]{:S(2)}, u32[]{:S(2)}) collective-permute-start(bf16[2,2,2,64,512]{4,3,2,1,0:T(8,128)(2,1)S(1)} %get-tuple-element.96), channel_id=1, source_target_pairs={{0,8},{1,9},{2,10},{3,11},{4,12},{5,13},{6,14},{7,15},{8,0},{9,1},... | collective-permute-start | bytes 1572872 | tf_op jit(solution)/shard_map/ppermute | solution.py:927
  307.7 69.4 %collective-permute-start.6 = (bf16[8,128,1536]{2,1,0:T(8,128)(2,1)}, bf16[8,128,1536]{2,1,0:T(8,128)(2,1)S(1)}, u32[]{:S(2)}, u32[]{:S(2)}) collective-permute-start(bf16[8,128,1536]{2,1,0:T(8,128)(2,1)} %get-tuple-element.70), channel_id=1, source_target_pairs={{0,2},{1,3},{2,0},{3,1},{4,6},{5,7},{6,4},{7,5},{8,10},{9,11},{10,... | collective-permute-start | bytes 9437192 | tf_op jit(solution)/shard_map/ppermute | solution.py:927
  308.6 53.4 %collective-permute-start.7 = (bf16[512,2048]{1,0:T(8,128)(2,1)}, bf16[512,2048]{1,0:T(8,128)(2,1)S(1)}, u32[]{:S(2)}, u32[]{:S(2)}) collective-permute-start(bf16[512,2048]{1,0:T(8,128)(2,1)} %get-tuple-element.71), channel_id=1, source_target_pairs={{0,16},{1,17},{2,18},{3,19},{4,20},{5,21},{6,22},{7,23},{8,24},{9,... | collective-permute-start | bytes 6291464 | tf_op jit(solution)/shard_map/ppermute | solution.py:927
  309.1 57.6 %collective-permute-start.8 = (bf16[8,64,2048]{2,1,0:T(8,128)(2,1)}, bf16[8,64,2048]{2,1,0:T(8,128)(2,1)S(1)}, u32[]{:S(2)}, u32[]{:S(2)}) collective-permute-start(bf16[8,64,2048]{2,1,0:T(8,128)(2,1)} %get-tuple-element.72), channel_id=1, source_target_pairs={{0,4},{1,5},{2,6},{3,7},{4,0},{5,1},{6,2},{7,3},{8,12},{9,13},{10,... | collective-permute-start | bytes 6291464 | tf_op jit(solution)/shard_map/ppermute | solution.py:927
  362.0 16.9 %copy-start.10 = (f32[2,1,1024]{2,1,0:T(1,128)S(1)}, f32[2,1,1024]{2,1,0:T(1,128)}, u32[]{:S(2)}) copy-start(f32[2,1,1024]{2,1,0:T(1,128)} %get-tuple-element.98) | copy-start | bytes 24580
  362.0 1.3 copy-start.3
  366.7 1.3 copy-start.4
  377.2 1.7 copy-start.2
  552.2 4.9 copy-start.8
  560.0 7.3 %copy-start = (f32[64,4096]{1,0:T(8,128)}, f32[64,4096]{1,0:T(8,128)S(1)}, u32[]{:S(2)}) copy-start(f32[64,4096]{1,0:T(8,128)S(1)} %reshape.116) | copy-start | bytes 3145732
  561.6 7.2 %copy-start.1 = (f32[64,4096]{1,0:T(8,128)}, f32[64,4096]{1,0:T(8,128)S(1)}, u32[]{:S(2)}) copy-start(f32[64,4096]{1,0:T(8,128)S(1)} %reshape.115) | copy-start | bytes 3145732
  564.2 7.3 %copy-start.5 = (bf16[256,2048]{1,0:T(8,128)(2,1)S(1)}, bf16[256,2048]{1,0:T(8,128)(2,1)}, u32[]{:S(2)}) copy-start(bf16[256,2048]{1,0:T(8,128)(2,1)} %get-tuple-element.59) | copy-start | bytes 3145732
  567.2 5.3 copy-start.7
  567.2 6.2 %copy-start.9 = (f32[64,2048]{1,0:T(8,128)S(1)}, f32[64,2048]{1,0:T(8,128)}, u32[]{:S(2)}) copy-start(f32[64,2048]{1,0:T(8,128)} %get-tuple-element.121) | copy-start | bytes 1572868
  568.9 5.4 copy-start.6

commit v8 on v7

--- a/solution.py
+++ b/solution.py
@@ -1000,6 +1000,15 @@
     output_ref,
     out_away,
     gains,
+    qkv_at,
+    gate_own_at,
+    gate_met_at,
+    up_at,
+    up_piece_at,
+    down_first_at,
+    down_second_at,
+    output_at,
+    out_at,
     raw,
     normed,
     weight_sem,
@@ -1009,6 +1018,7 @@
     side_send,
     side_recv,
     stripe_sem,
+    leave_sem,
 ):
     here, there = lax.axis_index("grp"), lax.axis_index("rep")
     core = there % 2
@@ -1109,14 +1119,14 @@
         first = (grp * reps + 8 * high + 2 * low + place) * LANES
         return weight.at[:, pl.ds(pl.multiple_of(first, LANES), LANES)]
 
-    for weight, target_ref in ((w_gate, gate_own), (w_up, up_ref)):
+    for weight, target_ref in ((w_gate, gate_own_at), (w_up, up_at)):
         for at, stripe in enumerate(stripes):
             load(columns_of(weight, *stripe), target_ref.at[:, pl.ds(at * LANES, LANES)])
     for at, (grp, high, low) in enumerate(stripes[: len(stripes) // 2]):
         first = (8 * high + 2 * low + place) * LANES
         load(
             w_down.at[pl.ds(pl.multiple_of(first, LANES), LANES)],
-            (down_first, down_second)[at // 2].at[pl.ds(at % 2 * LANES, LANES)],
+            (down_first_at, down_second_at)[at // 2].at[pl.ds(at % 2 * LANES, LANES)],
         )
     piece_rows = up_piece.shape[0]
     low = (there // 2) % 2
@@ -1125,24 +1135,30 @@
             columns_of(w_up, *stripe).at[
                 pl.ds(pl.multiple_of(low * piece_rows, piece_rows), piece_rows)
             ],
-            up_piece.at[:, pl.ds(at * LANES, LANES)],
-        )
-    load(out_rows, out_away)
+            up_piece_at.at[:, pl.ds(at * LANES, LANES)],
+        )
+    load(out_rows, out_at)
     for one in stripe_loads:
         one.start()
     quarter = output_ref.shape[0]
     output_copy = side(
         2,
         w_output.at[pl.ds(pl.multiple_of((there % 4) * quarter, quarter), quarter)],
-        output_ref,
+        output_at,
     )
     output_copy.start()
     gate_copy = side(
-        3, gate_own.at[pl.ds(pl.multiple_of(low * piece_rows, piece_rows), piece_rows)], gate_met
+        3, gate_own_at.at[pl.ds(pl.multiple_of(low * piece_rows, piece_rows), piece_rows)], gate_met_at
     )
     for one in stripe_loads[: len(stripes)]:
         one.wait()
     gate_copy.start()
+
+    leaving = []
+
+    def leave(at, source, target_ref):
+        leaving.append(pltpu.make_async_copy(source, target_ref, leave_sem.at[at]))
+        leaving[-1].start()
 
     written = {}
     used = [None] * slots
@@ -1174,8 +1190,11 @@
         product = jnp.dot(
             normed[slot, :, :half], weight_ref[0], preferred_element_type=jnp.float32
         ) + jnp.dot(normed[slot, :, half:], weight_ref[1], preferred_element_type=jnp.float32)
-        qkv_ref[pl.ds(2 * offset, 2)] = product.astype(jnp.bfloat16).reshape(
+        qkv_at[pl.ds(2 * offset, 2)] = product.astype(jnp.bfloat16).reshape(
             2, row_count, 3 * LANES
+        )
+        leave(
+            offset, qkv_at.at[pl.ds(2 * offset, 2)], qkv_ref.at[pl.ds(2 * offset, 2)]
         )
 
     count = 0
@@ -1192,16 +1211,32 @@
                 copies[what[0], part].wait_recv()
         project(count, what[0])
         count += 1
+        if count == reps // 2:
+            for one in stripe_loads[len(stripes) :]:
+                one.wait()
+            for at, pair in enumerate(
+                (
+                    (gate_own_at, gate_own),
+                    (up_at, up_ref),
+                    (up_piece_at, up_piece),
+                    (down_first_at, down_first),
+                    (down_second_at, down_second),
+                    (out_at, out_away),
+                )
+            ):
+                leave(reps + at, *pair)
     for offset in used:
         written[offset].wait()
     for one in copies.values():
         one.wait_send()
     gain_copy.wait_send()
     weight_copy.wait_send()
-    for one in stripe_loads[len(stripes) :]:
+    output_copy.wait()
+    leave(reps + 6, output_at, output_ref)
+    gate_copy.wait()
+    leave(reps + 7, gate_met_at, gate_met)
+    for one in leaving:
         one.wait()
-    gate_copy.wait()
-    output_copy.wait()
 
 
 def gather_heads(
@@ -1233,8 +1268,17 @@
             jax.ShapeDtypeStruct((2, 16, half), jnp.bfloat16),
         ),
         in_specs=[vmem, vmem] + [anywhere] * 8,
-        out_specs=(anywhere,) + (vmem,) * 11,
+        out_specs=(anywhere, anywhere, vmem) + (anywhere,) * 8 + (vmem,),
         scratch_shapes=[
+            pltpu.VMEM((2 * reps, row_count, 3 * LANES), jnp.bfloat16),
+            pltpu.VMEM((half, own_width), jnp.bfloat16),
+            pltpu.VMEM((half // 2, own_width), jnp.bfloat16),
+            pltpu.VMEM((half, own_width), jnp.bfloat16),
+            pltpu.VMEM((half // 2, own_width), jnp.bfloat16),
+            pltpu.VMEM((own_width // 4, width), jnp.bfloat16),
+            pltpu.VMEM((own_width // 4, width), jnp.bfloat16),
+            pltpu.VMEM((half // 4, width), jnp.bfloat16),
+            pltpu.VMEM(out_rows.shape, jnp.bfloat16),
             pltpu.VMEM((reps, 2, row_count, width), jnp.bfloat16),
             pltpu.VMEM((4, 2 * row_count, width), jnp.bfloat16),
             pltpu.SemaphoreType.DMA((3,)),
@@ -1244,6 +1288,7 @@
             pltpu.SemaphoreType.DMA((4,)),
             pltpu.SemaphoreType.DMA((4,)),
             pltpu.SemaphoreType.DMA((reps // 2 * 7 // 2 + 1,)),
+            pltpu.SemaphoreType.DMA((reps + 8,)),
         ],
         compiler_params=pltpu.CompilerParams(
             vmem_limit_bytes=KERNEL_VMEM, collective_id=0, has_side_effects=True
@@ -1256,20 +1301,20 @@
 
 
 SCATTER_PLAN = (
-    ("first", "down"), ("first", "up"), ("rows", 5, 0), ("rows", 4, 0), ("rows", 15, 0),
-    ("rows", 15, 1), ("weights", 1), ("first", "gate"), ("rows", 14, 1), ("weights", 1),
-    ("rows", 7, 0), ("first", "out"), ("sum", "down"), ("rows", 3, 1), ("rows", 13, 1),
-    ("rows", 11, 0), ("rows", 6, 0), ("rows", 11, 1), ("rows", 5, 1), ("rows", 10, 1),
-    ("sum", "up"), ("weights", 2), ("rows", 9, 1), ("rows", 1, 1), ("weights", 1),
-    ("rows", 14, 0), ("weights", 1), ("rows", 12, 1), ("weights", 1), ("sum", "gate"),
-    ("weights", 2), ("rows", 10, 0), ("weights", 1), ("rows", 7, 1), ("sum", "out"),
-    ("rows", 13, 0), ("rows", 6, 1), ("weights", 1), ("rows", 3, 0), ("rows", 12, 0),
-    ("rows", 1, 0), ("rows", 9, 0), ("weights", 3), ("rows", 8, 1), ("sum", "quad"),
-    ("rows", 2, 1), ("rows", 2, 0), ("weights", 2), ("sum", "out next"), ("rows", 8, 0),
-    ("weights over",), ("rows", 4, 1), ("sum", "quad next"), ("weights out",), ("rows", 0, 1),
-    ("rows", 0, 0),
+    ("first", "down"), ("rows", 13, 0), ("rows", 15, 0), ("rows", 7, 0), ("first", "up"),
+    ("first", "gate"), ("rows", 7, 1), ("first", "out"), ("rows", 14, 0), ("rows", 5, 1),
+    ("rows", 12, 0), ("sum", "down"), ("rows", 11, 0), ("rows", 1, 0), ("weights", 2),
+    ("rows", 11, 1), ("rows", 15, 1), ("weights", 1), ("sum", "up"), ("rows", 14, 1),
+    ("weights", 1), ("rows", 6, 1), ("rows", 13, 1), ("rows", 10, 1), ("rows", 12, 1),
+    ("rows", 9, 0), ("rows", 10, 0), ("weights", 1), ("rows", 5, 0), ("weights", 1),
+    ("rows", 4, 1), ("rows", 3, 1), ("weights", 2), ("rows", 6, 0), ("rows", 9, 1),
+    ("sum", "gate"), ("weights", 1), ("sum", "out"), ("rows", 2, 1), ("rows", 8, 1),
+    ("rows", 3, 0), ("weights", 2), ("rows", 8, 0), ("weights", 1), ("rows", 2, 0),
+    ("weights", 2), ("rows", 1, 1), ("sum", "quad"), ("rows", 4, 0), ("weights", 2),
+    ("weights over",), ("sum", "out next"), ("rows", 0, 1), ("sum", "quad next"),
+    ("weights out",), ("rows", 0, 0),
 )
-SCATTER_LINKS = {(6, 0): 4}
+SCATTER_LINKS = {(14, 0): 4}
 
 
 def scatter_kernel(
@@ -1772,6 +1817,121 @@
     )(back, weights, tokens, mixed_grad, gain, normed, *sums)
 
 
+def finish_kernel(
+    pieces_ref,
+    quad_ref,
+    down_ref,
+    output_ref,
+    token_ref,
+    block_ref,
+    gains_ref,
+    w_query,
+    w_key,
+    w_value,
+    w_gate,
+    w_up,
+    query_out,
+    key_out,
+    value_out,
+    gate_out,
+    up_out,
+    sums_out,
+    down_out,
+    output_out,
+    token_out,
+    block_out,
+    own_in,
+    own_up,
+    own_sem,
+):
+    reps, own_rows, _ = pieces_ref.shape
+    width = query_out.shape[1]
+    there = lax.axis_index("rep")
+    own_cut = pl.ds(pl.multiple_of(there * own_rows, own_rows), own_rows)
+    loads = [
+        pltpu.make_async_copy(weight.at[own_cut], target_ref, own_sem.at[at])
+        for at, (weight, target_ref) in enumerate(
+            (
+                (w_query, own_in.at[0]),
+                (w_key, own_in.at[1]),
+                (w_value, own_in.at[2]),
+                (w_gate, own_up.at[0]),
+                (w_up, own_up.at[1]),
+            )
+        )
+    ]
+    for one in loads:
+        one.start()
+    token_out[...] = token_ref[...]
+    block_out[...] = block_ref[...]
+    output_out[...] = output_ref[...]
+    for half in range(2):
+        down_out[pl.ds(half * own_rows, own_rows), :] = down_ref[half]
+    for kind, target_ref in enumerate((query_out, key_out, value_out)):
+        for place in range(reps):
+            target_ref[:, place * LANES : (place + 1) * LANES] = pieces_ref[
+                place, :, kind * LANES : (kind + 1) * LANES
+            ].astype(jnp.float32)
+    for kind, target_ref in enumerate((gate_out, up_out)):
+        for at in range(reps // 2):
+            source = (kind * (reps // 2) + at) * LANES
+            for far in range(2):
+                for near in range(2):
+                    target = ((at // 2) * 8 + far * 4 + (at % 2) * 2 + near) * LANES
+                    target_ref[:, target : target + LANES] = quad_ref[
+                        far, near, :, source : source + LANES
+                    ].astype(jnp.float32)
+    for one in loads:
+        one.wait()
+
+    def rows_sum(pairs):
+        total = jnp.zeros((own_rows, 1), jnp.float32)
+        for grad, weight in pairs:
+            total = total + jnp.sum(grad[...] * weight.astype(jnp.float32), axis=1, keepdims=True)
+        return jnp.broadcast_to(total, (own_rows, LANES))
+
+    sums_out[0] = (
+        rows_sum(((query_out, own_in[0]), (key_out, own_in[1]), (value_out, own_in[2])))
+        / gains_ref[0]
+    )
+    sums_out[1] = rows_sum(((gate_out, own_up[0]), (up_out, own_up[1]))) / gains_ref[1]
+
+
+def finish(pieces, quad, down, output, token_grad, block_out, gains, owned):
+    reps, own_rows, _ = pieces.shape
+    rows, width = token_grad.shape
+    hidden_width = owned[3].shape[1]
+    vmem = pl.BlockSpec(memory_space=pltpu.VMEM)
+    anywhere = pl.BlockSpec(memory_space=pl.ANY)
+    low, full = jnp.bfloat16, jnp.float32
+    narrow_rows = jax.ShapeDtypeStruct((own_rows, width), full)
+    wide_rows = jax.ShapeDtypeStruct((own_rows, hidden_width), full)
+    return pl.pallas_call(
+        finish_kernel,
+        out_shape=(
+            narrow_rows,
+            narrow_rows,
+            narrow_rows,
+            wide_rows,
+            wide_rows,
+            jax.ShapeDtypeStruct((2, own_rows, LANES), full),
+            jax.ShapeDtypeStruct((2 * own_rows, width), full),
+            narrow_rows,
+            jax.ShapeDtypeStruct((rows, width), low),
+            jax.ShapeDtypeStruct((rows, width), low),
+        ),
+        in_specs=[vmem] * 7 + [anywhere] * 5,
+        out_specs=(vmem,) * 10,
+        scratch_shapes=[
+            pltpu.VMEM((3, own_rows, width), low),
+            pltpu.VMEM((2, own_rows, hidden_width), low),
+            pltpu.SemaphoreType.DMA((5,)),
+        ],
+        compiler_params=pltpu.CompilerParams(vmem_limit_bytes=KERNEL_VMEM),
+        name="finish",
+    )(pieces, quad, down, output, token_grad, block_out, gains, *owned)
+
+
 def mlp_kernel(
     heads_ref,
     tokens_ref,
@@ -1792,13 +1952,15 @@
     block_ref,
     grad_ref,
     back_ref,
-    gate_ref,
+    gate_kept,
+    gate_sent,
     late_kept,
     late_sent,
     down_kept,
     down_sent,
     output_kept,
     output_sent,
+    gate_ref,
     mixed_ref,
     down_own_ref,
     down_far_landed,
@@ -1827,6 +1989,7 @@
     back_recv,
     piece_sem,
     late_sem,
+    gate_sem,
     place_sem,
     core_send,
     core_recv,
@@ -2331,6 +2494,13 @@
         return unused
 
     lax.fori_loop(0, half // tile, add_gate, 0)
+    gate_outs = []
+    for kind, (target_ref, flag) in enumerate(
+        ((gate_kept, there // 8 % 2), (gate_sent, 1 - there // 8 % 2))
+    ):
+        cut = pl.ds(pl.multiple_of(flag * (half // 2), half // 2), half // 2)
+        gate_outs.append(pltpu.make_async_copy(gate_ref.at[cut], target_ref, gate_sem.at[kind]))
+        gate_outs[-1].start()
     far_bit = (there // 4) % 2
     output_outs = []
     for at in range(2 * stripes):
@@ -2368,7 +2538,7 @@
             return unused
 
         lax.fori_loop(0, row_count // tile, block_rows, 0)
-    for one in up_outs + down_outs + output_outs:
+    for one in up_outs + down_outs + output_outs + gate_outs:
         one.wait()
     for one in back_copies:
         one.wait()
@@ -2384,7 +2554,7 @@
     rows, width = tokens.shape
     half = width // 2
     own_width = in_parts[0].shape[1]
-    early_width = own_width // 2
+    early_width = own_width * 6 // 8
     vmem = pl.BlockSpec(memory_space=pltpu.VMEM)
     anywhere = pl.BlockSpec(memory_space=pl.ANY)
     low, full = jnp.bfloat16, jnp.float32
@@ -2395,7 +2565,8 @@
             jax.ShapeDtypeStruct((rows, width), low),
             jax.ShapeDtypeStruct((rows, width), full),
             jax.ShapeDtypeStruct((count, row_count, LANES), low),
-            jax.ShapeDtypeStruct((half, early_width), low),
+            jax.ShapeDtypeStruct((half // 2, early_width), low),
+            jax.ShapeDtypeStruct((half // 2, early_width), low),
             jax.ShapeDtypeStruct((8, half // 8, 2 * own_width - early_width), low),
             jax.ShapeDtypeStruct((8, half // 8, 2 * own_width - early_width), low),
             jax.ShapeDtypeStruct((own_width // 2, width), low),
@@ -2404,8 +2575,9 @@
             jax.ShapeDtypeStruct((reps // 2, half // reps, width), low),
         ),
         in_specs=[vmem] * 3 + [anywhere] * 13,
-        out_specs=(vmem,) * 4 + (anywhere,) * 6,
+        out_specs=(vmem,) * 3 + (anywhere,) * 8,
         scratch_shapes=[
+            pltpu.VMEM((half, early_width), low),
             pltpu.VMEM((rows, width), full),
             pltpu.VMEM((2, 2, row_count, width), low),
             pltpu.VMEM((2, row_count, width), low),
@@ -2434,6 +2606,7 @@
             others,
             pltpu.SemaphoreType.DMA((2,)),
             pltpu.SemaphoreType.DMA((16,)),
+            pltpu.SemaphoreType.DMA((2,)),
             pltpu.SemaphoreType.DMA((reps,)),
             pltpu.SemaphoreType.DMA((reps,)),
             pltpu.SemaphoreType.DMA((reps,)),
@@ -2524,7 +2697,8 @@
         block_out,
         grad_mixed,
         grad_heads,
-        gate_part,
+        gate_kept,
+        gate_sent,
         late_kept,
         late_sent,
         down_kept,
@@ -2544,11 +2718,8 @@
 
     own_rows = width // (groups * reps)
     by_owner = (2, 2, 2, 2, own_rows, -1)
-    gate_part = gate_part.reshape(by_owner)
-    high_bit = there // 8 % 2
-    gate_kept = pick(gate_part, high_bit, 0)
     sums = (
-        swap(pick(gate_part, 1 - high_bit, 0), 0, 8),
+        swap(gate_sent, 0, 8),
         swap(late_sent, 0, 2),
         swap(down_sent, 1, 0),
         swap(output_sent, 0, 4),
@@ -2563,8 +2734,8 @@
         jnp.broadcast_to(gain_one[None], (8, width)),
         gathered_rows,
         (
-            gate_kept,
-            gate_met,
+            gate_kept.reshape(by_owner[1:]),
+            gate_met.reshape(by_owner[1:]),
             late_kept.reshape(by_owner),
             late_met.reshape(by_owner),
             down_kept.reshape(2, 2, 2, own_rows, width),
@@ -2573,42 +2744,45 @@
             output_met.reshape(2, 2, 2, own_rows, width),
         ),
     )
-    pieces = quad_grad.reshape(2, 2, own_rows, 2, groups, 2, 2, LANES)
-    pieces = pieces.transpose(3, 2, 4, 5, 0, 6, 1, 7).reshape(2, own_rows, hidden_width)
-    gate_grad, up_grad = pieces[0].astype(jnp.float32), pieces[1].astype(jnp.float32)
-    heads_grad = (
-        heads_grad.reshape(reps, own_rows, 3, LANES)
-        .transpose(2, 1, 0, 3)
-        .reshape(3, own_rows, width)
-        .astype(jnp.float32)
-    )
-
-    def own_part(value):
-        return lax.dynamic_slice_in_dim(value, there * own_rows, own_rows, axis=0).astype(
-            jnp.float32
-        )
-
-    attn_gain_grad = (
-        jnp.sum(own_part(w_query) * heads_grad[0], axis=1)
-        + jnp.sum(own_part(w_key) * heads_grad[1], axis=1)
-        + jnp.sum(own_part(w_value) * heads_grad[2], axis=1)
-    ) / own_part(attn_gain)
-    mlp_gain_grad = (
-        jnp.sum(own_part(w_gate) * gate_grad, axis=1) + jnp.sum(own_part(w_up) * up_grad, axis=1)
-    ) / own_part(mlp_gain)
+
+    def own_gain(gain):
+        own = lax.dynamic_slice_in_dim(gain, there * own_rows, own_rows, axis=0)
+        return jnp.broadcast_to(own.astype(jnp.float32)[:, None], (own_rows, LANES))
+
+    (
+        query_grad,
+        key_grad,
+        value_grad,
+        gate_grad,
+        up_grad,
+        gain_sums,
+        down_grad,
+        output_grad,
+        token_grad,
+        block_out,
+    ) = finish(
+        heads_grad,
+        quad_grad,
+        down_grad,
+        output_grad,
+        token_grad,
+        block_out,
+        jnp.stack([own_gain(attn_gain), own_gain(mlp_gain)], axis=0),
+        (w_query, w_key, w_value, w_gate, w_up),
+    )
     block_shape = tokens.shape
     return (
         block_out.reshape(block_shape),
         token_grad.reshape(block_shape),
-        attn_gain_grad,
-        heads_grad[0],
-        heads_grad[1],
-        heads_grad[2],
+        gain_sums[0, :, 0],
+        query_grad,
+        key_grad,
+        value_grad,
         output_grad,
-        mlp_gain_grad,
+        gain_sums[1, :, 0],
         gate_grad,
         up_grad,
-        down_grad.reshape(2 * own_rows, width),
+        down_grad,
     )
 
 

time: 585 us -> 554 us (0.947)
  local copies, waits for them, and re-layouts: 24.5 us -> 8.34 us
  other arithmetic: 12.1 us -> 3.55 us
    reduce_sum x3 -> x0, other arithmetic: 7.18 us -> none  [the longest x1 2.97 us: heads_body(): jnp.sum(own_part(w_value) * heads_grad[2], axis=1)]
    pallas_call x0 -> x1, Pallas kernels: none -> 7.1 us  [finish(): pl.pallas_call(finish_kernel, out_shape=(narrow_rows, narrow_rows, narrow...]
  transfers between devices with their start and end apart: 9 -> 9, of which waited for: 4 -> 3; matrix products, arithmetic and copies ran while one was open for 0% -> 1% of each run, Pallas kernels for 15% -> 16%
where the time goes in v8:
time: 554 us; the launch traced here: 545 us
  Pallas kernels  508 us (92%)
  waiting for transfers between devices  16.3 us (3%)
  local copies, waits for them, and re-layouts  8.34 us (2%)
  starting transfers between devices  7.3 us (1%)
    pallas_call x1, Pallas kernels, scatter_heads(): pl.pallas_call(scatter_kernel, out_shape=(jax.ShapeDtypeStruct((rows, wid...  165 us
    pallas_call x1, Pallas kernels, mlp(): pl.pallas_call(mlp_kernel, out_shape=(jax.ShapeDtypeStruct((rows, width),...  141 us
    pallas_call x1, Pallas kernels, gather_heads(): pl.pallas_call(gather_kernel, out_shape=(jax.ShapeDtypeStruct((reps, 2 *...  109 us
    pallas_call x1, Pallas kernels, attend_back(): pl.pallas_call(attend_back_kernel, out_shape=jax.ShapeDtypeStruct((parts,...  49.9 us
    pallas_call x1, Pallas kernels, attend(): pl.pallas_call(attend_kernel, out_shape=(jax.ShapeDtypeStruct((parts, uni...  35.9 us
    ppermute x9, waiting for transfers between devices, swap(): return lax.ppermute(value, BOTH, pairs)  16.3 us
  transfers between devices with their start and end apart: 9, of which 3 were waited for; matrix products, arithmetic and copies ran while one was open for 1% of the time, Pallas kernels for 16%

profile of v8, /device:TPU:0, one launch (start us, length us, event | category | flops | bytes accessed | tf_op | source)
XLA Modules:
  0.0 544.8 jit_solution(3020864107943823508)
XLA Ops:
  0.6 0.7 broadcast_in_dim.11
  1.3 0.7 broadcast_in_dim.10
  2.0 0.1 pad.4.clone
  2.1 0.7 maximum_maximum_fusion.gain_ref
  2.8 109.3 %gather_heads.1 = (bf16[16,256,2048]{2,1,0:T(8,128)(2,1)}, bf16[32,128,384]{2,1,0:T(8,128)(2,1)}, bf16[2,1024,384]{2,1,0:T(8,128)(2,1)}, bf16[1024,1024]{1,0:T(8...) custom-call(bf16[2,128,2048]{2,1,0:T(8,128)(2,1)} %tokens_ref.1, ...), custom_call_target="tpu_custom_call" | custom-call | flops 8000000000 | bytes 262144000 | tf_op jit(solution)/shard_map/gather_heads/pallas_call | solution.py:1254
  112.1 0.1 collective-permute-start
  112.2 0.6 collective-permute-start.1
  112.8 1.5 collective-permute-start.2
  114.3 1.5 collective-permute-start.3
  115.7 0.6 collective-permute-start.4
  116.3 35.9 %attend.1 = (bf16[32,128,128]{2,1,0:T(8,128)(2,1)}, f32[16,128,256]{2,1,0:T(8,128)}, f32[16,8,256]{2,1,0:T(8,128)}, bf16[16,256,128]{2,1,0:T(8,128)(2,1)}, bf16[...) custom-call(s32[2,4]{1,0:T(2,128)} %lengths_ref.3, bf16[32,128,384]{2,1,0:T(8,128)(2,1)} %get-tuple-element.59.qkv_ref), custom_call_target="tpu_custom_call" | custom-call | flops 20000000000 | bytes 16777216 | tf_op jit(solution)/shard_map/attend/pallas_call | solution.py:862
  152.2 0.8 dynamic-slice_convert_fusion
  153.0 0.1 stack_broadcast_in_dim.5
  153.1 0.1 stack_broadcast_in_dim.4
  153.1 0.6 pad_maximum_fusion.gains_ref
  153.8 1.4 slice_convert_fusion
  155.2 0.0 collective-permute-done.out_across
  155.2 0.0 copy-start.5
  155.2 0.0 collective-permute-done.1.output_beside
  155.2 0.0 copy-start.6
  155.2 4.4 collective-permute-done.2.gate_beside
  159.6 0.0 collective-permute-done.3.up_other
  159.6 1.5 collective-permute-done.4.down_other
  161.1 0.6 broadcast_in_dim.26.gain_ref
  161.7 0.0 copy-done.6
  161.7 0.0 copy-done.5
  161.7 140.8 %mlp.1 = (bf16[256,2048]{1,0:T(8,128)(2,1)}, f32[256,2048]{1,0:T(8,128)}, bf16[32,128,128]{2,1,0:T(8,128)(2,1)}, bf16[512,768]{1,0:T(8,128)(2,1)}, bf16[512,768]...) custom-call(bf16[32,128,128]{2,1,0:T(8,128)(2,1)} %get-tuple-element, ...), custom_call_target="tpu_custom_call" | custom-call | flops 149999992832 | bytes 157286400 | tf_op jit(solution)/shard_map/mlp/pallas_call | solution.py:2562
  302.5 0.1 collective-permute-start.5
  302.6 1.0 collective-permute-start.6
  303.6 0.5 collective-permute-start.7
  304.0 1.6 collective-permute-start.8
  305.7 49.9 %attend_back.1.refs_4_ = bf16[32,128,384]{2,1,0:T(8,128)(2,1)} custom-call(s32[2,4]{1,0:T(2,128)} %lengths_ref.3, bf16[16,256,128]{2,1,0:T(8,128)(2,1)} %get-tuple-element.60.query_ref, bf16[16,256,128]{2,1,0:T(8,128)(2,1)} %get-tuple-element.61.key_ref, bf16[16,256,128]{2,1,0:T(8,128)(2,1)} %get-tuple-element.62.value_ref, ...), custom_call_target="tpu_custom_call" | custom-call | flops 49999998976 | bytes 16777216 | tf_op jit(solution)/shard_map/attend_back/pallas_call | solution.py:899
  355.5 0.0 copy-start.4
  355.6 0.0 collective-permute-done.5.refs_0_
  355.6 0.0 copy-start.3
  355.6 0.0 collective-permute-done.7.refs_2_
  355.6 0.0 copy-start.1
  355.6 1.3 copy-done.1
  356.9 10.5 %collective-permute-done.8.refs_3_ = bf16[8,64,2048]{2,1,0:T(8,128)(2,1)S(1)} collective-permute-done((bf16[8,64,2048]{2,1,0:T(8,128)(2,1)}, bf16[8,64,2048]{2,1,0:T(8,128)(2,1)S(1)}, u32[]{:S(2)}, u32[]{:S(2)}) %collective-permute-start.8) | collective-permute-done | bytes 2097184 | tf_op jit(solution)/shard_map/ppermute | solution.py:927
  367.3 1.3 copy-done.2
  368.6 0.0 collective-permute-done.6.refs_1_
  368.6 0.0 copy-done.3
  368.6 1.5 copy-done
  370.1 0.0 copy-done.4
  370.1 0.6 broadcast_in_dim.27.gain_ref
  370.7 165.0 %scatter_heads.1 = (bf16[256,2048]{1,0:T(8,128)(2,1)}, bf16[16,64,384]{2,1,0:T(8,128)(2,1)}, bf16[2,2,64,2048]{3,2,1,0:T(8,128)(2,1)}, f32[2,64,2048]{2,1,0:T(8,128)}, f32[64,2048]{1,0:T(8,128)}) custom-call(bf16[16,256,384]{2,1,0:T(8,128)(2,1)} %bitcast.15, bf16[2,1024,384]{2,1,0:T(8,128)(2,1)} %get-tuple-element.76.weight_ref, bf16[256,2048]{1,0:T(8,128)(2,1)} %bitcast.22, ...), custom_call_target="tpu_custom_call" | custom-call | flops 14000000000 | bytes 262144000 | tf_op jit(solution)/shard_map/scatter_heads/pallas_call | solution.py:1760
  535.8 7.1 %finish.1 = (f32[64,2048]{1,0:T(8,128)}, f32[64,2048]{1,0:T(8,128)}, f32[64,2048]{1,0:T(8,128)}, f32[64,4096]{1,0:T(8,128)}, f32[64,4096]{1,0:T(8,128)}, /*index...) custom-call(bf16[16,64,384]{2,1,0:T(8,128)(2,1)} %get-tuple-element., ...), custom_call_target="tpu_custom_call" | custom-call | tf_op jit(solution)/shard_map/finish/pallas_call | solution.py:1909
  542.9 1.4 slice_reduce_fusion
  (4 shorter events, 0.0 us)
Async XLA Ops:
  112.1 43.1 %collective-permute-start = (bf16[256,2048]{1,0:T(8,128)(2,1)}, bf16[256,2048]{1,0:T(8,128)(2,1)S(1)}, u32[]{:S(2)}, u32[]{:S(2)}) collective-permute-start(bf16[256,2048]{1,0:T(8,128)(2,1)} %get-tuple-element.67), channel_id=1, source_target_pairs={{0,4},{1,5},{2,6},{3,7},{4,0},{5,1},{6,2},{7,3},{8,12},{9,13},{10,... | collective-permute-start | bytes 3145736 | tf_op jit(solution)/shard_map/ppermute | solution.py:927
  112.2 43.0 %collective-permute-start.1 = (bf16[256,2048]{1,0:T(8,128)(2,1)}, bf16[256,2048]{1,0:T(8,128)(2,1)S(1)}, u32[]{:S(2)}, u32[]{:S(2)}) collective-permute-start(bf16[256,2048]{1,0:T(8,128)(2,1)} %get-tuple-element.68.output_part), channel_id=1, source_target_pairs={{0,2},{1,3},{2,0},{3,1},{4,6},{5,7},{6,4},{7,5},{8,10},{9,11},{10,... | collective-permute-start | bytes 3145736 | tf_op jit(solution)/shard_map/ppermute | solution.py:927
  112.8 46.8 %collective-permute-start.2 = (bf16[512,1024]{1,0:T(8,128)(2,1)}, bf16[512,1024]{1,0:T(8,128)(2,1)}, u32[]{:S(2)}, u32[]{:S(2)}) collective-permute-start(bf16[512,1024]{1,0:T(8,128)(2,1)} %get-tuple-element.70.gate_met), channel_id=1, source_target_pairs={{0,2},{1,3},{2,0},{3,1},{4,6},{5,7},{6,4},{7,5},{8,10},{9,11},{10,... | collective-permute-start | bytes 3145736 | tf_op jit(solution)/shard_map/ppermute | solution.py:927
  114.3 45.3 %collective-permute-start.3 = (bf16[512,1024]{1,0:T(8,128)(2,1)}, bf16[512,1024]{1,0:T(8,128)(2,1)}, u32[]{:S(2)}, u32[]{:S(2)}) collective-permute-start(bf16[512,1024]{1,0:T(8,128)(2,1)} %get-tuple-element.72), channel_id=1, source_target_pairs={{0,16},{1,17},{2,18},{3,19},{4,20},{5,21},{6,22},{7,23},{8,24},{9,... | collective-permute-start | bytes 3145736 | tf_op jit(solution)/shard_map/ppermute | solution.py:927
  115.7 45.4 %collective-permute-start.4 = (bf16[256,2048]{1,0:T(8,128)(2,1)}, bf16[256,2048]{1,0:T(8,128)(2,1)}, u32[]{:S(2)}, u32[]{:S(2)}) collective-permute-start(bf16[256,2048]{1,0:T(8,128)(2,1)} %get-tuple-element.73.down_first), channel_id=1, source_target_pairs={{0,16},{1,17},{2,18},{3,19},{4,20},{5,21},{6,22},{7,23},{8,24},{9,... | collective-permute-start | bytes 3145736 | tf_op jit(solution)/shard_map/ppermute | solution.py:927
  155.2 6.5 %copy-start.5 = (bf16[256,2048]{1,0:T(8,128)(2,1)}, bf16[256,2048]{1,0:T(8,128)(2,1)S(1)}, u32[]{:S(2)}) copy-start(bf16[256,2048]{1,0:T(8,128)(2,1)S(1)} %collective-permute-done.out_across) | copy-start | bytes 3145732
  155.2 6.5 %copy-start.6 = (bf16[256,2048]{1,0:T(8,128)(2,1)}, bf16[256,2048]{1,0:T(8,128)(2,1)S(1)}, u32[]{:S(2)}) copy-start(bf16[256,2048]{1,0:T(8,128)(2,1)S(1)} %collective-permute-done.1.output_beside) | copy-start | bytes 3145732
  302.5 53.0 %collective-permute-start.5 = (bf16[512,768]{1,0:T(8,128)(2,1)}, bf16[512,768]{1,0:T(8,128)(2,1)S(1)}, u32[]{:S(2)}, u32[]{:S(2)}) collective-permute-start(bf16[512,768]{1,0:T(8,128)(2,1)} %get-tuple-element.80), channel_id=1, source_target_pairs={{0,8},{1,9},{2,10},{3,11},{4,12},{5,13},{6,14},{7,15},{8,0},{9,1},... | collective-permute-start | bytes 2359304 | tf_op jit(solution)/shard_map/ppermute | solution.py:927
  302.6 66.0 %collective-permute-start.6 = (bf16[8,128,1280]{2,1,0:T(8,128)(2,1)}, bf16[8,128,1280]{2,1,0:T(8,128)(2,1)S(1)}, u32[]{:S(2)}, u32[]{:S(2)}) collective-permute-start(bf16[8,128,1280]{2,1,0:T(8,128)(2,1)} %get-tuple-element.81), channel_id=1, source_target_pairs={{0,2},{1,3},{2,0},{3,1},{4,6},{5,7},{6,4},{7,5},{8,10},{9,11},{10,... | collective-permute-start | bytes 7864328 | tf_op jit(solution)/shard_map/ppermute | solution.py:927
  303.6 52.0 %collective-permute-start.7 = (bf16[512,2048]{1,0:T(8,128)(2,1)}, bf16[512,2048]{1,0:T(8,128)(2,1)S(1)}, u32[]{:S(2)}, u32[]{:S(2)}) collective-permute-start(bf16[512,2048]{1,0:T(8,128)(2,1)} %get-tuple-element.82), channel_id=1, source_target_pairs={{0,16},{1,17},{2,18},{3,19},{4,20},{5,21},{6,22},{7,23},{8,24},{9,... | collective-permute-start | bytes 6291464 | tf_op jit(solution)/shard_map/ppermute | solution.py:927
  304.0 63.3 %collective-permute-start.8 = (bf16[8,64,2048]{2,1,0:T(8,128)(2,1)}, bf16[8,64,2048]{2,1,0:T(8,128)(2,1)S(1)}, u32[]{:S(2)}, u32[]{:S(2)}) collective-permute-start(bf16[8,64,2048]{2,1,0:T(8,128)(2,1)} %get-tuple-element.83), channel_id=1, source_target_pairs={{0,4},{1,5},{2,6},{3,7},{4,0},{5,1},{6,2},{7,3},{8,12},{9,13},{10,... | collective-permute-start | bytes 6291464 | tf_op jit(solution)/shard_map/ppermute | solution.py:927
  355.5 14.6 %copy-start.4 = (f32[2,1,1024]{2,1,0:T(1,128)S(1)}, f32[2,1,1024]{2,1,0:T(1,128)}, u32[]{:S(2)}) copy-start(f32[2,1,1024]{2,1,0:T(1,128)} %get-tuple-element.109) | copy-start | bytes 24580
  355.6 13.1 %copy-start.3 = (bf16[512,768]{1,0:T(8,128)(2,1)}, bf16[512,768]{1,0:T(8,128)(2,1)S(1)}, u32[]{:S(2)}) copy-start(bf16[512,768]{1,0:T(8,128)(2,1)S(1)} %collective-permute-done.5.refs_0_) | copy-start | bytes 2359300
  355.6 1.3 copy-start.1
  367.3 1.3 copy-start.2
  368.6 1.5 copy-start
